TPU v7x, 32 devices: a whole 2x2x4 slice. The times are simulated.
32 devices in a mesh: strip: 4 (over x, core), sub: 8 (over z, y).
Axes of the slice: x: 2, y: 2, z: 4, core: 2. Of those that a mesh axis runs over, the one named last changes fastest.
Arguments:
- node_latents: bfloat16 [8192, 128], P(('strip', 'sub')), may hold values from -6 to 6
- edge_latents: bfloat16 [131072, 128], P(('strip', 'sub')), may hold values from -6 to 6
- senders: int32 [131072], P(('strip', 'sub')), may hold values from 0 to 8191, as said below
- receivers: int32 [131072], P(('strip', 'sub')), may hold values from 0 to 255
- edge_count: int32 [32], P(('strip', 'sub')), may hold values from 1024 to 4096, as said below
- w_edge_in: bfloat16 [384, 128], replicated, may hold values from -0.3125 to 0.3125
- w_edge_out: bfloat16 [128, 128], replicated, may hold values from -0.5 to 0.5
- w_node_in: bfloat16 [256, 128], replicated, may hold values from -0.375 to 0.375
- w_node_out: bfloat16 [128, 128], replicated, may hold values from -0.5 to 0.5
- node_cotangent: bfloat16 [8192, 128], P(('strip', 'sub')), may hold values from -6 to 6
- edge_cotangent: bfloat16 [131072, 128], P(('strip', 'sub')), may hold values from -6 to 6
Outputs:
- new_nodes: bfloat16 [8192, 128], P(('strip', 'sub'))
- new_edges: bfloat16 [131072, 128], P(('strip', 'sub'))
- node_grad: float32 [8192, 128], P(('strip', 'sub'))
- grad_edge_in: float32 [384, 128], replicated
- grad_edge_out: float32 [128, 128], replicated
- grad_node_in: float32 [256, 128], replicated
- grad_node_out: float32 [128, 128], replicated
Inputs may be any that keep to these rules, and one draw needn't show every extreme that they name: `senders`: devices are numbered strip * 8 + sub-block, each holding 256 consecutive particles and 4096 consecutive edge slots. The sender of an edge held by the device at strip i and sub-block j is a particle of a device at strip i - 1, i or i + 1 and sub-block j - 1, j or j + 1 (no wrap); if that device is not the edge's own, the sender is among its first 32 particles. A device's live edges are its first edge_count slots; some device is full.
All inputs are finite; a program needn't handle non-finite values.
Results may differ from a plain program's by a relative error of at most 0.012.
Values may be sent and summed in bfloat16 or wider, within the bound.
No kernel may reach another device: no remote copies, remote signals or barrier semaphores. Data moves between devices by JAX's collectives and lax.ppermute only.
A program may use at most 64 MiB of HBM per device.

v0:
```python
import math

import jax
import jax.numpy as jnp
from jax import lax
from jax.sharding import PartitionSpec as P

EPS = 1e-05


def padded_2(block, sides, width):
    for axis, dim in sides:
        count = lax.axis_size(axis)
        forward = [(i, i + 1) for i in range(count - 1)]
        backward = [(target, source) for source, target in forward]
        low = lax.ppermute(
            lax.slice_in_dim(block, block.shape[dim] - width, None, axis=dim), axis, forward
        )
        high = lax.ppermute(lax.slice_in_dim(block, 0, width, axis=dim), axis, backward)
        block = jnp.concatenate([low, block, high], axis=dim)
    return block


def shifted(value, axis, steps):
    count = lax.axis_size(axis)
    first, last = (max(0, -steps), min(count, count - steps))
    return lax.ppermute(value, axis, [(source, source + steps) for source in range(first, last)])


def norm_rows(values):
    centre = values - jnp.mean(values, axis=1, keepdims=True)
    scale = lax.rsqrt(jnp.mean(centre * centre, axis=1, keepdims=True) + EPS)
    return (centre * scale, scale)


def norm_back(normed, scale, upstream):
    first = jnp.mean(upstream, axis=1, keepdims=True)
    second = jnp.mean(upstream * normed, axis=1, keepdims=True)
    return scale * (upstream - first - normed * second)


def silu_grad(values):
    sig = jax.nn.sigmoid(values)
    return sig * (1.0 + values * (1.0 - sig))


def pick_rows(onehot, table):
    return jnp.dot(onehot, table, preferred_element_type=jnp.float32)


def pick_exact(onehot, table):
    return jnp.dot(
        onehot.astype(jnp.float32),
        table,
        precision=lax.Precision.HIGHEST,
        preferred_element_type=jnp.float32,
    )


def sum_rows(onehot, values):
    return jnp.dot(
        onehot.astype(jnp.float32).T,
        values,
        precision=lax.Precision.HIGHEST,
        preferred_element_type=jnp.float32,
    )


def shards(
    node_latents,
    edge_latents,
    senders,
    receivers,
    edge_count,
    w_edge_in,
    w_edge_out,
    w_node_in,
    w_node_out,
    node_cotangent,
    edge_cotangent,
):
    count_p = node_latents.shape[0]
    width = node_latents.shape[1]
    count_e = edge_latents.shape[0]
    border = count_p // 8
    subs_here = lax.axis_size("sub")
    my_strip = lax.axis_index("strip")
    my_sub = lax.axis_index("sub")
    rim_rows = node_latents[:border].reshape(1, 1, border, width)
    padded = padded_2(rim_rows, (("strip", 0), ("sub", 1)), 1)
    table = jnp.concatenate([node_latents, padded.reshape(9 * border, width)], axis=0)
    owner = senders // count_p
    within = senders % count_p
    is_local = owner == my_strip * subs_here + my_sub
    block = (owner // subs_here - my_strip + 1) * 3 + (owner % subs_here - my_sub + 1)
    send_index = jnp.where(
        is_local, within, count_p + block * border + jnp.minimum(within, border - 1)
    )
    valid = (jnp.arange(count_e, dtype=jnp.int32) < edge_count[0]).astype(jnp.float32)
    send_hot = (
        send_index[:, None] == jnp.arange(count_p + 9 * border, dtype=jnp.int32)[None, :]
    ).astype(jnp.bfloat16)
    recv_hot = (receivers[:, None] == jnp.arange(count_p, dtype=jnp.int32)[None, :]).astype(
        jnp.bfloat16
    )
    send_rows = pick_rows(send_hot, table).astype(jnp.bfloat16)
    recv_rows = pick_rows(recv_hot, node_latents).astype(jnp.bfloat16)
    stacked = jnp.concatenate([send_rows, recv_rows, edge_latents], axis=1)
    hidden_pre = jnp.dot(stacked, w_edge_in, preferred_element_type=jnp.float32)
    hidden = jax.nn.silu(hidden_pre).astype(jnp.bfloat16)
    outer = jnp.dot(hidden, w_edge_out, preferred_element_type=jnp.float32)
    normed, scale = norm_rows(outer)
    message = normed * valid[:, None]
    new_edges = (edge_latents.astype(jnp.float32) + message).astype(jnp.bfloat16)
    agg = sum_rows(recv_hot, message)
    joined = jnp.concatenate([node_latents, agg.astype(jnp.bfloat16)], axis=1)
    node_pre = jnp.dot(joined, w_node_in, preferred_element_type=jnp.float32)
    node_act = jax.nn.silu(node_pre).astype(jnp.bfloat16)
    node_outer = jnp.dot(node_act, w_node_out, preferred_element_type=jnp.float32)
    node_normed, node_scale = norm_rows(node_outer)
    new_nodes = (node_latents.astype(jnp.float32) + node_normed).astype(jnp.bfloat16)
    node_cot = node_cotangent.astype(jnp.float32)
    d_node_outer = norm_back(node_normed, node_scale, node_cot).astype(jnp.bfloat16)
    gn_out = jnp.dot(node_act.T, d_node_outer, preferred_element_type=jnp.float32)
    d_node_act = jnp.dot(d_node_outer, w_node_out.T, preferred_element_type=jnp.float32)
    d_node_pre = (d_node_act * silu_grad(node_pre)).astype(jnp.bfloat16)
    gn_in = jnp.dot(joined.T, d_node_pre, preferred_element_type=jnp.float32)
    d_joined = jnp.dot(d_node_pre, w_node_in.T, preferred_element_type=jnp.float32)
    upstream = edge_cotangent.astype(jnp.float32) + pick_exact(recv_hot, d_joined[:, width:])
    d_outer = norm_back(normed, scale, upstream * valid[:, None]).astype(jnp.bfloat16)
    ge_out = jnp.dot(hidden.T, d_outer, preferred_element_type=jnp.float32)
    d_hidden = jnp.dot(d_outer, w_edge_out.T, preferred_element_type=jnp.float32)
    d_pre = (d_hidden * silu_grad(hidden_pre)).astype(jnp.bfloat16)
    ge_in = jnp.dot(stacked.T, d_pre, preferred_element_type=jnp.float32)
    d_stacked = jnp.dot(d_pre, w_edge_in.T, preferred_element_type=jnp.float32)
    send_sums = sum_rows(send_hot, d_stacked[:, :width])
    owed = send_sums[count_p:].reshape(3, 3, border, width)
    local_grad = (
        node_cot
        + d_joined[:, :width]
        + sum_rows(recv_hot, d_stacked[:, width : 2 * width])
        + send_sums[:count_p]
    )
    column = (
        owed[:, 1]
        + shifted(owed[:, 0].astype(jnp.bfloat16), "sub", -1).astype(jnp.float32)
        + shifted(owed[:, 2].astype(jnp.bfloat16), "sub", 1).astype(jnp.float32)
    )
    returned = column[1] + shifted(column[0], "strip", -1) + shifted(column[2], "strip", 1)
    node_grad = local_grad.at[:border].add(returned)
    totals = lax.psum((ge_in, ge_out, gn_in, gn_out), ("strip", "sub"))
    factor = 1.0 / math.sqrt(count_e * lax.axis_size("strip") * subs_here)
    return (
        new_nodes,
        new_edges,
        node_grad,
        totals[0] * factor,
        totals[1] * factor,
        totals[2] * factor,
        totals[3] * factor,
    )


def solution(mesh):
    placed = (
        P(("strip", "sub"), None),
        P(("strip", "sub"), None),
        P(("strip", "sub")),
        P(("strip", "sub")),
        P(("strip", "sub")),
        P(),
        P(),
        P(),
        P(),
        P(("strip", "sub"), None),
        P(("strip", "sub"), None),
    )
    return jax.shard_map(
        shards,
        mesh=mesh,
        in_specs=placed,
        out_specs=(
            P(("strip", "sub"), None),
            P(("strip", "sub"), None),
            P(("strip", "sub"), None),
            P(),
            P(),
            P(),
            P(),
        ),
        check_vma=False,
    )
```

profile of v0, /device:TPU:0, one launch (start us, length us, event | category | flops | bytes accessed | tf_op | source)
XLA Modules:
  0.0 208.4 jit_solution(14302411649951955422)
XLA Ops:
  8.1 1.3 collective-permute-start.1
  9.4 3.0 %collective-permute-start = (bf16[1,1,32,128]{3,2,1,0:T(8,128)(2,1)S(1)}, bf16[1,1,32,128]{3,2,1,0:T(8,128)(2,1)S(1)}, u32[]{:S(2)}, u32[]{:S(2)}) collective-permute-start(bf16[1,1,32,128]{3,2,1,0:T(8,128)(2,1)S(1)} %slice_bitcast_fusion.6), channel_id=1, source_target_pairs={{0,8},{8,16},{16,24},{1,9},{9,17},{17,25},{2,10},{10,18},{18,26},{... | collective-permute-start | bytes 24584 | tf_op jit(solution)/shard_map/ppermute | solution.py:16
  12.4 2.9 %convolution_convert_fusion = bf16[4096,128]{0,1:T(8,128)(2,1)} fusion(bf16[256,128]{1,0:T(8,128)(2,1)} %param.13, s32[4096]{0:T(1024)} %param.16), kind=kOutput, calls=%fused_computation.8 | convolution fusion | flops 270008320 | bytes 1130496 | tf_op jit(solution)/shard_map/dot_general | solution.py:48
  16.7 1.3 collective-permute-start.3
  18.0 5.5 %collective-permute-start.2 = (bf16[3,1,32,128]{3,2,1,0:T(8,128)(2,1)S(1)}, bf16[3,1,32,128]{3,2,1,0:T(8,128)(2,1)S(1)}, u32[]{:S(2)}, u32[]{:S(2)}) collective-permute-start(bf16[3,1,32,128]{3,2,1,0:T(8,128)(2,1)S(1)} %pad_maximum_fusion.7), channel_id=1, source_target_pairs={{0,1},{1,2},{2,3},{3,4},{4,5},{5,6},{6,7},{8,9},{9,10},{10,11},{11... | collective-permute-start | bytes 73736 | tf_op jit(solution)/shard_map/ppermute | solution.py:16
  25.0 2.9 %fusion.4 = bf16[4096,128]{0,1:T(8,128)(2,1)S(1)} fusion(s32[4096]{0:T(1024)} %fusion.53, bf16[288,128]{1,0:T(8,128)(2,1)S(1)} %bitcast.50, bf16[256,128]{1,0:T(8,128)(2,1)S(1)} %copy-done.5), kind=kOutput, calls=%fused_computation.7 | convolution fusion | flops 573456384 | bytes 1204224 | tf_op jit(solution)/shard_map/dot_general | solution.py:48
  27.9 1.6 multiply_convert_fusion.1
  30.4 1.9 fusion.24
  33.4 2.6 %fusion.67 = (f32[4096]{0:T(1024)S(1)}, f32[4096]{0:T(1024)S(1)}, f32[4096,128]{0,1:T(8,128)S(1)}) fusion(f32[4096]{0:T(1024)S(1)} %add_rsqrt_fusion, f32[4096,128]{0,1:T(8,128)S(1)} %get-tuple-element.59, f32[4096]{0:T(1024)S(1)} %broadcast_multiply_fusion.6, f32[4096]{0:T(1024)S(1)} %fusion.61, f32[256,256]{1,0:T(8,128)S(1)} %fusion.70, ...), kind=kOutput, calls=%fused_computation.119 | convolution fusion | flops 1615847424 | bytes 5472256 | tf_op jit(solution)/shard_map/dot_general | solution.py:52
  36.8 1.1 fusion.72
  38.8 1.7 fusion.16
  40.5 1.0 fusion.71
  41.5 4.5 %fusion = f32[544,128]{1,0:T(8,128)S(1)} fusion(s32[4096]{0:T(1024)S(1)} %copy-done.11, f32[4096,384]{1,0:T(8,128)S(1)} %fusion.71), kind=kOutput, calls=%fused_computation.1 | convolution fusion | flops 3424780288 | bytes 2392064 | tf_op jit(solution)/shard_map/dot_general | solution.py:61
  46.6 1.3 collective-permute-start.4
  47.9 5.4 %collective-permute-start.5 = (bf16[3,32,128]{1,2,0:T(8,128)(2,1)S(1)}, bf16[3,32,128]{1,2,0:T(8,128)(2,1)S(1)}, u32[]{:S(2)}, u32[]{:S(2)}) collective-permute-start(bf16[3,32,128]{1,2,0:T(8,128)(2,1)S(1)} %get-tuple-element.51), channel_id=1, source_target_pairs={{0,1},{1,2},{2,3},{3,4},{4,5},{5,6},{6,7},{8,9},{9,10},{10,11},{11... | collective-permute-start | bytes 73736 | tf_op jit(solution)/shard_map/ppermute | solution.py:27
  53.4 4.0 %fusion.21 = f32[256,128]{0,1:T(8,128)S(1)} fusion(f32[256,128]{0,1:T(8,128)S(1)} %copy.60, f32[4096,384]{1,0:T(8,128)} %copy-done.1, s32[4096]{0:T(1024)S(1)} %copy-done.12, f32[256,128]{0,1:T(8,128)S(1)} %copy.59, bf16[256,128]{0,1:T(8,128)(2,1)S(1)} %copy.48), kind=kOutput, calls=%fused_computation.32 | convolution fusion | flops 1611792384 | bytes 2572288 | tf_op jit(solution)/shard_map/dot_general | solution.py:61
  58.2 1.3 collective-permute-start.6
  59.5 3.0 %collective-permute-start.7 = (f32[32,128]{0,1:T(8,128)S(1)}, f32[32,128]{0,1:T(8,128)S(1)}, u32[]{:S(2)}, u32[]{:S(2)}) collective-permute-start(f32[32,128]{0,1:T(8,128)S(1)} %get-tuple-element.53), channel_id=1, source_target_pairs={{0,8},{8,16},{16,24},{1,9},{9,17},{17,25},{2,10},{10,18},{18,26},{... | collective-permute-start | bytes 49160 | tf_op jit(solution)/shard_map/ppermute | solution.py:27
  64.1 1.3 copy.56
  66.9 128.5 %all-reduce.3.cloned.1.call-done = (f32[384,128]{1,0:T(8,128)}, f32[128,128]{1,0:T(8,128)}, f32[256,128]{1,0:T(8,128)}, f32[128,128]{1,0:T(8,128)}) async-done(((f32[384,128]{1,0:T(8,128)}, f32[128,128]{1,0:T(8,128)}, f32[256,128]{1,0:T(8,128)}, f32[128,128]{1,0:T(8,128)}), (f32[384,128]{1,0:T(8,128)}, f32[128,128]{1,0:T(8,128)}, f32[256,128]{1,0:T(8,128)}, ...) | async-done | bytes 458768 | tf_op jit(solution)/shard_map/psum | solution.py:151
  195.4 1.6 broadcast_multiply_fusion
  197.0 1.5 broadcast_multiply_fusion.3
  198.5 1.5 broadcast_multiply_fusion.2
  200.0 1.6 broadcast_multiply_fusion.1
  (82 shorter events, 10.8 us)
Async XLA Ops:
  7.2 20.7 %copy-start = (bf16[384,128]{1,0:T(8,128)(2,1)S(1)}, bf16[384,128]{1,0:T(8,128)(2,1)}, u32[]{:S(2)}) copy-start(bf16[384,128]{1,0:T(8,128)(2,1)} %param.18) | copy-start | bytes 294916
  7.2 16.3 %copy-start.5 = (bf16[256,128]{1,0:T(8,128)(2,1)S(1)}, bf16[256,128]{1,0:T(8,128)(2,1)}, u32[]{:S(2)}) copy-start(bf16[256,128]{1,0:T(8,128)(2,1)} %param.13) | copy-start | bytes 196612
  7.2 8.1 %copy-start.10 = (s32[4096]{0:T(1024)S(1)}, s32[4096]{0:T(1024)}, u32[]{:S(2)}) copy-start(s32[4096]{0:T(1024)} %param.15) | copy-start | bytes 49156
  7.2 16.4 %copy-start.6 = (bf16[256,128]{1,0:T(8,128)(2,1)S(1)}, bf16[256,128]{1,0:T(8,128)(2,1)}, u32[]{:S(2)}) copy-start(bf16[256,128]{1,0:T(8,128)(2,1)} %param.22) | copy-start | bytes 196612
  7.2 16.5 %copy-start.2 = (bf16[4096,128]{1,0:T(8,128)(2,1)S(1)}, bf16[4096,128]{1,0:T(8,128)(2,1)}, u32[]{:S(2)}) copy-start(bf16[4096,128]{1,0:T(8,128)(2,1)} %param.14) | copy-start | bytes 3145732
  7.2 188.2 %all-reduce.3.cloned.1.call-start = ((), (), s32[]{:S(2)}) async-start(), calls=%async_computation | async-start | bytes 917504 | tf_op jit(solution)/shard_map/psum | solution.py:151
  8.1 8.6 %collective-permute-start.1 = (bf16[1,1,32,128]{3,2,1,0:T(8,128)(2,1)S(1)}, bf16[1,1,32,128]{3,2,1,0:T(8,128)(2,1)S(1)}, u32[]{:S(2)}, u32[]{:S(2)}) collective-permute-start(bf16[1,1,32,128]{3,2,1,0:T(8,128)(2,1)S(1)} %slice_bitcast_fusion.6), channel_id=1, source_target_pairs={{8,0},{16,8},{24,16},{9,1},{17,9},{25,17},{10,2},{18,10},{26,18},{... | collective-permute-start | bytes 24584 | tf_op jit(solution)/shard_map/ppermute | solution.py:19
  9.4 7.3 %collective-permute-start = (bf16[1,1,32,128]{3,2,1,0:T(8,128)(2,1)S(1)}, bf16[1,1,32,128]{3,2,1,0:T(8,128)(2,1)S(1)}, u32[]{:S(2)}, u32[]{:S(2)}) collective-permute-start(bf16[1,1,32,128]{3,2,1,0:T(8,128)(2,1)S(1)} %slice_bitcast_fusion.6), channel_id=1, source_target_pairs={{0,8},{8,16},{16,24},{1,9},{9,17},{17,25},{2,10},{10,18},{18,26},{... | collective-permute-start | bytes 24584 | tf_op jit(solution)/shard_map/ppermute | solution.py:16
  15.3 9.0 %copy-start.3 = (bf16[4096,128]{1,0:T(8,128)(2,1)S(1)}, bf16[4096,128]{1,0:T(8,128)(2,1)}, u32[]{:S(2)}) copy-start(bf16[4096,128]{1,0:T(8,128)(2,1)} %param.23) | copy-start | bytes 3145732
  16.7 8.2 %collective-permute-start.3 = (bf16[3,1,32,128]{3,2,1,0:T(8,128)(2,1)S(1)}, bf16[3,1,32,128]{3,2,1,0:T(8,128)(2,1)S(1)}, u32[]{:S(2)}, u32[]{:S(2)}) collective-permute-start(bf16[3,1,32,128]{3,2,1,0:T(8,128)(2,1)S(1)} %pad_maximum_fusion.7), channel_id=1, source_target_pairs={{1,0},{2,1},{3,2},{4,3},{5,4},{6,5},{7,6},{9,8},{10,9},{11,10},{12... | collective-permute-start | bytes 73736 | tf_op jit(solution)/shard_map/ppermute | solution.py:19
  18.0 7.0 %collective-permute-start.2 = (bf16[3,1,32,128]{3,2,1,0:T(8,128)(2,1)S(1)}, bf16[3,1,32,128]{3,2,1,0:T(8,128)(2,1)S(1)}, u32[]{:S(2)}, u32[]{:S(2)}) collective-permute-start(bf16[3,1,32,128]{3,2,1,0:T(8,128)(2,1)S(1)} %pad_maximum_fusion.7), channel_id=1, source_target_pairs={{0,1},{1,2},{2,3},{3,4},{4,5},{5,6},{6,7},{8,9},{9,10},{10,11},{11... | collective-permute-start | bytes 73736 | tf_op jit(solution)/shard_map/ppermute | solution.py:16
  25.0 2.9 %copy-start.13 = (bf16[4096,128]{0,1:T(8,128)(2,1)S(1)}, bf16[4096,128]{0,1:T(8,128)(2,1)}, u32[]{:S(2)}) copy-start(bf16[4096,128]{0,1:T(8,128)(2,1)} %convolution_convert_fusion) | copy-start | bytes 3145732
  27.9 1.6 copy-start.8
  29.5 0.8 copy-start.12
  30.3 2.0 copy-start.7
  30.3 2.2 %copy-start.9 = (bf16[128,128]{1,0:T(8,128)(2,1)S(1)}, bf16[128,128]{1,0:T(8,128)(2,1)}, u32[]{:S(2)}) copy-start(bf16[128,128]{1,0:T(8,128)(2,1)} %param.21) | copy-start | bytes 98308
  33.4 2.6 %copy-start.4 = (f32[256,256]{1,0:T(8,128)}, f32[256,256]{1,0:T(8,128)S(1)}, u32[]{:S(2)}) copy-start(f32[256,256]{1,0:T(8,128)S(1)} %fusion.70) | copy-start | bytes 786436
  40.5 1.0 copy-start.11
  41.5 4.5 %copy-start.1 = (f32[4096,384]{1,0:T(8,128)}, f32[4096,384]{1,0:T(8,128)S(1)}, u32[]{:S(2)}) copy-start(f32[4096,384]{1,0:T(8,128)S(1)} %fusion.71) | copy-start | bytes 18874372
  41.5 4.6 %slice-start = ((f32[256,256]{1,0:T(8,128)}), f32[256,128]{1,0:T(8,128)S(1)}, s32[]{:S(2)}) async-start(f32[256,256]{1,0:T(8,128)} %copy-done.4), calls=%async_computation.1 | async-start | bytes 262144 | tf_op jit(solution)/shard_map/slice | solution.py:140
  46.6 11.6 %collective-permute-start.4 = (bf16[3,32,128]{1,2,0:T(8,128)(2,1)S(1)}, bf16[3,32,128]{1,2,0:T(8,128)(2,1)S(1)}, u32[]{:S(2)}, u32[]{:S(2)}) collective-permute-start(bf16[3,32,128]{1,2,0:T(8,128)(2,1)S(1)} %get-tuple-element.50), channel_id=1, source_target_pairs={{1,0},{2,1},{3,2},{4,3},{5,4},{6,5},{7,6},{9,8},{10,9},{11,10},{12... | collective-permute-start | bytes 73736 | tf_op jit(solution)/shard_map/ppermute | solution.py:27
  47.9 10.3 %collective-permute-start.5 = (bf16[3,32,128]{1,2,0:T(8,128)(2,1)S(1)}, bf16[3,32,128]{1,2,0:T(8,128)(2,1)S(1)}, u32[]{:S(2)}, u32[]{:S(2)}) collective-permute-start(bf16[3,32,128]{1,2,0:T(8,128)(2,1)S(1)} %get-tuple-element.51), channel_id=1, source_target_pairs={{0,1},{1,2},{2,3},{3,4},{4,5},{5,6},{6,7},{8,9},{9,10},{10,11},{11... | collective-permute-start | bytes 73736 | tf_op jit(solution)/shard_map/ppermute | solution.py:27
  58.2 7.2 %collective-permute-start.6 = (f32[32,128]{0,1:T(8,128)S(1)}, f32[32,128]{0,1:T(8,128)S(1)}, u32[]{:S(2)}, u32[]{:S(2)}) collective-permute-start(f32[32,128]{0,1:T(8,128)S(1)} %get-tuple-element.52), channel_id=1, source_target_pairs={{8,0},{16,8},{24,16},{9,1},{17,9},{25,17},{10,2},{18,10},{26,18},{... | collective-permute-start | bytes 49160 | tf_op jit(solution)/shard_map/ppermute | solution.py:27
  59.5 5.9 %collective-permute-start.7 = (f32[32,128]{0,1:T(8,128)S(1)}, f32[32,128]{0,1:T(8,128)S(1)}, u32[]{:S(2)}, u32[]{:S(2)}) collective-permute-start(f32[32,128]{0,1:T(8,128)S(1)} %get-tuple-element.53), channel_id=1, source_target_pairs={{0,8},{8,16},{16,24},{1,9},{9,17},{17,25},{2,10},{10,18},{18,26},{... | collective-permute-start | bytes 49160 | tf_op jit(solution)/shard_map/ppermute | solution.py:27
Sparse Core Ops, SparseCore 0:
  65.6 129.8 all-reduce.2
where the time goes:
time: 209 us; the launch traced here: 208 us
  waiting for transfers between devices  129 us (62%)
  matrix products  28.1 us (13%)
  starting transfers between devices  22.2 us (11%)
  between operations  15.3 us (7%)
  other arithmetic  8.02 us (4%)
  local copies, waits for them, and re-layouts  6.07 us (3%)
    psum x1, waiting for transfers between devices, shards(): totals = lax.psum((ge_in, ge_out, gn_in, gn_out), ('strip', 'sub'))  129 us
    ppermute x4, starting transfers between devices, shifted(): lax.ppermute(value, axis, [(source, source + steps) for source in range(f...  11.1 us
    dot_general x3, matrix products, sum_rows(): jnp.dot(onehot.astype(jnp.float32).T, values, precision=lax.Precision.HIG...  10.4 us
    ppermute x2, starting transfers between devices, padded_2(): lax.ppermute(lax.slice_in_dim(block, block.shape[dim] - width, None, axis...  8.53 us
    dot_general x2, matrix products, pick_rows(): return jnp.dot(onehot, table, preferred_element_type=jnp.float32)  5.81 us
    unnamed x37, local copies, waits for them, and re-layouts  4.33 us
  transfers between devices with their start and end apart: 9, of which 2 were waited for; matrix products, arithmetic and copies ran while one was open for 7% of the time, Pallas kernels for 0%

commit v1 on v0

--- a/solution.py
+++ b/solution.py
@@ -25,6 +25,23 @@
     count = lax.axis_size(axis)
     first, last = (max(0, -steps), min(count, count - steps))
     return lax.ppermute(value, axis, [(source, source + steps) for source in range(first, last)])
+
+
+def summed_over_devices(parts):
+    axes = ("strip", "sub")
+    count = lax.axis_size("strip") * lax.axis_size("sub")
+    width = parts[0].shape[1]
+    rows = [part.shape[0] for part in parts]
+    total = sum(rows)
+    share = -(-total // count)
+    packed = jnp.concatenate([part.astype(jnp.bfloat16) for part in parts], axis=0)
+    packed = jnp.pad(packed, ((0, share * count - total), (0, 0)))
+    mine = lax.all_to_all(packed.reshape(count, share, width), axes, 0, 0)
+    mine = jnp.sum(mine.astype(jnp.float32), axis=0).astype(jnp.bfloat16)
+    spread = jnp.broadcast_to(mine[None], (count, share, width))
+    whole = lax.all_to_all(spread, axes, 0, 0).reshape(count * share, width)
+    ends = [sum(rows[: i + 1]) for i in range(len(rows))]
+    return [whole[end - n : end].astype(jnp.float32) for end, n in zip(ends, rows)]
 
 
 def norm_rows(values):
@@ -87,7 +104,12 @@
     my_strip = lax.axis_index("strip")
     my_sub = lax.axis_index("sub")
     rim_rows = node_latents[:border].reshape(1, 1, border, width)
-    padded = padded_2(rim_rows, (("strip", 0), ("sub", 1)), 1)
+    strips_here = lax.axis_size("strip")
+    rims = jnp.broadcast_to(rim_rows[0], (strips_here * subs_here, border, width))
+    rims = lax.all_to_all(rims, ("strip", "sub"), 0, 0)
+    rims = rims.reshape(strips_here, subs_here, border, width)
+    rims = jnp.pad(rims, ((1, 1), (1, 1), (0, 0), (0, 0)))
+    padded = lax.dynamic_slice(rims, (my_strip, my_sub, 0, 0), (3, 3, border, width))
     table = jnp.concatenate([node_latents, padded.reshape(9 * border, width)], axis=0)
     owner = senders // count_p
     within = senders % count_p
@@ -148,7 +170,7 @@
     )
     returned = column[1] + shifted(column[0], "strip", -1) + shifted(column[2], "strip", 1)
     node_grad = local_grad.at[:border].add(returned)
-    totals = lax.psum((ge_in, ge_out, gn_in, gn_out), ("strip", "sub"))
+    totals = summed_over_devices((ge_in, ge_out, gn_in, gn_out))
     factor = 1.0 / math.sqrt(count_e * lax.axis_size("strip") * subs_here)
     return (
         new_nodes,

time: 209 us -> 78.7 us (0.38)
  waiting for transfers between devices: 129 us -> 11.1 us
  between operations: 15.3 us -> 1.91 us
  local copies, waits for them, and re-layouts: 6.07 us -> 12.3 us
  other arithmetic: 8.02 us -> 3.36 us
  matrix products: 28.1 us -> 25.4 us
    psum x1 -> x0, waiting for transfers between devices: 129 us -> none  [shards(): totals = lax.psum((ge_in, ge_out, gn_in, gn_out), ('strip', 'sub'))]
    all_to_all x0 -> x3, starting transfers between devices: none -> 13.9 us  [the longest x1 7.3 us: shards(): rims = lax.all_to_all(rims, ('strip', 'sub'), 0, 0)]
    ppermute x4 -> x0, starting transfers between devices: 11.1 us -> none  [the longest x2 8.53 us: padded_2(): lax.ppermute(lax.slice_in_dim(block, block.shape[dim] - width, None, axis...]
    all_to_all x0 -> x3, waiting for transfers between devices: none -> 11.1 us  [the longest x1 6.12 us: summed_over_devices(): mine = lax.all_to_all(packed.reshape(count, share, width), axes, 0, 0)]
    unnamed x37 -> x39, local copies, waits for them, and re-layouts: 4.33 us -> 8.24 us
  transfers between devices with their start and end apart: 9 -> 7, of which waited for: 2 -> 3; matrix products, arithmetic and copies ran while one was open for 7% -> 22% of each run, Pallas kernels for 0% -> 0%
where the time goes in v1:
time: 78.7 us; the launch traced here: 78.1 us
  matrix products  25.4 us (32%)
  starting transfers between devices  24 us (30%)
  local copies, waits for them, and re-layouts  12.3 us (16%)
  waiting for transfers between devices  11.1 us (14%)
  other arithmetic  3.36 us (4%)
  between operations  1.91 us (2%)
    dot_general x3, matrix products, sum_rows(): jnp.dot(onehot.astype(jnp.float32).T, values, precision=lax.Precision.HIG...  10.4 us
    ppermute x4, starting transfers between devices, shifted(): lax.ppermute(value, axis, [(source, source + steps) for source in range(f...  10.2 us
    unnamed x39, local copies, waits for them, and re-layouts  8.24 us
    all_to_all x1, starting transfers between devices, shards(): rims = lax.all_to_all(rims, ('strip', 'sub'), 0, 0)  7.3 us
    all_to_all x1, waiting for transfers between devices, summed_over_devices(): mine = lax.all_to_all(packed.reshape(count, share, width), axes, 0, 0)  6.12 us
    dot_general x2, matrix products, pick_rows(): return jnp.dot(onehot, table, preferred_element_type=jnp.float32)  5 us
    all_to_all x1, starting transfers between devices, summed_over_devices(): mine = lax.all_to_all(packed.reshape(count, share, width), axes, 0, 0)  3.99 us
    all_to_all x1, waiting for transfers between devices, summed_over_devices(): whole = lax.all_to_all(spread, axes, 0, 0).reshape(count * share, width)  3.18 us
  transfers between devices with their start and end apart: 7, of which 3 were waited for; matrix products, arithmetic and copies ran while one was open for 22% of the time, Pallas kernels for 0%

profile of v1, /device:TPU:0, one launch (start us, length us, event | category | flops | bytes accessed | tf_op | source)
XLA Modules:
  0.0 78.1 jit_solution(10650812496778107848)
XLA Ops:
  2.2 7.3 %all-to-all-start = ((bf16[32,32,128]{2,1,0:T(8,128)(2,1)}), bf16[32,32,128]{2,1,0:T(8,128)(2,1)S(1)}, u32[]{:S(2)}, u32[]{:S(2)}) async-start(bf16[32,32,128]{2,1,0:T(8,128)(2,1)} %broadcast_in_dim.4), calls=%async_computation | async-start | bytes 524288 | tf_op jit(solution)/shard_map/all_to_all | solution.py:109
  10.2 1.6 %copy.44 = bf16[256,128]{0,1:T(8,128)(2,1)} copy(bf16[256,128]{1,0:T(8,128)(2,1)} %param.13) | data formatting | bytes 131072 | tf_op args[0]
  11.7 1.6 %copy.48 = bf16[256,128]{0,1:T(8,128)(2,1)} copy(bf16[256,128]{1,0:T(8,128)(2,1)} %param.22) | data formatting | bytes 131072 | tf_op args[9]
  13.3 1.5 %copy.45 = bf16[4096,128]{0,1:T(8,128)(2,1)S(1)} copy(bf16[4096,128]{1,0:T(8,128)(2,1)} %param.14) | data formatting | bytes 2097152 | tf_op args[1]
  15.4 2.9 %convolution_convert_fusion = bf16[4096,128]{0,1:T(8,128)(2,1)} fusion(bf16[256,128]{1,0:T(8,128)(2,1)} %param.13, s32[4096]{0:T(1024)} %param.16), kind=kOutput, calls=%fused_computation.8 | convolution fusion | flops 270008320 | bytes 1130496 | tf_op jit(solution)/shard_map/dot_general | solution.py:65
  18.4 1.8 %all-to-all-done = bf16[32,32,128]{2,1,0:T(8,128)(2,1)S(1)} async-done(((bf16[32,32,128]{2,1,0:T(8,128)(2,1)}), bf16[32,32,128]{2,1,0:T(8,128)(2,1)S(1)}, u32[]{:S(2)}, u32[]{:S(2)}) %all-to-all-start) | async-done | bytes 262176 | tf_op jit(solution)/shard_map/all_to_all | solution.py:109
  20.2 2.1 %fusion.4 = bf16[4096,128]{0,1:T(8,128)(2,1)S(1)} fusion(s32[4096]{0:T(1024)S(1)} %fusion.53, bf16[288,128]{1,0:T(8,128)(2,1)S(1)} %bitcast.50, bf16[256,128]{1,0:T(8,128)(2,1)S(1)} %copy-done.6), kind=kOutput, calls=%fused_computation.7 | convolution fusion | flops 573456384 | bytes 1204224 | tf_op jit(solution)/shard_map/dot_general | solution.py:65
  22.3 1.6 %multiply_convert_fusion.1 = (bf16[4096,128]{1,0:T(8,128)(2,1)S(1)}, f32[4096,128]{1,0:T(8,128)S(1)}) fusion(bf16[384,128]{1,0:T(8,128)(2,1)S(1)} %copy-done, bf16[4096,128]{0,1:T(8,128)(2,1)S(1)} %copy.45, bf16[4096,128]{0,1:T(8,128)(2,1)S(1)} %copy-done.14, bf16[4096,128]{0,1:T(8,128)(2,1)S(1)} %fusion.4), kind=kOutput, calls=%fused_computation.21 | convolution fusion | flops 414711808 | bytes 6389760 | tf_op jit(solution)/shard_map/dot_general | solution.py:131
  24.8 1.9 %fusion.25 = bf16[256,128]{0,1:T(8,128)(2,1)S(1)} fusion(f32[4096,128]{0,1:T(8,128)S(1)} %get-tuple-element.57, s32[4096]{0:T(1024)S(1)} %copy-done.12, f32[4096]{0:T(1024)S(1)} %fusion.61, f32[4096]{0:T(1024)S(1)} %add_rsqrt_fusion, f32[4096]{0:T(1024)S(1)} %broadcast_multiply_fusion.2), kind=kOutput, calls=%fused_computation.35 | convolution fusion | flops 1613266944 | bytes 2228224 | tf_op jit(solution)/shard_map/dot_general | solution.py:78
  28.8 2.6 %fusion.67 = (f32[4096]{0:T(1024)S(1)}, f32[4096]{0:T(1024)S(1)}, f32[4096,128]{0,1:T(8,128)S(1)}) fusion(f32[4096]{0:T(1024)S(1)} %add_rsqrt_fusion, f32[4096,128]{0,1:T(8,128)S(1)} %get-tuple-element.57, f32[4096]{0:T(1024)S(1)} %broadcast_multiply_fusion.2, f32[4096]{0:T(1024)S(1)} %fusion.61, f32[256,256]{1,0:T(8,128)S(1)} %fusion.70, ...), kind=kOutput, calls=%fused_computation.121 | convolution fusion | flops 1615847424 | bytes 5472256 | tf_op jit(solution)/shard_map/dot_general | solution.py:69
  32.7 1.0 %fusion.3 = bf16[4096,128]{1,0:T(8,128)(2,1)S(1)} fusion(bf16[4096,128]{0,1:T(8,128)(2,1)S(1)} %get-tuple-element.44, bf16[128,128]{1,0:T(8,128)(2,1)S(1)} %copy-done.9, f32[4096,128]{1,0:T(8,128)S(1)} %get-tuple-element.55), kind=kOutput, calls=%fused_computation.6 | convolution fusion | flops 138936320 | bytes 4227072 | tf_op jit(solution)/shard_map/dot_general | solution.py:154
  33.6 1.0 %fusion.18 = bf16[384,128]{1,0:T(8,128)(2,1)S(1)} fusion(bf16[4096,128]{1,0:T(8,128)(2,1)S(1)} %fusion.3, bf16[4096,128]{0,1:T(8,128)(2,1)S(1)} %copy.45, bf16[4096,128]{0,1:T(8,128)(2,1)S(1)} %copy-done.14, bf16[4096,128]{0,1:T(8,128)(2,1)S(1)} %fusion.4), kind=kOutput, calls=%fused_computation.31 | convolution fusion | flops 412139520 | bytes 4292608 | tf_op jit(solution)/shard_map/dot_general | solution.py:156
  34.6 1.0 %fusion.71 = f32[4096,384]{1,0:T(8,128)S(1)} fusion(bf16[4096,128]{1,0:T(8,128)(2,1)S(1)} %fusion.3, bf16[384,128]{1,0:T(8,128)(2,1)S(1)} %copy-done), kind=kOutput, calls=%fused_computation.125 | convolution fusion | flops 402653184 | bytes 7438336 | tf_op jit(solution)/shard_map/dot_general | solution.py:157
  35.6 4.5 %fusion = f32[544,128]{1,0:T(8,128)S(1)} fusion(s32[4096]{0:T(1024)S(1)} %fusion.53, f32[4096,384]{1,0:T(8,128)S(1)} %fusion.71), kind=kOutput, calls=%fused_computation.1 | convolution fusion | flops 3424780288 | bytes 2392064 | tf_op jit(solution)/shard_map/dot_general | solution.py:78
  40.5 1.3 %collective-permute-start = (bf16[3,32,128]{1,2,0:T(8,128)(2,1)S(1)}, bf16[3,32,128]{1,2,0:T(8,128)(2,1)S(1)}, u32[]{:S(2)}, u32[]{:S(2)}) collective-permute-start(bf16[3,32,128]{1,2,0:T(8,128)(2,1)S(1)} %get-tuple-element.46), channel_id=1, source_target_pairs={{1,0},{2,1},{3,2},{4,3},{5,4},{6,5},{7,6},{9,8},{10,9},{11,10},{12... | collective-permute-start | bytes 73736 | tf_op jit(solution)/shard_map/ppermute | solution.py:27
  41.8 4.6 %collective-permute-start.1 = (bf16[3,32,128]{1,2,0:T(8,128)(2,1)S(1)}, bf16[3,32,128]{1,2,0:T(8,128)(2,1)S(1)}, u32[]{:S(2)}, u32[]{:S(2)}) collective-permute-start(bf16[3,32,128]{1,2,0:T(8,128)(2,1)S(1)} %get-tuple-element.47), channel_id=1, source_target_pairs={{0,1},{1,2},{2,3},{3,4},{4,5},{5,6},{6,7},{8,9},{9,10},{10,11},{11... | collective-permute-start | bytes 73736 | tf_op jit(solution)/shard_map/ppermute | solution.py:27
  47.3 4.0 %all-to-all-start.1 = ((bf16[32,28,128]{2,1,0:T(8,128)(2,1)}), bf16[32,28,128]{2,1,0:T(8,128)(2,1)S(1)}, u32[]{:S(2)}, u32[]{:S(2)}) async-start(bf16[32,28,128]{2,1,0:T(8,128)(2,1)} %reshape.109), calls=%async_computation.1 | async-start | bytes 524288 | tf_op jit(solution)/shard_map/all_to_all | solution.py:39
  51.5 1.3 %collective-permute-start.2 = (f32[32,128]{0,1:T(8,128)S(1)}, f32[32,128]{0,1:T(8,128)S(1)}, u32[]{:S(2)}, u32[]{:S(2)}) collective-permute-start(f32[32,128]{0,1:T(8,128)S(1)} %get-tuple-element.50), channel_id=1, source_target_pairs={{8,0},{16,8},{24,16},{9,1},{17,9},{25,17},{10,2},{18,10},{26,18},{... | collective-permute-start | bytes 49160 | tf_op jit(solution)/shard_map/ppermute | solution.py:27
  52.8 3.0 %collective-permute-start.3 = (f32[32,128]{0,1:T(8,128)S(1)}, f32[32,128]{0,1:T(8,128)S(1)}, u32[]{:S(2)}, u32[]{:S(2)}) collective-permute-start(f32[32,128]{0,1:T(8,128)S(1)} %get-tuple-element.51), channel_id=1, source_target_pairs={{0,8},{8,16},{16,24},{1,9},{9,17},{17,25},{2,10},{10,18},{18,26},{... | collective-permute-start | bytes 49160 | tf_op jit(solution)/shard_map/ppermute | solution.py:27
  55.8 6.1 %all-to-all-done.1 = bf16[32,28,128]{2,1,0:T(8,128)(2,1)S(1)} async-done(((bf16[32,28,128]{2,1,0:T(8,128)(2,1)}), bf16[32,28,128]{2,1,0:T(8,128)(2,1)S(1)}, u32[]{:S(2)}, u32[]{:S(2)}) %all-to-all-start.1) | async-done | bytes 229408 | tf_op jit(solution)/shard_map/all_to_all | solution.py:39
  62.8 2.6 %all-to-all-start.2 = ((bf16[32,28,128]{2,1,0:T(8,128)(2,1)}), bf16[32,28,128]{2,1,0:T(8,128)(2,1)S(1)}, u32[]{:S(2)}, u32[]{:S(2)}) async-start(bf16[32,28,128]{2,1,0:T(8,128)(2,1)} %broadcast_in_dim.5), calls=%async_computation.2 | async-start | bytes 524288 | tf_op jit(solution)/shard_map/all_to_all | solution.py:42
  65.4 4.0 %fusion.22 = f32[256,128]{0,1:T(8,128)S(1)} fusion(f32[256,128]{0,1:T(8,128)S(1)} %copy.60, f32[4096,384]{1,0:T(8,128)} %copy-done.1, s32[4096]{0:T(1024)S(1)} %copy-done.13, f32[256,128]{0,1:T(8,128)S(1)} %copy.59, bf16[256,128]{0,1:T(8,128)(2,1)S(1)} %copy-done.3), kind=kOutput, calls=%fused_computation.33 | convolution fusion | flops 1611792384 | bytes 2572288 | tf_op jit(solution)/shard_map/dot_general | solution.py:78
  70.1 1.3 %copy.56 = bf16[4096,128]{1,0:T(8,128)(2,1)} copy(bf16[4096,128]{0,1:T(8,128)(2,1)S(1)} %get-tuple-element.45) | data formatting | bytes 2097152
  72.8 3.2 %all-to-all-done.2 = bf16[32,28,128]{2,1,0:T(8,128)(2,1)S(1)} async-done(((bf16[32,28,128]{2,1,0:T(8,128)(2,1)}), bf16[32,28,128]{2,1,0:T(8,128)(2,1)S(1)}, u32[]{:S(2)}, u32[]{:S(2)}) %all-to-all-start.2) | async-done | bytes 229408 | tf_op jit(solution)/shard_map/all_to_all | solution.py:42
  (83 shorter events, 12.5 us)
Async XLA Ops:
  0.6 21.7 %copy-start = (bf16[384,128]{1,0:T(8,128)(2,1)S(1)}, bf16[384,128]{1,0:T(8,128)(2,1)}, u32[]{:S(2)}) copy-start(bf16[384,128]{1,0:T(8,128)(2,1)} %param.18) | copy-start | bytes 294916
  0.6 14.2 %copy-start.2 = (bf16[4096,128]{1,0:T(8,128)(2,1)S(1)}, bf16[4096,128]{1,0:T(8,128)(2,1)}, u32[]{:S(2)}) copy-start(bf16[4096,128]{1,0:T(8,128)(2,1)} %param.23) | copy-start | bytes 3145732
  2.2 18.0 %all-to-all-start = ((bf16[32,32,128]{2,1,0:T(8,128)(2,1)}), bf16[32,32,128]{2,1,0:T(8,128)(2,1)S(1)}, u32[]{:S(2)}, u32[]{:S(2)}) async-start(bf16[32,32,128]{2,1,0:T(8,128)(2,1)} %broadcast_in_dim.4), calls=%async_computation | async-start | bytes 524288 | tf_op jit(solution)/shard_map/all_to_all | solution.py:109
  13.3 2.1 %copy-start.11 = (s32[4096]{0:T(1024)S(1)}, s32[4096]{0:T(1024)}, u32[]{:S(2)}) copy-start(s32[4096]{0:T(1024)} %param.15) | copy-start | bytes 49156
  15.4 4.8 %copy-start.6 = (bf16[256,128]{1,0:T(8,128)(2,1)S(1)}, bf16[256,128]{1,0:T(8,128)(2,1)}, u32[]{:S(2)}) copy-start(bf16[256,128]{1,0:T(8,128)(2,1)} %param.13) | copy-start | bytes 196612
  20.2 2.1 %copy-start.14 = (bf16[4096,128]{0,1:T(8,128)(2,1)S(1)}, bf16[4096,128]{0,1:T(8,128)(2,1)}, u32[]{:S(2)}) copy-start(bf16[4096,128]{0,1:T(8,128)(2,1)} %convolution_convert_fusion) | copy-start | bytes 3145732
  22.3 1.6 %copy-start.9 = (bf16[128,128]{1,0:T(8,128)(2,1)S(1)}, bf16[128,128]{1,0:T(8,128)(2,1)}, u32[]{:S(2)}) copy-start(bf16[128,128]{1,0:T(8,128)(2,1)} %param.19) | copy-start | bytes 98308
  23.9 0.8 %copy-start.12 = (s32[4096]{0:T(1024)S(1)}, s32[4096]{0:T(1024)}, u32[]{:S(2)}) copy-start(s32[4096]{0:T(1024)} %param.16) | copy-start | bytes 49156
  24.7 2.0 %copy-start.5 = (bf16[256,128]{0,1:T(8,128)(2,1)S(1)}, bf16[256,128]{0,1:T(8,128)(2,1)}, u32[]{:S(2)}) copy-start(bf16[256,128]{0,1:T(8,128)(2,1)} %copy.44) | copy-start | bytes 196612
  24.7 2.0 %copy-start.8 = (bf16[256,128]{1,0:T(8,128)(2,1)S(1)}, bf16[256,128]{1,0:T(8,128)(2,1)}, u32[]{:S(2)}) copy-start(bf16[256,128]{1,0:T(8,128)(2,1)} %param.20) | copy-start | bytes 196612
  24.7 2.2 %copy-start.10 = (bf16[128,128]{1,0:T(8,128)(2,1)S(1)}, bf16[128,128]{1,0:T(8,128)(2,1)}, u32[]{:S(2)}) copy-start(bf16[128,128]{1,0:T(8,128)(2,1)} %param.21) | copy-start | bytes 98308
  24.8 2.5 %copy-start.3 = (bf16[256,128]{0,1:T(8,128)(2,1)S(1)}, bf16[256,128]{0,1:T(8,128)(2,1)}, u32[]{:S(2)}) copy-start(bf16[256,128]{0,1:T(8,128)(2,1)} %copy.48) | copy-start | bytes 196612
  28.8 2.7 %copy-start.4 = (f32[256,256]{1,0:T(8,128)}, f32[256,256]{1,0:T(8,128)S(1)}, u32[]{:S(2)}) copy-start(f32[256,256]{1,0:T(8,128)S(1)} %fusion.70) | copy-start | bytes 786436
  35.6 4.5 %copy-start.1 = (f32[4096,384]{1,0:T(8,128)}, f32[4096,384]{1,0:T(8,128)S(1)}, u32[]{:S(2)}) copy-start(f32[4096,384]{1,0:T(8,128)S(1)} %fusion.71) | copy-start | bytes 18874372
  40.2 6.2 %copy-start.7 = (bf16[256,128]{1,0:T(8,128)(2,1)S(1)}, bf16[256,128]{1,0:T(8,128)(2,1)}, u32[]{:S(2)}) copy-start(bf16[256,128]{1,0:T(8,128)(2,1)} %convolution_convert_fusion.1) | copy-start | bytes 196612
  40.2 6.3 %slice-start = ((f32[256,256]{1,0:T(8,128)}), f32[256,128]{1,0:T(8,128)S(1)}, s32[]{:S(2)}) async-start(f32[256,256]{1,0:T(8,128)} %copy-done.4), calls=%async_computation.3 | async-start | bytes 262144 | tf_op jit(solution)/shard_map/slice | solution.py:162
  40.5 10.9 %collective-permute-start = (bf16[3,32,128]{1,2,0:T(8,128)(2,1)S(1)}, bf16[3,32,128]{1,2,0:T(8,128)(2,1)S(1)}, u32[]{:S(2)}, u32[]{:S(2)}) collective-permute-start(bf16[3,32,128]{1,2,0:T(8,128)(2,1)S(1)} %get-tuple-element.46), channel_id=1, source_target_pairs={{1,0},{2,1},{3,2},{4,3},{5,4},{6,5},{7,6},{9,8},{10,9},{11,10},{12... | collective-permute-start | bytes 73736 | tf_op jit(solution)/shard_map/ppermute | solution.py:27
  41.8 9.6 %collective-permute-start.1 = (bf16[3,32,128]{1,2,0:T(8,128)(2,1)S(1)}, bf16[3,32,128]{1,2,0:T(8,128)(2,1)S(1)}, u32[]{:S(2)}, u32[]{:S(2)}) collective-permute-start(bf16[3,32,128]{1,2,0:T(8,128)(2,1)S(1)} %get-tuple-element.47), channel_id=1, source_target_pairs={{0,1},{1,2},{2,3},{3,4},{4,5},{5,6},{6,7},{8,9},{9,10},{10,11},{11... | collective-permute-start | bytes 73736 | tf_op jit(solution)/shard_map/ppermute | solution.py:27
  46.4 18.9 %copy-start.13 = (s32[4096]{0:T(1024)S(1)}, s32[4096]{0:T(1024)}, u32[]{:S(2)}) copy-start(s32[4096]{0:T(1024)} %param.16) | copy-start | bytes 49156
  47.3 14.6 %all-to-all-start.1 = ((bf16[32,28,128]{2,1,0:T(8,128)(2,1)}), bf16[32,28,128]{2,1,0:T(8,128)(2,1)S(1)}, u32[]{:S(2)}, u32[]{:S(2)}) async-start(bf16[32,28,128]{2,1,0:T(8,128)(2,1)} %reshape.109), calls=%async_computation.1 | async-start | bytes 524288 | tf_op jit(solution)/shard_map/all_to_all | solution.py:39
  51.5 19.9 %collective-permute-start.2 = (f32[32,128]{0,1:T(8,128)S(1)}, f32[32,128]{0,1:T(8,128)S(1)}, u32[]{:S(2)}, u32[]{:S(2)}) collective-permute-start(f32[32,128]{0,1:T(8,128)S(1)} %get-tuple-element.50), channel_id=1, source_target_pairs={{8,0},{16,8},{24,16},{9,1},{17,9},{25,17},{10,2},{18,10},{26,18},{... | collective-permute-start | bytes 49160 | tf_op jit(solution)/shard_map/ppermute | solution.py:27
  52.8 18.6 %collective-permute-start.3 = (f32[32,128]{0,1:T(8,128)S(1)}, f32[32,128]{0,1:T(8,128)S(1)}, u32[]{:S(2)}, u32[]{:S(2)}) collective-permute-start(f32[32,128]{0,1:T(8,128)S(1)} %get-tuple-element.51), channel_id=1, source_target_pairs={{0,8},{8,16},{16,24},{1,9},{9,17},{17,25},{2,10},{10,18},{18,26},{... | collective-permute-start | bytes 49160 | tf_op jit(solution)/shard_map/ppermute | solution.py:27
  62.8 13.2 %all-to-all-start.2 = ((bf16[32,28,128]{2,1,0:T(8,128)(2,1)}), bf16[32,28,128]{2,1,0:T(8,128)(2,1)S(1)}, u32[]{:S(2)}, u32[]{:S(2)}) async-start(bf16[32,28,128]{2,1,0:T(8,128)(2,1)} %broadcast_in_dim.5), calls=%async_computation.2 | async-start | bytes 524288 | tf_op jit(solution)/shard_map/all_to_all | solution.py:42

commit v2 on v0

v2 whole, which is shorter than its diff:
```python
import functools
import math

import jax
import jax.numpy as jnp
from jax import lax
from jax.experimental import pallas as pl
from jax.experimental.pallas import tpu as pltpu
from jax.sharding import Mesh
from jax.sharding import PartitionSpec as P

EPS = 1e-05
CHUNK = 512
PLANE = ("strip", "y")
ALL = ("strip", "z", "y")
F32 = jnp.float32
BF16 = jnp.bfloat16
VMEM = pl.BlockSpec(memory_space=pltpu.VMEM)
SMEM = pl.BlockSpec(memory_space=pltpu.SMEM)


def mm(left, right):
    return jnp.dot(left, right, preferred_element_type=F32)


def mm_nt(left, right):
    return lax.dot_general(left, right, (((1,), (1,)), ((), ())), preferred_element_type=F32)


def mm_tn(left, right):
    return lax.dot_general(left, right, (((0,), (0,)), ((), ())), preferred_element_type=F32)


def norm_rows(values):
    centre = values - jnp.mean(values, axis=1, keepdims=True)
    scale = lax.rsqrt(jnp.mean(centre * centre, axis=1, keepdims=True) + EPS)
    return (centre * scale, scale)


def norm_back(normed, scale, upstream):
    first = jnp.mean(upstream, axis=1, keepdims=True)
    second = jnp.mean(upstream * normed, axis=1, keepdims=True)
    return scale * (upstream - first - normed * second)


def silu_and_slope(values):
    sig = 0.5 + 0.5 * jnp.tanh(0.5 * values)
    act = values * sig
    return (act, sig + act * (1.0 - sig))


def call(kernel, outs, ins, scratch=()):
    return pl.pallas_call(
        kernel,
        out_shape=[jax.ShapeDtypeStruct(shape, dtype) for shape, dtype in outs],
        in_specs=[SMEM if value.ndim == 1 else VMEM for value in ins],
        out_specs=[VMEM] * len(outs),
        scratch_shapes=list(scratch),
        compiler_params=pltpu.CompilerParams(vmem_limit_bytes=48 * 2**20),
    )(*ins)


def rim_kernel(place, nodes, out):
    border = out.shape[1]
    for target in range(out.shape[0]):
        out[target] = nodes[:border]


def rim_plane_kernel(place, rims, out):
    border = rims.shape[1]
    zs = rims.shape[0]
    my_z, my_y = place[1], place[2]
    other = jnp.clip(my_z + 1 - 2 * my_y, 0, zs - 1)
    own = rims[my_z]
    beyond = rims[other]
    for target in range(out.shape[0]):
        out[target, :border] = own
        out[target, border:] = beyond


def layer_kernel(
    place,
    nodes,
    rims,
    edges,
    info,
    w_edge_in,
    w_edge_out,
    w_node_in,
    w_node_out,
    node_cot,
    edge_cot,
    new_nodes,
    new_edges,
    local_grad,
    parts,
    table,
    tables,
    recv_hot,
    recv_hot_t,
    hidden,
    slope,
    normed,
    scale,
    sums,
    ge_edge,
    ge_out,
    agg,
    packed,
):
    count_p, width = nodes.shape
    border = rims.shape[1] // 2
    chunks, _, chunk = info.shape
    slots = rims.shape[0]
    strips = slots // 2
    share = parts.shape[1] - 2 * border
    my_strip, my_y, live_count = place[0], place[2], place[3]

    table[:count_p] = nodes[...]
    spot = 0
    for d_strip in (-1, 0, 1):
        strip = jnp.clip(my_strip + d_strip, 0, strips - 1)
        for d_sub in (-1, 0, 1):
            if d_strip == 0 and d_sub == 0:
                continue
            if d_sub == 0:
                slot, part = 2 * strip + my_y, 0
            elif d_sub == 1:
                slot, part = 2 * strip + 1 - my_y, my_y
            else:
                slot, part = 2 * strip + 1 - my_y, 1 - my_y
            first = pl.multiple_of(part * border, border)
            rows = slice(count_p + spot * border, count_p + (spot + 1) * border)
            table[rows] = rims[slot, pl.ds(first, border), :]
            spot += 1
    send_rows = table.shape[0]
    tables[:send_rows] = mm(table[...], w_edge_in[:width]).astype(BF16)
    tables[send_rows : send_rows + count_p] = mm(
        nodes[...], w_edge_in[width : 2 * width]
    ).astype(BF16)
    tables[send_rows + count_p :] = w_edge_in[2 * width :]

    lane = lax.broadcasted_iota(jnp.int32, (chunk, width), 1)
    row = lax.broadcasted_iota(jnp.int32, (chunk, width), 0)

    def hot(column, blocks):
        return [(column == lane + width * k).astype(F32).astype(BF16) for k in range(blocks)]

    def hot_t(line, size):
        place_of = lax.broadcasted_iota(jnp.int32, (size, chunk), 0)
        return (place_of == line).astype(F32).astype(BF16)

    agg[...] = jnp.zeros_like(agg)

    def forward(step, carry):
        rows = pl.ds(pl.multiple_of(step * chunk, chunk), chunk)
        index = info[step]
        columns = index.T
        send = hot(columns[:, 0:1], send_rows // width)
        recv = hot(columns[:, 1:2], count_p // width)
        recv = jnp.concatenate(recv, axis=1)
        recv_hot[rows] = recv
        edge = edges[rows]
        pre = mm(jnp.concatenate(send + [recv, edge], axis=1), tables[...])
        act, slope[rows] = silu_and_slope(pre)
        act = act.astype(BF16)
        hidden[rows] = act
        unit, factor = norm_rows(mm(act, w_edge_out[...]))
        normed[rows] = unit
        scale[rows] = jnp.broadcast_to(factor, unit.shape)
        message = jnp.where(row + step * chunk < live_count, unit, 0.0)
        new_edges[rows] = (edge.astype(F32) + message).astype(BF16)
        recv_t = hot_t(index[1:2], count_p)
        recv_hot_t[step] = recv_t
        agg[...] += mm(recv_t, message.astype(BF16))
        return carry

    lax.fori_loop(0, chunks, forward, 0)

    joined = jnp.concatenate([nodes[...], agg[...].astype(BF16)], axis=1)
    node_pre = mm(joined, w_node_in[...])
    node_act, node_slope = silu_and_slope(node_pre)
    node_act = node_act.astype(BF16)
    node_unit, node_scale = norm_rows(mm(node_act, w_node_out[...]))
    new_nodes[...] = (nodes[...].astype(F32) + node_unit).astype(BF16)
    cot = node_cot[...].astype(F32)
    d_outer = norm_back(node_unit, node_scale, cot).astype(BF16)
    d_pre = (mm_nt(d_outer, w_node_out[...]) * node_slope).astype(BF16)
    d_joined = mm_nt(d_pre, w_node_in[...])
    d_agg = d_joined[:, width:].astype(BF16)
    agg[...] = cot + d_joined[:, :width]
    packed[4 * width : 6 * width] = mm_tn(joined, d_pre).astype(BF16)
    packed[6 * width : 7 * width] = mm_tn(node_act, d_outer).astype(BF16)

    sums[...] = jnp.zeros_like(sums)
    ge_edge[...] = jnp.zeros_like(ge_edge)
    ge_out[...] = jnp.zeros_like(ge_out)

    def backward(step, carry):
        rows = pl.ds(pl.multiple_of(step * chunk, chunk), chunk)
        upstream = edge_cot[rows].astype(F32) + mm(recv_hot[rows], d_agg)
        upstream = jnp.where(row + step * chunk < live_count, upstream, 0.0)
        d_out = norm_back(normed[rows], scale[rows], upstream).astype(BF16)
        ge_out[...] += mm_tn(hidden[rows], d_out)
        d_in = (mm_nt(d_out, w_edge_out[...]) * slope[rows]).astype(BF16)
        sums[:send_rows] += mm(hot_t(info[step][0:1], send_rows), d_in)
        sums[send_rows:] += mm(recv_hot_t[step], d_in)
        ge_edge[...] += mm_tn(edges[rows], d_in)
        return carry

    lax.fori_loop(0, chunks, backward, 0)

    send_sums = sums[:send_rows].astype(BF16)
    recv_sums = sums[send_rows:].astype(BF16)
    packed[:width] = mm_tn(table[...], send_sums).astype(BF16)
    packed[width : 2 * width] = mm_tn(nodes[...], recv_sums).astype(BF16)
    packed[2 * width : 3 * width] = ge_edge[...].astype(BF16)
    packed[3 * width : 4 * width] = ge_out[...].astype(BF16)
    if packed.shape[0] > 7 * width:
        packed[7 * width :] = jnp.zeros((packed.shape[0] - 7 * width, width), BF16)
    sent = mm_nt(send_sums, w_edge_in[:width])
    local_grad[...] = agg[...] + sent[:count_p] + mm_nt(recv_sums, w_edge_in[width : 2 * width])
    owed = sent[count_p:].astype(BF16)
    for slot in range(slots):
        parts[slot, :share] = packed[slot * share : (slot + 1) * share]
        parts[slot, share:] = jnp.zeros((2 * border, width), BF16)
    spot = 0
    for d_strip in (-1, 0, 1):
        strip = my_strip + d_strip
        for d_sub in (-1, 0, 1):
            if d_strip == 0 and d_sub == 0:
                continue
            if d_sub == 0:
                slot, part = 2 * strip + my_y, 0
            elif d_sub == 1:
                slot, part = 2 * strip + 1 - my_y, my_y
            else:
                slot, part = 2 * strip + 1 - my_y, 1 - my_y
            first = pl.multiple_of(share + part * border, 16)
            block = owed[spot * border : (spot + 1) * border]

            @pl.when((strip >= 0) & (strip < strips))
            def put(slot=slot, first=first, block=block):
                parts[slot, pl.ds(first, border), :] = block

            spot += 1


def plane_sum_kernel(place, came, out, mine):
    border = mine.shape[0]
    zs = out.shape[0]
    share = out.shape[1] - border
    total = came[0].astype(F32)
    for slot in range(1, came.shape[0]):
        total = total + came[slot].astype(F32)
    share_total = total[:share].astype(BF16)
    mine[...] = total[share : share + border]
    beyond = total[share + border :].astype(BF16)
    for target in range(zs):
        out[target, :share] = share_total
        out[target, share:] = jnp.zeros_like(beyond)
    target = place[1] + 1 - 2 * place[2]

    @pl.when((target >= 0) & (target < zs))
    def put():
        out[target, share:] = beyond


def line_sum_kernel(factor, place, came, mine, local_grad, out, node_grad):
    border = mine.shape[0]
    share = out.shape[1]
    total = came[0].astype(F32)
    for slot in range(1, came.shape[0]):
        total = total + came[slot].astype(F32)
    share_total = (total[:share] * factor).astype(BF16)
    for target in range(out.shape[0]):
        out[target] = share_total
    node_grad[...] = local_grad[...]
    node_grad[:border] += mine[...] + total[share:]


def spread_kernel(place, came, *outs):
    share = came.shape[1]
    start = 0
    for out in outs:
        size = out.shape[0]
        done = 0
        while done < size:
            slot, offset = divmod(start + done, share)
            step = min(size - done, share - offset)
            out[done : done + step] = came[slot, offset : offset + step].astype(F32)
            done += step
        start += size


def shards(
    node_latents,
    edge_latents,
    senders,
    receivers,
    edge_count,
    w_edge_in,
    w_edge_out,
    w_node_in,
    w_node_out,
    node_cotangent,
    edge_cotangent,
):
    count_p, width = node_latents.shape
    count_e = edge_latents.shape[0]
    border = count_p // 8
    strips, zs, ys = (lax.axis_size(axis) for axis in ALL)
    subs = zs * ys
    slots = strips * ys
    my_strip, my_z, my_y = (lax.axis_index(axis).astype(jnp.int32) for axis in ALL)
    my_sub = my_z * ys + my_y
    place = jnp.stack([my_strip, my_z, my_y, edge_count[0]])

    (rims,) = call(rim_kernel, [((zs, border, width), BF16)], [place, node_latents])
    rims = lax.all_to_all(rims, "z", 0, 0)
    (rims,) = call(rim_plane_kernel, [((slots, 2 * border, width), BF16)], [place, rims])
    rims = lax.all_to_all(rims, PLANE, 0, 0)

    owner = senders // count_p
    within = senders % count_p
    is_local = owner == my_strip * subs + my_sub
    block = (owner // subs - my_strip + 1) * 3 + (owner % subs - my_sub + 1)
    block = jnp.where(block > 4, block - 1, block)
    send_index = jnp.where(
        is_local, within, count_p + block * border + jnp.minimum(within, border - 1)
    )
    chunk = min(CHUNK, count_e)
    chunks = count_e // chunk
    info = jnp.concatenate(
        [
            send_index.reshape(chunks, 1, chunk),
            receivers.reshape(chunks, 1, chunk),
            jnp.zeros((chunks, 6, chunk), jnp.int32),
        ],
        axis=1,
    )

    total = 7 * width
    share = -(-total // (slots * 16)) * 16
    send_rows = 2 * count_p
    new_nodes, new_edges, local_grad, parts = call(
        layer_kernel,
        [
            ((count_p, width), BF16),
            ((count_e, width), BF16),
            ((count_p, width), F32),
            ((slots, share + 2 * border, width), BF16),
        ],
        [
            place,
            node_latents,
            rims,
            edge_latents,
            info,
            w_edge_in,
            w_edge_out,
            w_node_in,
            w_node_out,
            node_cotangent,
            edge_cotangent,
        ],
        [
            pltpu.VMEM((send_rows, width), BF16),
            pltpu.VMEM((send_rows + count_p + width, width), BF16),
            pltpu.VMEM((count_e, count_p), BF16),
            pltpu.VMEM((chunks, count_p, chunk), BF16),
            pltpu.VMEM((count_e, width), BF16),
            pltpu.VMEM((count_e, width), F32),
            pltpu.VMEM((count_e, width), F32),
            pltpu.VMEM((count_e, width), F32),
            pltpu.VMEM((send_rows + count_p, width), F32),
            pltpu.VMEM((width, width), F32),
            pltpu.VMEM((width, width), F32),
            pltpu.VMEM((count_p, width), F32),
            pltpu.VMEM((slots * share, width), BF16),
        ],
    )

    came = lax.all_to_all(parts, PLANE, 0, 0)
    parts, mine = call(
        plane_sum_kernel,
        [((zs, share + border, width), BF16), ((border, width), F32)],
        [place, came],
    )
    came = lax.all_to_all(parts, "z", 0, 0)
    factor = 1.0 / math.sqrt(count_e * strips * subs)
    parts, node_grad = call(
        functools.partial(line_sum_kernel, factor),
        [((slots, share, width), BF16), ((count_p, width), F32)],
        [place, came, mine, local_grad],
    )
    came = lax.all_to_all(parts, PLANE, 0, 0)
    grads = call(
        spread_kernel,
        [((rows, width), F32) for rows in (3 * width, width, 2 * width, width)],
        [place, came],
    )
    return (new_nodes, new_edges, node_grad, *grads)


def solution(mesh):
    strips, subs = mesh.devices.shape
    grid = Mesh(mesh.devices.reshape(strips, subs // 2, 2), ALL)
    rows = P(ALL, None)
    line = P(ALL)
    return jax.shard_map(
        shards,
        mesh=grid,
        in_specs=(rows, rows, line, line, line, P(), P(), P(), P(), rows, rows),
        out_specs=(rows, rows, rows, P(), P(), P(), P()),
        check_vma=False,
    )
```

time: 209 us -> 80.8 us (0.39)
  waiting for transfers between devices: 129 us -> 10.4 us
  matrix products: 28.1 us -> 0 us
  blocking collectives: 0 us -> 27.4 us
  Pallas kernels: 0 us -> 27.1 us
  between operations: 15.3 us -> 1.38 us
  starting transfers between devices: 22.2 us -> 10.3 us
  other arithmetic: 8.02 us -> 0.21 us
  local copies, waits for them, and re-layouts: 6.07 us -> 3.4 us
    psum x1 -> x0, waiting for transfers between devices: 129 us -> none  [shards(): totals = lax.psum((ge_in, ge_out, gn_in, gn_out), ('strip', 'sub'))]
    dot_general x18 -> x0, matrix products: 28.1 us -> none  [the longest x3 10.4 us: sum_rows(): jnp.dot(onehot.astype(jnp.float32).T, values, precision=lax.Precision.HIG...]
    all_to_all x0 -> x3, blocking collectives: none -> 27.4 us  [the longest x2 18 us: shards(): came = lax.all_to_all(parts, PLANE, 0, 0)]
    pallas_call x0 -> x6, Pallas kernels: none -> 27.1 us  [call(): pl.pallas_call(kernel, out_shape=[jax.ShapeDtypeStruct(shape, dtype) for...]
    ppermute x8 -> x0, starting transfers between devices: 22.2 us -> none  [the longest x4 11.1 us: shifted(): lax.ppermute(value, axis, [(source, source + steps) for source in range(f...]
    all_to_all x0 -> x2, waiting for transfers between devices: none -> 10.4 us  [the longest x1 5.52 us: shards(): rims = lax.all_to_all(rims, 'z', 0, 0)]
    all_to_all x0 -> x2, starting transfers between devices: none -> 10.3 us  [the longest x1 6.45 us: shards(): rims = lax.all_to_all(rims, 'z', 0, 0)]
    mul x4 -> x0, other arithmetic: 6.14 us -> none  [the longest x1 1.62 us: shards(): totals[0] * factor]
  transfers between devices with their start and end apart: 9 -> 2, of which waited for: 2 -> 2; matrix products, arithmetic and copies ran while one was open for 7% -> 0% of each run, Pallas kernels for 0% -> 0%
where the time goes in v2:
time: 80.8 us; the launch traced here: 80.2 us
  blocking collectives  27.4 us (34%)
  Pallas kernels  27.1 us (34%)
  waiting for transfers between devices  10.4 us (13%)
  starting transfers between devices  10.3 us (13%)
  local copies, waits for them, and re-layouts  3.4 us (4%)
  between operations  1.38 us (2%)
    pallas_call x6, Pallas kernels, call(): pl.pallas_call(kernel, out_shape=[jax.ShapeDtypeStruct(shape, dtype) for...  27.1 us
    all_to_all x2, blocking collectives, shards(): came = lax.all_to_all(parts, PLANE, 0, 0)  18 us
    all_to_all x1, blocking collectives, shards(): came = lax.all_to_all(parts, 'z', 0, 0)  9.35 us
    all_to_all x1, starting transfers between devices, shards(): rims = lax.all_to_all(rims, 'z', 0, 0)  6.45 us
    all_to_all x1, waiting for transfers between devices, shards(): rims = lax.all_to_all(rims, 'z', 0, 0)  5.52 us
    all_to_all x1, waiting for transfers between devices, shards(): rims = lax.all_to_all(rims, PLANE, 0, 0)  4.84 us
    all_to_all x1, starting transfers between devices, shards(): rims = lax.all_to_all(rims, PLANE, 0, 0)  3.87 us
    unnamed x22, local copies, waits for them, and re-layouts  3.32 us
  transfers between devices with their start and end apart: 2, of which 2 were waited for; matrix products, arithmetic and copies ran while one was open for 0% of the time, Pallas kernels for 0%

profile of v2, /device:TPU:0, one launch (start us, length us, event | category | flops | bytes accessed | tf_op | source)
XLA Modules:
  0.0 80.2 jit_solution(17841760476048039472)
XLA Ops:
  1.3 0.1 pad_add_fusion.place
  1.4 0.8 %copy-done.2 = bf16[256,128]{1,0:T(8,128)(2,1)S(1)} copy-done((bf16[256,128]{1,0:T(8,128)(2,1)S(1)}, bf16[256,128]{1,0:T(8,128)(2,1)}, u32[]{:S(2)}) %copy-start.2) | copy-done | bytes 65560
  2.2 1.2 %shard_map.162 = bf16[4,32,128]{2,1,0:T(8,128)(2,1)} custom-call(s32[4]{0:T(128)S(1)} %pad_add_fusion.place, bf16[256,128]{1,0:T(8,128)(2,1)S(1)} %copy-done.2), custom_call_target="tpu_custom_call" | custom-call | tf_op jit(solution)/shard_map/pallas_call | solution.py:53
  3.4 6.4 %all-to-all-start = ((bf16[4,32,128]{2,1,0:T(8,128)(2,1)}), bf16[4,32,128]{2,1,0:T(8,128)(2,1)S(1)}, u32[]{:S(2)}, u32[]{:S(2)}) async-start(bf16[4,32,128]{2,1,0:T(8,128)(2,1)} %shard_map.162), calls=%async_computation | async-start | bytes 65536 | tf_op jit(solution)/shard_map/all_to_all | solution.py:320
  9.8 0.0 copy-done.10
  9.8 0.1 fusion.9
  9.9 0.1 pad.2.clone
  10.0 5.5 %all-to-all-done.rims = bf16[4,32,128]{2,1,0:T(8,128)(2,1)S(1)} async-done(((bf16[4,32,128]{2,1,0:T(8,128)(2,1)}), bf16[4,32,128]{2,1,0:T(8,128)(2,1)S(1)}, u32[]{:S(2)}, u32[]{:S(2)}) %all-to-all-start) | async-done | bytes 32800 | tf_op jit(solution)/shard_map/all_to_all | solution.py:320
  15.5 1.2 %shard_map.163 = bf16[8,64,128]{2,1,0:T(8,128)(2,1)} custom-call(s32[4]{0:T(128)S(1)} %pad_add_fusion.place, bf16[4,32,128]{2,1,0:T(8,128)(2,1)S(1)} %all-to-all-done.rims), custom_call_target="tpu_custom_call" | custom-call | tf_op jit(solution)/shard_map/pallas_call | solution.py:53
  16.7 0.0 copy-start.8
  16.7 3.9 %all-to-all-start.1 = ((bf16[8,64,128]{2,1,0:T(8,128)(2,1)}), bf16[8,64,128]{2,1,0:T(8,128)(2,1)S(1)}, u32[]{:S(2)}, u32[]{:S(2)}) async-start(bf16[8,64,128]{2,1,0:T(8,128)(2,1)} %shard_map.163), calls=%async_computation.1 | async-start | bytes 262144 | tf_op jit(solution)/shard_map/all_to_all | solution.py:322
  20.6 0.0 copy-start.3
  20.6 0.1 add_add_fusion.info
  20.7 4.8 %all-to-all-done.1.rims = bf16[8,64,128]{2,1,0:T(8,128)(2,1)S(1)} async-done(((bf16[8,64,128]{2,1,0:T(8,128)(2,1)}), bf16[8,64,128]{2,1,0:T(8,128)(2,1)S(1)}, u32[]{:S(2)}, u32[]{:S(2)}) %all-to-all-start.1) | async-done | bytes 131104 | tf_op jit(solution)/shard_map/all_to_all | solution.py:322
  25.6 0.0 copy-start
  25.6 1.2 %copy-done = bf16[4096,128]{1,0:T(8,128)(2,1)S(1)} copy-done((bf16[4096,128]{1,0:T(8,128)(2,1)S(1)}, bf16[4096,128]{1,0:T(8,128)(2,1)}, u32[]{:S(2)}) %copy-start) | copy-done | bytes 1048600
  26.8 1.2 %copy-done.1 = bf16[4096,128]{1,0:T(8,128)(2,1)S(1)} copy-done((bf16[4096,128]{1,0:T(8,128)(2,1)S(1)}, bf16[4096,128]{1,0:T(8,128)(2,1)}, u32[]{:S(2)}) %copy-start.1) | copy-done | bytes 1048600
  28.0 21.6 %shard_map.164 = (bf16[256,128]{1,0:T(8,128)(2,1)}, bf16[4096,128]{1,0:T(8,128)(2,1)}, f32[256,128]{1,0:T(8,128)S(1)}, bf16[8,176,128]{2,1,0:T(8,128)(2,1)S(1)}) custom-call(s32[4]{0:T(128)S(1)} %pad_add_fusion.place, bf16[256,128]{1,0:T(8,128)(2,1)S(1)} %copy-done.3, bf16[8,64,128]{2,1,0:T(8,128)(2,1)S(1)} %all-to-all-done.1.rims, ...), custom_call_target="tpu_custom_call" | custom-call | tf_op jit(solution)/shard_map/pallas_call | solution.py:53
  49.6 10.0 %all_to_all.25.came = bf16[8,176,128]{2,1,0:T(8,128)(2,1)S(1)} all-to-all(bf16[8,176,128]{2,1,0:T(8,128)(2,1)S(1)} %get-tuple-element.21), channel_id=1, replica_groups=mesh['strip'=4,'z'=4,'y'=2] {'strip','y'}, dimensions={0} | all-to-all | bytes 720896 | tf_op jit(solution)/shard_map/all_to_all | solution.py:384
  59.6 0.6 shard_map.165
  60.2 9.3 %all_to_all.26.came = bf16[4,144,128]{2,1,0:T(8,128)(2,1)S(1)} all-to-all(bf16[4,144,128]{2,1,0:T(8,128)(2,1)S(1)} %get-tuple-element.22), channel_id=1, replica_groups=mesh['strip'=4,'z'=4,'y'=2] {'z'}, dimensions={0} | all-to-all | bytes 294912 | tf_op jit(solution)/shard_map/all_to_all | solution.py:390
  69.6 1.2 %shard_map.166 = (bf16[8,112,128]{2,1,0:T(8,128)(2,1)S(1)}, f32[256,128]{1,0:T(8,128)}) custom-call(s32[4]{0:T(128)S(1)} %pad_add_fusion.place, bf16[4,144,128]{2,1,0:T(8,128)(2,1)S(1)} %all_to_all.26.came, f32[32,128]{1,0:T(8,128)S(1)} %get-tuple-element.23.mine, f32[256,128]{1,0:T(8,128)S(1)} %get-tuple-element.24.local_grad), custom_call_target="tpu_custom_call" | custom-call | tf_op jit(solution)/shard_map/pallas_call | solution.py:53
  70.8 8.1 %all_to_all.27.came = bf16[8,112,128]{2,1,0:T(8,128)(2,1)S(1)} all-to-all(bf16[8,112,128]{2,1,0:T(8,128)(2,1)S(1)} %get-tuple-element.26), channel_id=1, replica_groups=mesh['strip'=4,'z'=4,'y'=2] {'strip','y'}, dimensions={0} | all-to-all | bytes 458752 | tf_op jit(solution)/shard_map/all_to_all | solution.py:397
  78.9 1.3 %shard_map.167 = (f32[384,128]{1,0:T(8,128)}, f32[128,128]{1,0:T(8,128)}, f32[256,128]{1,0:T(8,128)}, f32[128,128]{1,0:T(8,128)}) custom-call(s32[4]{0:T(128)S(1)} %pad_add_fusion.place, bf16[8,112,128]{2,1,0:T(8,128)(2,1)S(1)} %all_to_all.27.came), custom_call_target="tpu_custom_call" | custom-call | tf_op jit(solution)/shard_map/pallas_call | solution.py:53
  (16 shorter events, 0.0 us)
Async XLA Ops:
  1.4 0.8 %copy-start.2 = (bf16[256,128]{1,0:T(8,128)(2,1)S(1)}, bf16[256,128]{1,0:T(8,128)(2,1)}, u32[]{:S(2)}) copy-start(bf16[256,128]{1,0:T(8,128)(2,1)} %nodes.3) | copy-start | bytes 196612
  3.4 6.5 %copy-start.10 = (s32[4096]{0:T(1024)S(1)}, s32[4096]{0:T(1024)}, u32[]{:S(2)}) copy-start(s32[4096]{0:T(1024)} %param.13) | copy-start | bytes 49156
  3.4 12.1 %all-to-all-start = ((bf16[4,32,128]{2,1,0:T(8,128)(2,1)}), bf16[4,32,128]{2,1,0:T(8,128)(2,1)S(1)}, u32[]{:S(2)}, u32[]{:S(2)}) async-start(bf16[4,32,128]{2,1,0:T(8,128)(2,1)} %shard_map.162), calls=%async_computation | async-start | bytes 65536 | tf_op jit(solution)/shard_map/all_to_all | solution.py:320
  16.7 3.9 %copy-start.9 = (s32[4096]{0:T(1024)S(1)}, s32[4096]{0:T(1024)}, u32[]{:S(2)}) copy-start(s32[4096]{0:T(1024)} %param.14) | copy-start | bytes 49156
  16.7 8.8 %copy-start.5 = (bf16[256,128]{1,0:T(8,128)(2,1)S(1)}, bf16[256,128]{1,0:T(8,128)(2,1)}, u32[]{:S(2)}) copy-start(bf16[256,128]{1,0:T(8,128)(2,1)} %w_node_in.1) | copy-start | bytes 196612
  16.7 8.8 %copy-start.6 = (bf16[256,128]{1,0:T(8,128)(2,1)S(1)}, bf16[256,128]{1,0:T(8,128)(2,1)}, u32[]{:S(2)}) copy-start(bf16[256,128]{1,0:T(8,128)(2,1)} %node_cot.1) | copy-start | bytes 196612
  16.7 8.8 %copy-start.7 = (bf16[128,128]{1,0:T(8,128)(2,1)S(1)}, bf16[128,128]{1,0:T(8,128)(2,1)}, u32[]{:S(2)}) copy-start(bf16[128,128]{1,0:T(8,128)(2,1)} %w_edge_out.1) | copy-start | bytes 98308
  16.7 8.8 %copy-start.8 = (bf16[128,128]{1,0:T(8,128)(2,1)S(1)}, bf16[128,128]{1,0:T(8,128)(2,1)}, u32[]{:S(2)}) copy-start(bf16[128,128]{1,0:T(8,128)(2,1)} %w_node_out.1) | copy-start | bytes 98308
  16.7 8.8 %all-to-all-start.1 = ((bf16[8,64,128]{2,1,0:T(8,128)(2,1)}), bf16[8,64,128]{2,1,0:T(8,128)(2,1)S(1)}, u32[]{:S(2)}, u32[]{:S(2)}) async-start(bf16[8,64,128]{2,1,0:T(8,128)(2,1)} %shard_map.163), calls=%async_computation.1 | async-start | bytes 262144 | tf_op jit(solution)/shard_map/all_to_all | solution.py:322
  20.6 5.0 %copy-start.4 = (bf16[384,128]{1,0:T(8,128)(2,1)S(1)}, bf16[384,128]{1,0:T(8,128)(2,1)}, u32[]{:S(2)}) copy-start(bf16[384,128]{1,0:T(8,128)(2,1)} %w_edge_in.1) | copy-start | bytes 294916
  20.6 5.0 %copy-start.3 = (bf16[256,128]{1,0:T(8,128)(2,1)S(1)}, bf16[256,128]{1,0:T(8,128)(2,1)}, u32[]{:S(2)}) copy-start(bf16[256,128]{1,0:T(8,128)(2,1)} %nodes.3) | copy-start | bytes 196612
  25.6 1.2 %copy-start = (bf16[4096,128]{1,0:T(8,128)(2,1)S(1)}, bf16[4096,128]{1,0:T(8,128)(2,1)}, u32[]{:S(2)}) copy-start(bf16[4096,128]{1,0:T(8,128)(2,1)} %edges.1) | copy-start | bytes 3145732
  26.8 1.2 %copy-start.1 = (bf16[4096,128]{1,0:T(8,128)(2,1)S(1)}, bf16[4096,128]{1,0:T(8,128)(2,1)}, u32[]{:S(2)}) copy-start(bf16[4096,128]{1,0:T(8,128)(2,1)} %edge_cot.1) | copy-start | bytes 3145732

commit v3 on v2

v3 whole, which is shorter than its diff:
```python
import functools
import math

import jax
import jax.numpy as jnp
from jax import lax
from jax.experimental import pallas as pl
from jax.experimental.pallas import tpu as pltpu
from jax.sharding import PartitionSpec as P

EPS = 1e-05
CHUNK = 512
ALL = ("strip", "sub")
F32 = jnp.float32
BF16 = jnp.bfloat16
VMEM = pl.BlockSpec(memory_space=pltpu.VMEM)
SMEM = pl.BlockSpec(memory_space=pltpu.SMEM)


def mm(left, right):
    return jnp.dot(left, right, preferred_element_type=F32)


def mm_nt(left, right):
    return lax.dot_general(left, right, (((1,), (1,)), ((), ())), preferred_element_type=F32)


def mm_tn(left, right):
    return lax.dot_general(left, right, (((0,), (0,)), ((), ())), preferred_element_type=F32)


def norm_rows(values):
    centre = values - jnp.mean(values, axis=1, keepdims=True)
    scale = lax.rsqrt(jnp.mean(centre * centre, axis=1, keepdims=True) + EPS)
    return (centre * scale, scale)


def norm_back(normed, scale, upstream):
    first = jnp.mean(upstream, axis=1, keepdims=True)
    second = jnp.mean(upstream * normed, axis=1, keepdims=True)
    return scale * (upstream - first - normed * second)


def silu_and_slope(values):
    sig = 0.5 + 0.5 * jnp.tanh(0.5 * values)
    act = values * sig
    return (act, sig + act * (1.0 - sig))


def call(kernel, outs, ins, scratch=()):
    return pl.pallas_call(
        kernel,
        out_shape=[jax.ShapeDtypeStruct(shape, dtype) for shape, dtype in outs],
        in_specs=[SMEM if value.ndim == 1 else VMEM for value in ins],
        out_specs=[VMEM] * len(outs),
        scratch_shapes=list(scratch),
        compiler_params=pltpu.CompilerParams(vmem_limit_bytes=28 * 2**20),
    )(*ins)


def rim_kernel(nodes, out):
    border = out.shape[1]
    for target in range(out.shape[0]):
        out[target] = nodes[:border]


def early_kernel(
    nodes,
    edges,
    info,
    w_edge_in,
    send_hot,
    recv_hot,
    send_hot_t,
    recv_hot_t,
    edges_t,
    pre_part,
    tables,
):
    count_p, width = nodes.shape
    chunks, _, chunk = info.shape
    send_rows = send_hot.shape[1]
    tables[:count_p] = mm(nodes[...], w_edge_in[width : 2 * width]).astype(BF16)
    tables[count_p:] = w_edge_in[2 * width :]
    lane = lax.broadcasted_iota(jnp.int32, (chunk, width), 1)

    def hot(column, blocks):
        found = [(column == lane + width * k).astype(F32).astype(BF16) for k in range(blocks)]
        return jnp.concatenate(found, axis=1)

    def hot_t(line, size):
        place_of = lax.broadcasted_iota(jnp.int32, (size, chunk), 0)
        return (place_of == line).astype(F32).astype(BF16)

    def one(step, carry):
        rows = pl.ds(pl.multiple_of(step * chunk, chunk), chunk)
        index = info[step]
        columns = index.T
        send_hot[rows] = hot(columns[:, 0:1], send_rows // width)
        recv = hot(columns[:, 1:2], count_p // width)
        recv_hot[rows] = recv
        send_hot_t[step] = hot_t(index[0:1], send_rows)
        recv_hot_t[step] = hot_t(index[1:2], count_p)
        edge = edges[rows]
        edges_t[step] = edge.T
        pre_part[rows] = mm(jnp.concatenate([recv, edge], axis=1), tables[...])
        return carry

    lax.fori_loop(0, chunks, one, 0)


def layer_kernel(
    place,
    nodes,
    rims,
    edges,
    send_hot,
    recv_hot,
    send_hot_t,
    recv_hot_t,
    edges_t,
    pre_part,
    w_edge_in,
    w_edge_out,
    w_node_in,
    w_node_out,
    node_cot,
    edge_cot,
    new_nodes,
    new_edges,
    base_grad,
    packed,
    sums_out,
    table,
    tables,
    spread,
    means,
    hidden,
    slope,
    normed,
    scale,
    sums,
    ge_edge,
    ge_out,
    agg,
):
    count_p, width = nodes.shape
    border = rims.shape[1]
    chunks, _, chunk = recv_hot_t.shape
    my_strip, my_sub, strips, subs, live_count = (place[i] for i in range(5))

    table[:count_p] = nodes[...]
    spot = 0
    for d_strip in (-1, 0, 1):
        strip = jnp.clip(my_strip + d_strip, 0, strips - 1)
        for d_sub in (-1, 0, 1):
            if d_strip == 0 and d_sub == 0:
                continue
            sub = jnp.clip(my_sub + d_sub, 0, subs - 1)
            rows = slice(count_p + spot * border, count_p + (spot + 1) * border)
            table[rows] = rims[strip * subs + sub]
            spot += 1
    send_rows = table.shape[0]
    tables[...] = mm(table[...], w_edge_in[:width]).astype(BF16)
    spread[:, :width] = w_edge_out[...]
    spread[:, width:] = jnp.broadcast_to(
        jnp.mean(w_edge_out[...].astype(F32), axis=1, keepdims=True), (width, width)
    ).astype(BF16)
    high = lax.broadcasted_iota(jnp.int32, (2 * width, 2 * width), 0) >= width
    wide = lax.broadcasted_iota(jnp.int32, (2 * width, 2 * width), 1) >= width
    means[...] = jnp.where(high == wide, 1.0 / width, 0.0).astype(BF16)

    row = lax.broadcasted_iota(jnp.int32, (chunk, width), 0)
    agg[...] = jnp.zeros_like(agg)

    def forward(step, carry):
        rows = pl.ds(pl.multiple_of(step * chunk, chunk), chunk)
        pre = pre_part[rows] + mm(send_hot[rows], tables[...])
        act, slope[rows] = silu_and_slope(pre)
        act = act.astype(BF16)
        hidden[rows] = act
        outer = mm(act, spread[...])
        centre = outer[:, :width] - outer[:, width:]
        spare = mm((centre * centre).astype(BF16), means[:width, :width])
        factor = jnp.where(row < live_count - step * chunk, lax.rsqrt(spare + EPS), 0.0)
        unit = centre * factor
        scale[rows] = factor
        normed[rows] = unit
        new_edges[rows] = (edges[rows].astype(F32) + unit).astype(BF16)
        agg[...] += mm(recv_hot_t[step], unit.astype(BF16))
        return carry

    lax.fori_loop(0, chunks, forward, 0, unroll=2)

    joined = jnp.concatenate([nodes[...], agg[...].astype(BF16)], axis=1)
    node_pre = mm(joined, w_node_in[...])
    node_act, node_slope = silu_and_slope(node_pre)
    node_act = node_act.astype(BF16)
    node_unit, node_scale = norm_rows(mm(node_act, w_node_out[...]))
    new_nodes[...] = (nodes[...].astype(F32) + node_unit).astype(BF16)
    cot = node_cot[...].astype(F32)
    d_outer = norm_back(node_unit, node_scale, cot).astype(BF16)
    d_pre = (mm_nt(d_outer, w_node_out[...]) * node_slope).astype(BF16)
    d_joined = mm_nt(d_pre, w_node_in[...])
    d_agg = d_joined[:, width:].astype(BF16)
    base_grad[...] = cot + d_joined[:, :width]
    packed[4 * width : 6 * width] = mm_tn(joined, d_pre).astype(BF16)
    packed[6 * width : 7 * width] = mm_tn(node_act, d_outer).astype(BF16)

    sums[...] = jnp.zeros_like(sums)
    ge_edge[...] = jnp.zeros_like(ge_edge)
    ge_out[...] = jnp.zeros_like(ge_out)

    def backward(step, carry):
        rows = pl.ds(pl.multiple_of(step * chunk, chunk), chunk)
        upstream = edge_cot[rows].astype(F32) + mm(recv_hot[rows], d_agg)
        unit = normed[rows]
        both = jnp.concatenate([upstream.astype(BF16), (upstream * unit).astype(BF16)], axis=1)
        both = mm(both, means[...])
        d_out = scale[rows] * (upstream - both[:, :width] - unit * both[:, width:])
        d_out = d_out.astype(BF16)
        ge_out[...] += mm_tn(hidden[rows], d_out)
        d_in = (mm_nt(d_out, w_edge_out[...]) * slope[rows]).astype(BF16)
        sums[:send_rows] += mm(send_hot_t[step], d_in)
        sums[send_rows:] += mm(recv_hot_t[step], d_in)
        ge_edge[...] += mm(edges_t[step], d_in)
        return carry

    lax.fori_loop(0, chunks, backward, 0, unroll=2)

    sums_out[...] = sums[...].astype(BF16)
    packed[:width] = mm_tn(table[...], sums_out[:send_rows]).astype(BF16)
    packed[width : 2 * width] = mm_tn(nodes[...], sums_out[send_rows:]).astype(BF16)
    packed[2 * width : 3 * width] = ge_edge[...].astype(BF16)
    packed[3 * width : 4 * width] = ge_out[...].astype(BF16)
    if packed.shape[0] > 7 * width:
        packed[7 * width :] = jnp.zeros((packed.shape[0] - 7 * width, width), BF16)


def owed_kernel(base_grad, sums, w_edge_in, local_grad, low, high, middle):
    count_p, width = base_grad.shape
    border = low.shape[1]
    send_rows = sums.shape[0] - count_p
    sent = mm_nt(sums[:send_rows], w_edge_in[:width])
    local_grad[...] = (
        base_grad[...]
        + sent[:count_p]
        + mm_nt(sums[send_rows:], w_edge_in[width : 2 * width])
    )
    block = [sent[count_p + i * border : count_p + (i + 1) * border] for i in range(8)]
    for strip, (under, over) in enumerate(((0, 2), (3, 4), (5, 7))):
        low[strip] = block[under].astype(BF16)
        high[strip] = block[over].astype(BF16)
    middle[0] = block[1]
    middle[1] = jnp.zeros_like(block[1])
    middle[2] = block[6]


def share_kernel(factor, came, out):
    total = came[0].astype(F32)
    for source in range(1, came.shape[0]):
        total = total + came[source].astype(F32)
    total = (total * factor).astype(BF16)
    for target in range(out.shape[0]):
        out[target] = total


def column_kernel(middle, low, high, down, stay, up):
    column = [middle[i] + low[i].astype(F32) + high[i].astype(F32) for i in range(3)]
    down[...] = column[0].astype(BF16)
    stay[...] = column[1]
    up[...] = column[2].astype(BF16)


def finish_kernel(came, local_grad, stay, down, up, node_grad, *outs):
    border = stay.shape[0]
    node_grad[...] = local_grad[...]
    node_grad[:border] += stay[...] + down[...].astype(F32) + up[...].astype(F32)
    start = 0
    for out in outs:
        size = out.shape[0]
        out[...] = came[start : start + size].astype(F32)
        start += size


def shifted(value, axis, steps):
    count = lax.axis_size(axis)
    first, last = (max(0, -steps), min(count, count - steps))
    return lax.ppermute(value, axis, [(source, source + steps) for source in range(first, last)])


def shards(
    node_latents,
    edge_latents,
    senders,
    receivers,
    edge_count,
    w_edge_in,
    w_edge_out,
    w_node_in,
    w_node_out,
    node_cotangent,
    edge_cotangent,
):
    count_p, width = node_latents.shape
    count_e = edge_latents.shape[0]
    border = count_p // 8
    strips, subs = (lax.axis_size(axis) for axis in ALL)
    devices = strips * subs
    my_strip, my_sub = (lax.axis_index(axis).astype(jnp.int32) for axis in ALL)
    place = jnp.stack(
        [my_strip, my_sub, jnp.int32(strips), jnp.int32(subs), edge_count[0]]
    )

    (rims,) = call(rim_kernel, [((devices, border, width), BF16)], [node_latents])
    rims = lax.all_to_all(rims, ALL, 0, 0)

    owner = senders // count_p
    within = senders % count_p
    is_local = owner == my_strip * subs + my_sub
    block = (owner // subs - my_strip + 1) * 3 + (owner % subs - my_sub + 1)
    block = jnp.where(block > 4, block - 1, block)
    send_index = jnp.where(
        is_local, within, count_p + block * border + jnp.minimum(within, border - 1)
    )
    chunk = min(CHUNK, count_e)
    chunks = count_e // chunk
    info = jnp.concatenate(
        [
            send_index.reshape(chunks, 1, chunk),
            receivers.reshape(chunks, 1, chunk),
            jnp.zeros((chunks, 6, chunk), jnp.int32),
        ],
        axis=1,
    )
    send_rows = 2 * count_p
    early = call(
        early_kernel,
        [
            ((count_e, send_rows), BF16),
            ((count_e, count_p), BF16),
            ((chunks, send_rows, chunk), BF16),
            ((chunks, count_p, chunk), BF16),
            ((chunks, width, chunk), BF16),
            ((count_e, width), F32),
        ],
        [node_latents, edge_latents, info, w_edge_in],
        [pltpu.VMEM((count_p + width, width), BF16)],
    )

    share = -(-7 * width // (devices * 16)) * 16
    new_nodes, new_edges, base_grad, packed, sums = call(
        layer_kernel,
        [
            ((count_p, width), BF16),
            ((count_e, width), BF16),
            ((count_p, width), F32),
            ((devices * share, width), BF16),
            ((send_rows + count_p, width), BF16),
        ],
        [
            place,
            node_latents,
            rims,
            edge_latents,
            *early,
            w_edge_in,
            w_edge_out,
            w_node_in,
            w_node_out,
            node_cotangent,
            edge_cotangent,
        ],
        [
            pltpu.VMEM((send_rows, width), BF16),
            pltpu.VMEM((send_rows, width), BF16),
            pltpu.VMEM((width, 2 * width), BF16),
            pltpu.VMEM((2 * width, 2 * width), BF16),
            pltpu.VMEM((count_e, width), BF16),
            pltpu.VMEM((count_e, width), F32),
            pltpu.VMEM((count_e, width), F32),
            pltpu.VMEM((count_e, width), F32),
            pltpu.VMEM((send_rows + count_p, width), F32),
            pltpu.VMEM((width, width), F32),
            pltpu.VMEM((width, width), F32),
            pltpu.VMEM((count_p, width), F32),
        ],
    )

    came = lax.all_to_all(packed.reshape(devices, share, width), ALL, 0, 0)
    local_grad, low, high, middle = call(
        owed_kernel,
        [
            ((count_p, width), F32),
            ((3, border, width), BF16),
            ((3, border, width), BF16),
            ((3, border, width), F32),
        ],
        [base_grad, sums, w_edge_in],
    )
    low = shifted(low, "sub", -1)
    high = shifted(high, "sub", 1)
    factor = 1.0 / math.sqrt(count_e * devices)
    (parts,) = call(
        functools.partial(share_kernel, factor), [((devices, share, width), BF16)], [came]
    )
    parts, low, high, middle = lax.optimization_barrier((parts, low, high, middle))
    came = lax.all_to_all(parts, ALL, 0, 0)
    down, stay, up = call(
        column_kernel,
        [((border, width), BF16), ((border, width), F32), ((border, width), BF16)],
        [middle, low, high],
    )
    down = shifted(down, "strip", -1)
    up = shifted(up, "strip", 1)
    node_grad, *grads = call(
        finish_kernel,
        [((rows, width), F32) for rows in (count_p, 3 * width, width, 2 * width, width)],
        [came.reshape(devices * share, width), local_grad, stay, down, up],
    )
    return (new_nodes, new_edges, node_grad, *grads)


def solution(mesh):
    rows = P(ALL, None)
    line = P(ALL)
    return jax.shard_map(
        shards,
        mesh=mesh,
        in_specs=(rows, rows, line, line, line, P(), P(), P(), P(), rows, rows),
        out_specs=(rows, rows, rows, P(), P(), P(), P()),
        check_vma=False,
    )
```

time: 80.8 us -> 95.1 us (1.18)
  blocking collectives: 27.4 us -> 0 us
  local copies, waits for them, and re-layouts: 3.4 us -> 30.5 us
  starting transfers between devices: 10.3 us -> 28.8 us
  Pallas kernels: 27.1 us -> 22.5 us
  waiting for transfers between devices: 10.4 us -> 9.01 us
  other arithmetic: 0.21 us -> 1.56 us
    all_to_all x3 -> x0, blocking collectives: 27.4 us -> none  [the longest x2 18 us: shards(): came = lax.all_to_all(parts, PLANE, 0, 0)]
    unnamed x22 -> x56, local copies, waits for them, and re-layouts: 3.32 us -> 30.4 us
    ppermute x0 -> x4, starting transfers between devices: none -> 10.2 us  [shifted(): lax.ppermute(value, axis, [(source, source + steps) for source in range(f...]
    all_to_all x2 -> x3, starting transfers between devices: 10.3 us -> 18.7 us  [the longest x1 7.3 us: shards(): rims = lax.all_to_all(rims, ALL, 0, 0)]
    pallas_call x6 -> x7, Pallas kernels: 27.1 us -> 22.5 us  [call(): pl.pallas_call(kernel, out_shape=[jax.ShapeDtypeStruct(shape, dtype) for...]
    all_to_all x2 -> x3, waiting for transfers between devices: 10.4 us -> 8.2 us  [the longest x1 5.48 us: shards(): came = lax.all_to_all(parts, ALL, 0, 0)]
  transfers between devices with their start and end apart: 2 -> 7, of which waited for: 2 -> 3; matrix products, arithmetic and copies ran while one was open for 0% -> 2% of each run, Pallas kernels for 0% -> 7%
where the time goes in v3:
time: 95.1 us; the launch traced here: 93.9 us
  local copies, waits for them, and re-layouts  30.5 us (32%)
  starting transfers between devices  28.8 us (30%)
  Pallas kernels  22.5 us (24%)
  waiting for transfers between devices  9.01 us (9%)
  other arithmetic  1.56 us (2%)
  between operations  1.46 us (2%)
    unnamed x56, local copies, waits for them, and re-layouts  30.4 us
    pallas_call x7, Pallas kernels, call(): pl.pallas_call(kernel, out_shape=[jax.ShapeDtypeStruct(shape, dtype) for...  22.5 us
    ppermute x4, starting transfers between devices, shifted(): lax.ppermute(value, axis, [(source, source + steps) for source in range(f...  10.2 us
    all_to_all x1, starting transfers between devices, shards(): rims = lax.all_to_all(rims, ALL, 0, 0)  7.3 us
    all_to_all x1, starting transfers between devices, shards(): came = lax.all_to_all(packed.reshape(devices, share, width), ALL, 0, 0)  5.83 us
    all_to_all x1, starting transfers between devices, shards(): came = lax.all_to_all(parts, ALL, 0, 0)  5.54 us
    all_to_all x1, waiting for transfers between devices, shards(): came = lax.all_to_all(parts, ALL, 0, 0)  5.48 us
    all_to_all x1, waiting for transfers between devices, shards(): came = lax.all_to_all(packed.reshape(devices, share, width), ALL, 0, 0)  2.72 us
  transfers between devices with their start and end apart: 7, of which 3 were waited for; matrix products, arithmetic and copies ran while one was open for 2% of the time, Pallas kernels for 7%

profile of v3, /device:TPU:0, one launch (start us, length us, event | category | flops | bytes accessed | tf_op | source)
XLA Modules:
  0.0 93.9 jit_solution(12169182927444316248)
XLA Ops:
  2.3 7.3 %all-to-all-start = ((bf16[32,32,128]{2,1,0:T(8,128)(2,1)}), bf16[32,32,128]{2,1,0:T(8,128)(2,1)S(1)}, u32[]{:S(2)}, u32[]{:S(2)}) async-start(bf16[32,32,128]{2,1,0:T(8,128)(2,1)} %shard_map.162), calls=%async_computation | async-start | bytes 524288 | tf_op jit(solution)/shard_map/all_to_all | solution.py:316
  12.0 1.2 %copy-done.4 = bf16[4096,128]{1,0:T(8,128)(2,1)S(1)} copy-done((bf16[4096,128]{1,0:T(8,128)(2,1)S(1)}, bf16[4096,128]{1,0:T(8,128)(2,1)}, u32[]{:S(2)}) %copy-start.4) | copy-done | bytes 1048600
  14.9 5.4 %shard_map.163 = (bf16[4096,512]{1,0:T(8,128)(2,1)S(1)}, bf16[4096,256]{1,0:T(8,128)(2,1)S(1)}, bf16[8,512,512]{2,1,0:T(8,128)(2,1)S(1)}, bf16[8,256,512]{2,1,0:...) custom-call(bf16[256,128]{1,0:T(8,128)(2,1)S(1)} %copy-done.17, ...), custom_call_target="tpu_custom_call" | custom-call | tf_op jit(solution)/shard_map/pallas_call | solution.py:51
  20.3 2.0 %copy-done = bf16[4096,512]{1,0:T(8,128)(2,1)} copy-done((bf16[4096,512]{1,0:T(8,128)(2,1)}, bf16[4096,512]{1,0:T(8,128)(2,1)S(1)}, u32[]{:S(2)}) %copy-start) | copy-done | bytes 4194328
  22.3 2.0 %copy-done.2 = bf16[8,512,512]{2,1,0:T(8,128)(2,1)} copy-done((bf16[8,512,512]{2,1,0:T(8,128)(2,1)}, bf16[8,512,512]{2,1,0:T(8,128)(2,1)S(1)}, u32[]{:S(2)}) %copy-start.2) | copy-done | bytes 4194328
  24.3 1.4 %copy-done.6 = bf16[8,256,512]{2,1,0:T(8,128)(2,1)} copy-done((bf16[8,256,512]{2,1,0:T(8,128)(2,1)}, bf16[8,256,512]{2,1,0:T(8,128)(2,1)S(1)}, u32[]{:S(2)}) %copy-start.6) | copy-done | bytes 2097176
  25.7 1.4 %copy-done.8 = f32[4096,128]{1,0:T(8,128)} copy-done((f32[4096,128]{1,0:T(8,128)}, f32[4096,128]{1,0:T(8,128)S(1)}, u32[]{:S(2)}) %copy-start.8) | copy-done | bytes 2097176
  27.1 1.0 %copy-done.11 = bf16[8,128,512]{2,1,0:T(8,128)(2,1)} copy-done((bf16[8,128,512]{2,1,0:T(8,128)(2,1)}, bf16[8,128,512]{2,1,0:T(8,128)(2,1)S(1)}, u32[]{:S(2)}) %copy-start.11) | copy-done | bytes 1048600
  28.2 2.2 %copy-done.1 = bf16[4096,512]{1,0:T(8,128)(2,1)S(1)} copy-done((bf16[4096,512]{1,0:T(8,128)(2,1)S(1)}, bf16[4096,512]{1,0:T(8,128)(2,1)}, u32[]{:S(2)}) %copy-start.1) | copy-done | bytes 4194328
  30.3 2.2 %copy-done.3 = bf16[8,512,512]{2,1,0:T(8,128)(2,1)S(1)} copy-done((bf16[8,512,512]{2,1,0:T(8,128)(2,1)S(1)}, bf16[8,512,512]{2,1,0:T(8,128)(2,1)}, u32[]{:S(2)}) %copy-start.3) | copy-done | bytes 4194328
  32.5 1.6 %copy-done.7 = bf16[8,256,512]{2,1,0:T(8,128)(2,1)S(1)} copy-done((bf16[8,256,512]{2,1,0:T(8,128)(2,1)S(1)}, bf16[8,256,512]{2,1,0:T(8,128)(2,1)}, u32[]{:S(2)}) %copy-start.7) | copy-done | bytes 2097176
  34.1 1.6 %copy-done.9 = f32[4096,128]{1,0:T(8,128)S(1)} copy-done((f32[4096,128]{1,0:T(8,128)S(1)}, f32[4096,128]{1,0:T(8,128)}, u32[]{:S(2)}) %copy-start.9) | copy-done | bytes 2097176
  35.7 1.2 %copy-done.10 = bf16[4096,128]{1,0:T(8,128)(2,1)S(1)} copy-done((bf16[4096,128]{1,0:T(8,128)(2,1)S(1)}, bf16[4096,128]{1,0:T(8,128)(2,1)}, u32[]{:S(2)}) %copy-start.10) | copy-done | bytes 1048600
  36.9 1.2 %copy-done.12 = bf16[8,128,512]{2,1,0:T(8,128)(2,1)S(1)} copy-done((bf16[8,128,512]{2,1,0:T(8,128)(2,1)S(1)}, bf16[8,128,512]{2,1,0:T(8,128)(2,1)}, u32[]{:S(2)}) %copy-start.12) | copy-done | bytes 1048600
  43.1 14.5 %shard_map.164 = (bf16[256,128]{1,0:T(8,128)(2,1)}, bf16[4096,128]{1,0:T(8,128)(2,1)}, f32[256,128]{1,0:T(8,128)S(1)}, bf16[1024,128]{1,0:T(8,128)(2,1)S(1)}, bf16[768,128]{1,0:T(8,128)(2,1)S(1)}) custom-call(s32[5]{0:T(128)S(1)} %stack.11.place, bf16[256,128]{1,0:T(8,128)(2,1)S(1)} %copy-done.18, bf16[32,32,128]{2,1,0:T(8,128)(2,1)S(1)} %all-to-all-done.rims, ...), custom_call_target="tpu_custom_call" | custom-call | tf_op jit(solution)/shard_map/pallas_call | solution.py:51
  59.7 5.8 %all-to-all-start.1 = ((bf16[32,32,128]{2,1,0:T(8,128)(2,1)}), bf16[32,32,128]{2,1,0:T(8,128)(2,1)S(1)}, u32[]{:S(2)}, u32[]{:S(2)}) async-start(bf16[32,32,128]{2,1,0:T(8,128)(2,1)} %bitcast.7), calls=%async_computation.1 | async-start | bytes 524288 | tf_op jit(solution)/shard_map/all_to_all | solution.py:390
  65.5 0.9 copy-done.21
  67.6 1.3 %collective-permute-start = (bf16[3,32,128]{2,1,0:T(8,128)(2,1)S(1)}, bf16[3,32,128]{2,1,0:T(8,128)(2,1)S(1)}, u32[]{:S(2)}, u32[]{:S(2)}) collective-permute-start(bf16[3,32,128]{2,1,0:T(8,128)(2,1)S(1)} %get-tuple-element.45), channel_id=1, source_target_pairs={{1,0},{2,1},{3,2},{4,3},{5,4},{6,5},{7,6},{9,8},{10,9},{11,10},{12... | collective-permute-start | bytes 73736 | tf_op jit(solution)/shard_map/ppermute | solution.py:289
  68.9 4.5 %collective-permute-start.1 = (bf16[3,32,128]{2,1,0:T(8,128)(2,1)S(1)}, bf16[3,32,128]{2,1,0:T(8,128)(2,1)S(1)}, u32[]{:S(2)}, u32[]{:S(2)}) collective-permute-start(bf16[3,32,128]{2,1,0:T(8,128)(2,1)S(1)} %get-tuple-element.46), channel_id=1, source_target_pairs={{0,1},{1,2},{2,3},{3,4},{4,5},{5,6},{6,7},{8,9},{9,10},{10,11},{11... | collective-permute-start | bytes 73736 | tf_op jit(solution)/shard_map/ppermute | solution.py:289
  73.4 2.7 %all-to-all-done.1.came = bf16[32,32,128]{2,1,0:T(8,128)(2,1)S(1)} async-done(((bf16[32,32,128]{2,1,0:T(8,128)(2,1)}), bf16[32,32,128]{2,1,0:T(8,128)(2,1)S(1)}, u32[]{:S(2)}, u32[]{:S(2)}) %all-to-all-start.1) | async-done | bytes 262176 | tf_op jit(solution)/shard_map/all_to_all | solution.py:390
  76.9 5.5 %all-to-all-start.2 = ((bf16[32,32,128]{2,1,0:T(8,128)(2,1)}), bf16[32,32,128]{2,1,0:T(8,128)(2,1)S(1)}, u32[]{:S(2)}, u32[]{:S(2)}) async-start(bf16[32,32,128]{2,1,0:T(8,128)(2,1)} %shard_map.165), calls=%async_computation.2 | async-start | bytes 524288 | tf_op jit(solution)/shard_map/all_to_all | solution.py:408
  82.5 1.3 %collective-permute-start.2 = (bf16[32,128]{1,0:T(8,128)(2,1)S(1)}, bf16[32,128]{1,0:T(8,128)(2,1)S(1)}, u32[]{:S(2)}, u32[]{:S(2)}) collective-permute-start(bf16[32,128]{1,0:T(8,128)(2,1)S(1)} %get-tuple-element.54), channel_id=1, source_target_pairs={{8,0},{16,8},{24,16},{9,1},{17,9},{25,17},{10,2},{18,10},{26,18},{... | collective-permute-start | bytes 24584 | tf_op jit(solution)/shard_map/ppermute | solution.py:289
  83.8 3.0 %collective-permute-start.3 = (bf16[32,128]{1,0:T(8,128)(2,1)S(1)}, bf16[32,128]{1,0:T(8,128)(2,1)S(1)}, u32[]{:S(2)}, u32[]{:S(2)}) collective-permute-start(bf16[32,128]{1,0:T(8,128)(2,1)S(1)} %get-tuple-element.55), channel_id=1, source_target_pairs={{0,8},{8,16},{16,24},{1,9},{9,17},{17,25},{2,10},{10,18},{18,26},{... | collective-permute-start | bytes 24584 | tf_op jit(solution)/shard_map/ppermute | solution.py:289
  87.6 5.5 %all-to-all-done.2 = bf16[32,32,128]{2,1,0:T(8,128)(2,1)S(1)} async-done(((bf16[32,32,128]{2,1,0:T(8,128)(2,1)}), bf16[32,32,128]{2,1,0:T(8,128)(2,1)S(1)}, u32[]{:S(2)}, u32[]{:S(2)}) %all-to-all-start.2) | async-done | bytes 262176 | tf_op jit(solution)/shard_map/all_to_all | solution.py:408
  (58 shorter events, 15.6 us)
Async XLA Ops:
  0.6 27.5 %copy-start.5 = (bf16[4096,128]{1,0:T(8,128)(2,1)S(1)}, bf16[4096,128]{1,0:T(8,128)(2,1)}, u32[]{:S(2)}) copy-start(bf16[4096,128]{1,0:T(8,128)(2,1)} %edges.3) | copy-start | bytes 3145732
  0.6 0.9 copy-start.16
  2.3 25.8 %all-to-all-start = ((bf16[32,32,128]{2,1,0:T(8,128)(2,1)}), bf16[32,32,128]{2,1,0:T(8,128)(2,1)S(1)}, u32[]{:S(2)}, u32[]{:S(2)}) async-start(bf16[32,32,128]{2,1,0:T(8,128)(2,1)} %shard_map.162), calls=%async_computation | async-start | bytes 524288 | tf_op jit(solution)/shard_map/all_to_all | solution.py:316
  11.9 1.2 %copy-start.4 = (bf16[4096,128]{1,0:T(8,128)(2,1)S(1)}, bf16[4096,128]{1,0:T(8,128)(2,1)}, u32[]{:S(2)}) copy-start(bf16[4096,128]{1,0:T(8,128)(2,1)} %edges.3) | copy-start | bytes 3145732
  20.3 2.0 %copy-start = (bf16[4096,512]{1,0:T(8,128)(2,1)}, bf16[4096,512]{1,0:T(8,128)(2,1)S(1)}, u32[]{:S(2)}) copy-start(bf16[4096,512]{1,0:T(8,128)(2,1)S(1)} %get-tuple-element.34.send_hot) | copy-start | bytes 12582916
  22.3 2.0 %copy-start.2 = (bf16[8,512,512]{2,1,0:T(8,128)(2,1)}, bf16[8,512,512]{2,1,0:T(8,128)(2,1)S(1)}, u32[]{:S(2)}) copy-start(bf16[8,512,512]{2,1,0:T(8,128)(2,1)S(1)} %get-tuple-element.36.send_hot_t) | copy-start | bytes 12582916
  24.3 1.4 %copy-start.6 = (bf16[8,256,512]{2,1,0:T(8,128)(2,1)}, bf16[8,256,512]{2,1,0:T(8,128)(2,1)S(1)}, u32[]{:S(2)}) copy-start(bf16[8,256,512]{2,1,0:T(8,128)(2,1)S(1)} %get-tuple-element.37.recv_hot_t) | copy-start | bytes 6291460
  25.7 1.4 %copy-start.8 = (f32[4096,128]{1,0:T(8,128)}, f32[4096,128]{1,0:T(8,128)S(1)}, u32[]{:S(2)}) copy-start(f32[4096,128]{1,0:T(8,128)S(1)} %get-tuple-element.39.pre_part) | copy-start | bytes 6291460
  27.1 1.0 %copy-start.11 = (bf16[8,128,512]{2,1,0:T(8,128)(2,1)}, bf16[8,128,512]{2,1,0:T(8,128)(2,1)S(1)}, u32[]{:S(2)}) copy-start(bf16[8,128,512]{2,1,0:T(8,128)(2,1)S(1)} %get-tuple-element.38.edges_t) | copy-start | bytes 3145732
  28.2 2.2 %copy-start.1 = (bf16[4096,512]{1,0:T(8,128)(2,1)S(1)}, bf16[4096,512]{1,0:T(8,128)(2,1)}, u32[]{:S(2)}) copy-start(bf16[4096,512]{1,0:T(8,128)(2,1)} %copy-done) | copy-start | bytes 12582916
  30.3 2.2 %copy-start.3 = (bf16[8,512,512]{2,1,0:T(8,128)(2,1)S(1)}, bf16[8,512,512]{2,1,0:T(8,128)(2,1)}, u32[]{:S(2)}) copy-start(bf16[8,512,512]{2,1,0:T(8,128)(2,1)} %copy-done.2) | copy-start | bytes 12582916
  32.5 1.6 %copy-start.7 = (bf16[8,256,512]{2,1,0:T(8,128)(2,1)S(1)}, bf16[8,256,512]{2,1,0:T(8,128)(2,1)}, u32[]{:S(2)}) copy-start(bf16[8,256,512]{2,1,0:T(8,128)(2,1)} %copy-done.6) | copy-start | bytes 6291460
  34.1 1.6 %copy-start.9 = (f32[4096,128]{1,0:T(8,128)S(1)}, f32[4096,128]{1,0:T(8,128)}, u32[]{:S(2)}) copy-start(f32[4096,128]{1,0:T(8,128)} %copy-done.8) | copy-start | bytes 6291460
  35.7 1.2 %copy-start.10 = (bf16[4096,128]{1,0:T(8,128)(2,1)S(1)}, bf16[4096,128]{1,0:T(8,128)(2,1)}, u32[]{:S(2)}) copy-start(bf16[4096,128]{1,0:T(8,128)(2,1)} %edge_cot.1) | copy-start | bytes 3145732
  36.9 1.2 %copy-start.12 = (bf16[8,128,512]{2,1,0:T(8,128)(2,1)S(1)}, bf16[8,128,512]{2,1,0:T(8,128)(2,1)}, u32[]{:S(2)}) copy-start(bf16[8,128,512]{2,1,0:T(8,128)(2,1)} %copy-done.11) | copy-start | bytes 3145732
  43.1 22.4 %copy-start.15 = (bf16[384,128]{1,0:T(8,128)(2,1)S(1)}, bf16[384,128]{1,0:T(8,128)(2,1)}, u32[]{:S(2)}) copy-start(bf16[384,128]{1,0:T(8,128)(2,1)} %w_edge_in.5) | copy-start | bytes 294916
  59.7 16.5 %all-to-all-start.1 = ((bf16[32,32,128]{2,1,0:T(8,128)(2,1)}), bf16[32,32,128]{2,1,0:T(8,128)(2,1)S(1)}, u32[]{:S(2)}, u32[]{:S(2)}) async-start(bf16[32,32,128]{2,1,0:T(8,128)(2,1)} %bitcast.7), calls=%async_computation.1 | async-start | bytes 524288 | tf_op jit(solution)/shard_map/all_to_all | solution.py:390
  65.5 0.9 copy-start.21
  66.5 0.9 copy-start.23
  67.6 9.3 %collective-permute-start = (bf16[3,32,128]{2,1,0:T(8,128)(2,1)S(1)}, bf16[3,32,128]{2,1,0:T(8,128)(2,1)S(1)}, u32[]{:S(2)}, u32[]{:S(2)}) collective-permute-start(bf16[3,32,128]{2,1,0:T(8,128)(2,1)S(1)} %get-tuple-element.45), channel_id=1, source_target_pairs={{1,0},{2,1},{3,2},{4,3},{5,4},{6,5},{7,6},{9,8},{10,9},{11,10},{12... | collective-permute-start | bytes 73736 | tf_op jit(solution)/shard_map/ppermute | solution.py:289
  68.9 8.0 %collective-permute-start.1 = (bf16[3,32,128]{2,1,0:T(8,128)(2,1)S(1)}, bf16[3,32,128]{2,1,0:T(8,128)(2,1)S(1)}, u32[]{:S(2)}, u32[]{:S(2)}) collective-permute-start(bf16[3,32,128]{2,1,0:T(8,128)(2,1)S(1)} %get-tuple-element.46), channel_id=1, source_target_pairs={{0,1},{1,2},{2,3},{3,4},{4,5},{5,6},{6,7},{8,9},{9,10},{10,11},{11... | collective-permute-start | bytes 73736 | tf_op jit(solution)/shard_map/ppermute | solution.py:289
  76.9 16.2 %all-to-all-start.2 = ((bf16[32,32,128]{2,1,0:T(8,128)(2,1)}), bf16[32,32,128]{2,1,0:T(8,128)(2,1)S(1)}, u32[]{:S(2)}, u32[]{:S(2)}) async-start(bf16[32,32,128]{2,1,0:T(8,128)(2,1)} %shard_map.165), calls=%async_computation.2 | async-start | bytes 524288 | tf_op jit(solution)/shard_map/all_to_all | solution.py:408
  82.5 4.3 %collective-permute-start.2 = (bf16[32,128]{1,0:T(8,128)(2,1)S(1)}, bf16[32,128]{1,0:T(8,128)(2,1)S(1)}, u32[]{:S(2)}, u32[]{:S(2)}) collective-permute-start(bf16[32,128]{1,0:T(8,128)(2,1)S(1)} %get-tuple-element.54), channel_id=1, source_target_pairs={{8,0},{16,8},{24,16},{9,1},{17,9},{25,17},{10,2},{18,10},{26,18},{... | collective-permute-start | bytes 24584 | tf_op jit(solution)/shard_map/ppermute | solution.py:289
  83.8 3.8 %collective-permute-start.3 = (bf16[32,128]{1,0:T(8,128)(2,1)S(1)}, bf16[32,128]{1,0:T(8,128)(2,1)S(1)}, u32[]{:S(2)}, u32[]{:S(2)}) collective-permute-start(bf16[32,128]{1,0:T(8,128)(2,1)S(1)} %get-tuple-element.55), channel_id=1, source_target_pairs={{0,8},{8,16},{16,24},{1,9},{9,17},{17,25},{2,10},{10,18},{18,26},{... | collective-permute-start | bytes 24584 | tf_op jit(solution)/shard_map/ppermute | solution.py:289
  (11 other events, 8.7 us)

commit v4 on v2

v4 whole, which is shorter than its diff:
```python
import functools
import math

import jax
import jax.numpy as jnp
from jax import lax
from jax.experimental import pallas as pl
from jax.experimental.pallas import tpu as pltpu
from jax.sharding import Mesh
from jax.sharding import PartitionSpec as P

EPS = 1e-05
CHUNK = 1024
PLANE = ("strip", "y")
ALL = ("strip", "z", "y")
F32 = jnp.float32
BF16 = jnp.bfloat16
VMEM = pl.BlockSpec(memory_space=pltpu.VMEM)
SMEM = pl.BlockSpec(memory_space=pltpu.SMEM)
HBM = pl.BlockSpec(memory_space=pltpu.HBM)
SEM = pltpu.SemaphoreType.DMA


def mm(left, right):
    return jnp.dot(left, right, preferred_element_type=F32)


def mm_nt(left, right):
    return lax.dot_general(left, right, (((1,), (1,)), ((), ())), preferred_element_type=F32)


def mm_tn(left, right):
    return lax.dot_general(left, right, (((0,), (0,)), ((), ())), preferred_element_type=F32)


def norm_rows(values):
    centre = values - jnp.mean(values, axis=1, keepdims=True)
    scale = lax.rsqrt(jnp.mean(centre * centre, axis=1, keepdims=True) + EPS)
    return (centre * scale, scale)


def norm_back(normed, scale, upstream):
    first = jnp.mean(upstream, axis=1, keepdims=True)
    second = jnp.mean(upstream * normed, axis=1, keepdims=True)
    return scale * (upstream - first - normed * second)


def silu_and_slope(values):
    sig = 0.5 + 0.5 * jnp.tanh(0.5 * values)
    act = values * sig
    return (act, sig + act * (1.0 - sig))


def in_hbm(value):
    return pltpu.with_memory_space_constraint(value, pltpu.HBM)


def call(kernel, outs, ins, specs, scratch=(), out_specs=None, limit=24):
    out_specs = [VMEM] * len(outs) if out_specs is None else out_specs
    return pl.pallas_call(
        kernel,
        out_shape=[
            pltpu.HBM(shape, dtype) if spec is HBM else jax.ShapeDtypeStruct(shape, dtype)
            for (shape, dtype), spec in zip(outs, out_specs)
        ],
        in_specs=specs,
        out_specs=out_specs,
        scratch_shapes=list(scratch),
        compiler_params=pltpu.CompilerParams(vmem_limit_bytes=limit * 2**20),
    )(*[in_hbm(value) if spec is HBM else value for value, spec in zip(ins, specs)])


def rim_kernel(nodes, out, sems):
    border = out.shape[1]
    copies = [
        pltpu.make_async_copy(nodes.at[pl.ds(0, border)], out.at[target], sems.at[target])
        for target in range(out.shape[0])
    ]
    for copy in copies:
        copy.start()
    for copy in copies:
        copy.wait()


def early_kernel(
    nodes,
    edges,
    info,
    w_edge_in,
    send_hot,
    recv_hot,
    send_hot_t,
    recv_hot_t,
    edges_t,
    pre_part,
    tables,
):
    count_p, width = nodes.shape
    chunk = edges.shape[0]
    send_rows = send_hot.shape[1]

    @pl.when(pl.program_id(0) == 0)
    def prepare():
        tables[:count_p] = mm(nodes[...], w_edge_in[width : 2 * width]).astype(BF16)
        tables[count_p:] = w_edge_in[2 * width :]

    lane = lax.broadcasted_iota(jnp.int32, (chunk, width), 1)

    def hot(column, blocks):
        found = [(column == lane + width * k).astype(F32).astype(BF16) for k in range(blocks)]
        return jnp.concatenate(found, axis=1)

    def hot_t(line, size):
        place_of = lax.broadcasted_iota(jnp.int32, (size, chunk), 0)
        return (place_of == line).astype(F32).astype(BF16)

    index = info[0]
    columns = index.T
    edge = edges[...]
    recv = hot(columns[:, 1:2], count_p // width)
    pre_part[...] = mm(jnp.concatenate([recv, edge], axis=1), tables[...])
    recv_hot[...] = recv
    send_hot[...] = hot(columns[:, 0:1], send_rows // width)
    send_hot_t[0] = hot_t(index[0:1], send_rows)
    recv_hot_t[0] = hot_t(index[1:2], count_p)
    edges_t[0] = edge.T


def layer_kernel(
    place,
    nodes_in,
    rims_in,
    far_rims_in,
    edges_in,
    send_hot_in,
    recv_hot_in,
    send_hot_t_in,
    recv_hot_t_in,
    edges_t_in,
    pre_part_in,
    w_edge_in_in,
    w_edge_out_in,
    w_node_in_in,
    w_node_out_in,
    node_cot_in,
    edge_cot_in,
    new_nodes_out,
    new_edges_out,
    local_grad_out,
    parts,
    nodes,
    rims,
    edges,
    send_hot,
    recv_hot,
    send_hot_t,
    recv_hot_t,
    edges_t,
    pre_part,
    w_edge_in,
    w_edge_out,
    w_node_in,
    w_node_out,
    node_cot,
    edge_cot,
    new_nodes,
    new_edges,
    local_grad,
    table,
    tables,
    spread,
    means,
    hidden,
    slope,
    normed,
    scale,
    sums,
    ge_edge,
    ge_out,
    agg,
    packed,
    small_sems,
    sems,
    out_sems,
    last_sems,
):
    count_p, width = nodes.shape
    border = rims.shape[1]
    slots = parts.shape[0]
    strips = slots // 2
    chunks, _, chunk = recv_hot_t.shape
    share = parts.shape[1] - 2 * border
    my_strip, my_y, live_count = place[0], place[2], place[3]

    small = [
        pltpu.make_async_copy(source, target, small_sems.at[k])
        for k, (source, target) in enumerate(
            [
                (nodes_in, nodes),
                (rims_in, rims.at[pl.ds(0, slots)]),
                (far_rims_in, rims.at[pl.ds(slots, slots)]),
                (w_edge_in_in, w_edge_in),
                (w_edge_out_in, w_edge_out),
                (w_node_in_in, w_node_in),
                (w_node_out_in, w_node_out),
                (node_cot_in, node_cot),
            ]
        )
    ]

    def span(step):
        return pl.ds(pl.multiple_of(step * chunk, chunk), chunk)

    def fetch(step, which):
        rows = span(step)
        pairs = [
            (pre_part_in.at[rows], pre_part.at[rows]),
            (send_hot_in.at[rows], send_hot.at[rows]),
            (edges_in.at[rows], edges.at[rows]),
            (recv_hot_t_in.at[step], recv_hot_t.at[step]),
            (recv_hot_in.at[rows], recv_hot.at[rows]),
            (edge_cot_in.at[rows], edge_cot.at[rows]),
            (send_hot_t_in.at[step], send_hot_t.at[step]),
            (edges_t_in.at[step], edges_t.at[step]),
        ]
        return [
            pltpu.make_async_copy(*pairs[k], sems.at[k, step]) for k in which
        ]

    def emit(step):
        rows = span(step)
        return pltpu.make_async_copy(
            new_edges.at[rows], new_edges_out.at[rows], out_sems.at[step]
        )

    ahead, back = range(4), range(4, 8)
    for copy in small[:5] + fetch(0, ahead) + small[5:]:
        copy.start()
    for step in range(1, chunks):
        for copy in fetch(step, ahead):
            copy.start()
    for step in range(chunks):
        for copy in fetch(step, back):
            copy.start()
    for copy in small[:5]:
        copy.wait()

    table[:count_p] = nodes[...]
    spot = 0
    for d_strip in (-1, 0, 1):
        strip = jnp.clip(my_strip + d_strip, 0, strips - 1)
        for d_sub in (-1, 0, 1):
            if d_strip == 0 and d_sub == 0:
                continue
            if d_sub == 0:
                slot = 2 * strip + my_y
            elif d_sub == 1:
                slot = my_y * slots + 2 * strip + 1
            else:
                slot = (1 - my_y) * slots + 2 * strip
            rows = slice(count_p + spot * border, count_p + (spot + 1) * border)
            table[rows] = rims[slot]
            spot += 1
    send_rows = table.shape[0]
    tables[...] = mm(table[...], w_edge_in[:width]).astype(BF16)
    spread[:, :width] = w_edge_out[...]
    spread[:, width:] = jnp.broadcast_to(
        jnp.mean(w_edge_out[...].astype(F32), axis=1, keepdims=True), (width, width)
    ).astype(BF16)
    high = lax.broadcasted_iota(jnp.int32, (2 * width, 2 * width), 0) >= width
    wide = lax.broadcasted_iota(jnp.int32, (2 * width, 2 * width), 1) >= width
    means[...] = jnp.where(high == wide, 1.0 / width, 0.0).astype(BF16)

    row = lax.broadcasted_iota(jnp.int32, (chunk, width), 0)
    agg[...] = jnp.zeros_like(agg)

    def forward(step, carry):
        rows = span(step)
        for copy in fetch(step, ahead):
            copy.wait()
        begun = pre_part[rows]
        hot = send_hot[rows]
        hot_t = recv_hot_t[step]
        edge = edges[rows].astype(F32)
        so_far = agg[...]
        act, bend = silu_and_slope(begun + mm(hot, tables[...]))
        act = act.astype(BF16)
        outer = mm(act, spread[...])
        centre = outer[:, :width] - outer[:, width:]
        spare = mm((centre * centre).astype(BF16), means[:width, :width])
        factor = jnp.where(row < live_count - step * chunk, lax.rsqrt(spare + EPS), 0.0)
        unit = centre * factor
        so_far = so_far + mm(hot_t, unit.astype(BF16))
        slope[rows] = bend
        hidden[rows] = act
        scale[rows] = factor
        normed[rows] = unit
        new_edges[rows] = (edge + unit).astype(BF16)
        agg[...] = so_far
        emit(step).start()
        return carry

    lax.fori_loop(0, chunks, forward, 0)

    for copy in small[5:]:
        copy.wait()
    joined = jnp.concatenate([nodes[...], agg[...].astype(BF16)], axis=1)
    node_pre = mm(joined, w_node_in[...])
    node_act, node_slope = silu_and_slope(node_pre)
    node_act = node_act.astype(BF16)
    node_unit, node_scale = norm_rows(mm(node_act, w_node_out[...]))
    new_nodes[...] = (nodes[...].astype(F32) + node_unit).astype(BF16)
    cot = node_cot[...].astype(F32)
    d_outer = norm_back(node_unit, node_scale, cot).astype(BF16)
    d_pre = (mm_nt(d_outer, w_node_out[...]) * node_slope).astype(BF16)
    d_joined = mm_nt(d_pre, w_node_in[...])
    d_agg = d_joined[:, width:].astype(BF16)
    agg[...] = cot + d_joined[:, :width]
    packed[4 * width : 6 * width] = mm_tn(joined, d_pre).astype(BF16)
    packed[6 * width : 7 * width] = mm_tn(node_act, d_outer).astype(BF16)
    node_copy = pltpu.make_async_copy(new_nodes, new_nodes_out, last_sems.at[0])
    node_copy.start()

    sums[...] = jnp.zeros_like(sums)
    ge_edge[...] = jnp.zeros_like(ge_edge)
    ge_out[...] = jnp.zeros_like(ge_out)

    def backward(step, carry):
        rows = span(step)
        for copy in fetch(step, back):
            copy.wait()
        cot = edge_cot[rows].astype(F32)
        hot = recv_hot[rows]
        unit = normed[rows]
        factor = scale[rows]
        bend = slope[rows]
        act = hidden[rows]
        edge_t = edges_t[step]
        send_t = send_hot_t[step]
        recv_t = recv_hot_t[step]
        upstream = cot + mm(hot, d_agg)
        both = jnp.concatenate([upstream.astype(BF16), (upstream * unit).astype(BF16)], axis=1)
        both = mm(both, means[...])
        d_out = factor * (upstream - both[:, :width] - unit * both[:, width:])
        d_out = d_out.astype(BF16)
        d_in = (mm_nt(d_out, w_edge_out[...]) * bend).astype(BF16)
        ge_out[...] += mm_tn(act, d_out)
        sums[:send_rows] += mm(send_t, d_in)
        sums[send_rows:] += mm(recv_t, d_in)
        ge_edge[...] += mm(edge_t, d_in)
        return carry

    lax.fori_loop(0, chunks, backward, 0)

    send_sums = sums[:send_rows].astype(BF16)
    recv_sums = sums[send_rows:].astype(BF16)
    packed[:width] = mm_tn(table[...], send_sums).astype(BF16)
    packed[width : 2 * width] = mm_tn(nodes[...], recv_sums).astype(BF16)
    packed[2 * width : 3 * width] = ge_edge[...].astype(BF16)
    packed[3 * width : 4 * width] = ge_out[...].astype(BF16)
    if packed.shape[0] > 7 * width:
        packed[7 * width :] = jnp.zeros((packed.shape[0] - 7 * width, width), BF16)
    sent = mm_nt(send_sums, w_edge_in[:width])
    local_grad[...] = agg[...] + sent[:count_p] + mm_nt(recv_sums, w_edge_in[width : 2 * width])
    grad_copy = pltpu.make_async_copy(local_grad, local_grad_out, last_sems.at[1])
    grad_copy.start()
    owed = sent[count_p:].astype(BF16)
    for slot in range(slots):
        parts[slot, :share] = packed[slot * share : (slot + 1) * share]
        parts[slot, share:] = jnp.zeros((2 * border, width), BF16)
    spot = 0
    for d_strip in (-1, 0, 1):
        strip = my_strip + d_strip
        for d_sub in (-1, 0, 1):
            if d_strip == 0 and d_sub == 0:
                continue
            if d_sub == 0:
                slot, part = 2 * strip + my_y, 0
            elif d_sub == 1:
                slot, part = 2 * strip + 1 - my_y, my_y
            else:
                slot, part = 2 * strip + 1 - my_y, 1 - my_y
            first = pl.multiple_of(share + part * border, 16)
            block = owed[spot * border : (spot + 1) * border]

            @pl.when((strip >= 0) & (strip < strips))
            def put(slot=slot, first=first, block=block):
                parts[slot, pl.ds(first, border), :] = block

            spot += 1
    for step in range(chunks):
        emit(step).wait()
    node_copy.wait()
    grad_copy.wait()


def plane_sum_kernel(place, came, out, mine):
    border = mine.shape[0]
    zs = out.shape[0]
    share = out.shape[1] - border
    total = came[0].astype(F32)
    for slot in range(1, came.shape[0]):
        total = total + came[slot].astype(F32)
    share_total = total[:share].astype(BF16)
    mine[...] = total[share : share + border]
    beyond = total[share + border :].astype(BF16)
    for target in range(zs):
        out[target, :share] = share_total
        out[target, share:] = jnp.zeros_like(beyond)
    target = place[1] + 1 - 2 * place[2]

    @pl.when((target >= 0) & (target < zs))
    def put():
        out[target, share:] = beyond


def line_sum_kernel(factor, came, mine, out, rim_grad):
    share = out.shape[1]
    total = came[0].astype(F32)
    for slot in range(1, came.shape[0]):
        total = total + came[slot].astype(F32)
    share_total = (total[:share] * factor).astype(BF16)
    for target in range(out.shape[0]):
        out[target] = share_total
    rim_grad[...] = mine[...] + total[share:]


def finish_kernel(came, rim_grad, local_grad_in, *refs):
    outs, (local_grad, grads, in_sem, sems) = refs[:-4], refs[-4:]
    border = rim_grad.shape[0]
    slots, share, _ = came.shape
    fetch = pltpu.make_async_copy(local_grad_in, local_grad, in_sem)
    fetch.start()
    for slot in range(slots):
        grads[slot * share : (slot + 1) * share] = came[slot].astype(F32)
    copies = []
    start = 0
    for k, out in enumerate(outs[1:]):
        size = out.shape[0]
        copies.append(pltpu.make_async_copy(grads.at[pl.ds(start, size)], out, sems.at[k]))
        copies[-1].start()
        start += size
    fetch.wait()
    local_grad[:border] += rim_grad[...]
    copies.append(pltpu.make_async_copy(local_grad, outs[0], sems.at[len(outs) - 1]))
    copies[-1].start()
    for copy in copies:
        copy.wait()


def shards(
    node_latents,
    edge_latents,
    senders,
    receivers,
    edge_count,
    w_edge_in,
    w_edge_out,
    w_node_in,
    w_node_out,
    node_cotangent,
    edge_cotangent,
):
    count_p, width = node_latents.shape
    count_e = edge_latents.shape[0]
    border = count_p // 8
    strips, zs, ys = (lax.axis_size(axis) for axis in ALL)
    subs = zs * ys
    slots = strips * ys
    my_strip, my_z, my_y = (lax.axis_index(axis).astype(jnp.int32) for axis in ALL)
    my_sub = my_z * ys + my_y
    place = jnp.stack([my_strip, my_z, my_y, edge_count[0]])

    (rims,) = call(
        rim_kernel,
        [((slots, border, width), BF16)],
        [node_latents],
        [HBM],
        [SEM((slots,))],
        [HBM],
    )
    far_groups = [
        [s * subs + (2 * k + step) % subs for s in range(strips) for step in (1, 2)]
        for k in range(zs)
    ]
    near_rims = lax.all_to_all(rims, PLANE, 0, 0)
    far_rims = lax.all_to_all(rims, ALL, 0, 0, axis_index_groups=far_groups)

    owner = senders // count_p
    within = senders % count_p
    is_local = owner == my_strip * subs + my_sub
    block = (owner // subs - my_strip + 1) * 3 + (owner % subs - my_sub + 1)
    block = jnp.where(block > 4, block - 1, block)
    send_index = jnp.where(
        is_local, within, count_p + block * border + jnp.minimum(within, border - 1)
    )
    chunk = min(CHUNK, count_e)
    chunks = count_e // chunk
    info = jnp.concatenate(
        [
            send_index.reshape(chunks, 1, chunk),
            receivers.reshape(chunks, 1, chunk),
            jnp.zeros((chunks, 6, chunk), jnp.int32),
        ],
        axis=1,
    )
    send_rows = 2 * count_p

    def by_rows(*shape):
        return pl.BlockSpec(shape, lambda i: (i, 0))

    def by_chunk(*shape):
        return pl.BlockSpec((1, *shape), lambda i: (i, 0, 0))

    def whole(*shape):
        return pl.BlockSpec(shape, lambda i: (0, 0))

    early = pl.pallas_call(
        early_kernel,
        grid=(chunks,),
        out_shape=[
            pltpu.HBM(shape, dtype)
            for shape, dtype in [
                ((count_e, send_rows), BF16),
                ((count_e, count_p), BF16),
                ((chunks, send_rows, chunk), BF16),
                ((chunks, count_p, chunk), BF16),
                ((chunks, width, chunk), BF16),
                ((count_e, width), F32),
            ]
        ],
        in_specs=[
            whole(count_p, width),
            by_rows(chunk, width),
            by_chunk(8, chunk),
            whole(3 * width, width),
        ],
        out_specs=[
            by_rows(chunk, send_rows),
            by_rows(chunk, count_p),
            by_chunk(send_rows, chunk),
            by_chunk(count_p, chunk),
            by_chunk(width, chunk),
            by_rows(chunk, width),
        ],
        scratch_shapes=[pltpu.VMEM((count_p + width, width), BF16)],
        compiler_params=pltpu.CompilerParams(vmem_limit_bytes=32 * 2**20),
    )(in_hbm(node_latents), in_hbm(edge_latents), info, in_hbm(w_edge_in))

    share = -(-7 * width // (slots * 16)) * 16

    def like(value):
        return pltpu.VMEM(value.shape, value.dtype)

    new_nodes, new_edges, local_grad, parts = call(
        layer_kernel,
        [
            ((count_p, width), BF16),
            ((count_e, width), BF16),
            ((count_p, width), F32),
            ((slots, share + 2 * border, width), BF16),
        ],
        [
            place,
            node_latents,
            near_rims,
            far_rims,
            edge_latents,
            *early,
            w_edge_in,
            w_edge_out,
            w_node_in,
            w_node_out,
            node_cotangent,
            edge_cotangent,
        ],
        [SMEM] + [HBM] * 16,
        [
            like(node_latents),
            pltpu.VMEM((2 * slots, border, width), BF16),
            like(edge_latents),
            *[like(value) for value in early],
            like(w_edge_in),
            like(w_edge_out),
            like(w_node_in),
            like(w_node_out),
            like(node_cotangent),
            like(edge_cotangent),
            pltpu.VMEM((count_p, width), BF16),
            pltpu.VMEM((count_e, width), BF16),
            pltpu.VMEM((count_p, width), F32),
            pltpu.VMEM((send_rows, width), BF16),
            pltpu.VMEM((send_rows, width), BF16),
            pltpu.VMEM((width, 2 * width), BF16),
            pltpu.VMEM((2 * width, 2 * width), BF16),
            pltpu.VMEM((count_e, width), BF16),
            pltpu.VMEM((count_e, width), F32),
            pltpu.VMEM((count_e, width), F32),
            pltpu.VMEM((count_e, width), F32),
            pltpu.VMEM((send_rows + count_p, width), F32),
            pltpu.VMEM((width, width), F32),
            pltpu.VMEM((width, width), F32),
            pltpu.VMEM((count_p, width), F32),
            pltpu.VMEM((slots * share, width), BF16),
            SEM((8,)),
            SEM((8, chunks)),
            SEM((chunks,)),
            SEM((2,)),
        ],
        [HBM, HBM, HBM, VMEM],
        limit=48,
    )

    came = lax.all_to_all(parts, PLANE, 0, 0)
    parts, mine = call(
        plane_sum_kernel,
        [((zs, share + border, width), BF16), ((border, width), F32)],
        [place, came],
        [SMEM, VMEM],
    )
    came = lax.all_to_all(parts, "z", 0, 0)
    factor = 1.0 / math.sqrt(count_e * strips * subs)
    parts, rim_grad = call(
        functools.partial(line_sum_kernel, factor),
        [((slots, share, width), BF16), ((border, width), F32)],
        [came, mine],
        [VMEM, VMEM],
    )
    came = lax.all_to_all(parts, PLANE, 0, 0)
    node_grad, *grads = call(
        finish_kernel,
        [((rows, width), F32) for rows in (count_p, 3 * width, width, 2 * width, width)],
        [came, rim_grad, local_grad],
        [VMEM, VMEM, HBM],
        [
            pltpu.VMEM((count_p, width), F32),
            pltpu.VMEM((slots * share, width), F32),
            SEM,
            SEM((5,)),
        ],
        [HBM] * 5,
    )
    return (new_nodes, new_edges, node_grad, *grads)


def solution(mesh):
    strips, subs = mesh.devices.shape
    grid = Mesh(mesh.devices.reshape(strips, subs // 2, 2), ALL)
    rows = P(ALL, None)
    line = P(ALL)
    return jax.shard_map(
        shards,
        mesh=grid,
        in_specs=(rows, rows, line, line, line, P(), P(), P(), P(), rows, rows),
        out_specs=(rows, rows, rows, P(), P(), P(), P()),
        check_vma=False,
    )
```

time: 80.8 us -> 78.8 us (0.975)
  waiting for transfers between devices: 10.4 us -> 3.91 us
  Pallas kernels: 27.1 us -> 30.7 us
  local copies, waits for them, and re-layouts: 3.4 us -> 0.71 us
  starting transfers between devices: 10.3 us -> 12.3 us
  other arithmetic: 0.21 us -> 1.64 us
    all_to_all x2, waiting for transfers between devices: 10.4 us -> 3.91 us  [the longest x1 3.9 us: shards(): near_rims = lax.all_to_all(rims, PLANE, 0, 0)]
    pallas_call x6, Pallas kernels: 27.1 us -> 30.7 us  [the longest x5 22.8 us: call(): pl.pallas_call(kernel, out_shape=[pltpu.HBM(shape, dtype) if spec is HBM...]
    unnamed x22 -> x4, local copies, waits for them, and re-layouts: 3.32 us -> 0.63 us
    all_to_all x2, starting transfers between devices: 10.3 us -> 12.3 us  [the longest x1 7.12 us: shards(): far_rims = lax.all_to_all(rims, ALL, 0, 0, axis_index_groups=far_groups)]
  transfers between devices with their start and end apart: 2 -> 2, of which waited for: 2 -> 1; matrix products, arithmetic and copies ran while one was open for 0% -> 2% of each run, Pallas kernels for 0% -> 10%
where the time goes in v4:
time: 78.8 us; the launch traced here: 78.2 us
  Pallas kernels  30.7 us (39%)
  blocking collectives  27.6 us (35%)
  starting transfers between devices  12.3 us (16%)
  waiting for transfers between devices  3.91 us (5%)
  other arithmetic  1.64 us (2%)
  between operations  1.33 us (2%)
    pallas_call x5, Pallas kernels, call(): pl.pallas_call(kernel, out_shape=[pltpu.HBM(shape, dtype) if spec is HBM...  22.8 us
    all_to_all x2, blocking collectives, shards(): came = lax.all_to_all(parts, PLANE, 0, 0)  18.2 us
    all_to_all x1, blocking collectives, shards(): came = lax.all_to_all(parts, 'z', 0, 0)  9.35 us
    pallas_call x1, Pallas kernels, shards(): pl.pallas_call(early_kernel, grid=(chunks,), out_shape=[pltpu.HBM(shape,...  7.89 us
    all_to_all x1, starting transfers between devices, shards(): far_rims = lax.all_to_all(rims, ALL, 0, 0, axis_index_groups=far_groups)  7.12 us
    all_to_all x1, starting transfers between devices, shards(): near_rims = lax.all_to_all(rims, PLANE, 0, 0)  5.18 us
    all_to_all x1, waiting for transfers between devices, shards(): near_rims = lax.all_to_all(rims, PLANE, 0, 0)  3.9 us
  transfers between devices with their start and end apart: 2, of which 1 were waited for; matrix products, arithmetic and copies ran while one was open for 2% of the time, Pallas kernels for 10%

profile of v4, /device:TPU:0, one launch (start us, length us, event | category | flops | bytes accessed | tf_op | source)
XLA Modules:
  0.0 78.2 jit_solution(6765663613245858144)
XLA Ops:
  0.6 3.2 %shard_map.162 = bf16[8,32,128]{2,1,0:T(8,128)(2,1)} custom-call(bf16[256,128]{1,0:T(8,128)(2,1)} %nodes_in.1), custom_call_target="tpu_custom_call" | custom-call | tf_op jit(solution)/shard_map/pallas_call | solution.py:60
  3.8 5.2 %all-to-all-start = ((bf16[8,32,128]{2,1,0:T(8,128)(2,1)}), bf16[8,32,128]{2,1,0:T(8,128)(2,1)S(1)}, u32[]{:S(2)}, u32[]{:S(2)}) async-start(bf16[8,32,128]{2,1,0:T(8,128)(2,1)} %shard_map.162), calls=%async_computation | async-start | bytes 131072 | tf_op jit(solution)/shard_map/all_to_all | solution.py:486
  9.0 0.8 fusion.9
  9.8 0.1 pad.2.clone
  9.8 3.9 %all-to-all-done.rims_in = bf16[8,32,128]{2,1,0:T(8,128)(2,1)S(1)} async-done(((bf16[8,32,128]{2,1,0:T(8,128)(2,1)}), bf16[8,32,128]{2,1,0:T(8,128)(2,1)S(1)}, u32[]{:S(2)}, u32[]{:S(2)}) %all-to-all-start) | async-done | bytes 65568 | tf_op jit(solution)/shard_map/all_to_all | solution.py:486
  13.7 0.0 copy-start
  13.7 7.1 %all-to-all-start.1 = ((bf16[8,32,128]{2,1,0:T(8,128)(2,1)}), bf16[8,32,128]{2,1,0:T(8,128)(2,1)S(1)}, u32[]{:S(2)}, u32[]{:S(2)}) async-start(bf16[8,32,128]{2,1,0:T(8,128)(2,1)} %shard_map.162), calls=%async_computation.1 | async-start | bytes 131072 | tf_op jit(solution)/shard_map/all_to_all | solution.py:487
  20.9 0.8 %add_add_fusion.info = s32[4,8,1024]{2,1,0:T(8,128)S(1)} fusion(s32[4,1,1024]{2,1,0:T(1,128)} %bitcast.6, s32[4,1,1024]{2,1,0:T(1,128)S(1)} %bitcast.5, s32[8]{0:T(128)S(1)} %pad.2.clone), kind=kLoop, calls=%fused_computation | loop fusion | flops 65536 | bytes 163872 | tf_op jit(solution)/shard_map/concatenate | solution.py:499
  22.3 7.9 %shard_map.163 = (bf16[4096,512]{1,0:T(8,128)(2,1)}, bf16[4096,256]{1,0:T(8,128)(2,1)}, bf16[4,512,1024]{2,1,0:T(8,128)(2,1)}, bf16[4,256,1024]{2,1,0:T(8,128)(2...) custom-call(bf16[256,128]{1,0:T(8,128)(2,1)} %nodes_in.1, bf16[4096,128]{1,0:T(8,128)(2,1)} %edges_in.1, ...), custom_call_target="tpu_custom_call" | custom-call | tf_op jit(solution)/shard_map/pallas_call | solution.py:518
  30.2 0.1 pad_add_fusion.place
  30.3 0.0 all-to-all-done.1.far_rims_in
  30.3 0.0 copy-start.1
  30.3 0.0 copy-done
  30.3 0.6 copy-done.1
  30.9 17.4 %shard_map.164 = (bf16[256,128]{1,0:T(8,128)(2,1)}, bf16[4096,128]{1,0:T(8,128)(2,1)}, f32[256,128]{1,0:T(8,128)}, bf16[8,176,128]{2,1,0:T(8,128)(2,1)S(1)}) custom-call(s32[4]{0:T(128)S(1)} %pad_add_fusion.place, bf16[256,128]{1,0:T(8,128)(2,1)} %nodes_in.1, bf16[8,32,128]{2,1,0:T(8,128)(2,1)} %copy-done, bf16[8,32,128]{2,1,0:T(8,128)(2,1)} %copy-done.1, ...), custom_call_target="tpu_custom_call" | custom-call | tf_op jit(solution)/shard_map/pallas_call | solution.py:60
  48.3 10.2 %all_to_all.25.came = bf16[8,176,128]{2,1,0:T(8,128)(2,1)S(1)} all-to-all(bf16[8,176,128]{2,1,0:T(8,128)(2,1)S(1)} %get-tuple-element.34), channel_id=1, replica_groups=mesh['strip'=4,'z'=4,'y'=2] {'strip','y'}, dimensions={0} | all-to-all | bytes 720896 | tf_op jit(solution)/shard_map/all_to_all | solution.py:614
  58.4 0.6 shard_map.165
  59.0 9.3 %all_to_all.26.came = bf16[4,144,128]{2,1,0:T(8,128)(2,1)S(1)} all-to-all(bf16[4,144,128]{2,1,0:T(8,128)(2,1)S(1)} %get-tuple-element.35), channel_id=1, replica_groups=mesh['strip'=4,'z'=4,'y'=2] {'z'}, dimensions={0} | all-to-all | bytes 294912 | tf_op jit(solution)/shard_map/all_to_all | solution.py:621
  68.4 8.1 %all_to_all.27.came = bf16[8,112,128]{2,1,0:T(8,128)(2,1)S(1)} all-to-all(bf16[8,112,128]{2,1,0:T(8,128)(2,1)S(1)} %get-tuple-element.37), channel_id=1, replica_groups=mesh['strip'=4,'z'=4,'y'=2] {'strip','y'}, dimensions={0} | all-to-all | bytes 458752 | tf_op jit(solution)/shard_map/all_to_all | solution.py:629
  76.5 1.7 %shard_map.167 = (f32[256,128]{1,0:T(8,128)}, f32[384,128]{1,0:T(8,128)}, f32[128,128]{1,0:T(8,128)}, f32[256,128]{1,0:T(8,128)}, f32[128,128]{1,0:T(8,128)}) custom-call(bf16[8,112,128]{2,1,0:T(8,128)(2,1)S(1)} %all_to_all.27.came, f32[32,128]{1,0:T(8,128)S(1)} %get-tuple-element.38.rim_grad, f32[256,128]{1,0:T(8,128)} %get-tuple-element.39.local_grad_in), custom_call_target="tpu_custom_call" | custom-call | tf_op jit(solution)/shard_map/pallas_call | solution.py:60
  (2 shorter events, 0.0 us)
Async XLA Ops:
  3.8 9.9 %all-to-all-start = ((bf16[8,32,128]{2,1,0:T(8,128)(2,1)}), bf16[8,32,128]{2,1,0:T(8,128)(2,1)S(1)}, u32[]{:S(2)}, u32[]{:S(2)}) async-start(bf16[8,32,128]{2,1,0:T(8,128)(2,1)} %shard_map.162), calls=%async_computation | async-start | bytes 131072 | tf_op jit(solution)/shard_map/all_to_all | solution.py:486
  13.7 16.5 %copy-start = (bf16[8,32,128]{2,1,0:T(8,128)(2,1)}, bf16[8,32,128]{2,1,0:T(8,128)(2,1)S(1)}, u32[]{:S(2)}) copy-start(bf16[8,32,128]{2,1,0:T(8,128)(2,1)S(1)} %all-to-all-done.rims_in) | copy-start | bytes 196612
  13.7 16.5 %all-to-all-start.1 = ((bf16[8,32,128]{2,1,0:T(8,128)(2,1)}), bf16[8,32,128]{2,1,0:T(8,128)(2,1)S(1)}, u32[]{:S(2)}, u32[]{:S(2)}) async-start(bf16[8,32,128]{2,1,0:T(8,128)(2,1)} %shard_map.162), calls=%async_computation.1 | async-start | bytes 131072 | tf_op jit(solution)/shard_map/all_to_all | solution.py:487
  30.3 0.6 copy-start.1

commit v5 on v4

--- a/solution.py
+++ b/solution.py
@@ -70,34 +70,33 @@
     )(*[in_hbm(value) if spec is HBM else value for value, spec in zip(ins, specs)])
 
 
-def rim_kernel(nodes, out, sems):
+def rim_kernel(nodes, out, rim, many, in_sem, out_sem):
     border = out.shape[1]
-    copies = [
-        pltpu.make_async_copy(nodes.at[pl.ds(0, border)], out.at[target], sems.at[target])
-        for target in range(out.shape[0])
-    ]
-    for copy in copies:
-        copy.start()
-    for copy in copies:
-        copy.wait()
+    copy = pltpu.make_async_copy(nodes.at[pl.ds(0, border)], rim, in_sem)
+    copy.start()
+    copy.wait()
+    for target in range(out.shape[0]):
+        many[target] = rim[...]
+    copy = pltpu.make_async_copy(many, out, out_sem)
+    copy.start()
+    copy.wait()
 
 
 def early_kernel(
     nodes,
     edges,
+    edge_cot,
     info,
     w_edge_in,
-    send_hot,
-    recv_hot,
-    send_hot_t,
-    recv_hot_t,
-    edges_t,
+    hot,
+    hot_t,
+    far,
     pre_part,
+    cot_part,
     tables,
 ):
     count_p, width = nodes.shape
     chunk = edges.shape[0]
-    send_rows = send_hot.shape[1]
 
     @pl.when(pl.program_id(0) == 0)
     def prepare():
@@ -105,45 +104,45 @@
         tables[count_p:] = w_edge_in[2 * width :]
 
     lane = lax.broadcasted_iota(jnp.int32, (chunk, width), 1)
-
-    def hot(column, blocks):
-        found = [(column == lane + width * k).astype(F32).astype(BF16) for k in range(blocks)]
-        return jnp.concatenate(found, axis=1)
-
-    def hot_t(line, size):
-        place_of = lax.broadcasted_iota(jnp.int32, (size, chunk), 0)
-        return (place_of == line).astype(F32).astype(BF16)
+    line = lax.broadcasted_iota(jnp.int32, (count_p, chunk), 0)
+
+    def found(column):
+        blocks = [
+            (column == lane + width * k).astype(F32).astype(BF16)
+            for k in range(count_p // width)
+        ]
+        return jnp.concatenate(blocks, axis=1)
 
     index = info[0]
     columns = index.T
     edge = edges[...]
-    recv = hot(columns[:, 1:2], count_p // width)
+    cot = edge_cot[...].astype(F32)
+    recv = found(columns[:, 1:2])
     pre_part[...] = mm(jnp.concatenate([recv, edge], axis=1), tables[...])
-    recv_hot[...] = recv
-    send_hot[...] = hot(columns[:, 0:1], send_rows // width)
-    send_hot_t[0] = hot_t(index[0:1], send_rows)
-    recv_hot_t[0] = hot_t(index[1:2], count_p)
-    edges_t[0] = edge.T
+    hot[:, :count_p] = found(columns[:, 0:1])
+    hot[:, count_p:] = recv
+    hot_t[0, :count_p] = (line == index[1:2]).astype(F32).astype(BF16)
+    hot_t[0, count_p : 2 * count_p] = (line == index[0:1]).astype(F32).astype(BF16)
+    hot_t[0, 2 * count_p :] = edge.T
+    far[...] = jnp.broadcast_to(columns[:, 2:3], edge.shape).astype(F32).astype(BF16)
+    cot_part[...] = (cot - jnp.mean(cot, axis=1, keepdims=True)).astype(BF16)
 
 
 def layer_kernel(
     place,
     nodes_in,
     rims_in,
-    far_rims_in,
     edges_in,
-    send_hot_in,
-    recv_hot_in,
-    send_hot_t_in,
-    recv_hot_t_in,
-    edges_t_in,
+    hot_in,
+    hot_t_in,
+    far_in,
     pre_part_in,
+    cot_part_in,
     w_edge_in_in,
     w_edge_out_in,
     w_node_in_in,
     w_node_out_in,
     node_cot_in,
-    edge_cot_in,
     new_nodes_out,
     new_edges_out,
     local_grad_out,
@@ -151,31 +150,30 @@
     nodes,
     rims,
     edges,
-    send_hot,
-    recv_hot,
-    send_hot_t,
-    recv_hot_t,
-    edges_t,
+    hot,
+    hot_t,
+    far,
     pre_part,
+    cot_part,
     w_edge_in,
     w_edge_out,
     w_node_in,
     w_node_out,
     node_cot,
-    edge_cot,
     new_nodes,
     new_edges,
     local_grad,
-    table,
+    near_rows,
+    far_rows,
     tables,
-    spread,
+    centring,
+    back,
     means,
     hidden,
     slope,
     normed,
     scale,
     sums,
-    ge_edge,
     ge_out,
     agg,
     packed,
@@ -188,17 +186,17 @@
     border = rims.shape[1]
     slots = parts.shape[0]
     strips = slots // 2
-    chunks, _, chunk = recv_hot_t.shape
+    chunks, _, chunk = hot_t.shape
+    half = chunk // 2
     share = parts.shape[1] - 2 * border
-    my_strip, my_y, live_count = place[0], place[2], place[3]
+    my_strip, my_y, live_count, my_sub, subs = (place[k] for k in (0, 2, 3, 4, 5))
 
     small = [
         pltpu.make_async_copy(source, target, small_sems.at[k])
         for k, (source, target) in enumerate(
             [
                 (nodes_in, nodes),
-                (rims_in, rims.at[pl.ds(0, slots)]),
-                (far_rims_in, rims.at[pl.ds(slots, slots)]),
+                (rims_in, rims),
                 (w_edge_in_in, w_edge_in),
                 (w_edge_out_in, w_edge_out),
                 (w_node_in_in, w_node_in),
@@ -211,21 +209,24 @@
     def span(step):
         return pl.ds(pl.multiple_of(step * chunk, chunk), chunk)
 
+    def pairs_of(step):
+        return pl.ds(pl.multiple_of(step * half, half), half)
+
     def fetch(step, which):
         rows = span(step)
+        first, second = pl.ds(0, count_p), pl.ds(count_p, count_p)
+        rest = pl.ds(count_p, count_p + width)
         pairs = [
+            (hot_in.at[rows, first], hot.at[rows, first]),
+            (far_in.at[rows], far.at[rows]),
             (pre_part_in.at[rows], pre_part.at[rows]),
-            (send_hot_in.at[rows], send_hot.at[rows]),
             (edges_in.at[rows], edges.at[rows]),
-            (recv_hot_t_in.at[step], recv_hot_t.at[step]),
-            (recv_hot_in.at[rows], recv_hot.at[rows]),
-            (edge_cot_in.at[rows], edge_cot.at[rows]),
-            (send_hot_t_in.at[step], send_hot_t.at[step]),
-            (edges_t_in.at[step], edges_t.at[step]),
+            (hot_t_in.at[step, first], hot_t.at[step, first]),
+            (hot_in.at[rows, second], hot.at[rows, second]),
+            (cot_part_in.at[rows], cot_part.at[rows]),
+            (hot_t_in.at[step, rest], hot_t.at[step, rest]),
         ]
-        return [
-            pltpu.make_async_copy(*pairs[k], sems.at[k, step]) for k in which
-        ]
+        return [pltpu.make_async_copy(*pairs[k], sems.at[k, step]) for k in which]
 
     def emit(step):
         rows = span(step)
@@ -233,45 +234,54 @@
             new_edges.at[rows], new_edges_out.at[rows], out_sems.at[step]
         )
 
-    ahead, back = range(4), range(4, 8)
-    for copy in small[:5] + fetch(0, ahead) + small[5:]:
+    def paired(value):
+        return jnp.concatenate([value[:half], value[half:]], axis=1)
+
+    def unpaired(value):
+        return jnp.concatenate([value[:, :width], value[:, width:]], axis=0)
+
+    def twice(block):
+        zero = jnp.zeros_like(block)
+        return jnp.concatenate(
+            [
+                jnp.concatenate([block, zero], axis=1),
+                jnp.concatenate([zero, block], axis=1),
+            ],
+            axis=0,
+        )
+
+    ahead, behind = range(5), range(5, 8)
+    for copy in small[:4] + fetch(0, ahead) + small[4:]:
         copy.start()
     for step in range(1, chunks):
         for copy in fetch(step, ahead):
             copy.start()
     for step in range(chunks):
-        for copy in fetch(step, back):
+        for copy in fetch(step, behind):
             copy.start()
-    for copy in small[:5]:
+    for copy in small[:4]:
         copy.wait()
 
-    table[:count_p] = nodes[...]
+    near_rows[...] = nodes[...]
     spot = 0
     for d_strip in (-1, 0, 1):
         strip = jnp.clip(my_strip + d_strip, 0, strips - 1)
         for d_sub in (-1, 0, 1):
             if d_strip == 0 and d_sub == 0:
                 continue
-            if d_sub == 0:
-                slot = 2 * strip + my_y
-            elif d_sub == 1:
-                slot = my_y * slots + 2 * strip + 1
-            else:
-                slot = (1 - my_y) * slots + 2 * strip
-            rows = slice(count_p + spot * border, count_p + (spot + 1) * border)
-            table[rows] = rims[slot]
+            sub = jnp.clip(my_sub + d_sub, 0, subs - 1)
+            far_rows[spot * border : (spot + 1) * border] = rims[strip * subs + sub]
             spot += 1
-    send_rows = table.shape[0]
-    tables[...] = mm(table[...], w_edge_in[:width]).astype(BF16)
-    spread[:, :width] = w_edge_out[...]
-    spread[:, width:] = jnp.broadcast_to(
-        jnp.mean(w_edge_out[...].astype(F32), axis=1, keepdims=True), (width, width)
-    ).astype(BF16)
-    high = lax.broadcasted_iota(jnp.int32, (2 * width, 2 * width), 0) >= width
-    wide = lax.broadcasted_iota(jnp.int32, (2 * width, 2 * width), 1) >= width
-    means[...] = jnp.where(high == wide, 1.0 / width, 0.0).astype(BF16)
-
-    row = lax.broadcasted_iota(jnp.int32, (chunk, width), 0)
+    tables[:, :width] = mm(near_rows[...], w_edge_in[:width]).astype(BF16)
+    tables[:, width:] = mm(far_rows[...], w_edge_in[:width]).astype(BF16)
+    weight = w_edge_out[...].astype(F32)
+    centring[...] = twice(weight - jnp.mean(weight, axis=1, keepdims=True)).astype(BF16)
+    back[...] = twice(weight).astype(BF16)
+    means[...] = twice(jnp.full((width, width), 1.0 / width, F32)).astype(BF16)
+
+    row = lax.broadcasted_iota(jnp.int32, (half, 2 * width), 0)
+    lane = lax.broadcasted_iota(jnp.int32, (half, 2 * width), 1)
+    edge_row = jnp.where(lane < width, row, row + half)
     agg[...] = jnp.zeros_like(agg)
 
     def forward(step, carry):
@@ -279,30 +289,31 @@
         for copy in fetch(step, ahead):
             copy.wait()
         begun = pre_part[rows]
-        hot = send_hot[rows]
-        hot_t = recv_hot_t[step]
-        edge = edges[rows].astype(F32)
+        beyond = far[rows] > 0
+        picked = mm(hot[rows, :count_p], tables[...])
+        edge = paired(edges[rows].astype(F32))
+        recv_t = hot_t[step, :count_p]
         so_far = agg[...]
-        act, bend = silu_and_slope(begun + mm(hot, tables[...]))
+        pre = begun + jnp.where(beyond, picked[:, width:], picked[:, :width])
+        act, bend = silu_and_slope(paired(pre))
         act = act.astype(BF16)
-        outer = mm(act, spread[...])
-        centre = outer[:, :width] - outer[:, width:]
-        spare = mm((centre * centre).astype(BF16), means[:width, :width])
-        factor = jnp.where(row < live_count - step * chunk, lax.rsqrt(spare + EPS), 0.0)
+        centre = mm(act, centring[...])
+        spare = mm((centre * centre).astype(BF16), means[...])
+        factor = jnp.where(edge_row < live_count - step * chunk, lax.rsqrt(spare + EPS), 0.0)
         unit = centre * factor
-        so_far = so_far + mm(hot_t, unit.astype(BF16))
-        slope[rows] = bend
-        hidden[rows] = act
-        scale[rows] = factor
-        normed[rows] = unit
-        new_edges[rows] = (edge + unit).astype(BF16)
+        so_far = so_far + mm(recv_t, unpaired(unit.astype(BF16)))
+        slope[pairs_of(step)] = bend
+        hidden[rows] = unpaired(act)
+        scale[pairs_of(step)] = factor
+        normed[pairs_of(step)] = unit
+        new_edges[rows] = unpaired((edge + unit).astype(BF16))
         agg[...] = so_far
         emit(step).start()
         return carry
 
     lax.fori_loop(0, chunks, forward, 0)
 
-    for copy in small[5:]:
+    for copy in small[4:]:
         copy.wait()
     joined = jnp.concatenate([nodes[...], agg[...].astype(BF16)], axis=1)
     node_pre = mm(joined, w_node_in[...])
@@ -314,7 +325,8 @@
     d_outer = norm_back(node_unit, node_scale, cot).astype(BF16)
     d_pre = (mm_nt(d_outer, w_node_out[...]) * node_slope).astype(BF16)
     d_joined = mm_nt(d_pre, w_node_in[...])
-    d_agg = d_joined[:, width:].astype(BF16)
+    d_agg = d_joined[:, width:]
+    d_agg = (d_agg - jnp.mean(d_agg, axis=1, keepdims=True)).astype(BF16)
     agg[...] = cot + d_joined[:, :width]
     packed[4 * width : 6 * width] = mm_tn(joined, d_pre).astype(BF16)
     packed[6 * width : 7 * width] = mm_tn(node_act, d_outer).astype(BF16)
@@ -322,49 +334,56 @@
     node_copy.start()
 
     sums[...] = jnp.zeros_like(sums)
-    ge_edge[...] = jnp.zeros_like(ge_edge)
     ge_out[...] = jnp.zeros_like(ge_out)
 
     def backward(step, carry):
         rows = span(step)
-        for copy in fetch(step, back):
+        for copy in fetch(step, behind):
             copy.wait()
-        cot = edge_cot[rows].astype(F32)
-        hot = recv_hot[rows]
-        unit = normed[rows]
-        factor = scale[rows]
-        bend = slope[rows]
+        cot = cot_part[rows].astype(F32)
+        recv = hot[rows, count_p:]
+        unit = normed[pairs_of(step)]
+        factor = scale[pairs_of(step)]
+        bend = slope[pairs_of(step)]
         act = hidden[rows]
-        edge_t = edges_t[step]
-        send_t = send_hot_t[step]
-        recv_t = recv_hot_t[step]
-        upstream = cot + mm(hot, d_agg)
-        both = jnp.concatenate([upstream.astype(BF16), (upstream * unit).astype(BF16)], axis=1)
-        both = mm(both, means[...])
-        d_out = factor * (upstream - both[:, :width] - unit * both[:, width:])
-        d_out = d_out.astype(BF16)
-        d_in = (mm_nt(d_out, w_edge_out[...]) * bend).astype(BF16)
-        ge_out[...] += mm_tn(act, d_out)
-        sums[:send_rows] += mm(send_t, d_in)
-        sums[send_rows:] += mm(recv_t, d_in)
-        ge_edge[...] += mm(edge_t, d_in)
+        beyond = far[rows] > 0
+        turned = hot_t[step]
+        upstream = paired(cot + mm(recv, d_agg))
+        along = mm((upstream * unit).astype(BF16), means[...])
+        d_out = (factor * (upstream - unit * along)).astype(BF16)
+        d_in = unpaired(mm_nt(d_out, back[...]) * bend)
+        zero = jnp.zeros_like(d_in)
+        near_far = jnp.concatenate(
+            [
+                jnp.where(beyond, zero, d_in).astype(BF16),
+                jnp.where(beyond, d_in, zero).astype(BF16),
+            ],
+            axis=1,
+        )
+        ge_out[...] += mm_tn(act, unpaired(d_out))
+        sums[...] += mm(turned, near_far)
         return carry
 
     lax.fori_loop(0, chunks, backward, 0)
 
-    send_sums = sums[:send_rows].astype(BF16)
-    recv_sums = sums[send_rows:].astype(BF16)
-    packed[:width] = mm_tn(table[...], send_sums).astype(BF16)
+    recv_sums = (sums[:count_p, :width] + sums[:count_p, width:]).astype(BF16)
+    near_sums = sums[count_p : 2 * count_p, :width].astype(BF16)
+    far_sums = sums[count_p : 2 * count_p, width:].astype(BF16)
+    edge_sums = sums[2 * count_p :, :width] + sums[2 * count_p :, width:]
+    packed[:width] = (mm_tn(near_rows[...], near_sums) + mm_tn(far_rows[...], far_sums)).astype(BF16)
     packed[width : 2 * width] = mm_tn(nodes[...], recv_sums).astype(BF16)
-    packed[2 * width : 3 * width] = ge_edge[...].astype(BF16)
+    packed[2 * width : 3 * width] = edge_sums.astype(BF16)
     packed[3 * width : 4 * width] = ge_out[...].astype(BF16)
     if packed.shape[0] > 7 * width:
         packed[7 * width :] = jnp.zeros((packed.shape[0] - 7 * width, width), BF16)
-    sent = mm_nt(send_sums, w_edge_in[:width])
-    local_grad[...] = agg[...] + sent[:count_p] + mm_nt(recv_sums, w_edge_in[width : 2 * width])
+    local_grad[...] = (
+        agg[...]
+        + mm_nt(near_sums, w_edge_in[:width])
+        + mm_nt(recv_sums, w_edge_in[width : 2 * width])
+    )
     grad_copy = pltpu.make_async_copy(local_grad, local_grad_out, last_sems.at[1])
     grad_copy.start()
-    owed = sent[count_p:].astype(BF16)
+    owed = mm_nt(far_sums, w_edge_in[:width]).astype(BF16)
     for slot in range(slots):
         parts[slot, :share] = packed[slot * share : (slot + 1) * share]
         parts[slot, share:] = jnp.zeros((2 * border, width), BF16)
@@ -469,42 +488,40 @@
     slots = strips * ys
     my_strip, my_z, my_y = (lax.axis_index(axis).astype(jnp.int32) for axis in ALL)
     my_sub = my_z * ys + my_y
-    place = jnp.stack([my_strip, my_z, my_y, edge_count[0]])
+    devices = strips * subs
+    place = jnp.stack([my_strip, my_z, my_y, edge_count[0], my_sub, jnp.int32(subs)])
 
     (rims,) = call(
         rim_kernel,
-        [((slots, border, width), BF16)],
+        [((devices, border, width), BF16)],
         [node_latents],
         [HBM],
-        [SEM((slots,))],
+        [
+            pltpu.VMEM((border, width), BF16),
+            pltpu.VMEM((devices, border, width), BF16),
+            SEM,
+            SEM,
+        ],
         [HBM],
     )
-    far_groups = [
-        [s * subs + (2 * k + step) % subs for s in range(strips) for step in (1, 2)]
-        for k in range(zs)
-    ]
-    near_rims = lax.all_to_all(rims, PLANE, 0, 0)
-    far_rims = lax.all_to_all(rims, ALL, 0, 0, axis_index_groups=far_groups)
+    rims = lax.all_to_all(rims, ALL, 0, 0)
 
     owner = senders // count_p
     within = senders % count_p
     is_local = owner == my_strip * subs + my_sub
     block = (owner // subs - my_strip + 1) * 3 + (owner % subs - my_sub + 1)
     block = jnp.where(block > 4, block - 1, block)
-    send_index = jnp.where(
-        is_local, within, count_p + block * border + jnp.minimum(within, border - 1)
-    )
+    send_index = jnp.where(is_local, within, block * border + jnp.minimum(within, border - 1))
     chunk = min(CHUNK, count_e)
     chunks = count_e // chunk
-    info = jnp.concatenate(
+    info = jnp.stack(
         [
-            send_index.reshape(chunks, 1, chunk),
-            receivers.reshape(chunks, 1, chunk),
-            jnp.zeros((chunks, 6, chunk), jnp.int32),
+            value.reshape(chunks, chunk)
+            for value in [send_index, receivers, 1 - is_local.astype(jnp.int32)]
+            + [jnp.zeros_like(receivers)] * 5
         ],
         axis=1,
     )
-    send_rows = 2 * count_p
 
     def by_rows(*shape):
         return pl.BlockSpec(shape, lambda i: (i, 0))
@@ -521,31 +538,36 @@
         out_shape=[
             pltpu.HBM(shape, dtype)
             for shape, dtype in [
-                ((count_e, send_rows), BF16),
-                ((count_e, count_p), BF16),
-                ((chunks, send_rows, chunk), BF16),
-                ((chunks, count_p, chunk), BF16),
-                ((chunks, width, chunk), BF16),
+                ((count_e, 2 * count_p), BF16),
+                ((chunks, 2 * count_p + width, chunk), BF16),
+                ((count_e, width), BF16),
                 ((count_e, width), F32),
+                ((count_e, width), BF16),
             ]
         ],
         in_specs=[
             whole(count_p, width),
             by_rows(chunk, width),
+            by_rows(chunk, width),
             by_chunk(8, chunk),
             whole(3 * width, width),
         ],
         out_specs=[
-            by_rows(chunk, send_rows),
-            by_rows(chunk, count_p),
-            by_chunk(send_rows, chunk),
-            by_chunk(count_p, chunk),
-            by_chunk(width, chunk),
+            by_rows(chunk, 2 * count_p),
+            by_chunk(2 * count_p + width, chunk),
+            by_rows(chunk, width),
+            by_rows(chunk, width),
             by_rows(chunk, width),
         ],
         scratch_shapes=[pltpu.VMEM((count_p + width, width), BF16)],
         compiler_params=pltpu.CompilerParams(vmem_limit_bytes=32 * 2**20),
-    )(in_hbm(node_latents), in_hbm(edge_latents), info, in_hbm(w_edge_in))
+    )(
+        in_hbm(node_latents),
+        in_hbm(edge_latents),
+        in_hbm(edge_cotangent),
+        info,
+        in_hbm(w_edge_in),
+    )
 
     share = -(-7 * width // (slots * 16)) * 16
 
@@ -563,8 +585,7 @@
         [
             place,
             node_latents,
-            near_rims,
-            far_rims,
+            rims,
             edge_latents,
             *early,
             w_edge_in,
@@ -572,12 +593,11 @@
             w_node_in,
             w_node_out,
             node_cotangent,
-            edge_cotangent,
-        ],
-        [SMEM] + [HBM] * 16,
+        ],
+        [SMEM] + [HBM] * 13,
         [
             like(node_latents),
-            pltpu.VMEM((2 * slots, border, width), BF16),
+            like(rims),
             like(edge_latents),
             *[like(value) for value in early],
             like(w_edge_in),
@@ -585,24 +605,24 @@
             like(w_node_in),
             like(w_node_out),
             like(node_cotangent),
-            like(edge_cotangent),
             pltpu.VMEM((count_p, width), BF16),
             pltpu.VMEM((count_e, width), BF16),
             pltpu.VMEM((count_p, width), F32),
-            pltpu.VMEM((send_rows, width), BF16),
-            pltpu.VMEM((send_rows, width), BF16),
-            pltpu.VMEM((width, 2 * width), BF16),
+            pltpu.VMEM((count_p, width), BF16),
+            pltpu.VMEM((8 * border, width), BF16),
+            pltpu.VMEM((count_p, 2 * width), BF16),
+            pltpu.VMEM((2 * width, 2 * width), BF16),
+            pltpu.VMEM((2 * width, 2 * width), BF16),
             pltpu.VMEM((2 * width, 2 * width), BF16),
             pltpu.VMEM((count_e, width), BF16),
-            pltpu.VMEM((count_e, width), F32),
-            pltpu.VMEM((count_e, width), F32),
-            pltpu.VMEM((count_e, width), F32),
-            pltpu.VMEM((send_rows + count_p, width), F32),
-            pltpu.VMEM((width, width), F32),
+            pltpu.VMEM((count_e // 2, 2 * width), F32),
+            pltpu.VMEM((count_e // 2, 2 * width), F32),
+            pltpu.VMEM((count_e // 2, 2 * width), F32),
+            pltpu.VMEM((2 * count_p + width, 2 * width), F32),
             pltpu.VMEM((width, width), F32),
             pltpu.VMEM((count_p, width), F32),
             pltpu.VMEM((slots * share, width), BF16),
-            SEM((8,)),
+            SEM((7,)),
             SEM((8, chunks)),
             SEM((chunks,)),
             SEM((2,)),

time: 78.8 us -> 70.6 us (0.90)
  starting transfers between devices: 12.3 us -> 7.3 us
  waiting for transfers between devices: 3.91 us -> 0.46 us
  blocking collectives: 27.6 us -> 30.2 us
  Pallas kernels: 30.7 us -> 28.3 us
  local copies, waits for them, and re-layouts: 0.71 us -> 1.64 us
  other arithmetic: 1.64 us -> 0.77 us
    all_to_all x2 -> x1, starting transfers between devices: 12.3 us -> 7.3 us  [shards(): rims = lax.all_to_all(rims, ALL, 0, 0)]
    all_to_all x2 -> x1, waiting for transfers between devices: 3.91 us -> 0.46 us  [shards(): rims = lax.all_to_all(rims, ALL, 0, 0)]
    pallas_call x5, Pallas kernels: 22.8 us -> 20.5 us  [call(): pl.pallas_call(kernel, out_shape=[pltpu.HBM(shape, dtype) if spec is HBM...]
    all_to_all x1, blocking collectives: 9.35 us -> 11.2 us  [shards(): came = lax.all_to_all(parts, 'z', 0, 0)]
    another operation x0 -> x4, local copies, waits for them, and re-layouts: none -> 0.94 us  [the longest x3 0.86 us: shards(): jnp.stack([value.reshape(chunks, chunk) for value in [send_index, receive...]
    concatenate x1 -> x0, other arithmetic: 0.79 us -> none  [shards(): jnp.concatenate([send_index.reshape(chunks, 1, chunk), receivers.reshape(...]
  transfers between devices with their start and end apart: 2 -> 1, of which waited for: 1 -> 1; matrix products, arithmetic and copies ran while one was open for 2% -> 2% of each run, Pallas kernels for 10% -> 11%
where the time goes in v5:
time: 70.6 us; the launch traced here: 70 us
  blocking collectives  30.2 us (43%)
  Pallas kernels  28.3 us (40%)
  starting transfers between devices  7.3 us (10%)
  local copies, waits for them, and re-layouts  1.64 us (2%)
  between operations  1.35 us (2%)
  other arithmetic  0.77 us (1%)
    pallas_call x5, Pallas kernels, call(): pl.pallas_call(kernel, out_shape=[pltpu.HBM(shape, dtype) if spec is HBM...  20.5 us
    all_to_all x2, blocking collectives, shards(): came = lax.all_to_all(parts, PLANE, 0, 0)  19 us
    all_to_all x1, blocking collectives, shards(): came = lax.all_to_all(parts, 'z', 0, 0)  11.2 us
    pallas_call x1, Pallas kernels, shards(): pl.pallas_call(early_kernel, grid=(chunks,), out_shape=[pltpu.HBM(shape,...  7.8 us
    all_to_all x1, starting transfers between devices, shards(): rims = lax.all_to_all(rims, ALL, 0, 0)  7.3 us
  transfers between devices with their start and end apart: 1, of which 1 were waited for; matrix products, arithmetic and copies ran while one was open for 2% of the time, Pallas kernels for 11%

profile of v5, /device:TPU:0, one launch (start us, length us, event | category | flops | bytes accessed | tf_op | source)
XLA Modules:
  0.0 70.0 jit_solution(7816117375464106517)
XLA Ops:
  0.6 1.5 %shard_map.162 = bf16[32,32,128]{2,1,0:T(8,128)(2,1)} custom-call(bf16[256,128]{1,0:T(8,128)(2,1)} %nodes_in.1), custom_call_target="tpu_custom_call" | custom-call | tf_op jit(solution)/shard_map/pallas_call | solution.py:60
  2.1 7.3 %all-to-all-start = ((bf16[32,32,128]{2,1,0:T(8,128)(2,1)}), bf16[32,32,128]{2,1,0:T(8,128)(2,1)S(1)}, u32[]{:S(2)}, u32[]{:S(2)}) async-start(bf16[32,32,128]{2,1,0:T(8,128)(2,1)} %shard_map.162), calls=%async_computation | async-start | bytes 524288 | tf_op jit(solution)/shard_map/all_to_all | solution.py:507
  10.1 0.8 %convert_subtract_fusion = (s32[4096]{0:T(1024)S(1)}, s32[4096]{0:T(1024)S(1)}) fusion(s32[]{:T(128)S(6)} %add.32, s32[4096]{0:T(1024)} %param.13, s32[]{:T(128)} %add.31, s32[]{:T(128)} %axis_index.33), kind=kLoop, calls=%fused_computation.20 | loop fusion | flops 221184 | bytes 49164 | tf_op jit(solution)/shard_map/sub | solution.py:520
  10.9 0.8 %stack.27.info = s32[4,8,1024]{2,1,0:T(8,128)S(1)} concatenate(s32[4,1,1024]{2,1,0:T(1,128)S(1)} %bitcast.8, s32[4,1,1024]{2,1,0:T(1,128)} %bitcast.9, s32[4,1,1024]{2,1,0:T(1,128)S(1)} %bitcast.7, s32[4,1,1024]{2,1,0:T(1,128)S(1)} %stack_reshape.15, s32[4,4,1024]{2,1,0:T(4,128)S(1)} %stack.26), dimensions={1} | concatenate | bytes 262144 | tf_op jit(solution)/shard_map/stack | solution.py:517
  11.7 7.8 %shard_map.163 = (bf16[4096,512]{1,0:T(8,128)(2,1)}, bf16[4,640,1024]{2,1,0:T(8,128)(2,1)}, bf16[4096,128]{1,0:T(8,128)(2,1)}, f32[4096,128]{1,0:T(8,128)}, bf16[4096,128]{1,0:T(8,128)(2,1)}) custom-call(bf16[256,128]{1,0:T(8,128)(2,1)} %nodes_in.1, bf16[4096,128]{1,0:T(8,128)(2,1)} %edges_in.1, bf16[4096,128]{1,0:T(8,128)(2,1)} %edge_cot.1, ...), custom_call_target="tpu_custom_call" | custom-call | tf_op jit(solution)/shard_map/pallas_call | solution.py:535
  19.5 0.1 stack.25.place
  19.6 0.5 all-to-all-done.rims_in
  20.0 0.0 copy-start
  20.1 0.7 copy-done
  20.8 16.8 %shard_map.164 = (bf16[256,128]{1,0:T(8,128)(2,1)}, bf16[4096,128]{1,0:T(8,128)(2,1)}, f32[256,128]{1,0:T(8,128)}, bf16[8,176,128]{2,1,0:T(8,128)(2,1)S(1)}) custom-call(s32[6]{0:T(128)S(1)} %stack.25.place, bf16[256,128]{1,0:T(8,128)(2,1)} %nodes_in.1, bf16[32,32,128]{2,1,0:T(8,128)(2,1)} %copy-done, bf16[4096,128]{1,0:T(8,128)(2,1)} %edges_in.1, ...), custom_call_target="tpu_custom_call" | custom-call | tf_op jit(solution)/shard_map/pallas_call | solution.py:60
  37.6 10.9 %all_to_all.20.came = bf16[8,176,128]{2,1,0:T(8,128)(2,1)S(1)} all-to-all(bf16[8,176,128]{2,1,0:T(8,128)(2,1)S(1)} %get-tuple-element.32), channel_id=1, replica_groups=mesh['strip'=4,'z'=4,'y'=2] {'strip','y'}, dimensions={0} | all-to-all | bytes 720896 | tf_op jit(solution)/shard_map/all_to_all | solution.py:634
  48.5 0.6 shard_map.165
  49.1 11.2 %all_to_all.21.came = bf16[4,144,128]{2,1,0:T(8,128)(2,1)S(1)} all-to-all(bf16[4,144,128]{2,1,0:T(8,128)(2,1)S(1)} %get-tuple-element.33), channel_id=1, replica_groups=mesh['strip'=4,'z'=4,'y'=2] {'z'}, dimensions={0} | all-to-all | bytes 294912 | tf_op jit(solution)/shard_map/all_to_all | solution.py:641
  60.3 8.1 %all_to_all.22.came = bf16[8,112,128]{2,1,0:T(8,128)(2,1)S(1)} all-to-all(bf16[8,112,128]{2,1,0:T(8,128)(2,1)S(1)} %get-tuple-element.35), channel_id=1, replica_groups=mesh['strip'=4,'z'=4,'y'=2] {'strip','y'}, dimensions={0} | all-to-all | bytes 458752 | tf_op jit(solution)/shard_map/all_to_all | solution.py:649
  68.4 1.7 %shard_map.167 = (f32[256,128]{1,0:T(8,128)}, f32[384,128]{1,0:T(8,128)}, f32[128,128]{1,0:T(8,128)}, f32[256,128]{1,0:T(8,128)}, f32[128,128]{1,0:T(8,128)}) custom-call(bf16[8,112,128]{2,1,0:T(8,128)(2,1)S(1)} %all_to_all.22.came, f32[32,128]{1,0:T(8,128)S(1)} %get-tuple-element.36.rim_grad, f32[256,128]{1,0:T(8,128)} %get-tuple-element.37.local_grad_in), custom_call_target="tpu_custom_call" | custom-call | tf_op jit(solution)/shard_map/pallas_call | solution.py:60
  (3 shorter events, 0.0 us)
Async XLA Ops:
  2.1 18.0 %all-to-all-start = ((bf16[32,32,128]{2,1,0:T(8,128)(2,1)}), bf16[32,32,128]{2,1,0:T(8,128)(2,1)S(1)}, u32[]{:S(2)}, u32[]{:S(2)}) async-start(bf16[32,32,128]{2,1,0:T(8,128)(2,1)} %shard_map.162), calls=%async_computation | async-start | bytes 524288 | tf_op jit(solution)/shard_map/all_to_all | solution.py:507
  20.0 0.7 %copy-start = (bf16[32,32,128]{2,1,0:T(8,128)(2,1)}, bf16[32,32,128]{2,1,0:T(8,128)(2,1)S(1)}, u32[]{:S(2)}) copy-start(bf16[32,32,128]{2,1,0:T(8,128)(2,1)S(1)} %all-to-all-done.rims_in) | copy-start | bytes 786436

commit v6 on v5

--- a/solution.py
+++ b/solution.py
@@ -10,7 +10,7 @@
 from jax.sharding import PartitionSpec as P
 
 EPS = 1e-05
-CHUNK = 1024
+CHUNK = 512
 PLANE = ("strip", "y")
 ALL = ("strip", "z", "y")
 F32 = jnp.float32
@@ -129,7 +129,7 @@
 
 
 def layer_kernel(
-    place,
+    edge_count,
     nodes_in,
     rims_in,
     edges_in,
@@ -145,7 +145,7 @@
     node_cot_in,
     new_nodes_out,
     new_edges_out,
-    local_grad_out,
+    local_grad,
     parts,
     nodes,
     rims,
@@ -162,7 +162,6 @@
     node_cot,
     new_nodes,
     new_edges,
-    local_grad,
     near_rows,
     far_rows,
     tables,
@@ -177,10 +176,16 @@
     ge_out,
     agg,
     packed,
+    act_now,
+    centre_now,
+    unit_now,
+    out_now,
+    in_now,
+    last_now,
     small_sems,
     sems,
     out_sems,
-    last_sems,
+    last_sem,
 ):
     count_p, width = nodes.shape
     border = rims.shape[1]
@@ -189,7 +194,10 @@
     chunks, _, chunk = hot_t.shape
     half = chunk // 2
     share = parts.shape[1] - 2 * border
-    my_strip, my_y, live_count, my_sub, subs = (place[k] for k in (0, 2, 3, 4, 5))
+    my_strip, my_y = lax.axis_index("strip"), lax.axis_index("y")
+    subs = lax.axis_size("z") * lax.axis_size("y")
+    my_sub = lax.axis_index("z") * lax.axis_size("y") + my_y
+    live_count = edge_count[0]
 
     small = [
         pltpu.make_async_copy(source, target, small_sems.at[k])
@@ -283,35 +291,50 @@
     lane = lax.broadcasted_iota(jnp.int32, (half, 2 * width), 1)
     edge_row = jnp.where(lane < width, row, row + half)
     agg[...] = jnp.zeros_like(agg)
+    for buffer in (act_now, centre_now, unit_now):
+        buffer[...] = jnp.zeros_like(buffer)
+
+    def clamped(step):
+        return jnp.clip(step, 0, chunks - 1)
 
     def forward(step, carry):
-        rows = span(step)
-        for copy in fetch(step, ahead):
-            copy.wait()
-        begun = pre_part[rows]
+        @pl.when(step < chunks)
+        def arrive():
+            for copy in fetch(step, ahead):
+                copy.wait()
+
+        agg[...] += mm(hot_t[clamped(step - 3), :count_p], unit_now[...])
+
+        place = clamped(step - 2)
+        centre = centre_now[...]
+        spare = mm((centre * centre).astype(BF16), means[...])
+        factor = jnp.where(edge_row < live_count - place * chunk, lax.rsqrt(spare + EPS), 0.0)
+        unit = centre * factor
+        scale[pairs_of(place)] = factor
+        normed[pairs_of(place)] = unit
+        unit_now[...] = unpaired(unit.astype(BF16))
+        new_edges[span(place)] = unpaired((paired(edges[span(place)].astype(F32)) + unit).astype(BF16))
+
+        centre_now[...] = mm(act_now[...], centring[...])
+
+        place = clamped(step)
+        rows = span(place)
         beyond = far[rows] > 0
         picked = mm(hot[rows, :count_p], tables[...])
-        edge = paired(edges[rows].astype(F32))
-        recv_t = hot_t[step, :count_p]
-        so_far = agg[...]
-        pre = begun + jnp.where(beyond, picked[:, width:], picked[:, :width])
+        pre = pre_part[rows] + jnp.where(beyond, picked[:, width:], picked[:, :width])
         act, bend = silu_and_slope(paired(pre))
         act = act.astype(BF16)
-        centre = mm(act, centring[...])
-        spare = mm((centre * centre).astype(BF16), means[...])
-        factor = jnp.where(edge_row < live_count - step * chunk, lax.rsqrt(spare + EPS), 0.0)
-        unit = centre * factor
-        so_far = so_far + mm(recv_t, unpaired(unit.astype(BF16)))
-        slope[pairs_of(step)] = bend
+        slope[pairs_of(place)] = bend
+        act_now[...] = act
         hidden[rows] = unpaired(act)
-        scale[pairs_of(step)] = factor
-        normed[pairs_of(step)] = unit
-        new_edges[rows] = unpaired((edge + unit).astype(BF16))
-        agg[...] = so_far
-        emit(step).start()
+
+        @pl.when(step >= 3)
+        def leave():
+            emit(step - 3).start()
+
         return carry
 
-    lax.fori_loop(0, chunks, forward, 0)
+    lax.fori_loop(0, chunks + 3, forward, 0)
 
     for copy in small[4:]:
         copy.wait()
@@ -330,41 +353,47 @@
     agg[...] = cot + d_joined[:, :width]
     packed[4 * width : 6 * width] = mm_tn(joined, d_pre).astype(BF16)
     packed[6 * width : 7 * width] = mm_tn(node_act, d_outer).astype(BF16)
-    node_copy = pltpu.make_async_copy(new_nodes, new_nodes_out, last_sems.at[0])
+    node_copy = pltpu.make_async_copy(new_nodes, new_nodes_out, last_sem)
     node_copy.start()
 
     sums[...] = jnp.zeros_like(sums)
     ge_out[...] = jnp.zeros_like(ge_out)
+    for buffer in (act_now, centre_now, out_now, in_now, last_now):
+        buffer[...] = jnp.zeros_like(buffer)
 
     def backward(step, carry):
-        rows = span(step)
-        for copy in fetch(step, behind):
-            copy.wait()
-        cot = cot_part[rows].astype(F32)
-        recv = hot[rows, count_p:]
-        unit = normed[pairs_of(step)]
-        factor = scale[pairs_of(step)]
-        bend = slope[pairs_of(step)]
-        act = hidden[rows]
+        @pl.when(step < chunks)
+        def arrive():
+            for copy in fetch(step, behind):
+                copy.wait()
+
+        place = clamped(step - 3)
+        sums[...] += mm(hot_t[place], in_now[...])
+        ge_out[...] += mm_tn(hidden[span(place)], last_now[...])
+
+        place = clamped(step - 2)
+        rows = span(place)
+        d_out = out_now[...]
+        d_in = unpaired(mm_nt(d_out, back[...]) * slope[pairs_of(place)])
         beyond = far[rows] > 0
-        turned = hot_t[step]
-        upstream = paired(cot + mm(recv, d_agg))
-        along = mm((upstream * unit).astype(BF16), means[...])
-        d_out = (factor * (upstream - unit * along)).astype(BF16)
-        d_in = unpaired(mm_nt(d_out, back[...]) * bend)
         zero = jnp.zeros_like(d_in)
-        near_far = jnp.concatenate(
-            [
-                jnp.where(beyond, zero, d_in).astype(BF16),
-                jnp.where(beyond, d_in, zero).astype(BF16),
-            ],
-            axis=1,
-        )
-        ge_out[...] += mm_tn(act, unpaired(d_out))
-        sums[...] += mm(turned, near_far)
+        in_now[:, :width] = jnp.where(beyond, zero, d_in).astype(BF16)
+        in_now[:, width:] = jnp.where(beyond, d_in, zero).astype(BF16)
+        last_now[...] = unpaired(d_out)
+
+        place = clamped(step - 1)
+        along = mm(act_now[...], means[...])
+        d_out = centre_now[...] - normed[pairs_of(place)] * along
+        out_now[...] = (scale[pairs_of(place)] * d_out).astype(BF16)
+
+        place = clamped(step)
+        rows = span(place)
+        upstream = paired(cot_part[rows].astype(F32) + mm(hot[rows, count_p:], d_agg))
+        centre_now[...] = upstream
+        act_now[...] = (upstream * normed[pairs_of(place)]).astype(BF16)
         return carry
 
-    lax.fori_loop(0, chunks, backward, 0)
+    lax.fori_loop(0, chunks + 3, backward, 0)
 
     recv_sums = (sums[:count_p, :width] + sums[:count_p, width:]).astype(BF16)
     near_sums = sums[count_p : 2 * count_p, :width].astype(BF16)
@@ -381,8 +410,6 @@
         + mm_nt(near_sums, w_edge_in[:width])
         + mm_nt(recv_sums, w_edge_in[width : 2 * width])
     )
-    grad_copy = pltpu.make_async_copy(local_grad, local_grad_out, last_sems.at[1])
-    grad_copy.start()
     owed = mm_nt(far_sums, w_edge_in[:width]).astype(BF16)
     for slot in range(slots):
         parts[slot, :share] = packed[slot * share : (slot + 1) * share]
@@ -410,10 +437,9 @@
     for step in range(chunks):
         emit(step).wait()
     node_copy.wait()
-    grad_copy.wait()
-
-
-def plane_sum_kernel(place, came, out, mine):
+
+
+def plane_sum_kernel(came, out, mine):
     border = mine.shape[0]
     zs = out.shape[0]
     share = out.shape[1] - border
@@ -426,7 +452,7 @@
     for target in range(zs):
         out[target, :share] = share_total
         out[target, share:] = jnp.zeros_like(beyond)
-    target = place[1] + 1 - 2 * place[2]
+    target = lax.axis_index("z") + 1 - 2 * lax.axis_index("y")
 
     @pl.when((target >= 0) & (target < zs))
     def put():
@@ -444,27 +470,21 @@
     rim_grad[...] = mine[...] + total[share:]
 
 
-def finish_kernel(came, rim_grad, local_grad_in, *refs):
-    outs, (local_grad, grads, in_sem, sems) = refs[:-4], refs[-4:]
+def finish_kernel(came, rim_grad, local_grad, node_grad, *outs):
     border = rim_grad.shape[0]
-    slots, share, _ = came.shape
-    fetch = pltpu.make_async_copy(local_grad_in, local_grad, in_sem)
-    fetch.start()
-    for slot in range(slots):
-        grads[slot * share : (slot + 1) * share] = came[slot].astype(F32)
-    copies = []
+    share = came.shape[1]
+    node_grad[...] = local_grad[...]
+    node_grad[:border] += rim_grad[...]
     start = 0
-    for k, out in enumerate(outs[1:]):
+    for out in outs:
         size = out.shape[0]
-        copies.append(pltpu.make_async_copy(grads.at[pl.ds(start, size)], out, sems.at[k]))
-        copies[-1].start()
+        done = 0
+        while done < size:
+            slot, offset = divmod(start + done, share)
+            step = min(size - done, share - offset)
+            out[done : done + step] = came[slot, offset : offset + step].astype(F32)
+            done += step
         start += size
-    fetch.wait()
-    local_grad[:border] += rim_grad[...]
-    copies.append(pltpu.make_async_copy(local_grad, outs[0], sems.at[len(outs) - 1]))
-    copies[-1].start()
-    for copy in copies:
-        copy.wait()
 
 
 def shards(
@@ -489,7 +509,6 @@
     my_strip, my_z, my_y = (lax.axis_index(axis).astype(jnp.int32) for axis in ALL)
     my_sub = my_z * ys + my_y
     devices = strips * subs
-    place = jnp.stack([my_strip, my_z, my_y, edge_count[0], my_sub, jnp.int32(subs)])
 
     (rims,) = call(
         rim_kernel,
@@ -583,7 +602,7 @@
             ((slots, share + 2 * border, width), BF16),
         ],
         [
-            place,
+            edge_count,
             node_latents,
             rims,
             edge_latents,
@@ -607,7 +626,6 @@
             like(node_cotangent),
             pltpu.VMEM((count_p, width), BF16),
             pltpu.VMEM((count_e, width), BF16),
-            pltpu.VMEM((count_p, width), F32),
             pltpu.VMEM((count_p, width), BF16),
             pltpu.VMEM((8 * border, width), BF16),
             pltpu.VMEM((count_p, 2 * width), BF16),
@@ -622,12 +640,18 @@
             pltpu.VMEM((width, width), F32),
             pltpu.VMEM((count_p, width), F32),
             pltpu.VMEM((slots * share, width), BF16),
+            pltpu.VMEM((chunk // 2, 2 * width), BF16),
+            pltpu.VMEM((chunk // 2, 2 * width), F32),
+            pltpu.VMEM((chunk, width), BF16),
+            pltpu.VMEM((chunk // 2, 2 * width), BF16),
+            pltpu.VMEM((chunk, 2 * width), BF16),
+            pltpu.VMEM((chunk, width), BF16),
             SEM((7,)),
             SEM((8, chunks)),
             SEM((chunks,)),
-            SEM((2,)),
-        ],
-        [HBM, HBM, HBM, VMEM],
+            SEM,
+        ],
+        [HBM, HBM, VMEM, VMEM],
         limit=48,
     )
 
@@ -635,8 +659,8 @@
     parts, mine = call(
         plane_sum_kernel,
         [((zs, share + border, width), BF16), ((border, width), F32)],
-        [place, came],
-        [SMEM, VMEM],
+        [came],
+        [VMEM],
     )
     came = lax.all_to_all(parts, "z", 0, 0)
     factor = 1.0 / math.sqrt(count_e * strips * subs)
@@ -651,14 +675,7 @@
         finish_kernel,
         [((rows, width), F32) for rows in (count_p, 3 * width, width, 2 * width, width)],
         [came, rim_grad, local_grad],
-        [VMEM, VMEM, HBM],
-        [
-            pltpu.VMEM((count_p, width), F32),
-            pltpu.VMEM((slots * share, width), F32),
-            SEM,
-            SEM((5,)),
-        ],
-        [HBM] * 5,
+        [VMEM, VMEM, VMEM],
     )
     return (new_nodes, new_edges, node_grad, *grads)
 

time: 70.6 us -> 72.6 us (1.028)
  Pallas kernels: 28.3 us -> 30.4 us
    pallas_call x1, Pallas kernels: 7.8 us -> 9.82 us  [shards(): pl.pallas_call(early_kernel, grid=(chunks,), out_shape=[pltpu.HBM(shape,...]
  transfers between devices with their start and end apart: 1 -> 1, of which waited for: 1 -> 0; matrix products, arithmetic and copies ran while one was open for 2% -> 2% of each run, Pallas kernels for 11% -> 14%
where the time goes in v6:
time: 72.6 us; the launch traced here: 72 us
  blocking collectives  30.6 us (42%)
  Pallas kernels  30.4 us (42%)
  starting transfers between devices  7.3 us (10%)
  local copies, waits for them, and re-layouts  1.55 us (2%)
  between operations  1.35 us (2%)
  other arithmetic  0.77 us (1%)
    pallas_call x5, Pallas kernels, call(): pl.pallas_call(kernel, out_shape=[pltpu.HBM(shape, dtype) if spec is HBM...  20.5 us
    all_to_all x2, blocking collectives, shards(): came = lax.all_to_all(parts, PLANE, 0, 0)  19.4 us
    all_to_all x1, blocking collectives, shards(): came = lax.all_to_all(parts, 'z', 0, 0)  11.2 us
    pallas_call x1, Pallas kernels, shards(): pl.pallas_call(early_kernel, grid=(chunks,), out_shape=[pltpu.HBM(shape,...  9.82 us
    all_to_all x1, starting transfers between devices, shards(): rims = lax.all_to_all(rims, ALL, 0, 0)  7.3 us
  transfers between devices with their start and end apart: 1, of which 0 were waited for; matrix products, arithmetic and copies ran while one was open for 2% of the time, Pallas kernels for 14%

profile of v6, /device:TPU:0, one launch (start us, length us, event | category | flops | bytes accessed | tf_op | source)
XLA Modules:
  0.0 72.0 jit_solution(7635390925795762976)
XLA Ops:
  0.6 1.5 %shard_map.162 = bf16[32,32,128]{2,1,0:T(8,128)(2,1)} custom-call(bf16[256,128]{1,0:T(8,128)(2,1)} %nodes_in.1), custom_call_target="tpu_custom_call" | custom-call | tf_op jit(solution)/shard_map/pallas_call | solution.py:60
  2.1 7.3 %all-to-all-start = ((bf16[32,32,128]{2,1,0:T(8,128)(2,1)}), bf16[32,32,128]{2,1,0:T(8,128)(2,1)S(1)}, u32[]{:S(2)}, u32[]{:S(2)}) async-start(bf16[32,32,128]{2,1,0:T(8,128)(2,1)} %shard_map.162), calls=%async_computation | async-start | bytes 524288 | tf_op jit(solution)/shard_map/all_to_all | solution.py:526
  10.1 0.8 %convert_subtract_fusion = (s32[4096]{0:T(1024)S(1)}, s32[4096]{0:T(1024)S(1)}) fusion(s32[]{:T(128)S(6)} %add.32, s32[4096]{0:T(1024)} %param.13, s32[]{:T(128)S(6)} %add.31, s32[]{:T(128)S(6)} %axis_index.33), kind=kLoop, calls=%fused_computation.20 | loop fusion | flops 221184 | bytes 49164 | tf_op jit(solution)/shard_map/sub | solution.py:539
  10.9 0.8 %stack.7.info = s32[8,8,512]{2,1,0:T(8,128)S(1)} concatenate(s32[8,1,512]{2,1,0:T(1,128)S(1)} %bitcast.4, s32[8,1,512]{2,1,0:T(1,128)} %bitcast.5, s32[8,1,512]{2,1,0:T(1,128)S(1)} %bitcast.3, s32[8,1,512]{2,1,0:T(1,128)S(1)} %stack_reshape.15, s32[8,4,512]{2,1,0:T(4,128)S(1)} %stack.6), dimensions={1} | concatenate | bytes 262144 | tf_op jit(solution)/shard_map/stack | solution.py:536
  11.7 9.8 %shard_map.163 = (bf16[4096,512]{1,0:T(8,128)(2,1)}, bf16[8,640,512]{2,1,0:T(8,128)(2,1)}, bf16[4096,128]{1,0:T(8,128)(2,1)}, f32[4096,128]{1,0:T(8,128)}, bf16[4096,128]{1,0:T(8,128)(2,1)}) custom-call(bf16[256,128]{1,0:T(8,128)(2,1)} %nodes_in.1, bf16[4096,128]{1,0:T(8,128)(2,1)} %edges_in.1, bf16[4096,128]{1,0:T(8,128)(2,1)} %edge_cot.1, ...), custom_call_target="tpu_custom_call" | custom-call | tf_op jit(solution)/shard_map/pallas_call | solution.py:554
  21.5 0.0 all-to-all-done.rims_in
  21.5 0.0 copy-start
  21.5 0.7 copy-done
  22.2 18.2 %shard_map.164 = (bf16[256,128]{1,0:T(8,128)(2,1)}, bf16[4096,128]{1,0:T(8,128)(2,1)}, f32[256,128]{1,0:T(8,128)S(1)}, bf16[8,176,128]{2,1,0:T(8,128)(2,1)S(1)}) custom-call(s32[1]{0:T(128)S(6)} %copy.18.edge_count, bf16[256,128]{1,0:T(8,128)(2,1)} %nodes_in.1, bf16[32,32,128]{2,1,0:T(8,128)(2,1)} %copy-done, bf16[4096,128]{1,0:T(8,128)(2,1)} %edges_in.1, ...), custom_call_target="tpu_custom_call" | custom-call | tf_op jit(solution)/shard_map/pallas_call | solution.py:60
  40.4 11.3 %all_to_all.20.came = bf16[8,176,128]{2,1,0:T(8,128)(2,1)S(1)} all-to-all(bf16[8,176,128]{2,1,0:T(8,128)(2,1)S(1)} %get-tuple-element.32), channel_id=1, replica_groups=mesh['strip'=4,'z'=4,'y'=2] {'strip','y'}, dimensions={0} | all-to-all | bytes 720896 | tf_op jit(solution)/shard_map/all_to_all | solution.py:658
  51.8 0.1 shard_map.165
  51.8 11.2 %all_to_all.21.came = bf16[4,144,128]{2,1,0:T(8,128)(2,1)S(1)} all-to-all(bf16[4,144,128]{2,1,0:T(8,128)(2,1)S(1)} %get-tuple-element.33), channel_id=1, replica_groups=mesh['strip'=4,'z'=4,'y'=2] {'z'}, dimensions={0} | all-to-all | bytes 294912 | tf_op jit(solution)/shard_map/all_to_all | solution.py:665
  63.1 8.1 %all_to_all.22.came = bf16[8,112,128]{2,1,0:T(8,128)(2,1)S(1)} all-to-all(bf16[8,112,128]{2,1,0:T(8,128)(2,1)S(1)} %get-tuple-element.35), channel_id=1, replica_groups=mesh['strip'=4,'z'=4,'y'=2] {'strip','y'}, dimensions={0} | all-to-all | bytes 458752 | tf_op jit(solution)/shard_map/all_to_all | solution.py:673
  71.1 0.8 %shard_map.167 = (f32[256,128]{1,0:T(8,128)}, f32[384,128]{1,0:T(8,128)}, f32[128,128]{1,0:T(8,128)}, f32[256,128]{1,0:T(8,128)}, f32[128,128]{1,0:T(8,128)}) custom-call(bf16[8,112,128]{2,1,0:T(8,128)(2,1)S(1)} %all_to_all.22.came, f32[32,128]{1,0:T(8,128)S(1)} %get-tuple-element.36.rim_grad, f32[256,128]{1,0:T(8,128)S(1)} %get-tuple-element.37.local_grad), custom_call_target="tpu_custom_call" | custom-call | tf_op jit(solution)/shard_map/pallas_call | solution.py:60
  (3 shorter events, 0.0 us)
Async XLA Ops:
  2.1 19.4 %all-to-all-start = ((bf16[32,32,128]{2,1,0:T(8,128)(2,1)}), bf16[32,32,128]{2,1,0:T(8,128)(2,1)S(1)}, u32[]{:S(2)}, u32[]{:S(2)}) async-start(bf16[32,32,128]{2,1,0:T(8,128)(2,1)} %shard_map.162), calls=%async_computation | async-start | bytes 524288 | tf_op jit(solution)/shard_map/all_to_all | solution.py:526
  21.5 0.7 copy-start

commit v7 on v6

--- a/solution.py
+++ b/solution.py
@@ -10,7 +10,8 @@
 from jax.sharding import PartitionSpec as P
 
 EPS = 1e-05
-CHUNK = 512
+CHUNK = 1024
+SPLIT = 2
 PLANE = ("strip", "y")
 ALL = ("strip", "z", "y")
 F32 = jnp.float32
@@ -49,6 +50,25 @@
     sig = 0.5 + 0.5 * jnp.tanh(0.5 * values)
     act = values * sig
     return (act, sig + act * (1.0 - sig))
+
+
+def found(codes, blocks):
+    lane = lax.broadcasted_iota(jnp.int32, codes.shape, 1)
+    one, zero = jnp.ones((), BF16), jnp.zeros((), BF16)
+    width = codes.shape[1]
+    return jnp.concatenate(
+        [
+            jnp.where(codes == (lane + width * k).astype(F32).astype(BF16), one, zero)
+            for k in range(blocks)
+        ],
+        axis=1,
+    )
+
+
+def found_t(line, size):
+    place = lax.broadcasted_iota(jnp.int32, (size, line.shape[1]), 0).astype(F32).astype(BF16)
+    one, zero = jnp.ones((), BF16), jnp.zeros((), BF16)
+    return jnp.where(place == line.astype(F32).astype(BF16), one, zero)
 
 
 def in_hbm(value):
@@ -88,43 +108,29 @@
     edge_cot,
     info,
     w_edge_in,
-    hot,
-    hot_t,
-    far,
+    send_codes,
+    recv_codes,
+    edges_t,
     pre_part,
     cot_part,
     tables,
 ):
     count_p, width = nodes.shape
-    chunk = edges.shape[0]
 
     @pl.when(pl.program_id(0) == 0)
     def prepare():
         tables[:count_p] = mm(nodes[...], w_edge_in[width : 2 * width]).astype(BF16)
         tables[count_p:] = w_edge_in[2 * width :]
 
-    lane = lax.broadcasted_iota(jnp.int32, (chunk, width), 1)
-    line = lax.broadcasted_iota(jnp.int32, (count_p, chunk), 0)
-
-    def found(column):
-        blocks = [
-            (column == lane + width * k).astype(F32).astype(BF16)
-            for k in range(count_p // width)
-        ]
-        return jnp.concatenate(blocks, axis=1)
-
-    index = info[0]
-    columns = index.T
+    columns = info[0].T
     edge = edges[...]
     cot = edge_cot[...].astype(F32)
-    recv = found(columns[:, 1:2])
+    recv = jnp.broadcast_to(columns[:, 1:2], edge.shape).astype(F32).astype(BF16)
+    recv_codes[...] = recv
+    send_codes[...] = jnp.broadcast_to(columns[:, 2:3], edge.shape).astype(F32).astype(BF16)
+    recv = found(recv, count_p // width)
     pre_part[...] = mm(jnp.concatenate([recv, edge], axis=1), tables[...])
-    hot[:, :count_p] = found(columns[:, 0:1])
-    hot[:, count_p:] = recv
-    hot_t[0, :count_p] = (line == index[1:2]).astype(F32).astype(BF16)
-    hot_t[0, count_p : 2 * count_p] = (line == index[0:1]).astype(F32).astype(BF16)
-    hot_t[0, 2 * count_p :] = edge.T
-    far[...] = jnp.broadcast_to(columns[:, 2:3], edge.shape).astype(F32).astype(BF16)
+    edges_t[0] = edge.T
     cot_part[...] = (cot - jnp.mean(cot, axis=1, keepdims=True)).astype(BF16)
 
 
@@ -133,9 +139,10 @@
     nodes_in,
     rims_in,
     edges_in,
-    hot_in,
-    hot_t_in,
-    far_in,
+    info_in,
+    send_codes_in,
+    recv_codes_in,
+    edges_t_in,
     pre_part_in,
     cot_part_in,
     w_edge_in_in,
@@ -150,9 +157,10 @@
     nodes,
     rims,
     edges,
-    hot,
-    hot_t,
-    far,
+    info,
+    send_codes,
+    recv_codes,
+    edges_t,
     pre_part,
     cot_part,
     w_edge_in,
@@ -176,12 +184,6 @@
     ge_out,
     agg,
     packed,
-    act_now,
-    centre_now,
-    unit_now,
-    out_now,
-    in_now,
-    last_now,
     small_sems,
     sems,
     out_sems,
@@ -191,8 +193,9 @@
     border = rims.shape[1]
     slots = parts.shape[0]
     strips = slots // 2
-    chunks, _, chunk = hot_t.shape
-    half = chunk // 2
+    chunks, _, chunk = edges_t.shape
+    block = chunk // SPLIT
+    half = block // 2
     share = parts.shape[1] - 2 * border
     my_strip, my_y = lax.axis_index("strip"), lax.axis_index("y")
     subs = lax.axis_size("z") * lax.axis_size("y")
@@ -217,22 +220,22 @@
     def span(step):
         return pl.ds(pl.multiple_of(step * chunk, chunk), chunk)
 
-    def pairs_of(step):
-        return pl.ds(pl.multiple_of(step * half, half), half)
+    def block_rows(step, part):
+        return pl.ds(pl.multiple_of(step * chunk + part * block, block), block)
+
+    def block_pairs(step, part):
+        return pl.ds(pl.multiple_of((step * SPLIT + part) * half, half), half)
 
     def fetch(step, which):
         rows = span(step)
-        first, second = pl.ds(0, count_p), pl.ds(count_p, count_p)
-        rest = pl.ds(count_p, count_p + width)
         pairs = [
-            (hot_in.at[rows, first], hot.at[rows, first]),
-            (far_in.at[rows], far.at[rows]),
+            (send_codes_in.at[rows], send_codes.at[rows]),
             (pre_part_in.at[rows], pre_part.at[rows]),
+            (info_in.at[step], info.at[step]),
             (edges_in.at[rows], edges.at[rows]),
-            (hot_t_in.at[step, first], hot_t.at[step, first]),
-            (hot_in.at[rows, second], hot.at[rows, second]),
+            (recv_codes_in.at[rows], recv_codes.at[rows]),
             (cot_part_in.at[rows], cot_part.at[rows]),
-            (hot_t_in.at[step, rest], hot_t.at[step, rest]),
+            (edges_t_in.at[step], edges_t.at[step]),
         ]
         return [pltpu.make_async_copy(*pairs[k], sems.at[k, step]) for k in which]
 
@@ -258,7 +261,7 @@
             axis=0,
         )
 
-    ahead, behind = range(5), range(5, 8)
+    ahead, behind = range(4), range(4, 7)
     for copy in small[:4] + fetch(0, ahead) + small[4:]:
         copy.start()
     for step in range(1, chunks):
@@ -291,50 +294,39 @@
     lane = lax.broadcasted_iota(jnp.int32, (half, 2 * width), 1)
     edge_row = jnp.where(lane < width, row, row + half)
     agg[...] = jnp.zeros_like(agg)
-    for buffer in (act_now, centre_now, unit_now):
-        buffer[...] = jnp.zeros_like(buffer)
-
-    def clamped(step):
-        return jnp.clip(step, 0, chunks - 1)
 
     def forward(step, carry):
-        @pl.when(step < chunks)
-        def arrive():
-            for copy in fetch(step, ahead):
-                copy.wait()
-
-        agg[...] += mm(hot_t[clamped(step - 3), :count_p], unit_now[...])
-
-        place = clamped(step - 2)
-        centre = centre_now[...]
-        spare = mm((centre * centre).astype(BF16), means[...])
-        factor = jnp.where(edge_row < live_count - place * chunk, lax.rsqrt(spare + EPS), 0.0)
-        unit = centre * factor
-        scale[pairs_of(place)] = factor
-        normed[pairs_of(place)] = unit
-        unit_now[...] = unpaired(unit.astype(BF16))
-        new_edges[span(place)] = unpaired((paired(edges[span(place)].astype(F32)) + unit).astype(BF16))
-
-        centre_now[...] = mm(act_now[...], centring[...])
-
-        place = clamped(step)
-        rows = span(place)
-        beyond = far[rows] > 0
-        picked = mm(hot[rows, :count_p], tables[...])
-        pre = pre_part[rows] + jnp.where(beyond, picked[:, width:], picked[:, :width])
-        act, bend = silu_and_slope(paired(pre))
-        act = act.astype(BF16)
-        slope[pairs_of(place)] = bend
-        act_now[...] = act
-        hidden[rows] = unpaired(act)
-
-        @pl.when(step >= 3)
-        def leave():
-            emit(step - 3).start()
-
+        for copy in fetch(step, ahead):
+            copy.wait()
+        recv_t = found_t(info[step][1:2], count_p)
+        units = []
+        for part in range(SPLIT):
+            rows, pairs = block_rows(step, part), block_pairs(step, part)
+            codes = send_codes[rows]
+            begun = pre_part[rows]
+            edge = paired(edges[rows].astype(F32))
+            place = jnp.where(codes < 0, -1 - codes, codes)
+            picked = mm(found(place, count_p // width), tables[...])
+            beyond = codes.astype(F32) < 0.0
+            pre = begun + jnp.where(beyond, picked[:, width:], picked[:, :width])
+            act, bend = silu_and_slope(paired(pre))
+            act = act.astype(BF16)
+            centre = mm(act, centring[...])
+            spare = mm((centre * centre).astype(BF16), means[...])
+            live = edge_row < live_count - step * chunk - part * block
+            factor = jnp.where(live, lax.rsqrt(spare + EPS), 0.0)
+            unit = centre * factor
+            slope[pairs] = bend
+            hidden[rows] = unpaired(act)
+            scale[pairs] = factor
+            normed[pairs] = unit
+            new_edges[rows] = unpaired((edge + unit).astype(BF16))
+            units.append(unpaired(unit.astype(BF16)))
+        agg[...] += mm(recv_t, jnp.concatenate(units, axis=0))
+        emit(step).start()
         return carry
 
-    lax.fori_loop(0, chunks + 3, forward, 0)
+    lax.fori_loop(0, chunks, forward, 0)
 
     for copy in small[4:]:
         copy.wait()
@@ -358,42 +350,38 @@
 
     sums[...] = jnp.zeros_like(sums)
     ge_out[...] = jnp.zeros_like(ge_out)
-    for buffer in (act_now, centre_now, out_now, in_now, last_now):
-        buffer[...] = jnp.zeros_like(buffer)
 
     def backward(step, carry):
-        @pl.when(step < chunks)
-        def arrive():
-            for copy in fetch(step, behind):
-                copy.wait()
-
-        place = clamped(step - 3)
-        sums[...] += mm(hot_t[place], in_now[...])
-        ge_out[...] += mm_tn(hidden[span(place)], last_now[...])
-
-        place = clamped(step - 2)
-        rows = span(place)
-        d_out = out_now[...]
-        d_in = unpaired(mm_nt(d_out, back[...]) * slope[pairs_of(place)])
-        beyond = far[rows] > 0
-        zero = jnp.zeros_like(d_in)
-        in_now[:, :width] = jnp.where(beyond, zero, d_in).astype(BF16)
-        in_now[:, width:] = jnp.where(beyond, d_in, zero).astype(BF16)
-        last_now[...] = unpaired(d_out)
-
-        place = clamped(step - 1)
-        along = mm(act_now[...], means[...])
-        d_out = centre_now[...] - normed[pairs_of(place)] * along
-        out_now[...] = (scale[pairs_of(place)] * d_out).astype(BF16)
-
-        place = clamped(step)
-        rows = span(place)
-        upstream = paired(cot_part[rows].astype(F32) + mm(hot[rows, count_p:], d_agg))
-        centre_now[...] = upstream
-        act_now[...] = (upstream * normed[pairs_of(place)]).astype(BF16)
+        for copy in fetch(step, behind):
+            copy.wait()
+        index = info[step]
+        turned = jnp.concatenate(
+            [found_t(index[1:2], count_p), found_t(index[0:1], count_p), edges_t[step]], axis=0
+        )
+        acts, outs, ins = [], [], []
+        for part in range(SPLIT):
+            rows, pairs = block_rows(step, part), block_pairs(step, part)
+            cot = cot_part[rows].astype(F32)
+            recv = found(recv_codes[rows], count_p // width)
+            unit = normed[pairs]
+            acts.append(hidden[rows])
+            beyond = send_codes[rows] < 0
+            upstream = paired(cot + mm(recv, d_agg))
+            along = mm((upstream * unit).astype(BF16), means[...])
+            d_out = (scale[pairs] * (upstream - unit * along)).astype(BF16)
+            outs.append(unpaired(d_out))
+            d_in = unpaired((mm_nt(d_out, back[...]) * slope[pairs]).astype(BF16))
+            zero = jnp.zeros_like(d_in)
+            ins.append(
+                jnp.concatenate(
+                    [jnp.where(beyond, zero, d_in), jnp.where(beyond, d_in, zero)], axis=1
+                )
+            )
+        ge_out[...] += mm_tn(jnp.concatenate(acts, axis=0), jnp.concatenate(outs, axis=0))
+        sums[...] += mm(turned, jnp.concatenate(ins, axis=0))
         return carry
 
-    lax.fori_loop(0, chunks + 3, backward, 0)
+    lax.fori_loop(0, chunks, backward, 0)
 
     recv_sums = (sums[:count_p, :width] + sums[:count_p, width:]).astype(BF16)
     near_sums = sums[count_p : 2 * count_p, :width].astype(BF16)
@@ -531,12 +519,13 @@
     block = (owner // subs - my_strip + 1) * 3 + (owner % subs - my_sub + 1)
     block = jnp.where(block > 4, block - 1, block)
     send_index = jnp.where(is_local, within, block * border + jnp.minimum(within, border - 1))
+    codes = jnp.where(is_local, send_index, -1 - send_index)
     chunk = min(CHUNK, count_e)
     chunks = count_e // chunk
     info = jnp.stack(
         [
             value.reshape(chunks, chunk)
-            for value in [send_index, receivers, 1 - is_local.astype(jnp.int32)]
+            for value in [send_index, receivers, codes]
             + [jnp.zeros_like(receivers)] * 5
         ],
         axis=1,
@@ -557,9 +546,9 @@
         out_shape=[
             pltpu.HBM(shape, dtype)
             for shape, dtype in [
-                ((count_e, 2 * count_p), BF16),
-                ((chunks, 2 * count_p + width, chunk), BF16),
                 ((count_e, width), BF16),
+                ((count_e, width), BF16),
+                ((chunks, width, chunk), BF16),
                 ((count_e, width), F32),
                 ((count_e, width), BF16),
             ]
@@ -572,9 +561,9 @@
             whole(3 * width, width),
         ],
         out_specs=[
-            by_rows(chunk, 2 * count_p),
-            by_chunk(2 * count_p + width, chunk),
             by_rows(chunk, width),
+            by_rows(chunk, width),
+            by_chunk(width, chunk),
             by_rows(chunk, width),
             by_rows(chunk, width),
         ],
@@ -606,6 +595,7 @@
             node_latents,
             rims,
             edge_latents,
+            info,
             *early,
             w_edge_in,
             w_edge_out,
@@ -613,11 +603,12 @@
             w_node_out,
             node_cotangent,
         ],
-        [SMEM] + [HBM] * 13,
+        [SMEM] + [HBM] * 14,
         [
             like(node_latents),
             like(rims),
             like(edge_latents),
+            like(info),
             *[like(value) for value in early],
             like(w_edge_in),
             like(w_edge_out),
@@ -640,14 +631,8 @@
             pltpu.VMEM((width, width), F32),
             pltpu.VMEM((count_p, width), F32),
             pltpu.VMEM((slots * share, width), BF16),
-            pltpu.VMEM((chunk // 2, 2 * width), BF16),
-            pltpu.VMEM((chunk // 2, 2 * width), F32),
-            pltpu.VMEM((chunk, width), BF16),
-            pltpu.VMEM((chunk // 2, 2 * width), BF16),
-            pltpu.VMEM((chunk, 2 * width), BF16),
-            pltpu.VMEM((chunk, width), BF16),
             SEM((7,)),
-            SEM((8, chunks)),
+            SEM((7, chunks)),
             SEM((chunks,)),
             SEM,
         ],

time: 72.6 us -> 63.9 us (0.88)
  Pallas kernels: 30.4 us -> 21.7 us
  waiting for transfers between devices: 0.01 us -> 2.27 us
  blocking collectives: 30.6 us -> 28.4 us
    pallas_call x5, Pallas kernels: 20.5 us -> 15.6 us  [call(): pl.pallas_call(kernel, out_shape=[pltpu.HBM(shape, dtype) if spec is HBM...]
    pallas_call x1, Pallas kernels: 9.82 us -> 6.06 us  [shards(): pl.pallas_call(early_kernel, grid=(chunks,), out_shape=[pltpu.HBM(shape,...]
    all_to_all x1, waiting for transfers between devices: 0.01 us -> 2.27 us  [shards(): rims = lax.all_to_all(rims, ALL, 0, 0)]
    all_to_all x2, blocking collectives: 19.4 us -> 18.1 us  [shards(): came = lax.all_to_all(parts, PLANE, 0, 0)]
    all_to_all x1, blocking collectives: 11.2 us -> 10.3 us  [shards(): came = lax.all_to_all(parts, 'z', 0, 0)]
    select_n x0 -> x1, other arithmetic: none -> 0.77 us  [shards(): codes = jnp.where(is_local, send_index, -1 - send_index)]
    sub x1 -> x0, other arithmetic: 0.77 us -> none  [shards(): 1 - is_local.astype(jnp.int32)]
  transfers between devices with their start and end apart: 1 -> 1, of which waited for: 0 -> 1; matrix products, arithmetic and copies ran while one was open for 2% -> 3% of each run, Pallas kernels for 14% -> 10%
where the time goes in v7:
time: 63.9 us; the launch traced here: 63.3 us
  blocking collectives  28.4 us (44%)
  Pallas kernels  21.7 us (34%)
  starting transfers between devices  7.3 us (11%)
  waiting for transfers between devices  2.27 us (4%)
  local copies, waits for them, and re-layouts  1.56 us (2%)
  between operations  1.35 us (2%)
  other arithmetic  0.77 us (1%)
    all_to_all x2, blocking collectives, shards(): came = lax.all_to_all(parts, PLANE, 0, 0)  18.1 us
    pallas_call x5, Pallas kernels, call(): pl.pallas_call(kernel, out_shape=[pltpu.HBM(shape, dtype) if spec is HBM...  15.6 us
    all_to_all x1, blocking collectives, shards(): came = lax.all_to_all(parts, 'z', 0, 0)  10.3 us
    all_to_all x1, starting transfers between devices, shards(): rims = lax.all_to_all(rims, ALL, 0, 0)  7.3 us
    pallas_call x1, Pallas kernels, shards(): pl.pallas_call(early_kernel, grid=(chunks,), out_shape=[pltpu.HBM(shape,...  6.06 us
    all_to_all x1, waiting for transfers between devices, shards(): rims = lax.all_to_all(rims, ALL, 0, 0)  2.27 us
  transfers between devices with their start and end apart: 1, of which 1 were waited for; matrix products, arithmetic and copies ran while one was open for 3% of the time, Pallas kernels for 10%

profile of v7, /device:TPU:0, one launch (start us, length us, event | category | flops | bytes accessed | tf_op | source)
XLA Modules:
  0.0 63.3 jit_solution(5402079110244707506)
XLA Ops:
  0.6 1.5 %shard_map.162 = bf16[32,32,128]{2,1,0:T(8,128)(2,1)} custom-call(bf16[256,128]{1,0:T(8,128)(2,1)} %nodes_in.1), custom_call_target="tpu_custom_call" | custom-call | tf_op jit(solution)/shard_map/pallas_call | solution.py:80
  2.1 7.3 %all-to-all-start = ((bf16[32,32,128]{2,1,0:T(8,128)(2,1)}), bf16[32,32,128]{2,1,0:T(8,128)(2,1)S(1)}, u32[]{:S(2)}, u32[]{:S(2)}) async-start(bf16[32,32,128]{2,1,0:T(8,128)(2,1)} %shard_map.162), calls=%async_computation | async-start | bytes 524288 | tf_op jit(solution)/shard_map/all_to_all | solution.py:514
  10.1 0.8 %subtract_select_fusion = (s32[4096]{0:T(1024)S(1)}, s32[4096]{0:T(1024)S(1)}) fusion(s32[]{:T(128)S(6)} %add.32, s32[4096]{0:T(1024)} %param.13, s32[]{:T(128)S(6)} %add.31, s32[]{:T(128)S(6)} %axis_index.33), kind=kLoop, calls=%fused_computation.1 | loop fusion | flops 221184 | bytes 49164 | tf_op jit(solution)/shard_map/jit(_where)/select_n | solution.py:522
  10.9 0.8 %stack.7.info.info_in = s32[4,8,1024]{2,1,0:T(8,128)S(1)} concatenate(s32[4,1,1024]{2,1,0:T(1,128)S(1)} %bitcast.4, s32[4,1,1024]{2,1,0:T(1,128)} %bitcast.5, s32[4,1,1024]{2,1,0:T(1,128)S(1)} %bitcast.3, s32[4,1,1024]{2,1,0:T(1,128)S(1)} %stack_reshape.15, s32[4,4,1024]{2,1,0:T(4,128)S(1)} %stack.6), dimensions={1} | concatenate | bytes 262144 | tf_op jit(solution)/shard_map/stack | solution.py:525
  11.7 0.0 copy-start
  11.7 6.1 %shard_map.163 = (bf16[4096,128]{1,0:T(8,128)(2,1)}, bf16[4096,128]{1,0:T(8,128)(2,1)}, bf16[4,128,1024]{2,1,0:T(8,128)(2,1)}, f32[4096,128]{1,0:T(8,128)}, bf16[4096,128]{1,0:T(8,128)(2,1)}) custom-call(bf16[256,128]{1,0:T(8,128)(2,1)} %nodes_in.1, bf16[4096,128]{1,0:T(8,128)(2,1)} %edges_in.1, bf16[4096,128]{1,0:T(8,128)(2,1)} %edge_cot.1, ...), custom_call_target="tpu_custom_call" | custom-call | tf_op jit(solution)/shard_map/pallas_call | solution.py:543
  17.8 2.3 %all-to-all-done.rims_in = bf16[32,32,128]{2,1,0:T(8,128)(2,1)S(1)} async-done(((bf16[32,32,128]{2,1,0:T(8,128)(2,1)}), bf16[32,32,128]{2,1,0:T(8,128)(2,1)S(1)}, u32[]{:S(2)}, u32[]{:S(2)}) %all-to-all-start) | async-done | bytes 262176 | tf_op jit(solution)/shard_map/all_to_all | solution.py:514
  20.0 0.0 copy-start.1
  20.1 0.0 copy-done
  20.1 0.7 %copy-done.1 = bf16[32,32,128]{2,1,0:T(8,128)(2,1)} copy-done((bf16[32,32,128]{2,1,0:T(8,128)(2,1)}, bf16[32,32,128]{2,1,0:T(8,128)(2,1)S(1)}, u32[]{:S(2)}) %copy-start.1) | copy-done | bytes 262168
  20.7 13.3 %shard_map.164 = (bf16[256,128]{1,0:T(8,128)(2,1)}, bf16[4096,128]{1,0:T(8,128)(2,1)}, f32[256,128]{1,0:T(8,128)S(1)}, bf16[8,176,128]{2,1,0:T(8,128)(2,1)S(1)}) custom-call(s32[1]{0:T(128)S(6)} %copy.18.edge_count, bf16[256,128]{1,0:T(8,128)(2,1)} %nodes_in.1, bf16[32,32,128]{2,1,0:T(8,128)(2,1)} %copy-done.1, bf16[4096,128]{1,0:T(8,128)(2,1)} %edges_in.1, ...), custom_call_target="tpu_custom_call" | custom-call | tf_op jit(solution)/shard_map/pallas_call | solution.py:80
  34.0 10.0 %all_to_all.20.came = bf16[8,176,128]{2,1,0:T(8,128)(2,1)S(1)} all-to-all(bf16[8,176,128]{2,1,0:T(8,128)(2,1)S(1)} %get-tuple-element.32), channel_id=1, replica_groups=mesh['strip'=4,'z'=4,'y'=2] {'strip','y'}, dimensions={0} | all-to-all | bytes 720896 | tf_op jit(solution)/shard_map/all_to_all | solution.py:643
  44.0 0.1 shard_map.165
  44.1 10.3 %all_to_all.21.came = bf16[4,144,128]{2,1,0:T(8,128)(2,1)S(1)} all-to-all(bf16[4,144,128]{2,1,0:T(8,128)(2,1)S(1)} %get-tuple-element.33), channel_id=1, replica_groups=mesh['strip'=4,'z'=4,'y'=2] {'z'}, dimensions={0} | all-to-all | bytes 294912 | tf_op jit(solution)/shard_map/all_to_all | solution.py:650
  54.4 8.1 %all_to_all.22.came = bf16[8,112,128]{2,1,0:T(8,128)(2,1)S(1)} all-to-all(bf16[8,112,128]{2,1,0:T(8,128)(2,1)S(1)} %get-tuple-element.35), channel_id=1, replica_groups=mesh['strip'=4,'z'=4,'y'=2] {'strip','y'}, dimensions={0} | all-to-all | bytes 458752 | tf_op jit(solution)/shard_map/all_to_all | solution.py:658
  62.5 0.8 %shard_map.167 = (f32[256,128]{1,0:T(8,128)}, f32[384,128]{1,0:T(8,128)}, f32[128,128]{1,0:T(8,128)}, f32[256,128]{1,0:T(8,128)}, f32[128,128]{1,0:T(8,128)}) custom-call(bf16[8,112,128]{2,1,0:T(8,128)(2,1)S(1)} %all_to_all.22.came, f32[32,128]{1,0:T(8,128)S(1)} %get-tuple-element.36.rim_grad, f32[256,128]{1,0:T(8,128)S(1)} %get-tuple-element.37.local_grad), custom_call_target="tpu_custom_call" | custom-call | tf_op jit(solution)/shard_map/pallas_call | solution.py:80
  (3 shorter events, 0.0 us)
Async XLA Ops:
  2.1 18.0 %all-to-all-start = ((bf16[32,32,128]{2,1,0:T(8,128)(2,1)}), bf16[32,32,128]{2,1,0:T(8,128)(2,1)S(1)}, u32[]{:S(2)}, u32[]{:S(2)}) async-start(bf16[32,32,128]{2,1,0:T(8,128)(2,1)} %shard_map.162), calls=%async_computation | async-start | bytes 524288 | tf_op jit(solution)/shard_map/all_to_all | solution.py:514
  11.7 8.3 %copy-start = (s32[4,8,1024]{2,1,0:T(8,128)}, s32[4,8,1024]{2,1,0:T(8,128)S(1)}, u32[]{:S(2)}) copy-start(s32[4,8,1024]{2,1,0:T(8,128)S(1)} %stack.7.info.info_in) | copy-start | bytes 393220
  20.0 0.7 %copy-start.1 = (bf16[32,32,128]{2,1,0:T(8,128)(2,1)}, bf16[32,32,128]{2,1,0:T(8,128)(2,1)S(1)}, u32[]{:S(2)}) copy-start(bf16[32,32,128]{2,1,0:T(8,128)(2,1)S(1)} %all-to-all-done.rims_in) | copy-start | bytes 786436

commit v8 on v7

--- a/solution.py
+++ b/solution.py
@@ -137,7 +137,7 @@
 def layer_kernel(
     edge_count,
     nodes_in,
-    rims_in,
+    rims,
     edges_in,
     info_in,
     send_codes_in,
@@ -155,7 +155,6 @@
     local_grad,
     parts,
     nodes,
-    rims,
     edges,
     info,
     send_codes,
@@ -184,6 +183,7 @@
     ge_out,
     agg,
     packed,
+    kept,
     small_sems,
     sems,
     out_sems,
@@ -207,7 +207,6 @@
         for k, (source, target) in enumerate(
             [
                 (nodes_in, nodes),
-                (rims_in, rims),
                 (w_edge_in_in, w_edge_in),
                 (w_edge_out_in, w_edge_out),
                 (w_node_in_in, w_node_in),
@@ -262,7 +261,7 @@
         )
 
     ahead, behind = range(4), range(4, 7)
-    for copy in small[:4] + fetch(0, ahead) + small[4:]:
+    for copy in small[:3] + fetch(0, ahead) + small[3:]:
         copy.start()
     for step in range(1, chunks):
         for copy in fetch(step, ahead):
@@ -270,7 +269,7 @@
     for step in range(chunks):
         for copy in fetch(step, behind):
             copy.start()
-    for copy in small[:4]:
+    for copy in small[:3]:
         copy.wait()
 
     near_rows[...] = nodes[...]
@@ -328,7 +327,7 @@
 
     lax.fori_loop(0, chunks, forward, 0)
 
-    for copy in small[4:]:
+    for copy in small[3:]:
         copy.wait()
     joined = jnp.concatenate([nodes[...], agg[...].astype(BF16)], axis=1)
     node_pre = mm(joined, w_node_in[...])
@@ -343,8 +342,10 @@
     d_agg = d_joined[:, width:]
     d_agg = (d_agg - jnp.mean(d_agg, axis=1, keepdims=True)).astype(BF16)
     agg[...] = cot + d_joined[:, :width]
-    packed[4 * width : 6 * width] = mm_tn(joined, d_pre).astype(BF16)
-    packed[6 * width : 7 * width] = mm_tn(node_act, d_outer).astype(BF16)
+    kept[:, : 2 * width] = joined
+    kept[:, 2 * width : 3 * width] = node_act
+    kept[:, 3 * width : 4 * width] = d_outer
+    kept[:, 4 * width :] = d_pre
     node_copy = pltpu.make_async_copy(new_nodes, new_nodes_out, last_sem)
     node_copy.start()
 
@@ -389,6 +390,10 @@
     edge_sums = sums[2 * count_p :, :width] + sums[2 * count_p :, width:]
     packed[:width] = (mm_tn(near_rows[...], near_sums) + mm_tn(far_rows[...], far_sums)).astype(BF16)
     packed[width : 2 * width] = mm_tn(nodes[...], recv_sums).astype(BF16)
+    packed[4 * width : 6 * width] = mm_tn(kept[:, : 2 * width], kept[:, 4 * width :]).astype(BF16)
+    packed[6 * width : 7 * width] = mm_tn(
+        kept[:, 2 * width : 3 * width], kept[:, 3 * width : 4 * width]
+    ).astype(BF16)
     packed[2 * width : 3 * width] = edge_sums.astype(BF16)
     packed[3 * width : 4 * width] = ge_out[...].astype(BF16)
     if packed.shape[0] > 7 * width:
@@ -427,35 +432,39 @@
     node_copy.wait()
 
 
-def plane_sum_kernel(came, out, mine):
+def plane_sum_kernel(came, message, mine):
     border = mine.shape[0]
-    zs = out.shape[0]
-    share = out.shape[1] - border
+    share = message.shape[0] - border
     total = came[0].astype(F32)
     for slot in range(1, came.shape[0]):
         total = total + came[slot].astype(F32)
-    share_total = total[:share].astype(BF16)
     mine[...] = total[share : share + border]
-    beyond = total[share + border :].astype(BF16)
-    for target in range(zs):
-        out[target, :share] = share_total
-        out[target, share:] = jnp.zeros_like(beyond)
-    target = lax.axis_index("z") + 1 - 2 * lax.axis_index("y")
-
-    @pl.when((target >= 0) & (target < zs))
-    def put():
-        out[target, share:] = beyond
-
-
-def line_sum_kernel(factor, came, mine, out, rim_grad):
-    share = out.shape[1]
-    total = came[0].astype(F32)
-    for slot in range(1, came.shape[0]):
-        total = total + came[slot].astype(F32)
-    share_total = (total[:share] * factor).astype(BF16)
+    message[:share] = total[:share].astype(BF16)
+    message[share:] = total[share + border :].astype(BF16)
+
+
+def joined_line(bit, own, came, mine):
+    share = came.shape[0] - mine.shape[0]
+    total = own[:share].astype(F32) + came[:share].astype(F32)
+    passing = came[share:].astype(F32)
+    mine_bit = lax.rem(lax.div(lax.axis_index("z"), 2**bit), 2)
+    here = jnp.where(mine_bit != lax.axis_index("y"), 1.0, 0.0)
+    return total, mine[...] + here * passing, (1.0 - here) * passing
+
+
+def line_step_kernel(bit, own, came, mine, message, next_mine):
+    share = came.shape[0] - mine.shape[0]
+    total, arrived, passing = joined_line(bit, own, came, mine)
+    next_mine[...] = arrived
+    message[:share] = total.astype(BF16)
+    message[share:] = passing.astype(BF16)
+
+
+def line_last_kernel(bit, factor, own, came, mine, out, rim_grad):
+    total, rim_grad[...], _ = joined_line(bit, own, came, mine)
+    total = (total * factor).astype(BF16)
     for target in range(out.shape[0]):
-        out[target] = share_total
-    rim_grad[...] = mine[...] + total[share:]
+        out[target] = total
 
 
 def finish_kernel(came, rim_grad, local_grad, node_grad, *outs):
@@ -603,10 +612,9 @@
             w_node_out,
             node_cotangent,
         ],
-        [SMEM] + [HBM] * 14,
+        [SMEM, HBM, VMEM] + [HBM] * 12,
         [
             like(node_latents),
-            like(rims),
             like(edge_latents),
             like(info),
             *[like(value) for value in early],
@@ -631,7 +639,8 @@
             pltpu.VMEM((width, width), F32),
             pltpu.VMEM((count_p, width), F32),
             pltpu.VMEM((slots * share, width), BF16),
-            SEM((7,)),
+            pltpu.VMEM((count_p, 5 * width), BF16),
+            SEM((6,)),
             SEM((7, chunks)),
             SEM((chunks,)),
             SEM,
@@ -641,19 +650,21 @@
     )
 
     came = lax.all_to_all(parts, PLANE, 0, 0)
-    parts, mine = call(
-        plane_sum_kernel,
-        [((zs, share + border, width), BF16), ((border, width), F32)],
-        [came],
-        [VMEM],
-    )
-    came = lax.all_to_all(parts, "z", 0, 0)
+    state = [((share + border, width), BF16), ((border, width), F32)]
+    message, mine = call(plane_sum_kernel, state, [came], [VMEM])
     factor = 1.0 / math.sqrt(count_e * strips * subs)
+    bits = zs.bit_length() - 1
+    for bit in range(bits):
+        came = lax.ppermute(message, "z", [(z, z ^ (1 << bit)) for z in range(zs)])
+        if bit < bits - 1:
+            message, mine = call(
+                functools.partial(line_step_kernel, bit), state, [message, came, mine], [VMEM] * 3
+            )
     parts, rim_grad = call(
-        functools.partial(line_sum_kernel, factor),
+        functools.partial(line_last_kernel, bits - 1, factor),
         [((slots, share, width), BF16), ((border, width), F32)],
-        [came, mine],
-        [VMEM, VMEM],
+        [message, came, mine],
+        [VMEM] * 3,
     )
     came = lax.all_to_all(parts, PLANE, 0, 0)
     node_grad, *grads = call(

time: 63.9 us -> 61.9 us (0.969)
  blocking collectives: 28.4 us -> 18.1 us
  waiting for transfers between devices: 2.27 us -> 8.58 us
  starting transfers between devices: 7.3 us -> 9.92 us
  local copies, waits for them, and re-layouts: 1.56 us -> 0.87 us
    all_to_all x1 -> x0, blocking collectives: 10.3 us -> none  [shards(): came = lax.all_to_all(parts, 'z', 0, 0)]
    ppermute x0 -> x2, waiting for transfers between devices: none -> 6.33 us  [shards(): came = lax.ppermute(message, 'z', [(z, z ^ 1 << bit) for z in range(zs)])]
    ppermute x0 -> x2, starting transfers between devices: none -> 2.61 us  [shards(): came = lax.ppermute(message, 'z', [(z, z ^ 1 << bit) for z in range(zs)])]
    unnamed x4 -> x2, local copies, waits for them, and re-layouts: 0.7 us -> 0.01 us
    pallas_call x5 -> x6, Pallas kernels: 15.6 us -> 15.7 us  [call(): pl.pallas_call(kernel, out_shape=[pltpu.HBM(shape, dtype) if spec is HBM...]
  transfers between devices with their start and end apart: 1 -> 3, of which waited for: 1 -> 3; matrix products, arithmetic and copies ran while one was open for 3% -> 3% of each run, Pallas kernels for 10% -> 10%
where the time goes in v8:
time: 61.9 us; the launch traced here: 61.3 us
  Pallas kernels  21.8 us (35%)
  blocking collectives  18.1 us (29%)
  starting transfers between devices  9.92 us (16%)
  waiting for transfers between devices  8.58 us (14%)
  between operations  1.35 us (2%)
  local copies, waits for them, and re-layouts  0.87 us (1%)
  other arithmetic  0.77 us (1%)
    all_to_all x2, blocking collectives, shards(): came = lax.all_to_all(parts, PLANE, 0, 0)  18.1 us
    pallas_call x6, Pallas kernels, call(): pl.pallas_call(kernel, out_shape=[pltpu.HBM(shape, dtype) if spec is HBM...  15.7 us
    all_to_all x1, starting transfers between devices, shards(): rims = lax.all_to_all(rims, ALL, 0, 0)  7.3 us
    ppermute x2, waiting for transfers between devices, shards(): came = lax.ppermute(message, 'z', [(z, z ^ 1 << bit) for z in range(zs)])  6.33 us
    pallas_call x1, Pallas kernels, shards(): pl.pallas_call(early_kernel, grid=(chunks,), out_shape=[pltpu.HBM(shape,...  6.08 us
    ppermute x2, starting transfers between devices, shards(): came = lax.ppermute(message, 'z', [(z, z ^ 1 << bit) for z in range(zs)])  2.61 us
    all_to_all x1, waiting for transfers between devices, shards(): rims = lax.all_to_all(rims, ALL, 0, 0)  2.25 us
  transfers between devices with their start and end apart: 3, of which 3 were waited for; matrix products, arithmetic and copies ran while one was open for 3% of the time, Pallas kernels for 10%

profile of v8, /device:TPU:0, one launch (start us, length us, event | category | flops | bytes accessed | tf_op | source)
XLA Modules:
  0.0 61.3 jit_solution(10941991169233415655)
XLA Ops:
  0.6 1.5 %shard_map.162 = bf16[32,32,128]{2,1,0:T(8,128)(2,1)} custom-call(bf16[256,128]{1,0:T(8,128)(2,1)} %nodes_in.1), custom_call_target="tpu_custom_call" | custom-call | tf_op jit(solution)/shard_map/pallas_call | solution.py:80
  2.1 7.3 %all-to-all-start = ((bf16[32,32,128]{2,1,0:T(8,128)(2,1)}), bf16[32,32,128]{2,1,0:T(8,128)(2,1)S(1)}, u32[]{:S(2)}, u32[]{:S(2)}) async-start(bf16[32,32,128]{2,1,0:T(8,128)(2,1)} %shard_map.162), calls=%async_computation | async-start | bytes 524288 | tf_op jit(solution)/shard_map/all_to_all | solution.py:523
  10.1 0.8 %subtract_select_fusion = (s32[4096]{0:T(1024)S(1)}, s32[4096]{0:T(1024)S(1)}) fusion(s32[]{:T(128)S(6)} %add.32, s32[4096]{0:T(1024)} %param.13, s32[]{:T(128)S(6)} %add.31, s32[]{:T(128)S(6)} %axis_index.33), kind=kLoop, calls=%fused_computation.1 | loop fusion | flops 221184 | bytes 49164 | tf_op jit(solution)/shard_map/jit(_where)/select_n | solution.py:531
  10.9 0.8 %stack.7.info.info_in = s32[4,8,1024]{2,1,0:T(8,128)S(1)} concatenate(s32[4,1,1024]{2,1,0:T(1,128)S(1)} %bitcast.4, s32[4,1,1024]{2,1,0:T(1,128)} %bitcast.5, s32[4,1,1024]{2,1,0:T(1,128)S(1)} %bitcast.3, s32[4,1,1024]{2,1,0:T(1,128)S(1)} %stack_reshape.15, s32[4,4,1024]{2,1,0:T(4,128)S(1)} %stack.6), dimensions={1} | concatenate | bytes 262144 | tf_op jit(solution)/shard_map/stack | solution.py:534
  11.7 0.0 copy-start
  11.7 6.1 %shard_map.163 = (bf16[4096,128]{1,0:T(8,128)(2,1)}, bf16[4096,128]{1,0:T(8,128)(2,1)}, bf16[4,128,1024]{2,1,0:T(8,128)(2,1)}, f32[4096,128]{1,0:T(8,128)}, bf16[4096,128]{1,0:T(8,128)(2,1)}) custom-call(bf16[256,128]{1,0:T(8,128)(2,1)} %nodes_in.1, bf16[4096,128]{1,0:T(8,128)(2,1)} %edges_in.1, bf16[4096,128]{1,0:T(8,128)(2,1)} %edge_cot.1, ...), custom_call_target="tpu_custom_call" | custom-call | tf_op jit(solution)/shard_map/pallas_call | solution.py:552
  17.8 2.2 %all-to-all-done.rims = bf16[32,32,128]{2,1,0:T(8,128)(2,1)S(1)} async-done(((bf16[32,32,128]{2,1,0:T(8,128)(2,1)}), bf16[32,32,128]{2,1,0:T(8,128)(2,1)S(1)}, u32[]{:S(2)}, u32[]{:S(2)}) %all-to-all-start) | async-done | bytes 262176 | tf_op jit(solution)/shard_map/all_to_all | solution.py:523
  20.0 0.0 copy-done
  20.1 13.4 %shard_map.164 = (bf16[256,128]{1,0:T(8,128)(2,1)}, bf16[4096,128]{1,0:T(8,128)(2,1)}, f32[256,128]{1,0:T(8,128)S(1)}, bf16[8,176,128]{2,1,0:T(8,128)(2,1)S(1)}) custom-call(s32[1]{0:T(128)S(6)} %copy.18.edge_count, bf16[256,128]{1,0:T(8,128)(2,1)} %nodes_in.1, bf16[32,32,128]{2,1,0:T(8,128)(2,1)S(1)} %all-to-all-done.rims, bf16[4096,128]{1,0:T(8,128)(2,1)} %edges_in.1, ...), custom_call_target="tpu_custom_call" | custom-call | tf_op jit(solution)/shard_map/pallas_call | solution.py:80
  33.4 10.0 %all_to_all.15.came = bf16[8,176,128]{2,1,0:T(8,128)(2,1)S(1)} all-to-all(bf16[8,176,128]{2,1,0:T(8,128)(2,1)S(1)} %get-tuple-element.34), channel_id=1, replica_groups=mesh['strip'=4,'z'=4,'y'=2] {'strip','y'}, dimensions={0} | all-to-all | bytes 720896 | tf_op jit(solution)/shard_map/all_to_all | solution.py:652
  43.4 0.1 shard_map.165
  43.4 1.0 %collective-permute-start = (bf16[144,128]{1,0:T(8,128)(2,1)S(1)}, bf16[144,128]{1,0:T(8,128)(2,1)S(1)}, u32[]{:S(2)}, u32[]{:S(2)}) collective-permute-start(bf16[144,128]{1,0:T(8,128)(2,1)S(1)} %get-tuple-element.35.own), channel_id=1, source_target_pairs={{0,2},{2,0},{4,6},{6,4},{1,3},{3,1},{5,7},{7,5},{8,10},{10,8},{12,... | collective-permute-start | bytes 110600 | tf_op jit(solution)/shard_map/ppermute | solution.py:658
  44.5 3.0 %collective-permute-done.came = bf16[144,128]{1,0:T(8,128)(2,1)S(1)} collective-permute-done((bf16[144,128]{1,0:T(8,128)(2,1)S(1)}, bf16[144,128]{1,0:T(8,128)(2,1)S(1)}, u32[]{:S(2)}, u32[]{:S(2)}) %collective-permute-start) | collective-permute-done | bytes 36896 | tf_op jit(solution)/shard_map/ppermute | solution.py:658
  47.5 1.6 %collective-permute-start.1 = (bf16[144,128]{1,0:T(8,128)(2,1)S(1)}, bf16[144,128]{1,0:T(8,128)(2,1)S(1)}, u32[]{:S(2)}, u32[]{:S(2)}) collective-permute-start(bf16[144,128]{1,0:T(8,128)(2,1)S(1)} %get-tuple-element.37.own), channel_id=1, source_target_pairs={{0,4},{2,6},{4,0},{6,2},{1,5},{3,7},{5,1},{7,3},{8,12},{10,14},{12... | collective-permute-start | bytes 110600 | tf_op jit(solution)/shard_map/ppermute | solution.py:658
  49.1 3.3 %collective-permute-done.1.came = bf16[144,128]{1,0:T(8,128)(2,1)S(1)} collective-permute-done((bf16[144,128]{1,0:T(8,128)(2,1)S(1)}, bf16[144,128]{1,0:T(8,128)(2,1)S(1)}, u32[]{:S(2)}, u32[]{:S(2)}) %collective-permute-start.1) | collective-permute-done | bytes 36896 | tf_op jit(solution)/shard_map/ppermute | solution.py:658
  52.4 8.1 %all_to_all.16.came = bf16[8,112,128]{2,1,0:T(8,128)(2,1)S(1)} all-to-all(bf16[8,112,128]{2,1,0:T(8,128)(2,1)S(1)} %get-tuple-element.39), channel_id=1, replica_groups=mesh['strip'=4,'z'=4,'y'=2] {'strip','y'}, dimensions={0} | all-to-all | bytes 458752 | tf_op jit(solution)/shard_map/all_to_all | solution.py:669
  60.5 0.8 %shard_map.168 = (f32[256,128]{1,0:T(8,128)}, f32[384,128]{1,0:T(8,128)}, f32[128,128]{1,0:T(8,128)}, f32[256,128]{1,0:T(8,128)}, f32[128,128]{1,0:T(8,128)}) custom-call(bf16[8,112,128]{2,1,0:T(8,128)(2,1)S(1)} %all_to_all.16.came, f32[32,128]{1,0:T(8,128)S(1)} %get-tuple-element.40.rim_grad, f32[256,128]{1,0:T(8,128)S(1)} %get-tuple-element.41.local_grad), custom_call_target="tpu_custom_call" | custom-call | tf_op jit(solution)/shard_map/pallas_call | solution.py:80
  (4 shorter events, 0.1 us)
Async XLA Ops:
  2.1 18.0 %all-to-all-start = ((bf16[32,32,128]{2,1,0:T(8,128)(2,1)}), bf16[32,32,128]{2,1,0:T(8,128)(2,1)S(1)}, u32[]{:S(2)}, u32[]{:S(2)}) async-start(bf16[32,32,128]{2,1,0:T(8,128)(2,1)} %shard_map.162), calls=%async_computation | async-start | bytes 524288 | tf_op jit(solution)/shard_map/all_to_all | solution.py:523
  11.7 8.3 %copy-start = (s32[4,8,1024]{2,1,0:T(8,128)}, s32[4,8,1024]{2,1,0:T(8,128)S(1)}, u32[]{:S(2)}) copy-start(s32[4,8,1024]{2,1,0:T(8,128)S(1)} %stack.7.info.info_in) | copy-start | bytes 393220
  43.4 4.0 %collective-permute-start = (bf16[144,128]{1,0:T(8,128)(2,1)S(1)}, bf16[144,128]{1,0:T(8,128)(2,1)S(1)}, u32[]{:S(2)}, u32[]{:S(2)}) collective-permute-start(bf16[144,128]{1,0:T(8,128)(2,1)S(1)} %get-tuple-element.35.own), channel_id=1, source_target_pairs={{0,2},{2,0},{4,6},{6,4},{1,3},{3,1},{5,7},{7,5},{8,10},{10,8},{12,... | collective-permute-start | bytes 110600 | tf_op jit(solution)/shard_map/ppermute | solution.py:658
  47.5 4.9 %collective-permute-start.1 = (bf16[144,128]{1,0:T(8,128)(2,1)S(1)}, bf16[144,128]{1,0:T(8,128)(2,1)S(1)}, u32[]{:S(2)}, u32[]{:S(2)}) collective-permute-start(bf16[144,128]{1,0:T(8,128)(2,1)S(1)} %get-tuple-element.37.own), channel_id=1, source_target_pairs={{0,4},{2,6},{4,0},{6,2},{1,5},{3,7},{5,1},{7,3},{8,12},{10,14},{12... | collective-permute-start | bytes 110600 | tf_op jit(solution)/shard_map/ppermute | solution.py:658

commit v9 on v8

--- a/solution.py
+++ b/solution.py
@@ -90,16 +90,18 @@
     )(*[in_hbm(value) if spec is HBM else value for value, spec in zip(ins, specs)])
 
 
-def rim_kernel(nodes, out, rim, many, in_sem, out_sem):
-    border = out.shape[1]
-    copy = pltpu.make_async_copy(nodes.at[pl.ds(0, border)], rim, in_sem)
-    copy.start()
-    copy.wait()
-    for target in range(out.shape[0]):
-        many[target] = rim[...]
-    copy = pltpu.make_async_copy(many, out, out_sem)
-    copy.start()
-    copy.wait()
+def column_kernel(nodes, even, odd, out):
+    border = even.shape[0]
+    out[:border] = nodes[:border]
+    out[border : 2 * border] = even[...]
+    out[2 * border :] = odd[...]
+
+
+def swapped(value, axes):
+    count = lax.axis_size(axes)
+    even = [(k, k ^ 1) for k in range(count)]
+    odd = [(k, min(max(((k + 1) ^ 1) - 1, 0), count - 1)) for k in range(count)]
+    return lax.ppermute(value, axes, even), lax.ppermute(value, axes, odd)
 
 
 def early_kernel(
@@ -137,7 +139,9 @@
 def layer_kernel(
     edge_count,
     nodes_in,
-    rims,
+    own_column,
+    even_column,
+    odd_column,
     edges_in,
     info_in,
     send_codes_in,
@@ -184,13 +188,14 @@
     agg,
     packed,
     kept,
+    columns,
     small_sems,
     sems,
     out_sems,
     last_sem,
 ):
     count_p, width = nodes.shape
-    border = rims.shape[1]
+    border = own_column.shape[0] // 3
     slots = parts.shape[0]
     strips = slots // 2
     chunks, _, chunk = edges_t.shape
@@ -198,8 +203,6 @@
     half = block // 2
     share = parts.shape[1] - 2 * border
     my_strip, my_y = lax.axis_index("strip"), lax.axis_index("y")
-    subs = lax.axis_size("z") * lax.axis_size("y")
-    my_sub = lax.axis_index("z") * lax.axis_size("y") + my_y
     live_count = edge_count[0]
 
     small = [
@@ -273,14 +276,24 @@
         copy.wait()
 
     near_rows[...] = nodes[...]
+    for k, column in enumerate((own_column, even_column, odd_column)):
+        for part in range(3):
+            columns[3 * k + part] = column[part * border : (part + 1) * border]
+
+    def partner(mine, step):
+        if step == 0:
+            return 0
+        is_odd = lax.rem(mine, 2)
+        return 1 + is_odd if step > 0 else 2 - is_odd
+
     spot = 0
     for d_strip in (-1, 0, 1):
-        strip = jnp.clip(my_strip + d_strip, 0, strips - 1)
+        column = partner(my_strip, d_strip)
         for d_sub in (-1, 0, 1):
             if d_strip == 0 and d_sub == 0:
                 continue
-            sub = jnp.clip(my_sub + d_sub, 0, subs - 1)
-            far_rows[spot * border : (spot + 1) * border] = rims[strip * subs + sub]
+            rows = slice(spot * border, (spot + 1) * border)
+            far_rows[rows] = columns[3 * column + partner(my_y, d_sub)]
             spot += 1
     tables[:, :width] = mm(near_rows[...], w_edge_in[:width]).astype(BF16)
     tables[:, width:] = mm(far_rows[...], w_edge_in[:width]).astype(BF16)
@@ -443,28 +456,23 @@
     message[share:] = total[share + border :].astype(BF16)
 
 
-def joined_line(bit, own, came, mine):
-    share = came.shape[0] - mine.shape[0]
-    total = own[:share].astype(F32) + came[:share].astype(F32)
-    passing = came[share:].astype(F32)
-    mine_bit = lax.rem(lax.div(lax.axis_index("z"), 2**bit), 2)
-    here = jnp.where(mine_bit != lax.axis_index("y"), 1.0, 0.0)
-    return total, mine[...] + here * passing, (1.0 - here) * passing
-
-
-def line_step_kernel(bit, own, came, mine, message, next_mine):
-    share = came.shape[0] - mine.shape[0]
-    total, arrived, passing = joined_line(bit, own, came, mine)
-    next_mine[...] = arrived
-    message[:share] = total.astype(BF16)
-    message[share:] = passing.astype(BF16)
-
-
-def line_last_kernel(bit, factor, own, came, mine, out, rim_grad):
-    total, rim_grad[...], _ = joined_line(bit, own, came, mine)
+def line_sum_kernel(factor, mine, *refs):
+    messages, (out, rim_grad, held) = refs[:-3], refs[-3:]
+    border = mine.shape[0]
+    share = out.shape[1]
+    for k, message in enumerate(messages):
+        held[k] = message[...].astype(F32)
+    my_z, my_y = lax.axis_index("z"), lax.axis_index("y")
+    total = held[lax.bitwise_xor(my_z, 0), :share]
+    for z in range(1, len(messages)):
+        total = total + held[lax.bitwise_xor(my_z, z), :share]
     total = (total * factor).astype(BF16)
     for target in range(out.shape[0]):
         out[target] = total
+    source = my_z - 1 + 2 * my_y
+    inside = (source >= 0) & (source < len(messages))
+    passed = held[lax.bitwise_xor(my_z, jnp.clip(source, 0, len(messages) - 1)), share:]
+    rim_grad[...] = mine[...] + jnp.where(inside, passed, 0.0)
 
 
 def finish_kernel(came, rim_grad, local_grad, node_grad, *outs):
@@ -505,22 +513,12 @@
     slots = strips * ys
     my_strip, my_z, my_y = (lax.axis_index(axis).astype(jnp.int32) for axis in ALL)
     my_sub = my_z * ys + my_y
-    devices = strips * subs
-
-    (rims,) = call(
-        rim_kernel,
-        [((devices, border, width), BF16)],
-        [node_latents],
-        [HBM],
-        [
-            pltpu.VMEM((border, width), BF16),
-            pltpu.VMEM((devices, border, width), BF16),
-            SEM,
-            SEM,
-        ],
-        [HBM],
-    )
-    rims = lax.all_to_all(rims, ALL, 0, 0)
+
+    even, odd = swapped(node_latents[:border], ("z", "y"))
+    (own_column,) = call(
+        column_kernel, [((3 * border, width), BF16)], [node_latents[:border], even, odd], [VMEM] * 3
+    )
+    even_column, odd_column = swapped(own_column, "strip")
 
     owner = senders // count_p
     within = senders % count_p
@@ -549,6 +547,7 @@
     def whole(*shape):
         return pl.BlockSpec(shape, lambda i: (0, 0))
 
+    info, own_column = lax.optimization_barrier((info, own_column))
     early = pl.pallas_call(
         early_kernel,
         grid=(chunks,),
@@ -602,7 +601,9 @@
         [
             edge_count,
             node_latents,
-            rims,
+            own_column,
+            even_column,
+            odd_column,
             edge_latents,
             info,
             *early,
@@ -612,7 +613,7 @@
             w_node_out,
             node_cotangent,
         ],
-        [SMEM, HBM, VMEM] + [HBM] * 12,
+        [SMEM, HBM] + [VMEM] * 3 + [HBM] * 12,
         [
             like(node_latents),
             like(edge_latents),
@@ -640,6 +641,7 @@
             pltpu.VMEM((count_p, width), F32),
             pltpu.VMEM((slots * share, width), BF16),
             pltpu.VMEM((count_p, 5 * width), BF16),
+            pltpu.VMEM((9, border, width), BF16),
             SEM((6,)),
             SEM((7, chunks)),
             SEM((chunks,)),
@@ -653,18 +655,15 @@
     state = [((share + border, width), BF16), ((border, width), F32)]
     message, mine = call(plane_sum_kernel, state, [came], [VMEM])
     factor = 1.0 / math.sqrt(count_e * strips * subs)
-    bits = zs.bit_length() - 1
-    for bit in range(bits):
-        came = lax.ppermute(message, "z", [(z, z ^ (1 << bit)) for z in range(zs)])
-        if bit < bits - 1:
-            message, mine = call(
-                functools.partial(line_step_kernel, bit), state, [message, came, mine], [VMEM] * 3
-            )
+    messages = [message] + [
+        lax.ppermute(message, "z", [(z, z ^ k) for z in range(zs)]) for k in range(1, zs)
+    ]
     parts, rim_grad = call(
-        functools.partial(line_last_kernel, bits - 1, factor),
+        functools.partial(line_sum_kernel, factor),
         [((slots, share, width), BF16), ((border, width), F32)],
-        [message, came, mine],
-        [VMEM] * 3,
+        [mine, *messages],
+        [VMEM] * (1 + zs),
+        [pltpu.VMEM((zs, share + border, width), F32)],
     )
     came = lax.all_to_all(parts, PLANE, 0, 0)
     node_grad, *grads = call(

time: 61.9 us -> 63.2 us (1.021)
  starting transfers between devices: 9.92 us -> 14.5 us
  waiting for transfers between devices: 8.58 us -> 5.38 us
  Pallas kernels: 21.8 us -> 20.4 us
  local copies, waits for them, and re-layouts: 0.87 us -> 1.57 us
  blocking collectives: 18.1 us -> 18.8 us
    ppermute x2 -> x7, starting transfers between devices: 2.61 us -> 14.5 us  [the longest x4 10 us: swapped(): return (lax.ppermute(value, axes, even), lax.ppermute(value, axes, odd))]
    all_to_all x1 -> x0, starting transfers between devices: 7.3 us -> none  [shards(): rims = lax.all_to_all(rims, ALL, 0, 0)]
    all_to_all x1 -> x0, waiting for transfers between devices: 2.25 us -> none  [shards(): rims = lax.all_to_all(rims, ALL, 0, 0)]
    pallas_call x6 -> x5, Pallas kernels: 15.7 us -> 14.3 us  [call(): pl.pallas_call(kernel, out_shape=[pltpu.HBM(shape, dtype) if spec is HBM...]
    ppermute x2 -> x7, waiting for transfers between devices: 6.33 us -> 5.38 us  [the longest x3 3.74 us: shards(): lax.ppermute(message, 'z', [(z, z ^ k) for z in range(zs)])]
    all_to_all x2, blocking collectives: 18.1 us -> 18.8 us  [shards(): came = lax.all_to_all(parts, PLANE, 0, 0)]
    slice x0 -> x1, local copies, waits for them, and re-layouts: none -> 0.7 us  [shards(): node_latents[:border]]
  transfers between devices with their start and end apart: 3 -> 7, of which waited for: 3 -> 3; matrix products, arithmetic and copies ran while one was open for 3% -> 3% of each run, Pallas kernels for 10% -> 10%
where the time goes in v9:
time: 63.2 us; the launch traced here: 62.7 us
  Pallas kernels  20.4 us (32%)
  blocking collectives  18.8 us (30%)
  starting transfers between devices  14.5 us (23%)
  waiting for transfers between devices  5.38 us (9%)
  local copies, waits for them, and re-layouts  1.57 us (2%)
  between operations  1.37 us (2%)
  other arithmetic  0.77 us (1%)
    all_to_all x2, blocking collectives, shards(): came = lax.all_to_all(parts, PLANE, 0, 0)  18.8 us
    pallas_call x5, Pallas kernels, call(): pl.pallas_call(kernel, out_shape=[pltpu.HBM(shape, dtype) if spec is HBM...  14.3 us
    ppermute x4, starting transfers between devices, swapped(): return (lax.ppermute(value, axes, even), lax.ppermute(value, axes, odd))  10 us
    pallas_call x1, Pallas kernels, shards(): pl.pallas_call(early_kernel, grid=(chunks,), out_shape=[pltpu.HBM(shape,...  6.07 us
    ppermute x3, starting transfers between devices, shards(): lax.ppermute(message, 'z', [(z, z ^ k) for z in range(zs)])  4.45 us
    ppermute x3, waiting for transfers between devices, shards(): lax.ppermute(message, 'z', [(z, z ^ k) for z in range(zs)])  3.74 us
    ppermute x4, waiting for transfers between devices, swapped(): return (lax.ppermute(value, axes, even), lax.ppermute(value, axes, odd))  1.64 us
  transfers between devices with their start and end apart: 7, of which 3 were waited for; matrix products, arithmetic and copies ran while one was open for 3% of the time, Pallas kernels for 10%

profile of v9, /device:TPU:0, one launch (start us, length us, event | category | flops | bytes accessed | tf_op | source)
XLA Modules:
  0.0 62.7 jit_solution(4445529770893029002)
XLA Ops:
  0.6 0.7 %slice.4.nodes = bf16[32,128]{1,0:T(8,128)(2,1)S(1)} slice(bf16[256,128]{1,0:T(8,128)(2,1)} %nodes_in.1), slice={[0:32], [0:128]} | slice | bytes 16384 | tf_op jit(solution)/shard_map/slice | solution.py:519
  1.3 0.6 %collective-permute-start.1 = (bf16[32,128]{1,0:T(8,128)(2,1)S(1)}, bf16[32,128]{1,0:T(8,128)(2,1)S(1)}, u32[]{:S(2)}, u32[]{:S(2)}) collective-permute-start(bf16[32,128]{1,0:T(8,128)(2,1)S(1)} %slice.4.nodes), channel_id=1, source_target_pairs={{0,0},{1,2},{2,1},{3,4},{4,3},{5,6},{6,5},{7,7},{8,8},{9,10},{10,9... | collective-permute-start | bytes 24584 | tf_op jit(solution)/shard_map/ppermute | solution.py:104
  2.0 5.8 %collective-permute-start = (bf16[32,128]{1,0:T(8,128)(2,1)S(1)}, bf16[32,128]{1,0:T(8,128)(2,1)S(1)}, u32[]{:S(2)}, u32[]{:S(2)}) collective-permute-start(bf16[32,128]{1,0:T(8,128)(2,1)S(1)} %slice.4.nodes), channel_id=1, source_target_pairs={{0,1},{1,0},{2,3},{3,2},{4,5},{5,4},{6,7},{7,6},{8,9},{9,8},{10,11... | collective-permute-start | bytes 24584 | tf_op jit(solution)/shard_map/ppermute | solution.py:104
  7.8 0.0 collective-permute-done.1.odd
  7.8 1.6 %collective-permute-done.even = bf16[32,128]{1,0:T(8,128)(2,1)S(1)} collective-permute-done((bf16[32,128]{1,0:T(8,128)(2,1)S(1)}, bf16[32,128]{1,0:T(8,128)(2,1)S(1)}, u32[]{:S(2)}, u32[]{:S(2)}) %collective-permute-start) | collective-permute-done | bytes 8224 | tf_op jit(solution)/shard_map/ppermute | solution.py:104
  9.4 0.7 %collective-permute-start.3 = (bf16[96,128]{1,0:T(8,128)(2,1)S(1)}, bf16[96,128]{1,0:T(8,128)(2,1)S(1)}, u32[]{:S(2)}, u32[]{:S(2)}) collective-permute-start(bf16[96,128]{1,0:T(8,128)(2,1)S(1)} %shard_map.162.own_column), channel_id=1, source_target_pairs={{0,0},{8,16},{16,8},{24,24},{1,1},{9,17},{17,9},{25,25},{2,2},{10,... | collective-permute-start | bytes 73736 | tf_op jit(solution)/shard_map/ppermute | solution.py:104
  10.1 2.9 %collective-permute-start.2 = (bf16[96,128]{1,0:T(8,128)(2,1)S(1)}, bf16[96,128]{1,0:T(8,128)(2,1)S(1)}, u32[]{:S(2)}, u32[]{:S(2)}) collective-permute-start(bf16[96,128]{1,0:T(8,128)(2,1)S(1)} %shard_map.162.own_column), channel_id=1, source_target_pairs={{0,8},{8,0},{16,24},{24,16},{1,9},{9,1},{17,25},{25,17},{2,10},{10... | collective-permute-start | bytes 73736 | tf_op jit(solution)/shard_map/ppermute | solution.py:104
  13.0 0.8 %subtract_select_fusion = (s32[4096]{0:T(1024)S(1)}, s32[4096]{0:T(1024)S(1)}) fusion(s32[]{:T(128)S(6)} %add.32, s32[4096]{0:T(1024)} %param.13, s32[]{:T(128)S(6)} %add.31, s32[]{:T(128)S(6)} %axis_index.33), kind=kLoop, calls=%fused_computation.1 | loop fusion | flops 221184 | bytes 49164 | tf_op jit(solution)/shard_map/jit(_where)/select_n | solution.py:529
  14.5 0.8 %stack.7.info.info_in = s32[4,8,1024]{2,1,0:T(8,128)S(1)} concatenate(s32[4,1,1024]{2,1,0:T(1,128)S(1)} %bitcast.4, s32[4,1,1024]{2,1,0:T(1,128)} %bitcast.5, s32[4,1,1024]{2,1,0:T(1,128)S(1)} %bitcast.3, s32[4,1,1024]{2,1,0:T(1,128)S(1)} %stack_reshape.15, s32[4,4,1024]{2,1,0:T(4,128)S(1)} %stack.6), dimensions={1} | concatenate | bytes 262144 | tf_op jit(solution)/shard_map/stack | solution.py:532
  15.3 0.0 copy-start
  15.3 6.1 %shard_map.163 = (bf16[4096,128]{1,0:T(8,128)(2,1)}, bf16[4096,128]{1,0:T(8,128)(2,1)}, bf16[4,128,1024]{2,1,0:T(8,128)(2,1)}, f32[4096,128]{1,0:T(8,128)}, bf16[4096,128]{1,0:T(8,128)(2,1)}) custom-call(bf16[256,128]{1,0:T(8,128)(2,1)} %nodes_in.1, bf16[4096,128]{1,0:T(8,128)(2,1)} %edges_in.1, bf16[4096,128]{1,0:T(8,128)(2,1)} %edge_cot.1, ...), custom_call_target="tpu_custom_call" | custom-call | tf_op jit(solution)/shard_map/pallas_call | solution.py:551
  21.4 0.0 collective-permute-done.2.even_column
  21.4 13.4 %shard_map.164 = (bf16[256,128]{1,0:T(8,128)(2,1)}, bf16[4096,128]{1,0:T(8,128)(2,1)}, f32[256,128]{1,0:T(8,128)S(1)}, bf16[8,176,128]{2,1,0:T(8,128)(2,1)S(1)}) custom-call(s32[1]{0:T(128)S(6)} %copy.18.edge_count, bf16[256,128]{1,0:T(8,128)(2,1)} %nodes_in.1, bf16[96,128]{1,0:T(8,128)(2,1)S(1)} %shard_map.162.own_column, ...), custom_call_target="tpu_custom_call" | custom-call | tf_op jit(solution)/shard_map/pallas_call | solution.py:80
  34.8 10.7 %all_to_all.10.came = bf16[8,176,128]{2,1,0:T(8,128)(2,1)S(1)} all-to-all(bf16[8,176,128]{2,1,0:T(8,128)(2,1)S(1)} %get-tuple-element.36), channel_id=1, replica_groups=mesh['strip'=4,'z'=4,'y'=2] {'strip','y'}, dimensions={0} | all-to-all | bytes 720896 | tf_op jit(solution)/shard_map/all_to_all | solution.py:654
  45.5 0.1 shard_map.165
  45.5 3.3 %collective-permute-start.6 = (bf16[144,128]{1,0:T(8,128)(2,1)S(1)}, bf16[144,128]{1,0:T(8,128)(2,1)S(1)}, u32[]{:S(2)}, u32[]{:S(2)}) collective-permute-start(bf16[144,128]{1,0:T(8,128)(2,1)S(1)} %get-tuple-element.38.refs_0_), channel_id=1, source_target_pairs={{0,6},{2,4},{4,2},{6,0},{1,7},{3,5},{5,3},{7,1},{8,14},{10,12},{12... | collective-permute-start | bytes 110600 | tf_op jit(solution)/shard_map/ppermute | solution.py:659
  48.9 0.0 collective-permute-start.5
  48.9 1.1 %collective-permute-start.4 = (bf16[144,128]{1,0:T(8,128)(2,1)S(1)}, bf16[144,128]{1,0:T(8,128)(2,1)S(1)}, u32[]{:S(2)}, u32[]{:S(2)}) collective-permute-start(bf16[144,128]{1,0:T(8,128)(2,1)S(1)} %get-tuple-element.38.refs_0_), channel_id=1, source_target_pairs={{0,2},{2,0},{4,6},{6,4},{1,3},{3,1},{5,7},{7,5},{8,10},{10,8},{12,... | collective-permute-start | bytes 110600 | tf_op jit(solution)/shard_map/ppermute | solution.py:659
  50.0 1.4 %collective-permute-done.6.refs_3_ = bf16[144,128]{1,0:T(8,128)(2,1)S(1)} collective-permute-done((bf16[144,128]{1,0:T(8,128)(2,1)S(1)}, bf16[144,128]{1,0:T(8,128)(2,1)S(1)}, u32[]{:S(2)}, u32[]{:S(2)}) %collective-permute-start.6) | collective-permute-done | bytes 36896 | tf_op jit(solution)/shard_map/ppermute | solution.py:659
  51.4 2.4 %collective-permute-done.5.refs_2_ = bf16[144,128]{1,0:T(8,128)(2,1)S(1)} collective-permute-done((bf16[144,128]{1,0:T(8,128)(2,1)S(1)}, bf16[144,128]{1,0:T(8,128)(2,1)S(1)}, u32[]{:S(2)}, u32[]{:S(2)}) %collective-permute-start.5) | collective-permute-done | bytes 36896 | tf_op jit(solution)/shard_map/ppermute | solution.py:659
  53.7 0.0 collective-permute-done.4.refs_1_
  53.7 0.1 shard_map.166
  53.8 8.1 %all_to_all.11.came = bf16[8,112,128]{2,1,0:T(8,128)(2,1)S(1)} all-to-all(bf16[8,112,128]{2,1,0:T(8,128)(2,1)S(1)} %get-tuple-element.39), channel_id=1, replica_groups=mesh['strip'=4,'z'=4,'y'=2] {'strip','y'}, dimensions={0} | all-to-all | bytes 458752 | tf_op jit(solution)/shard_map/all_to_all | solution.py:668
  61.9 0.8 %shard_map.167 = (f32[256,128]{1,0:T(8,128)}, f32[384,128]{1,0:T(8,128)}, f32[128,128]{1,0:T(8,128)}, f32[256,128]{1,0:T(8,128)}, f32[128,128]{1,0:T(8,128)}) custom-call(bf16[8,112,128]{2,1,0:T(8,128)(2,1)S(1)} %all_to_all.11.came, f32[32,128]{1,0:T(8,128)S(1)} %get-tuple-element.40.rim_grad, f32[256,128]{1,0:T(8,128)S(1)} %get-tuple-element.41.local_grad), custom_call_target="tpu_custom_call" | custom-call | tf_op jit(solution)/shard_map/pallas_call | solution.py:80
  (5 shorter events, 0.0 us)
Async XLA Ops:
  1.3 6.5 %collective-permute-start.1 = (bf16[32,128]{1,0:T(8,128)(2,1)S(1)}, bf16[32,128]{1,0:T(8,128)(2,1)S(1)}, u32[]{:S(2)}, u32[]{:S(2)}) collective-permute-start(bf16[32,128]{1,0:T(8,128)(2,1)S(1)} %slice.4.nodes), channel_id=1, source_target_pairs={{0,0},{1,2},{2,1},{3,4},{4,3},{5,6},{6,5},{7,7},{8,8},{9,10},{10,9... | collective-permute-start | bytes 24584 | tf_op jit(solution)/shard_map/ppermute | solution.py:104
  2.0 7.4 %collective-permute-start = (bf16[32,128]{1,0:T(8,128)(2,1)S(1)}, bf16[32,128]{1,0:T(8,128)(2,1)S(1)}, u32[]{:S(2)}, u32[]{:S(2)}) collective-permute-start(bf16[32,128]{1,0:T(8,128)(2,1)S(1)} %slice.4.nodes), channel_id=1, source_target_pairs={{0,1},{1,0},{2,3},{3,2},{4,5},{5,4},{6,7},{7,6},{8,9},{9,8},{10,11... | collective-permute-start | bytes 24584 | tf_op jit(solution)/shard_map/ppermute | solution.py:104
  9.4 12.0 %collective-permute-start.3 = (bf16[96,128]{1,0:T(8,128)(2,1)S(1)}, bf16[96,128]{1,0:T(8,128)(2,1)S(1)}, u32[]{:S(2)}, u32[]{:S(2)}) collective-permute-start(bf16[96,128]{1,0:T(8,128)(2,1)S(1)} %shard_map.162.own_column), channel_id=1, source_target_pairs={{0,0},{8,16},{16,8},{24,24},{1,1},{9,17},{17,9},{25,25},{2,2},{10,... | collective-permute-start | bytes 73736 | tf_op jit(solution)/shard_map/ppermute | solution.py:104
  10.1 11.3 %collective-permute-start.2 = (bf16[96,128]{1,0:T(8,128)(2,1)S(1)}, bf16[96,128]{1,0:T(8,128)(2,1)S(1)}, u32[]{:S(2)}, u32[]{:S(2)}) collective-permute-start(bf16[96,128]{1,0:T(8,128)(2,1)S(1)} %shard_map.162.own_column), channel_id=1, source_target_pairs={{0,8},{8,0},{16,24},{24,16},{1,9},{9,1},{17,25},{25,17},{2,10},{10... | collective-permute-start | bytes 73736 | tf_op jit(solution)/shard_map/ppermute | solution.py:104
  15.3 6.1 %copy-start = (s32[4,8,1024]{2,1,0:T(8,128)}, s32[4,8,1024]{2,1,0:T(8,128)S(1)}, u32[]{:S(2)}) copy-start(s32[4,8,1024]{2,1,0:T(8,128)S(1)} %stack.7.info.info_in) | copy-start | bytes 393220
  45.5 5.8 %collective-permute-start.6 = (bf16[144,128]{1,0:T(8,128)(2,1)S(1)}, bf16[144,128]{1,0:T(8,128)(2,1)S(1)}, u32[]{:S(2)}, u32[]{:S(2)}) collective-permute-start(bf16[144,128]{1,0:T(8,128)(2,1)S(1)} %get-tuple-element.38.refs_0_), channel_id=1, source_target_pairs={{0,6},{2,4},{4,2},{6,0},{1,7},{3,5},{5,3},{7,1},{8,14},{10,12},{12... | collective-permute-start | bytes 110600 | tf_op jit(solution)/shard_map/ppermute | solution.py:659
  48.9 4.9 %collective-permute-start.5 = (bf16[144,128]{1,0:T(8,128)(2,1)S(1)}, bf16[144,128]{1,0:T(8,128)(2,1)S(1)}, u32[]{:S(2)}, u32[]{:S(2)}) collective-permute-start(bf16[144,128]{1,0:T(8,128)(2,1)S(1)} %get-tuple-element.38.refs_0_), channel_id=1, source_target_pairs={{0,4},{2,6},{4,0},{6,2},{1,5},{3,7},{5,1},{7,3},{8,12},{10,14},{12... | collective-permute-start | bytes 110600 | tf_op jit(solution)/shard_map/ppermute | solution.py:659
  48.9 4.9 %collective-permute-start.4 = (bf16[144,128]{1,0:T(8,128)(2,1)S(1)}, bf16[144,128]{1,0:T(8,128)(2,1)S(1)}, u32[]{:S(2)}, u32[]{:S(2)}) collective-permute-start(bf16[144,128]{1,0:T(8,128)(2,1)S(1)} %get-tuple-element.38.refs_0_), channel_id=1, source_target_pairs={{0,2},{2,0},{4,6},{6,4},{1,3},{3,1},{5,7},{7,5},{8,10},{10,8},{12,... | collective-permute-start | bytes 110600 | tf_op jit(solution)/shard_map/ppermute | solution.py:659

commit v10 on v9

--- a/solution.py
+++ b/solution.py
@@ -105,72 +105,119 @@
 
 
 def early_kernel(
-    nodes,
+    nodes_in,
+    edges_in,
+    edge_cot_in,
+    senders_in,
+    receivers_in,
+    w_edge_in_in,
     edges,
-    edge_cot,
-    info,
-    w_edge_in,
     send_codes,
     recv_codes,
     edges_t,
     pre_part,
     cot_part,
+    info,
     tables,
+    nodes,
+    edge_cot,
+    senders,
+    receivers,
+    w_edge_in,
+    small_sems,
+    sems,
 ):
-    count_p, width = nodes.shape
-
-    @pl.when(pl.program_id(0) == 0)
-    def prepare():
-        tables[:count_p] = mm(nodes[...], w_edge_in[width : 2 * width]).astype(BF16)
-        tables[count_p:] = w_edge_in[2 * width :]
-
-    columns = info[0].T
-    edge = edges[...]
-    cot = edge_cot[...].astype(F32)
-    recv = jnp.broadcast_to(columns[:, 1:2], edge.shape).astype(F32).astype(BF16)
-    recv_codes[...] = recv
-    send_codes[...] = jnp.broadcast_to(columns[:, 2:3], edge.shape).astype(F32).astype(BF16)
-    recv = found(recv, count_p // width)
-    pre_part[...] = mm(jnp.concatenate([recv, edge], axis=1), tables[...])
-    edges_t[0] = edge.T
-    cot_part[...] = (cot - jnp.mean(cot, axis=1, keepdims=True)).astype(BF16)
+    count_p, width = nodes_in.shape
+    chunks, _, chunk = info.shape
+    border = count_p // 8
+    my_strip = lax.axis_index("strip")
+    subs = lax.axis_size("z") * lax.axis_size("y")
+    my_sub = lax.axis_index("z") * lax.axis_size("y") + lax.axis_index("y")
+    place_bits, sub_bits = count_p.bit_length() - 1, subs.bit_length() - 1
+
+    def fetch(step):
+        rows = pl.ds(pl.multiple_of(step * chunk, chunk), chunk)
+        return [
+            pltpu.make_async_copy(edges_in.at[rows], edges.at[rows], sems.at[0, step]),
+            pltpu.make_async_copy(edge_cot_in.at[rows], edge_cot.at[rows], sems.at[1, step]),
+        ]
+
+    small = [
+        pltpu.make_async_copy(source, target, small_sems.at[k])
+        for k, (source, target) in enumerate(
+            [
+                (nodes_in, nodes),
+                (w_edge_in_in, w_edge_in),
+                (senders_in, senders),
+                (receivers_in, receivers),
+            ]
+        )
+    ]
+    for copy in small:
+        copy.start()
+    for step in range(chunks):
+        for copy in fetch(step):
+            copy.start()
+    for copy in small:
+        copy.wait()
+    tables[:count_p] = mm(nodes[...], w_edge_in[width : 2 * width]).astype(BF16)
+    tables[count_p:] = w_edge_in[2 * width :]
+    line = lax.broadcasted_iota(jnp.int32, (8, chunk), 0)
+
+    def one(step, carry):
+        rows = pl.ds(pl.multiple_of(step * chunk, chunk), chunk)
+        sender = jnp.broadcast_to(senders[step], (8, chunk))
+        receiver = jnp.broadcast_to(receivers[step], (8, chunk))
+        owner = lax.shift_right_logical(sender, place_bits)
+        within = lax.bitwise_and(sender, count_p - 1)
+        d_strip = lax.shift_right_logical(owner, sub_bits) - my_strip
+        d_sub = lax.bitwise_and(owner, subs - 1) - my_sub
+        spot = 3 * d_strip + d_sub + 4
+        spot = jnp.where(spot > 4, spot - 1, spot)
+        near = (d_strip == 0) & (d_sub == 0)
+        spot = jnp.where(near, within, spot * border + jnp.minimum(within, border - 1))
+        index = jnp.where(line == 0, spot, receiver)
+        index = jnp.where(line == 2, jnp.where(near, spot, -1 - spot), index)
+        info[step] = index
+        columns = index.T
+        for copy in fetch(step):
+            copy.wait()
+        edge = edges[rows]
+        cot = edge_cot[rows].astype(F32)
+        recv = jnp.broadcast_to(columns[:, 1:2], edge.shape).astype(F32).astype(BF16)
+        recv_codes[rows] = recv
+        send_codes[rows] = jnp.broadcast_to(columns[:, 2:3], edge.shape).astype(F32).astype(BF16)
+        recv = found(recv, count_p // width)
+        pre_part[rows] = mm(jnp.concatenate([recv, edge], axis=1), tables[...])
+        edges_t[step] = edge.T
+        cot_part[rows] = (cot - jnp.mean(cot, axis=1, keepdims=True)).astype(BF16)
+        return carry
+
+    lax.fori_loop(0, chunks, one, 0)
 
 
 def layer_kernel(
     edge_count,
-    nodes_in,
+    nodes,
     own_column,
     even_column,
     odd_column,
-    edges_in,
-    info_in,
-    send_codes_in,
-    recv_codes_in,
-    edges_t_in,
-    pre_part_in,
-    cot_part_in,
-    w_edge_in_in,
-    w_edge_out_in,
-    w_node_in_in,
-    w_node_out_in,
-    node_cot_in,
-    new_nodes_out,
-    new_edges_out,
-    local_grad,
-    parts,
-    nodes,
     edges,
-    info,
     send_codes,
     recv_codes,
     edges_t,
     pre_part,
     cot_part,
+    info,
     w_edge_in,
     w_edge_out,
     w_node_in,
     w_node_out,
     node_cot,
+    new_nodes_out,
+    new_edges_out,
+    local_grad,
+    parts,
     new_nodes,
     new_edges,
     near_rows,
@@ -189,8 +236,6 @@
     packed,
     kept,
     columns,
-    small_sems,
-    sems,
     out_sems,
     last_sem,
 ):
@@ -205,20 +250,6 @@
     my_strip, my_y = lax.axis_index("strip"), lax.axis_index("y")
     live_count = edge_count[0]
 
-    small = [
-        pltpu.make_async_copy(source, target, small_sems.at[k])
-        for k, (source, target) in enumerate(
-            [
-                (nodes_in, nodes),
-                (w_edge_in_in, w_edge_in),
-                (w_edge_out_in, w_edge_out),
-                (w_node_in_in, w_node_in),
-                (w_node_out_in, w_node_out),
-                (node_cot_in, node_cot),
-            ]
-        )
-    ]
-
     def span(step):
         return pl.ds(pl.multiple_of(step * chunk, chunk), chunk)
 
@@ -227,19 +258,6 @@
 
     def block_pairs(step, part):
         return pl.ds(pl.multiple_of((step * SPLIT + part) * half, half), half)
-
-    def fetch(step, which):
-        rows = span(step)
-        pairs = [
-            (send_codes_in.at[rows], send_codes.at[rows]),
-            (pre_part_in.at[rows], pre_part.at[rows]),
-            (info_in.at[step], info.at[step]),
-            (edges_in.at[rows], edges.at[rows]),
-            (recv_codes_in.at[rows], recv_codes.at[rows]),
-            (cot_part_in.at[rows], cot_part.at[rows]),
-            (edges_t_in.at[step], edges_t.at[step]),
-        ]
-        return [pltpu.make_async_copy(*pairs[k], sems.at[k, step]) for k in which]
 
     def emit(step):
         rows = span(step)
@@ -262,18 +280,6 @@
             ],
             axis=0,
         )
-
-    ahead, behind = range(4), range(4, 7)
-    for copy in small[:3] + fetch(0, ahead) + small[3:]:
-        copy.start()
-    for step in range(1, chunks):
-        for copy in fetch(step, ahead):
-            copy.start()
-    for step in range(chunks):
-        for copy in fetch(step, behind):
-            copy.start()
-    for copy in small[:3]:
-        copy.wait()
 
     near_rows[...] = nodes[...]
     for k, column in enumerate((own_column, even_column, odd_column)):
@@ -308,8 +314,6 @@
     agg[...] = jnp.zeros_like(agg)
 
     def forward(step, carry):
-        for copy in fetch(step, ahead):
-            copy.wait()
         recv_t = found_t(info[step][1:2], count_p)
         units = []
         for part in range(SPLIT):
@@ -340,8 +344,6 @@
 
     lax.fori_loop(0, chunks, forward, 0)
 
-    for copy in small[3:]:
-        copy.wait()
     joined = jnp.concatenate([nodes[...], agg[...].astype(BF16)], axis=1)
     node_pre = mm(joined, w_node_in[...])
     node_act, node_slope = silu_and_slope(node_pre)
@@ -366,8 +368,6 @@
     ge_out[...] = jnp.zeros_like(ge_out)
 
     def backward(step, carry):
-        for copy in fetch(step, behind):
-            copy.wait()
         index = info[step]
         turned = jnp.concatenate(
             [found_t(index[1:2], count_p), found_t(index[0:1], count_p), edges_t[step]], axis=0
@@ -511,84 +511,47 @@
     strips, zs, ys = (lax.axis_size(axis) for axis in ALL)
     subs = zs * ys
     slots = strips * ys
-    my_strip, my_z, my_y = (lax.axis_index(axis).astype(jnp.int32) for axis in ALL)
-    my_sub = my_z * ys + my_y
-
     even, odd = swapped(node_latents[:border], ("z", "y"))
     (own_column,) = call(
         column_kernel, [((3 * border, width), BF16)], [node_latents[:border], even, odd], [VMEM] * 3
     )
     even_column, odd_column = swapped(own_column, "strip")
 
-    owner = senders // count_p
-    within = senders % count_p
-    is_local = owner == my_strip * subs + my_sub
-    block = (owner // subs - my_strip + 1) * 3 + (owner % subs - my_sub + 1)
-    block = jnp.where(block > 4, block - 1, block)
-    send_index = jnp.where(is_local, within, block * border + jnp.minimum(within, border - 1))
-    codes = jnp.where(is_local, send_index, -1 - send_index)
     chunk = min(CHUNK, count_e)
     chunks = count_e // chunk
-    info = jnp.stack(
+    early = call(
+        early_kernel,
         [
-            value.reshape(chunks, chunk)
-            for value in [send_index, receivers, codes]
-            + [jnp.zeros_like(receivers)] * 5
-        ],
-        axis=1,
-    )
-
-    def by_rows(*shape):
-        return pl.BlockSpec(shape, lambda i: (i, 0))
-
-    def by_chunk(*shape):
-        return pl.BlockSpec((1, *shape), lambda i: (i, 0, 0))
-
-    def whole(*shape):
-        return pl.BlockSpec(shape, lambda i: (0, 0))
-
-    info, own_column = lax.optimization_barrier((info, own_column))
-    early = pl.pallas_call(
-        early_kernel,
-        grid=(chunks,),
-        out_shape=[
-            pltpu.HBM(shape, dtype)
-            for shape, dtype in [
-                ((count_e, width), BF16),
-                ((count_e, width), BF16),
-                ((chunks, width, chunk), BF16),
-                ((count_e, width), F32),
-                ((count_e, width), BF16),
-            ]
-        ],
-        in_specs=[
-            whole(count_p, width),
-            by_rows(chunk, width),
-            by_rows(chunk, width),
-            by_chunk(8, chunk),
-            whole(3 * width, width),
-        ],
-        out_specs=[
-            by_rows(chunk, width),
-            by_rows(chunk, width),
-            by_chunk(width, chunk),
-            by_rows(chunk, width),
-            by_rows(chunk, width),
-        ],
-        scratch_shapes=[pltpu.VMEM((count_p + width, width), BF16)],
-        compiler_params=pltpu.CompilerParams(vmem_limit_bytes=32 * 2**20),
-    )(
-        in_hbm(node_latents),
-        in_hbm(edge_latents),
-        in_hbm(edge_cotangent),
-        info,
-        in_hbm(w_edge_in),
+            ((count_e, width), BF16),
+            ((count_e, width), BF16),
+            ((count_e, width), BF16),
+            ((chunks, width, chunk), BF16),
+            ((count_e, width), F32),
+            ((count_e, width), BF16),
+            ((chunks, 8, chunk), jnp.int32),
+        ],
+        [
+            node_latents,
+            edge_latents,
+            edge_cotangent,
+            senders.reshape(chunks, 1, chunk),
+            receivers.reshape(chunks, 1, chunk),
+            w_edge_in,
+        ],
+        [HBM] * 6,
+        [
+            pltpu.VMEM((count_p + width, width), BF16),
+            pltpu.VMEM((count_p, width), BF16),
+            pltpu.VMEM((count_e, width), BF16),
+            pltpu.VMEM((chunks, 1, chunk), jnp.int32),
+            pltpu.VMEM((chunks, 1, chunk), jnp.int32),
+            pltpu.VMEM((3 * width, width), BF16),
+            SEM((4,)),
+            SEM((2, chunks)),
+        ],
     )
 
     share = -(-7 * width // (slots * 16)) * 16
-
-    def like(value):
-        return pltpu.VMEM(value.shape, value.dtype)
 
     new_nodes, new_edges, local_grad, parts = call(
         layer_kernel,
@@ -604,8 +567,6 @@
             own_column,
             even_column,
             odd_column,
-            edge_latents,
-            info,
             *early,
             w_edge_in,
             w_edge_out,
@@ -613,17 +574,8 @@
             w_node_out,
             node_cotangent,
         ],
-        [SMEM, HBM] + [VMEM] * 3 + [HBM] * 12,
+        [SMEM] + [VMEM] * 16,
         [
-            like(node_latents),
-            like(edge_latents),
-            like(info),
-            *[like(value) for value in early],
-            like(w_edge_in),
-            like(w_edge_out),
-            like(w_node_in),
-            like(w_node_out),
-            like(node_cotangent),
             pltpu.VMEM((count_p, width), BF16),
             pltpu.VMEM((count_e, width), BF16),
             pltpu.VMEM((count_p, width), BF16),
@@ -642,13 +594,11 @@
             pltpu.VMEM((slots * share, width), BF16),
             pltpu.VMEM((count_p, 5 * width), BF16),
             pltpu.VMEM((9, border, width), BF16),
-            SEM((6,)),
-            SEM((7, chunks)),
             SEM((chunks,)),
             SEM,
         ],
         [HBM, HBM, VMEM, VMEM],
-        limit=48,
+        limit=24,
     )
 
     came = lax.all_to_all(parts, PLANE, 0, 0)

time: 63.2 us -> 57.4 us (0.908)
  Pallas kernels: 20.4 us -> 16.2 us
  other arithmetic: 0.77 us -> 0 us
  local copies, waits for them, and re-layouts: 1.57 us -> 0.81 us
    pallas_call x1 -> x0, Pallas kernels: 6.07 us -> none  [shards(): pl.pallas_call(early_kernel, grid=(chunks,), out_shape=[pltpu.HBM(shape,...]
    pallas_call x5 -> x6, Pallas kernels: 14.3 us -> 16.2 us  [call(): pl.pallas_call(kernel, out_shape=[pltpu.HBM(shape, dtype) if spec is HBM...]
    another operation x3 -> x0, local copies, waits for them, and re-layouts: 0.86 us -> none  [shards(): jnp.stack([value.reshape(chunks, chunk) for value in [send_index, receive...]
    select_n x1 -> x0, other arithmetic: 0.77 us -> none  [shards(): codes = jnp.where(is_local, send_index, -1 - send_index)]
  transfers between devices with their start and end apart: 7 -> 7, of which waited for: 3 -> 3; matrix products, arithmetic and copies ran while one was open for 3% -> 0% of each run, Pallas kernels for 10% -> 9%
where the time goes in v10:
time: 57.4 us; the launch traced here: 57.1 us
  blocking collectives  18.8 us (33%)
  Pallas kernels  16.2 us (28%)
  starting transfers between devices  14.5 us (25%)
  waiting for transfers between devices  5.39 us (9%)
  between operations  1.44 us (3%)
  local copies, waits for them, and re-layouts  0.81 us (1%)
    all_to_all x2, blocking collectives, shards(): came = lax.all_to_all(parts, PLANE, 0, 0)  18.8 us
    pallas_call x6, Pallas kernels, call(): pl.pallas_call(kernel, out_shape=[pltpu.HBM(shape, dtype) if spec is HBM...  16.2 us
    ppermute x4, starting transfers between devices, swapped(): return (lax.ppermute(value, axes, even), lax.ppermute(value, axes, odd))  10 us
    ppermute x3, starting transfers between devices, shards(): lax.ppermute(message, 'z', [(z, z ^ k) for z in range(zs)])  4.45 us
    ppermute x3, waiting for transfers between devices, shards(): lax.ppermute(message, 'z', [(z, z ^ k) for z in range(zs)])  3.76 us
    ppermute x4, waiting for transfers between devices, swapped(): return (lax.ppermute(value, axes, even), lax.ppermute(value, axes, odd))  1.64 us
  transfers between devices with their start and end apart: 7, of which 3 were waited for; matrix products, arithmetic and copies ran while one was open for 0% of the time, Pallas kernels for 9%

profile of v10, /device:TPU:0, one launch (start us, length us, event | category | flops | bytes accessed | tf_op | source)
XLA Modules:
  0.0 57.1 jit_solution(46915060858528530)
XLA Ops:
  0.6 0.0 copy-start.1
  0.6 0.0 copy-start
  0.7 0.8 %slice.4.nodes = bf16[32,128]{1,0:T(8,128)(2,1)S(1)} slice(bf16[256,128]{1,0:T(8,128)(2,1)} %nodes.1), slice={[0:32], [0:128]} | slice | bytes 16384 | tf_op jit(solution)/shard_map/slice | solution.py:516
  1.5 0.6 %collective-permute-start.1 = (bf16[32,128]{1,0:T(8,128)(2,1)S(1)}, bf16[32,128]{1,0:T(8,128)(2,1)S(1)}, u32[]{:S(2)}, u32[]{:S(2)}) collective-permute-start(bf16[32,128]{1,0:T(8,128)(2,1)S(1)} %slice.4.nodes), channel_id=1, source_target_pairs={{0,0},{1,2},{2,1},{3,4},{4,3},{5,6},{6,5},{7,7},{8,8},{9,10},{10,9... | collective-permute-start | bytes 24584 | tf_op jit(solution)/shard_map/ppermute | solution.py:104
  2.1 5.8 %collective-permute-start = (bf16[32,128]{1,0:T(8,128)(2,1)S(1)}, bf16[32,128]{1,0:T(8,128)(2,1)S(1)}, u32[]{:S(2)}, u32[]{:S(2)}) collective-permute-start(bf16[32,128]{1,0:T(8,128)(2,1)S(1)} %slice.4.nodes), channel_id=1, source_target_pairs={{0,1},{1,0},{2,3},{3,2},{4,5},{5,4},{6,7},{7,6},{8,9},{9,8},{10,11... | collective-permute-start | bytes 24584 | tf_op jit(solution)/shard_map/ppermute | solution.py:104
  7.9 0.0 collective-permute-done.1.odd
  7.9 1.6 %collective-permute-done.even = bf16[32,128]{1,0:T(8,128)(2,1)S(1)} collective-permute-done((bf16[32,128]{1,0:T(8,128)(2,1)S(1)}, bf16[32,128]{1,0:T(8,128)(2,1)S(1)}, u32[]{:S(2)}, u32[]{:S(2)}) %collective-permute-start) | collective-permute-done | bytes 8224 | tf_op jit(solution)/shard_map/ppermute | solution.py:104
  9.6 0.7 %collective-permute-start.3 = (bf16[96,128]{1,0:T(8,128)(2,1)S(1)}, bf16[96,128]{1,0:T(8,128)(2,1)S(1)}, u32[]{:S(2)}, u32[]{:S(2)}) collective-permute-start(bf16[96,128]{1,0:T(8,128)(2,1)S(1)} %shard_map.162.own_column), channel_id=1, source_target_pairs={{0,0},{8,16},{16,8},{24,24},{1,1},{9,17},{17,9},{25,25},{2,2},{10,... | collective-permute-start | bytes 73736 | tf_op jit(solution)/shard_map/ppermute | solution.py:104
  10.2 2.9 %collective-permute-start.2 = (bf16[96,128]{1,0:T(8,128)(2,1)S(1)}, bf16[96,128]{1,0:T(8,128)(2,1)S(1)}, u32[]{:S(2)}, u32[]{:S(2)}) collective-permute-start(bf16[96,128]{1,0:T(8,128)(2,1)S(1)} %shard_map.162.own_column), channel_id=1, source_target_pairs={{0,8},{8,0},{16,24},{24,16},{1,9},{9,1},{17,25},{25,17},{2,10},{10... | collective-permute-start | bytes 73736 | tf_op jit(solution)/shard_map/ppermute | solution.py:104
  13.8 4.9 %shard_map.163 = (bf16[4096,128]{1,0:T(8,128)(2,1)S(1)}, bf16[4096,128]{1,0:T(8,128)(2,1)S(1)}, bf16[4096,128]{1,0:T(8,128)(2,1)S(1)}, bf16[4,128,1024]{2,1,0:T(...) custom-call(bf16[256,128]{1,0:T(8,128)(2,1)} %nodes.1, ...), custom_call_target="tpu_custom_call" | custom-call | tf_op jit(solution)/shard_map/pallas_call | solution.py:80
  18.7 0.0 collective-permute-done.3.odd_column
  18.7 0.0 collective-permute-done.2.even_column
  18.8 10.4 %shard_map.164 = (bf16[256,128]{1,0:T(8,128)(2,1)}, bf16[4096,128]{1,0:T(8,128)(2,1)}, f32[256,128]{1,0:T(8,128)S(1)}, bf16[8,176,128]{2,1,0:T(8,128)(2,1)S(1)}) custom-call(s32[1]{0:T(128)S(6)} %copy.18.edge_count, bf16[256,128]{1,0:T(8,128)(2,1)S(1)} %copy-done.1, bf16[96,128]{1,0:T(8,128)(2,1)S(1)} %shard_map.162.own_column, ...), custom_call_target="tpu_custom_call" | custom-call | tf_op jit(solution)/shard_map/pallas_call | solution.py:80
  29.2 10.7 %all_to_all.10.came = bf16[8,176,128]{2,1,0:T(8,128)(2,1)S(1)} all-to-all(bf16[8,176,128]{2,1,0:T(8,128)(2,1)S(1)} %get-tuple-element.36), channel_id=1, replica_groups=mesh['strip'=4,'z'=4,'y'=2] {'strip','y'}, dimensions={0} | all-to-all | bytes 720896 | tf_op jit(solution)/shard_map/all_to_all | solution.py:604
  39.8 0.1 shard_map.165
  39.9 3.4 %collective-permute-start.6 = (bf16[144,128]{1,0:T(8,128)(2,1)S(1)}, bf16[144,128]{1,0:T(8,128)(2,1)S(1)}, u32[]{:S(2)}, u32[]{:S(2)}) collective-permute-start(bf16[144,128]{1,0:T(8,128)(2,1)S(1)} %get-tuple-element.38.refs_0_), channel_id=1, source_target_pairs={{0,6},{2,4},{4,2},{6,0},{1,7},{3,5},{5,3},{7,1},{8,14},{10,12},{12... | collective-permute-start | bytes 110600 | tf_op jit(solution)/shard_map/ppermute | solution.py:609
  43.2 0.0 collective-permute-start.5
  43.2 1.1 %collective-permute-start.4 = (bf16[144,128]{1,0:T(8,128)(2,1)S(1)}, bf16[144,128]{1,0:T(8,128)(2,1)S(1)}, u32[]{:S(2)}, u32[]{:S(2)}) collective-permute-start(bf16[144,128]{1,0:T(8,128)(2,1)S(1)} %get-tuple-element.38.refs_0_), channel_id=1, source_target_pairs={{0,2},{2,0},{4,6},{6,4},{1,3},{3,1},{5,7},{7,5},{8,10},{10,8},{12,... | collective-permute-start | bytes 110600 | tf_op jit(solution)/shard_map/ppermute | solution.py:609
  44.3 1.4 %collective-permute-done.6.refs_3_ = bf16[144,128]{1,0:T(8,128)(2,1)S(1)} collective-permute-done((bf16[144,128]{1,0:T(8,128)(2,1)S(1)}, bf16[144,128]{1,0:T(8,128)(2,1)S(1)}, u32[]{:S(2)}, u32[]{:S(2)}) %collective-permute-start.6) | collective-permute-done | bytes 36896 | tf_op jit(solution)/shard_map/ppermute | solution.py:609
  45.7 2.4 %collective-permute-done.5.refs_2_ = bf16[144,128]{1,0:T(8,128)(2,1)S(1)} collective-permute-done((bf16[144,128]{1,0:T(8,128)(2,1)S(1)}, bf16[144,128]{1,0:T(8,128)(2,1)S(1)}, u32[]{:S(2)}, u32[]{:S(2)}) %collective-permute-start.5) | collective-permute-done | bytes 36896 | tf_op jit(solution)/shard_map/ppermute | solution.py:609
  48.1 0.0 collective-permute-done.4.refs_1_
  48.1 0.1 shard_map.166
  48.2 8.1 %all_to_all.11.came = bf16[8,112,128]{2,1,0:T(8,128)(2,1)S(1)} all-to-all(bf16[8,112,128]{2,1,0:T(8,128)(2,1)S(1)} %get-tuple-element.39), channel_id=1, replica_groups=mesh['strip'=4,'z'=4,'y'=2] {'strip','y'}, dimensions={0} | all-to-all | bytes 458752 | tf_op jit(solution)/shard_map/all_to_all | solution.py:618
  56.2 0.8 %shard_map.167 = (f32[256,128]{1,0:T(8,128)}, f32[384,128]{1,0:T(8,128)}, f32[128,128]{1,0:T(8,128)}, f32[256,128]{1,0:T(8,128)}, f32[128,128]{1,0:T(8,128)}) custom-call(bf16[8,112,128]{2,1,0:T(8,128)(2,1)S(1)} %all_to_all.11.came, f32[32,128]{1,0:T(8,128)S(1)} %get-tuple-element.40.rim_grad, f32[256,128]{1,0:T(8,128)S(1)} %get-tuple-element.41.local_grad), custom_call_target="tpu_custom_call" | custom-call | tf_op jit(solution)/shard_map/pallas_call | solution.py:80
  (11 shorter events, 0.0 us)
Async XLA Ops:
  0.6 18.1 %copy-start.1 = (bf16[256,128]{1,0:T(8,128)(2,1)S(1)}, bf16[256,128]{1,0:T(8,128)(2,1)}, u32[]{:S(2)}) copy-start(bf16[256,128]{1,0:T(8,128)(2,1)} %nodes.1) | copy-start | bytes 196612
  0.6 18.1 %copy-start = (bf16[384,128]{1,0:T(8,128)(2,1)S(1)}, bf16[384,128]{1,0:T(8,128)(2,1)}, u32[]{:S(2)}) copy-start(bf16[384,128]{1,0:T(8,128)(2,1)} %w_edge_in.1) | copy-start | bytes 294916
  0.7 18.1 %copy-start.3 = (bf16[256,128]{1,0:T(8,128)(2,1)S(1)}, bf16[256,128]{1,0:T(8,128)(2,1)}, u32[]{:S(2)}) copy-start(bf16[256,128]{1,0:T(8,128)(2,1)} %node_cot.1) | copy-start | bytes 196612
  0.7 18.1 %copy-start.5 = (bf16[128,128]{1,0:T(8,128)(2,1)S(1)}, bf16[128,128]{1,0:T(8,128)(2,1)}, u32[]{:S(2)}) copy-start(bf16[128,128]{1,0:T(8,128)(2,1)} %w_node_out.1) | copy-start | bytes 98308
  0.7 18.1 %copy-start.2 = (bf16[256,128]{1,0:T(8,128)(2,1)S(1)}, bf16[256,128]{1,0:T(8,128)(2,1)}, u32[]{:S(2)}) copy-start(bf16[256,128]{1,0:T(8,128)(2,1)} %w_node_in.1) | copy-start | bytes 196612
  0.7 18.1 %copy-start.4 = (bf16[128,128]{1,0:T(8,128)(2,1)S(1)}, bf16[128,128]{1,0:T(8,128)(2,1)}, u32[]{:S(2)}) copy-start(bf16[128,128]{1,0:T(8,128)(2,1)} %w_edge_out.1) | copy-start | bytes 98308
  1.5 6.5 %collective-permute-start.1 = (bf16[32,128]{1,0:T(8,128)(2,1)S(1)}, bf16[32,128]{1,0:T(8,128)(2,1)S(1)}, u32[]{:S(2)}, u32[]{:S(2)}) collective-permute-start(bf16[32,128]{1,0:T(8,128)(2,1)S(1)} %slice.4.nodes), channel_id=1, source_target_pairs={{0,0},{1,2},{2,1},{3,4},{4,3},{5,6},{6,5},{7,7},{8,8},{9,10},{10,9... | collective-permute-start | bytes 24584 | tf_op jit(solution)/shard_map/ppermute | solution.py:104
  2.1 7.4 %collective-permute-start = (bf16[32,128]{1,0:T(8,128)(2,1)S(1)}, bf16[32,128]{1,0:T(8,128)(2,1)S(1)}, u32[]{:S(2)}, u32[]{:S(2)}) collective-permute-start(bf16[32,128]{1,0:T(8,128)(2,1)S(1)} %slice.4.nodes), channel_id=1, source_target_pairs={{0,1},{1,0},{2,3},{3,2},{4,5},{5,4},{6,7},{7,6},{8,9},{9,8},{10,11... | collective-permute-start | bytes 24584 | tf_op jit(solution)/shard_map/ppermute | solution.py:104
  9.6 9.1 %collective-permute-start.3 = (bf16[96,128]{1,0:T(8,128)(2,1)S(1)}, bf16[96,128]{1,0:T(8,128)(2,1)S(1)}, u32[]{:S(2)}, u32[]{:S(2)}) collective-permute-start(bf16[96,128]{1,0:T(8,128)(2,1)S(1)} %shard_map.162.own_column), channel_id=1, source_target_pairs={{0,0},{8,16},{16,8},{24,24},{1,1},{9,17},{17,9},{25,25},{2,2},{10,... | collective-permute-start | bytes 73736 | tf_op jit(solution)/shard_map/ppermute | solution.py:104
  10.2 8.5 %collective-permute-start.2 = (bf16[96,128]{1,0:T(8,128)(2,1)S(1)}, bf16[96,128]{1,0:T(8,128)(2,1)S(1)}, u32[]{:S(2)}, u32[]{:S(2)}) collective-permute-start(bf16[96,128]{1,0:T(8,128)(2,1)S(1)} %shard_map.162.own_column), channel_id=1, source_target_pairs={{0,8},{8,0},{16,24},{24,16},{1,9},{9,1},{17,25},{25,17},{2,10},{10... | collective-permute-start | bytes 73736 | tf_op jit(solution)/shard_map/ppermute | solution.py:104
  39.9 5.8 %collective-permute-start.6 = (bf16[144,128]{1,0:T(8,128)(2,1)S(1)}, bf16[144,128]{1,0:T(8,128)(2,1)S(1)}, u32[]{:S(2)}, u32[]{:S(2)}) collective-permute-start(bf16[144,128]{1,0:T(8,128)(2,1)S(1)} %get-tuple-element.38.refs_0_), channel_id=1, source_target_pairs={{0,6},{2,4},{4,2},{6,0},{1,7},{3,5},{5,3},{7,1},{8,14},{10,12},{12... | collective-permute-start | bytes 110600 | tf_op jit(solution)/shard_map/ppermute | solution.py:609
  43.2 4.9 %collective-permute-start.5 = (bf16[144,128]{1,0:T(8,128)(2,1)S(1)}, bf16[144,128]{1,0:T(8,128)(2,1)S(1)}, u32[]{:S(2)}, u32[]{:S(2)}) collective-permute-start(bf16[144,128]{1,0:T(8,128)(2,1)S(1)} %get-tuple-element.38.refs_0_), channel_id=1, source_target_pairs={{0,4},{2,6},{4,0},{6,2},{1,5},{3,7},{5,1},{7,3},{8,12},{10,14},{12... | collective-permute-start | bytes 110600 | tf_op jit(solution)/shard_map/ppermute | solution.py:609
  43.2 4.9 %collective-permute-start.4 = (bf16[144,128]{1,0:T(8,128)(2,1)S(1)}, bf16[144,128]{1,0:T(8,128)(2,1)S(1)}, u32[]{:S(2)}, u32[]{:S(2)}) collective-permute-start(bf16[144,128]{1,0:T(8,128)(2,1)S(1)} %get-tuple-element.38.refs_0_), channel_id=1, source_target_pairs={{0,2},{2,0},{4,6},{6,4},{1,3},{3,1},{5,7},{7,5},{8,10},{10,8},{12,... | collective-permute-start | bytes 110600 | tf_op jit(solution)/shard_map/ppermute | solution.py:609

commit v11 on v10

--- a/solution.py
+++ b/solution.py
@@ -12,6 +12,7 @@
 EPS = 1e-05
 CHUNK = 1024
 SPLIT = 2
+UNROLL = 4
 PLANE = ("strip", "y")
 ALL = ("strip", "z", "y")
 F32 = jnp.float32
@@ -90,7 +91,7 @@
     )(*[in_hbm(value) if spec is HBM else value for value, spec in zip(ins, specs)])
 
 
-def column_kernel(nodes, even, odd, out):
+def column_kernel(edge_count, nodes, odd, even, out):
     border = even.shape[0]
     out[:border] = nodes[:border]
     out[border : 2 * border] = even[...]
@@ -101,7 +102,9 @@
     count = lax.axis_size(axes)
     even = [(k, k ^ 1) for k in range(count)]
     odd = [(k, min(max(((k + 1) ^ 1) - 1, 0), count - 1)) for k in range(count)]
-    return lax.ppermute(value, axes, even), lax.ppermute(value, axes, odd)
+    from_odd = lax.ppermute(value, axes, odd)
+    from_even = lax.ppermute(value, axes, even)
+    return from_even, from_odd
 
 
 def early_kernel(
@@ -200,8 +203,8 @@
     edge_count,
     nodes,
     own_column,
+    odd_column,
     even_column,
-    odd_column,
     edges,
     send_codes,
     recv_codes,
@@ -342,7 +345,7 @@
         emit(step).start()
         return carry
 
-    lax.fori_loop(0, chunks, forward, 0)
+    lax.fori_loop(0, chunks, forward, 0, unroll=UNROLL)
 
     joined = jnp.concatenate([nodes[...], agg[...].astype(BF16)], axis=1)
     node_pre = mm(joined, w_node_in[...])
@@ -395,7 +398,7 @@
         sums[...] += mm(turned, jnp.concatenate(ins, axis=0))
         return carry
 
-    lax.fori_loop(0, chunks, backward, 0)
+    lax.fori_loop(0, chunks, backward, 0, unroll=UNROLL)
 
     recv_sums = (sums[:count_p, :width] + sums[:count_p, width:]).astype(BF16)
     near_sums = sums[count_p : 2 * count_p, :width].astype(BF16)
@@ -513,7 +516,10 @@
     slots = strips * ys
     even, odd = swapped(node_latents[:border], ("z", "y"))
     (own_column,) = call(
-        column_kernel, [((3 * border, width), BF16)], [node_latents[:border], even, odd], [VMEM] * 3
+        column_kernel,
+        [((3 * border, width), BF16)],
+        [edge_count, node_latents[:border], odd, even],
+        [SMEM] + [VMEM] * 3,
     )
     even_column, odd_column = swapped(own_column, "strip")
 
@@ -565,8 +571,8 @@
             edge_count,
             node_latents,
             own_column,
+            odd_column,
             even_column,
-            odd_column,
             *early,
             w_edge_in,
             w_edge_out,

time: 57.4 us -> 55.5 us (0.967)
  blocking collectives: 18.8 us -> 24.5 us
  starting transfers between devices: 14.5 us -> 9.01 us
  Pallas kernels: 16.2 us -> 14.8 us
  waiting for transfers between devices: 5.39 us -> 4.55 us
    all_to_all x2, blocking collectives: 18.8 us -> 24.5 us  [shards(): came = lax.all_to_all(parts, PLANE, 0, 0)]
    ppermute x4, starting transfers between devices: 10 us -> 4.28 us  [the longest x2 2.97 us: swapped(): from_even = lax.ppermute(value, axes, even)]
    pallas_call x6, Pallas kernels: 16.2 us -> 14.8 us  [call(): pl.pallas_call(kernel, out_shape=[pltpu.HBM(shape, dtype) if spec is HBM...]
    ppermute x4, waiting for transfers between devices: 1.64 us -> 0.33 us  [the longest x2 0.33 us: swapped(): from_even = lax.ppermute(value, axes, even)]
where the time goes in v11:
time: 55.5 us; the launch traced here: 55.1 us
  blocking collectives  24.5 us (44%)
  Pallas kernels  14.8 us (27%)
  starting transfers between devices  9.01 us (16%)
  waiting for transfers between devices  4.55 us (8%)
  between operations  1.44 us (3%)
  local copies, waits for them, and re-layouts  0.81 us (1%)
    all_to_all x2, blocking collectives, shards(): came = lax.all_to_all(parts, PLANE, 0, 0)  24.5 us
    pallas_call x6, Pallas kernels, call(): pl.pallas_call(kernel, out_shape=[pltpu.HBM(shape, dtype) if spec is HBM...  14.8 us
    ppermute x3, starting transfers between devices, shards(): lax.ppermute(message, 'z', [(z, z ^ k) for z in range(zs)])  4.73 us
    ppermute x3, waiting for transfers between devices, shards(): lax.ppermute(message, 'z', [(z, z ^ k) for z in range(zs)])  4.22 us
    ppermute x2, starting transfers between devices, swapped(): from_even = lax.ppermute(value, axes, even)  2.97 us
    ppermute x2, starting transfers between devices, swapped(): from_odd = lax.ppermute(value, axes, odd)  1.31 us
  transfers between devices with their start and end apart: 7, of which 3 were waited for; matrix products, arithmetic and copies ran while one was open for 0% of the time, Pallas kernels for 9%

profile of v11, /device:TPU:0, one launch (start us, length us, event | category | flops | bytes accessed | tf_op | source)
XLA Modules:
  0.0 55.1 jit_solution(5034402102614903598)
XLA Ops:
  0.6 0.0 copy-start.1
  0.6 0.0 copy-start
  0.7 0.8 %slice.4.nodes = bf16[32,128]{1,0:T(8,128)(2,1)S(1)} slice(bf16[256,128]{1,0:T(8,128)(2,1)} %nodes.1), slice={[0:32], [0:128]} | slice | bytes 16384 | tf_op jit(solution)/shard_map/slice | solution.py:521
  1.5 3.0 %collective-permute-start.1 = (bf16[32,128]{1,0:T(8,128)(2,1)S(1)}, bf16[32,128]{1,0:T(8,128)(2,1)S(1)}, u32[]{:S(2)}, u32[]{:S(2)}) collective-permute-start(bf16[32,128]{1,0:T(8,128)(2,1)S(1)} %slice.4.nodes), channel_id=1, source_target_pairs={{0,1},{1,0},{2,3},{3,2},{4,5},{5,4},{6,7},{7,6},{8,9},{9,8},{10,11... | collective-permute-start | bytes 24584 | tf_op jit(solution)/shard_map/ppermute | solution.py:106
  4.4 0.6 %collective-permute-start = (bf16[32,128]{1,0:T(8,128)(2,1)S(1)}, bf16[32,128]{1,0:T(8,128)(2,1)S(1)}, u32[]{:S(2)}, u32[]{:S(2)}) collective-permute-start(bf16[32,128]{1,0:T(8,128)(2,1)S(1)} %slice.4.nodes), channel_id=1, source_target_pairs={{0,0},{1,2},{2,1},{3,4},{4,3},{5,6},{6,5},{7,7},{8,8},{9,10},{10,9... | collective-permute-start | bytes 24584 | tf_op jit(solution)/shard_map/ppermute | solution.py:105
  5.8 0.3 collective-permute-done.1.even
  6.1 0.0 collective-permute-done.odd
  6.1 0.0 collective-permute-start.3
  6.1 0.7 %collective-permute-start.2 = (bf16[96,128]{1,0:T(8,128)(2,1)S(1)}, bf16[96,128]{1,0:T(8,128)(2,1)S(1)}, u32[]{:S(2)}, u32[]{:S(2)}) collective-permute-start(bf16[96,128]{1,0:T(8,128)(2,1)S(1)} %shard_map.162.own_column), channel_id=1, source_target_pairs={{0,0},{8,16},{16,8},{24,24},{1,1},{9,17},{17,9},{25,25},{2,2},{10,... | collective-permute-start | bytes 73736 | tf_op jit(solution)/shard_map/ppermute | solution.py:105
  6.8 4.9 %shard_map.163 = (bf16[4096,128]{1,0:T(8,128)(2,1)S(1)}, bf16[4096,128]{1,0:T(8,128)(2,1)S(1)}, bf16[4096,128]{1,0:T(8,128)(2,1)S(1)}, bf16[4,128,1024]{2,1,0:T(...) custom-call(bf16[256,128]{1,0:T(8,128)(2,1)} %nodes.1, ...), custom_call_target="tpu_custom_call" | custom-call | tf_op jit(solution)/shard_map/pallas_call | solution.py:81
  11.7 0.0 collective-permute-done.3.even_column
  11.7 0.0 collective-permute-done.2.odd_column
  11.8 9.0 %shard_map.164 = (bf16[256,128]{1,0:T(8,128)(2,1)}, bf16[4096,128]{1,0:T(8,128)(2,1)}, f32[256,128]{1,0:T(8,128)S(1)}, bf16[8,176,128]{2,1,0:T(8,128)(2,1)S(1)}) custom-call(s32[1]{0:T(128)S(6)} %copy.18.edge_count, bf16[256,128]{1,0:T(8,128)(2,1)S(1)} %copy-done.1, bf16[96,128]{1,0:T(8,128)(2,1)S(1)} %shard_map.162.own_column, ...), custom_call_target="tpu_custom_call" | custom-call | tf_op jit(solution)/shard_map/pallas_call | solution.py:81
  20.8 16.4 %all_to_all.10.came = bf16[8,176,128]{2,1,0:T(8,128)(2,1)S(1)} all-to-all(bf16[8,176,128]{2,1,0:T(8,128)(2,1)S(1)} %get-tuple-element.36), channel_id=1, replica_groups=mesh['strip'=4,'z'=4,'y'=2] {'strip','y'}, dimensions={0} | all-to-all | bytes 720896 | tf_op jit(solution)/shard_map/all_to_all | solution.py:610
  37.2 0.1 shard_map.165
  37.2 4.1 %collective-permute-start.6 = (bf16[144,128]{1,0:T(8,128)(2,1)S(1)}, bf16[144,128]{1,0:T(8,128)(2,1)S(1)}, u32[]{:S(2)}, u32[]{:S(2)}) collective-permute-start(bf16[144,128]{1,0:T(8,128)(2,1)S(1)} %get-tuple-element.38.refs_0_), channel_id=1, source_target_pairs={{0,6},{2,4},{4,2},{6,0},{1,7},{3,5},{5,3},{7,1},{8,14},{10,12},{12... | collective-permute-start | bytes 110600 | tf_op jit(solution)/shard_map/ppermute | solution.py:615
  41.3 0.0 collective-permute-start.5
  41.3 0.6 %collective-permute-start.4 = (bf16[144,128]{1,0:T(8,128)(2,1)S(1)}, bf16[144,128]{1,0:T(8,128)(2,1)S(1)}, u32[]{:S(2)}, u32[]{:S(2)}) collective-permute-start(bf16[144,128]{1,0:T(8,128)(2,1)S(1)} %get-tuple-element.38.refs_0_), channel_id=1, source_target_pairs={{0,2},{2,0},{4,6},{6,4},{1,3},{3,1},{5,7},{7,5},{8,10},{10,8},{12,... | collective-permute-start | bytes 110600 | tf_op jit(solution)/shard_map/ppermute | solution.py:615
  42.0 1.3 %collective-permute-done.6.refs_3_ = bf16[144,128]{1,0:T(8,128)(2,1)S(1)} collective-permute-done((bf16[144,128]{1,0:T(8,128)(2,1)S(1)}, bf16[144,128]{1,0:T(8,128)(2,1)S(1)}, u32[]{:S(2)}, u32[]{:S(2)}) %collective-permute-start.6) | collective-permute-done | bytes 36896 | tf_op jit(solution)/shard_map/ppermute | solution.py:615
  43.3 2.9 %collective-permute-done.5.refs_2_ = bf16[144,128]{1,0:T(8,128)(2,1)S(1)} collective-permute-done((bf16[144,128]{1,0:T(8,128)(2,1)S(1)}, bf16[144,128]{1,0:T(8,128)(2,1)S(1)}, u32[]{:S(2)}, u32[]{:S(2)}) %collective-permute-start.5) | collective-permute-done | bytes 36896 | tf_op jit(solution)/shard_map/ppermute | solution.py:615
  46.2 0.0 collective-permute-done.4.refs_1_
  46.2 0.1 shard_map.166
  46.2 8.1 %all_to_all.11.came = bf16[8,112,128]{2,1,0:T(8,128)(2,1)S(1)} all-to-all(bf16[8,112,128]{2,1,0:T(8,128)(2,1)S(1)} %get-tuple-element.39), channel_id=1, replica_groups=mesh['strip'=4,'z'=4,'y'=2] {'strip','y'}, dimensions={0} | all-to-all | bytes 458752 | tf_op jit(solution)/shard_map/all_to_all | solution.py:624
  54.3 0.8 %shard_map.167 = (f32[256,128]{1,0:T(8,128)}, f32[384,128]{1,0:T(8,128)}, f32[128,128]{1,0:T(8,128)}, f32[256,128]{1,0:T(8,128)}, f32[128,128]{1,0:T(8,128)}) custom-call(bf16[8,112,128]{2,1,0:T(8,128)(2,1)S(1)} %all_to_all.11.came, f32[32,128]{1,0:T(8,128)S(1)} %get-tuple-element.40.rim_grad, f32[256,128]{1,0:T(8,128)S(1)} %get-tuple-element.41.local_grad), custom_call_target="tpu_custom_call" | custom-call | tf_op jit(solution)/shard_map/pallas_call | solution.py:81
  (11 shorter events, 0.0 us)
Async XLA Ops:
  0.6 11.1 %copy-start.1 = (bf16[256,128]{1,0:T(8,128)(2,1)S(1)}, bf16[256,128]{1,0:T(8,128)(2,1)}, u32[]{:S(2)}) copy-start(bf16[256,128]{1,0:T(8,128)(2,1)} %nodes.1) | copy-start | bytes 196612
  0.6 11.1 %copy-start = (bf16[384,128]{1,0:T(8,128)(2,1)S(1)}, bf16[384,128]{1,0:T(8,128)(2,1)}, u32[]{:S(2)}) copy-start(bf16[384,128]{1,0:T(8,128)(2,1)} %w_edge_in.1) | copy-start | bytes 294916
  0.7 11.1 %copy-start.3 = (bf16[256,128]{1,0:T(8,128)(2,1)S(1)}, bf16[256,128]{1,0:T(8,128)(2,1)}, u32[]{:S(2)}) copy-start(bf16[256,128]{1,0:T(8,128)(2,1)} %node_cot.1) | copy-start | bytes 196612
  0.7 11.1 %copy-start.5 = (bf16[128,128]{1,0:T(8,128)(2,1)S(1)}, bf16[128,128]{1,0:T(8,128)(2,1)}, u32[]{:S(2)}) copy-start(bf16[128,128]{1,0:T(8,128)(2,1)} %w_node_out.1) | copy-start | bytes 98308
  0.7 11.1 %copy-start.2 = (bf16[256,128]{1,0:T(8,128)(2,1)S(1)}, bf16[256,128]{1,0:T(8,128)(2,1)}, u32[]{:S(2)}) copy-start(bf16[256,128]{1,0:T(8,128)(2,1)} %w_node_in.1) | copy-start | bytes 196612
  0.7 11.1 %copy-start.4 = (bf16[128,128]{1,0:T(8,128)(2,1)S(1)}, bf16[128,128]{1,0:T(8,128)(2,1)}, u32[]{:S(2)}) copy-start(bf16[128,128]{1,0:T(8,128)(2,1)} %w_edge_out.1) | copy-start | bytes 98308
  1.5 4.6 %collective-permute-start.1 = (bf16[32,128]{1,0:T(8,128)(2,1)S(1)}, bf16[32,128]{1,0:T(8,128)(2,1)S(1)}, u32[]{:S(2)}, u32[]{:S(2)}) collective-permute-start(bf16[32,128]{1,0:T(8,128)(2,1)S(1)} %slice.4.nodes), channel_id=1, source_target_pairs={{0,1},{1,0},{2,3},{3,2},{4,5},{5,4},{6,7},{7,6},{8,9},{9,8},{10,11... | collective-permute-start | bytes 24584 | tf_op jit(solution)/shard_map/ppermute | solution.py:106
  4.4 1.6 %collective-permute-start = (bf16[32,128]{1,0:T(8,128)(2,1)S(1)}, bf16[32,128]{1,0:T(8,128)(2,1)S(1)}, u32[]{:S(2)}, u32[]{:S(2)}) collective-permute-start(bf16[32,128]{1,0:T(8,128)(2,1)S(1)} %slice.4.nodes), channel_id=1, source_target_pairs={{0,0},{1,2},{2,1},{3,4},{4,3},{5,6},{6,5},{7,7},{8,8},{9,10},{10,9... | collective-permute-start | bytes 24584 | tf_op jit(solution)/shard_map/ppermute | solution.py:105
  6.1 5.6 %collective-permute-start.3 = (bf16[96,128]{1,0:T(8,128)(2,1)S(1)}, bf16[96,128]{1,0:T(8,128)(2,1)S(1)}, u32[]{:S(2)}, u32[]{:S(2)}) collective-permute-start(bf16[96,128]{1,0:T(8,128)(2,1)S(1)} %shard_map.162.own_column), channel_id=1, source_target_pairs={{0,8},{8,0},{16,24},{24,16},{1,9},{9,1},{17,25},{25,17},{2,10},{10... | collective-permute-start | bytes 73736 | tf_op jit(solution)/shard_map/ppermute | solution.py:106
  6.1 5.6 %collective-permute-start.2 = (bf16[96,128]{1,0:T(8,128)(2,1)S(1)}, bf16[96,128]{1,0:T(8,128)(2,1)S(1)}, u32[]{:S(2)}, u32[]{:S(2)}) collective-permute-start(bf16[96,128]{1,0:T(8,128)(2,1)S(1)} %shard_map.162.own_column), channel_id=1, source_target_pairs={{0,0},{8,16},{16,8},{24,24},{1,1},{9,17},{17,9},{25,25},{2,2},{10,... | collective-permute-start | bytes 73736 | tf_op jit(solution)/shard_map/ppermute | solution.py:105
  37.2 6.1 %collective-permute-start.6 = (bf16[144,128]{1,0:T(8,128)(2,1)S(1)}, bf16[144,128]{1,0:T(8,128)(2,1)S(1)}, u32[]{:S(2)}, u32[]{:S(2)}) collective-permute-start(bf16[144,128]{1,0:T(8,128)(2,1)S(1)} %get-tuple-element.38.refs_0_), channel_id=1, source_target_pairs={{0,6},{2,4},{4,2},{6,0},{1,7},{3,5},{5,3},{7,1},{8,14},{10,12},{12... | collective-permute-start | bytes 110600 | tf_op jit(solution)/shard_map/ppermute | solution.py:615
  41.3 4.9 %collective-permute-start.5 = (bf16[144,128]{1,0:T(8,128)(2,1)S(1)}, bf16[144,128]{1,0:T(8,128)(2,1)S(1)}, u32[]{:S(2)}, u32[]{:S(2)}) collective-permute-start(bf16[144,128]{1,0:T(8,128)(2,1)S(1)} %get-tuple-element.38.refs_0_), channel_id=1, source_target_pairs={{0,4},{2,6},{4,0},{6,2},{1,5},{3,7},{5,1},{7,3},{8,12},{10,14},{12... | collective-permute-start | bytes 110600 | tf_op jit(solution)/shard_map/ppermute | solution.py:615
  41.3 4.9 %collective-permute-start.4 = (bf16[144,128]{1,0:T(8,128)(2,1)S(1)}, bf16[144,128]{1,0:T(8,128)(2,1)S(1)}, u32[]{:S(2)}, u32[]{:S(2)}) collective-permute-start(bf16[144,128]{1,0:T(8,128)(2,1)S(1)} %get-tuple-element.38.refs_0_), channel_id=1, source_target_pairs={{0,2},{2,0},{4,6},{6,4},{1,3},{3,1},{5,7},{7,5},{8,10},{10,8},{12,... | collective-permute-start | bytes 110600 | tf_op jit(solution)/shard_map/ppermute | solution.py:615

commit v12 on v11

--- a/solution.py
+++ b/solution.py
@@ -33,18 +33,6 @@
 
 def mm_tn(left, right):
     return lax.dot_general(left, right, (((0,), (0,)), ((), ())), preferred_element_type=F32)
-
-
-def norm_rows(values):
-    centre = values - jnp.mean(values, axis=1, keepdims=True)
-    scale = lax.rsqrt(jnp.mean(centre * centre, axis=1, keepdims=True) + EPS)
-    return (centre * scale, scale)
-
-
-def norm_back(normed, scale, upstream):
-    first = jnp.mean(upstream, axis=1, keepdims=True)
-    second = jnp.mean(upstream * normed, axis=1, keepdims=True)
-    return scale * (upstream - first - normed * second)
 
 
 def silu_and_slope(values):
@@ -196,7 +184,7 @@
         cot_part[rows] = (cot - jnp.mean(cot, axis=1, keepdims=True)).astype(BF16)
         return carry
 
-    lax.fori_loop(0, chunks, one, 0)
+    lax.fori_loop(0, chunks, one, 0, unroll=UNROLL)
 
 
 def layer_kernel(
@@ -239,6 +227,9 @@
     packed,
     kept,
     columns,
+    node_centring,
+    agg_centring,
+    node_cot_c,
     out_sems,
     last_sem,
 ):
@@ -309,6 +300,12 @@
     weight = w_edge_out[...].astype(F32)
     centring[...] = twice(weight - jnp.mean(weight, axis=1, keepdims=True)).astype(BF16)
     back[...] = twice(weight).astype(BF16)
+    weight = w_node_out[...].astype(F32)
+    node_centring[...] = (weight - jnp.mean(weight, axis=1, keepdims=True)).astype(BF16)
+    weight = w_node_in[width:].astype(F32)
+    agg_centring[...] = (weight - jnp.mean(weight, axis=0, keepdims=True)).astype(BF16)
+    cot = node_cot[...].astype(F32)
+    node_cot_c[...] = cot - jnp.mean(cot, axis=1, keepdims=True)
     means[...] = twice(jnp.full((width, width), 1.0 / width, F32)).astype(BF16)
 
     row = lax.broadcasted_iota(jnp.int32, (half, 2 * width), 0)
@@ -351,15 +348,17 @@
     node_pre = mm(joined, w_node_in[...])
     node_act, node_slope = silu_and_slope(node_pre)
     node_act = node_act.astype(BF16)
-    node_unit, node_scale = norm_rows(mm(node_act, w_node_out[...]))
+    centre = mm(node_act, node_centring[...])
+    spare = jnp.mean(centre * centre, axis=1, keepdims=True)
+    along = jnp.mean(node_cot_c[...] * centre, axis=1, keepdims=True)
+    node_scale = lax.rsqrt(spare + EPS)
+    node_unit = centre * node_scale
+    d_outer = node_scale * (node_cot_c[...] - node_unit * (along * node_scale))
+    d_outer = d_outer.astype(BF16)
+    d_pre = (mm_nt(d_outer, w_node_out[...]) * node_slope).astype(BF16)
+    d_agg = mm_nt(d_pre, agg_centring[...]).astype(BF16)
     new_nodes[...] = (nodes[...].astype(F32) + node_unit).astype(BF16)
-    cot = node_cot[...].astype(F32)
-    d_outer = norm_back(node_unit, node_scale, cot).astype(BF16)
-    d_pre = (mm_nt(d_outer, w_node_out[...]) * node_slope).astype(BF16)
-    d_joined = mm_nt(d_pre, w_node_in[...])
-    d_agg = d_joined[:, width:]
-    d_agg = (d_agg - jnp.mean(d_agg, axis=1, keepdims=True)).astype(BF16)
-    agg[...] = cot + d_joined[:, :width]
+    agg[...] = node_cot[...].astype(F32) + mm_nt(d_pre, w_node_in[:width])
     kept[:, : 2 * width] = joined
     kept[:, 2 * width : 3 * width] = node_act
     kept[:, 3 * width : 4 * width] = d_outer
@@ -515,14 +514,6 @@
     subs = zs * ys
     slots = strips * ys
     even, odd = swapped(node_latents[:border], ("z", "y"))
-    (own_column,) = call(
-        column_kernel,
-        [((3 * border, width), BF16)],
-        [edge_count, node_latents[:border], odd, even],
-        [SMEM] + [VMEM] * 3,
-    )
-    even_column, odd_column = swapped(own_column, "strip")
-
     chunk = min(CHUNK, count_e)
     chunks = count_e // chunk
     early = call(
@@ -556,6 +547,15 @@
             SEM((2, chunks)),
         ],
     )
+
+    *early, even, odd = lax.optimization_barrier((*early, even, odd))
+    (own_column,) = call(
+        column_kernel,
+        [((3 * border, width), BF16)],
+        [edge_count, node_latents[:border], odd, even],
+        [SMEM] + [VMEM] * 3,
+    )
+    even_column, odd_column = swapped(own_column, "strip")
 
     share = -(-7 * width // (slots * 16)) * 16
 
@@ -600,6 +600,9 @@
             pltpu.VMEM((slots * share, width), BF16),
             pltpu.VMEM((count_p, 5 * width), BF16),
             pltpu.VMEM((9, border, width), BF16),
+            pltpu.VMEM((width, width), BF16),
+            pltpu.VMEM((width, width), BF16),
+            pltpu.VMEM((count_p, width), F32),
             SEM((chunks,)),
             SEM,
         ],

time: 55.5 us -> 55 us (level)
  starting transfers between devices: 9.01 us -> 11.6 us
  blocking collectives: 24.5 us -> 22.2 us
  Pallas kernels: 14.8 us -> 14.1 us
    ppermute x2, starting transfers between devices: 2.97 us -> 5.87 us  [swapped(): from_even = lax.ppermute(value, axes, even)]
    all_to_all x2, blocking collectives: 24.5 us -> 22.2 us  [shards(): came = lax.all_to_all(parts, PLANE, 0, 0)]
    pallas_call x6, Pallas kernels: 14.8 us -> 14.1 us  [call(): pl.pallas_call(kernel, out_shape=[pltpu.HBM(shape, dtype) if spec is HBM...]
  transfers between devices with their start and end apart: 7 -> 7, of which waited for: 3 -> 3; matrix products, arithmetic and copies ran while one was open for 0% -> 0% of each run, Pallas kernels for 9% -> 8%
where the time goes in v12:
time: 55 us; the launch traced here: 54.7 us
  blocking collectives  22.2 us (40%)
  Pallas kernels  14.1 us (26%)
  starting transfers between devices  11.6 us (21%)
  waiting for transfers between devices  4.42 us (8%)
  between operations  1.44 us (3%)
  local copies, waits for them, and re-layouts  0.81 us (1%)
    all_to_all x2, blocking collectives, shards(): came = lax.all_to_all(parts, PLANE, 0, 0)  22.2 us
    pallas_call x6, Pallas kernels, call(): pl.pallas_call(kernel, out_shape=[pltpu.HBM(shape, dtype) if spec is HBM...  14.1 us
    ppermute x2, starting transfers between devices, swapped(): from_even = lax.ppermute(value, axes, even)  5.87 us
    ppermute x3, starting transfers between devices, shards(): lax.ppermute(message, 'z', [(z, z ^ k) for z in range(zs)])  4.45 us
    ppermute x3, waiting for transfers between devices, shards(): lax.ppermute(message, 'z', [(z, z ^ k) for z in range(zs)])  3.9 us
    ppermute x2, starting transfers between devices, swapped(): from_odd = lax.ppermute(value, axes, odd)  1.31 us
  transfers between devices with their start and end apart: 7, of which 3 were waited for; matrix products, arithmetic and copies ran while one was open for 0% of the time, Pallas kernels for 8%

profile of v12, /device:TPU:0, one launch (start us, length us, event | category | flops | bytes accessed | tf_op | source)
XLA Modules:
  0.0 54.7 jit_solution(15367048087657037042)
XLA Ops:
  0.6 0.0 copy-start.1
  0.6 0.0 copy-start
  0.7 0.8 %slice.4.nodes = bf16[32,128]{1,0:T(8,128)(2,1)S(1)} slice(bf16[256,128]{1,0:T(8,128)(2,1)} %nodes.1), slice={[0:32], [0:128]} | slice | bytes 16384 | tf_op jit(solution)/shard_map/slice | solution.py:555
  1.5 0.6 %collective-permute-start.1 = (bf16[32,128]{1,0:T(8,128)(2,1)S(1)}, bf16[32,128]{1,0:T(8,128)(2,1)S(1)}, u32[]{:S(2)}, u32[]{:S(2)}) collective-permute-start(bf16[32,128]{1,0:T(8,128)(2,1)S(1)} %slice.4.nodes), channel_id=1, source_target_pairs={{0,0},{1,2},{2,1},{3,4},{4,3},{5,6},{6,5},{7,7},{8,8},{9,10},{10,9... | collective-permute-start | bytes 24584 | tf_op jit(solution)/shard_map/ppermute | solution.py:93
  2.1 5.8 %collective-permute-start = (bf16[32,128]{1,0:T(8,128)(2,1)S(1)}, bf16[32,128]{1,0:T(8,128)(2,1)S(1)}, u32[]{:S(2)}, u32[]{:S(2)}) collective-permute-start(bf16[32,128]{1,0:T(8,128)(2,1)S(1)} %slice.4.nodes), channel_id=1, source_target_pairs={{0,1},{1,0},{2,3},{3,2},{4,5},{5,4},{6,7},{7,6},{8,9},{9,8},{10,11... | collective-permute-start | bytes 24584 | tf_op jit(solution)/shard_map/ppermute | solution.py:94
  8.6 4.5 %shard_map.162 = (bf16[4096,128]{1,0:T(8,128)(2,1)S(1)}, bf16[4096,128]{1,0:T(8,128)(2,1)S(1)}, bf16[4096,128]{1,0:T(8,128)(2,1)S(1)}, bf16[4,128,1024]{2,1,0:T(...) custom-call(bf16[256,128]{1,0:T(8,128)(2,1)} %nodes.1, ...), custom_call_target="tpu_custom_call" | custom-call | tf_op jit(solution)/shard_map/pallas_call | solution.py:69
  13.1 0.0 collective-permute-done.1.odd
  13.1 0.0 collective-permute-done.even
  13.1 0.1 collective-permute-start.3
  13.2 0.7 %collective-permute-start.2 = (bf16[96,128]{1,0:T(8,128)(2,1)S(1)}, bf16[96,128]{1,0:T(8,128)(2,1)S(1)}, u32[]{:S(2)}, u32[]{:S(2)}) collective-permute-start(bf16[96,128]{1,0:T(8,128)(2,1)S(1)} %shard_map.163.own_column), channel_id=1, source_target_pairs={{0,0},{8,16},{16,8},{24,24},{1,1},{9,17},{17,9},{25,25},{2,2},{10,... | collective-permute-start | bytes 73736 | tf_op jit(solution)/shard_map/ppermute | solution.py:93
  13.9 0.5 collective-permute-done.3.even_column
  14.4 0.0 collective-permute-done.2.odd_column
  14.4 8.7 %shard_map.164 = (bf16[256,128]{1,0:T(8,128)(2,1)}, bf16[4096,128]{1,0:T(8,128)(2,1)}, f32[256,128]{1,0:T(8,128)S(1)}, bf16[8,176,128]{2,1,0:T(8,128)(2,1)S(1)}) custom-call(s32[1]{0:T(128)S(6)} %copy.18.edge_count, bf16[256,128]{1,0:T(8,128)(2,1)S(1)} %copy-done.1, bf16[96,128]{1,0:T(8,128)(2,1)S(1)} %shard_map.163.own_column, ...), custom_call_target="tpu_custom_call" | custom-call | tf_op jit(solution)/shard_map/pallas_call | solution.py:69
  23.2 14.1 %all_to_all.10.came = bf16[8,176,128]{2,1,0:T(8,128)(2,1)S(1)} all-to-all(bf16[8,176,128]{2,1,0:T(8,128)(2,1)S(1)} %get-tuple-element.54), channel_id=1, replica_groups=mesh['strip'=4,'z'=4,'y'=2] {'strip','y'}, dimensions={0} | all-to-all | bytes 720896 | tf_op jit(solution)/shard_map/all_to_all | solution.py:613
  37.3 0.1 shard_map.165
  37.3 3.5 %collective-permute-start.6 = (bf16[144,128]{1,0:T(8,128)(2,1)S(1)}, bf16[144,128]{1,0:T(8,128)(2,1)S(1)}, u32[]{:S(2)}, u32[]{:S(2)}) collective-permute-start(bf16[144,128]{1,0:T(8,128)(2,1)S(1)} %get-tuple-element.56.refs_0_), channel_id=1, source_target_pairs={{0,6},{2,4},{4,2},{6,0},{1,7},{3,5},{5,3},{7,1},{8,14},{10,12},{12... | collective-permute-start | bytes 110600 | tf_op jit(solution)/shard_map/ppermute | solution.py:618
  40.8 0.0 collective-permute-start.5
  40.8 1.0 %collective-permute-start.4 = (bf16[144,128]{1,0:T(8,128)(2,1)S(1)}, bf16[144,128]{1,0:T(8,128)(2,1)S(1)}, u32[]{:S(2)}, u32[]{:S(2)}) collective-permute-start(bf16[144,128]{1,0:T(8,128)(2,1)S(1)} %get-tuple-element.56.refs_0_), channel_id=1, source_target_pairs={{0,2},{2,0},{4,6},{6,4},{1,3},{3,1},{5,7},{7,5},{8,10},{10,8},{12,... | collective-permute-start | bytes 110600 | tf_op jit(solution)/shard_map/ppermute | solution.py:618
  41.8 1.4 %collective-permute-done.6.refs_3_ = bf16[144,128]{1,0:T(8,128)(2,1)S(1)} collective-permute-done((bf16[144,128]{1,0:T(8,128)(2,1)S(1)}, bf16[144,128]{1,0:T(8,128)(2,1)S(1)}, u32[]{:S(2)}, u32[]{:S(2)}) %collective-permute-start.6) | collective-permute-done | bytes 36896 | tf_op jit(solution)/shard_map/ppermute | solution.py:618
  43.2 2.5 %collective-permute-done.5.refs_2_ = bf16[144,128]{1,0:T(8,128)(2,1)S(1)} collective-permute-done((bf16[144,128]{1,0:T(8,128)(2,1)S(1)}, bf16[144,128]{1,0:T(8,128)(2,1)S(1)}, u32[]{:S(2)}, u32[]{:S(2)}) %collective-permute-start.5) | collective-permute-done | bytes 36896 | tf_op jit(solution)/shard_map/ppermute | solution.py:618
  45.7 0.0 collective-permute-done.4.refs_1_
  45.7 0.1 shard_map.166
  45.8 8.1 %all_to_all.11.came = bf16[8,112,128]{2,1,0:T(8,128)(2,1)S(1)} all-to-all(bf16[8,112,128]{2,1,0:T(8,128)(2,1)S(1)} %get-tuple-element.57), channel_id=1, replica_groups=mesh['strip'=4,'z'=4,'y'=2] {'strip','y'}, dimensions={0} | all-to-all | bytes 458752 | tf_op jit(solution)/shard_map/all_to_all | solution.py:627
  53.8 0.8 %shard_map.167 = (f32[256,128]{1,0:T(8,128)}, f32[384,128]{1,0:T(8,128)}, f32[128,128]{1,0:T(8,128)}, f32[256,128]{1,0:T(8,128)}, f32[128,128]{1,0:T(8,128)}) custom-call(bf16[8,112,128]{2,1,0:T(8,128)(2,1)S(1)} %all_to_all.11.came, f32[32,128]{1,0:T(8,128)S(1)} %get-tuple-element.58.rim_grad, f32[256,128]{1,0:T(8,128)S(1)} %get-tuple-element.59.local_grad), custom_call_target="tpu_custom_call" | custom-call | tf_op jit(solution)/shard_map/pallas_call | solution.py:69
  (11 shorter events, 0.0 us)
Async XLA Ops:
  0.6 13.8 %copy-start.1 = (bf16[256,128]{1,0:T(8,128)(2,1)S(1)}, bf16[256,128]{1,0:T(8,128)(2,1)}, u32[]{:S(2)}) copy-start(bf16[256,128]{1,0:T(8,128)(2,1)} %nodes.1) | copy-start | bytes 196612
  0.6 13.8 %copy-start = (bf16[384,128]{1,0:T(8,128)(2,1)S(1)}, bf16[384,128]{1,0:T(8,128)(2,1)}, u32[]{:S(2)}) copy-start(bf16[384,128]{1,0:T(8,128)(2,1)} %w_edge_in.1) | copy-start | bytes 294916
  0.7 13.7 %copy-start.3 = (bf16[256,128]{1,0:T(8,128)(2,1)S(1)}, bf16[256,128]{1,0:T(8,128)(2,1)}, u32[]{:S(2)}) copy-start(bf16[256,128]{1,0:T(8,128)(2,1)} %node_cot.1) | copy-start | bytes 196612
  0.7 13.7 %copy-start.5 = (bf16[128,128]{1,0:T(8,128)(2,1)S(1)}, bf16[128,128]{1,0:T(8,128)(2,1)}, u32[]{:S(2)}) copy-start(bf16[128,128]{1,0:T(8,128)(2,1)} %w_node_out.1) | copy-start | bytes 98308
  0.7 13.7 %copy-start.2 = (bf16[256,128]{1,0:T(8,128)(2,1)S(1)}, bf16[256,128]{1,0:T(8,128)(2,1)}, u32[]{:S(2)}) copy-start(bf16[256,128]{1,0:T(8,128)(2,1)} %w_node_in.1) | copy-start | bytes 196612
  0.7 13.7 %copy-start.4 = (bf16[128,128]{1,0:T(8,128)(2,1)S(1)}, bf16[128,128]{1,0:T(8,128)(2,1)}, u32[]{:S(2)}) copy-start(bf16[128,128]{1,0:T(8,128)(2,1)} %w_edge_out.1) | copy-start | bytes 98308
  1.5 11.6 %collective-permute-start.1 = (bf16[32,128]{1,0:T(8,128)(2,1)S(1)}, bf16[32,128]{1,0:T(8,128)(2,1)S(1)}, u32[]{:S(2)}, u32[]{:S(2)}) collective-permute-start(bf16[32,128]{1,0:T(8,128)(2,1)S(1)} %slice.4.nodes), channel_id=1, source_target_pairs={{0,0},{1,2},{2,1},{3,4},{4,3},{5,6},{6,5},{7,7},{8,8},{9,10},{10,9... | collective-permute-start | bytes 24584 | tf_op jit(solution)/shard_map/ppermute | solution.py:93
  2.1 11.0 %collective-permute-start = (bf16[32,128]{1,0:T(8,128)(2,1)S(1)}, bf16[32,128]{1,0:T(8,128)(2,1)S(1)}, u32[]{:S(2)}, u32[]{:S(2)}) collective-permute-start(bf16[32,128]{1,0:T(8,128)(2,1)S(1)} %slice.4.nodes), channel_id=1, source_target_pairs={{0,1},{1,0},{2,3},{3,2},{4,5},{5,4},{6,7},{7,6},{8,9},{9,8},{10,11... | collective-permute-start | bytes 24584 | tf_op jit(solution)/shard_map/ppermute | solution.py:94
  13.1 1.3 %collective-permute-start.3 = (bf16[96,128]{1,0:T(8,128)(2,1)S(1)}, bf16[96,128]{1,0:T(8,128)(2,1)S(1)}, u32[]{:S(2)}, u32[]{:S(2)}) collective-permute-start(bf16[96,128]{1,0:T(8,128)(2,1)S(1)} %shard_map.163.own_column), channel_id=1, source_target_pairs={{0,8},{8,0},{16,24},{24,16},{1,9},{9,1},{17,25},{25,17},{2,10},{10... | collective-permute-start | bytes 73736 | tf_op jit(solution)/shard_map/ppermute | solution.py:94
  13.2 1.2 %collective-permute-start.2 = (bf16[96,128]{1,0:T(8,128)(2,1)S(1)}, bf16[96,128]{1,0:T(8,128)(2,1)S(1)}, u32[]{:S(2)}, u32[]{:S(2)}) collective-permute-start(bf16[96,128]{1,0:T(8,128)(2,1)S(1)} %shard_map.163.own_column), channel_id=1, source_target_pairs={{0,0},{8,16},{16,8},{24,24},{1,1},{9,17},{17,9},{25,25},{2,2},{10,... | collective-permute-start | bytes 73736 | tf_op jit(solution)/shard_map/ppermute | solution.py:93
  37.3 5.8 %collective-permute-start.6 = (bf16[144,128]{1,0:T(8,128)(2,1)S(1)}, bf16[144,128]{1,0:T(8,128)(2,1)S(1)}, u32[]{:S(2)}, u32[]{:S(2)}) collective-permute-start(bf16[144,128]{1,0:T(8,128)(2,1)S(1)} %get-tuple-element.56.refs_0_), channel_id=1, source_target_pairs={{0,6},{2,4},{4,2},{6,0},{1,7},{3,5},{5,3},{7,1},{8,14},{10,12},{12... | collective-permute-start | bytes 110600 | tf_op jit(solution)/shard_map/ppermute | solution.py:618
  40.8 4.9 %collective-permute-start.5 = (bf16[144,128]{1,0:T(8,128)(2,1)S(1)}, bf16[144,128]{1,0:T(8,128)(2,1)S(1)}, u32[]{:S(2)}, u32[]{:S(2)}) collective-permute-start(bf16[144,128]{1,0:T(8,128)(2,1)S(1)} %get-tuple-element.56.refs_0_), channel_id=1, source_target_pairs={{0,4},{2,6},{4,0},{6,2},{1,5},{3,7},{5,1},{7,3},{8,12},{10,14},{12... | collective-permute-start | bytes 110600 | tf_op jit(solution)/shard_map/ppermute | solution.py:618
  40.8 4.9 %collective-permute-start.4 = (bf16[144,128]{1,0:T(8,128)(2,1)S(1)}, bf16[144,128]{1,0:T(8,128)(2,1)S(1)}, u32[]{:S(2)}, u32[]{:S(2)}) collective-permute-start(bf16[144,128]{1,0:T(8,128)(2,1)S(1)} %get-tuple-element.56.refs_0_), channel_id=1, source_target_pairs={{0,2},{2,0},{4,6},{6,4},{1,3},{3,1},{5,7},{7,5},{8,10},{10,8},{12,... | collective-permute-start | bytes 110600 | tf_op jit(solution)/shard_map/ppermute | solution.py:618

commit v13 on v12

--- a/solution.py
+++ b/solution.py
@@ -79,11 +79,11 @@
     )(*[in_hbm(value) if spec is HBM else value for value, spec in zip(ins, specs)])
 
 
-def column_kernel(edge_count, nodes, odd, even, out):
-    border = even.shape[0]
+def column_kernel(nodes, odd, even, out):
+    border = out.shape[0] // 3
     out[:border] = nodes[:border]
-    out[border : 2 * border] = even[...]
-    out[2 * border :] = odd[...]
+    out[border : 2 * border] = even[:border]
+    out[2 * border :] = odd[:border]
 
 
 def swapped(value, axes):
@@ -187,6 +187,47 @@
     lax.fori_loop(0, chunks, one, 0, unroll=UNROLL)
 
 
+def prepare_kernel(
+    column,
+    nodes,
+    w_edge_in,
+    w_edge_out,
+    w_node_in,
+    w_node_out,
+    node_cot,
+    near_table,
+    centring,
+    back,
+    means,
+    node_centring,
+    agg_centring,
+    node_cot_c,
+):
+    width = nodes.shape[1]
+
+    def twice(block):
+        zero = jnp.zeros_like(block)
+        return jnp.concatenate(
+            [
+                jnp.concatenate([block, zero], axis=1),
+                jnp.concatenate([zero, block], axis=1),
+            ],
+            axis=0,
+        )
+
+    near_table[...] = mm(nodes[...], w_edge_in[:width]).astype(BF16)
+    weight = w_edge_out[...].astype(F32)
+    centring[...] = twice(weight - jnp.mean(weight, axis=1, keepdims=True)).astype(BF16)
+    back[...] = twice(weight).astype(BF16)
+    weight = w_node_out[...].astype(F32)
+    node_centring[...] = (weight - jnp.mean(weight, axis=1, keepdims=True)).astype(BF16)
+    weight = w_node_in[width:].astype(F32)
+    agg_centring[...] = (weight - jnp.mean(weight, axis=0, keepdims=True)).astype(BF16)
+    cot = node_cot[...].astype(F32)
+    node_cot_c[...] = cot - jnp.mean(cot, axis=1, keepdims=True)
+    means[...] = twice(jnp.full((width, width), 1.0 / width, F32)).astype(BF16)
+
+
 def layer_kernel(
     edge_count,
     nodes,
@@ -205,18 +246,21 @@
     w_node_in,
     w_node_out,
     node_cot,
+    near_table,
+    centring,
+    back,
+    means,
+    node_centring,
+    agg_centring,
+    node_cot_c,
     new_nodes_out,
     new_edges_out,
     local_grad,
     parts,
     new_nodes,
     new_edges,
-    near_rows,
     far_rows,
     tables,
-    centring,
-    back,
-    means,
     hidden,
     slope,
     normed,
@@ -227,9 +271,6 @@
     packed,
     kept,
     columns,
-    node_centring,
-    agg_centring,
-    node_cot_c,
     out_sems,
     last_sem,
 ):
@@ -265,17 +306,6 @@
     def unpaired(value):
         return jnp.concatenate([value[:, :width], value[:, width:]], axis=0)
 
-    def twice(block):
-        zero = jnp.zeros_like(block)
-        return jnp.concatenate(
-            [
-                jnp.concatenate([block, zero], axis=1),
-                jnp.concatenate([zero, block], axis=1),
-            ],
-            axis=0,
-        )
-
-    near_rows[...] = nodes[...]
     for k, column in enumerate((own_column, even_column, odd_column)):
         for part in range(3):
             columns[3 * k + part] = column[part * border : (part + 1) * border]
@@ -295,19 +325,8 @@
             rows = slice(spot * border, (spot + 1) * border)
             far_rows[rows] = columns[3 * column + partner(my_y, d_sub)]
             spot += 1
-    tables[:, :width] = mm(near_rows[...], w_edge_in[:width]).astype(BF16)
+    tables[:, :width] = near_table[...]
     tables[:, width:] = mm(far_rows[...], w_edge_in[:width]).astype(BF16)
-    weight = w_edge_out[...].astype(F32)
-    centring[...] = twice(weight - jnp.mean(weight, axis=1, keepdims=True)).astype(BF16)
-    back[...] = twice(weight).astype(BF16)
-    weight = w_node_out[...].astype(F32)
-    node_centring[...] = (weight - jnp.mean(weight, axis=1, keepdims=True)).astype(BF16)
-    weight = w_node_in[width:].astype(F32)
-    agg_centring[...] = (weight - jnp.mean(weight, axis=0, keepdims=True)).astype(BF16)
-    cot = node_cot[...].astype(F32)
-    node_cot_c[...] = cot - jnp.mean(cot, axis=1, keepdims=True)
-    means[...] = twice(jnp.full((width, width), 1.0 / width, F32)).astype(BF16)
-
     row = lax.broadcasted_iota(jnp.int32, (half, 2 * width), 0)
     lane = lax.broadcasted_iota(jnp.int32, (half, 2 * width), 1)
     edge_row = jnp.where(lane < width, row, row + half)
@@ -403,7 +422,7 @@
     near_sums = sums[count_p : 2 * count_p, :width].astype(BF16)
     far_sums = sums[count_p : 2 * count_p, width:].astype(BF16)
     edge_sums = sums[2 * count_p :, :width] + sums[2 * count_p :, width:]
-    packed[:width] = (mm_tn(near_rows[...], near_sums) + mm_tn(far_rows[...], far_sums)).astype(BF16)
+    packed[:width] = (mm_tn(nodes[...], near_sums) + mm_tn(far_rows[...], far_sums)).astype(BF16)
     packed[width : 2 * width] = mm_tn(nodes[...], recv_sums).astype(BF16)
     packed[4 * width : 6 * width] = mm_tn(kept[:, : 2 * width], kept[:, 4 * width :]).astype(BF16)
     packed[6 * width : 7 * width] = mm_tn(
@@ -513,7 +532,7 @@
     strips, zs, ys = (lax.axis_size(axis) for axis in ALL)
     subs = zs * ys
     slots = strips * ys
-    even, odd = swapped(node_latents[:border], ("z", "y"))
+    even, odd = swapped(node_latents, ("z", "y"))
     chunk = min(CHUNK, count_e)
     chunks = count_e // chunk
     early = call(
@@ -548,17 +567,39 @@
         ],
     )
 
-    *early, even, odd = lax.optimization_barrier((*early, even, odd))
+    *early, odd, even = lax.optimization_barrier((*early, odd, even))
     (own_column,) = call(
         column_kernel,
         [((3 * border, width), BF16)],
-        [edge_count, node_latents[:border], odd, even],
-        [SMEM] + [VMEM] * 3,
+        [node_latents, odd, even],
+        [VMEM] * 3,
     )
     even_column, odd_column = swapped(own_column, "strip")
 
     share = -(-7 * width // (slots * 16)) * 16
 
+    prepared = call(
+        prepare_kernel,
+        [
+            ((count_p, width), BF16),
+            ((2 * width, 2 * width), BF16),
+            ((2 * width, 2 * width), BF16),
+            ((2 * width, 2 * width), BF16),
+            ((width, width), BF16),
+            ((width, width), BF16),
+            ((count_p, width), F32),
+        ],
+        [
+            own_column,
+            node_latents,
+            w_edge_in,
+            w_edge_out,
+            w_node_in,
+            w_node_out,
+            node_cotangent,
+        ],
+        [VMEM] * 7,
+    )
     new_nodes, new_edges, local_grad, parts = call(
         layer_kernel,
         [
@@ -579,17 +620,14 @@
             w_node_in,
             w_node_out,
             node_cotangent,
-        ],
-        [SMEM] + [VMEM] * 16,
+            *prepared,
+        ],
+        [SMEM] + [VMEM] * 23,
         [
             pltpu.VMEM((count_p, width), BF16),
             pltpu.VMEM((count_e, width), BF16),
-            pltpu.VMEM((count_p, width), BF16),
             pltpu.VMEM((8 * border, width), BF16),
             pltpu.VMEM((count_p, 2 * width), BF16),
-            pltpu.VMEM((2 * width, 2 * width), BF16),
-            pltpu.VMEM((2 * width, 2 * width), BF16),
-            pltpu.VMEM((2 * width, 2 * width), BF16),
             pltpu.VMEM((count_e, width), BF16),
             pltpu.VMEM((count_e // 2, 2 * width), F32),
             pltpu.VMEM((count_e // 2, 2 * width), F32),
@@ -600,9 +638,6 @@
             pltpu.VMEM((slots * share, width), BF16),
             pltpu.VMEM((count_p, 5 * width), BF16),
             pltpu.VMEM((9, border, width), BF16),
-            pltpu.VMEM((width, width), BF16),
-            pltpu.VMEM((width, width), BF16),
-            pltpu.VMEM((count_p, width), F32),
             SEM((chunks,)),
             SEM,
         ],

time: 55 us -> 53.5 us (0.973)
  blocking collectives: 22.2 us -> 24.7 us
  starting transfers between devices: 11.6 us -> 9.7 us
  waiting for transfers between devices: 4.42 us -> 2.89 us
  local copies, waits for them, and re-layouts: 0.81 us -> 0.03 us
    ppermute x2, starting transfers between devices: 5.87 us -> 3.1 us  [swapped(): from_even = lax.ppermute(value, axes, even)]
    all_to_all x2, blocking collectives: 22.2 us -> 24.7 us  [shards(): came = lax.all_to_all(parts, PLANE, 0, 0)]
    ppermute x3, waiting for transfers between devices: 3.9 us -> 2.88 us  [shards(): lax.ppermute(message, 'z', [(z, z ^ k) for z in range(zs)])]
    ppermute x2, starting transfers between devices: 1.31 us -> 2.15 us  [swapped(): from_odd = lax.ppermute(value, axes, odd)]
    slice x1 -> x0, local copies, waits for them, and re-layouts: 0.78 us -> none  [shards(): node_latents[:border]]
    pallas_call x6 -> x7, Pallas kernels: 14.1 us -> 14.4 us  [call(): pl.pallas_call(kernel, out_shape=[pltpu.HBM(shape, dtype) if spec is HBM...]
  transfers between devices with their start and end apart: 7 -> 7, of which waited for: 3 -> 3; matrix products, arithmetic and copies ran while one was open for 0% -> 0% of each run, Pallas kernels for 8% -> 9%
where the time goes in v13:
time: 53.5 us; the launch traced here: 53.2 us
  blocking collectives  24.7 us (46%)
  Pallas kernels  14.4 us (27%)
  starting transfers between devices  9.7 us (18%)
  waiting for transfers between devices  2.89 us (5%)
  between operations  1.47 us (3%)
    all_to_all x2, blocking collectives, shards(): came = lax.all_to_all(parts, PLANE, 0, 0)  24.7 us
    pallas_call x7, Pallas kernels, call(): pl.pallas_call(kernel, out_shape=[pltpu.HBM(shape, dtype) if spec is HBM...  14.4 us
    ppermute x3, starting transfers between devices, shards(): lax.ppermute(message, 'z', [(z, z ^ k) for z in range(zs)])  4.45 us
    ppermute x2, starting transfers between devices, swapped(): from_even = lax.ppermute(value, axes, even)  3.1 us
    ppermute x3, waiting for transfers between devices, shards(): lax.ppermute(message, 'z', [(z, z ^ k) for z in range(zs)])  2.88 us
    ppermute x2, starting transfers between devices, swapped(): from_odd = lax.ppermute(value, axes, odd)  2.15 us
  transfers between devices with their start and end apart: 7, of which 3 were waited for; matrix products, arithmetic and copies ran while one was open for 0% of the time, Pallas kernels for 9%

profile of v13, /device:TPU:0, one launch (start us, length us, event | category | flops | bytes accessed | tf_op | source)
XLA Modules:
  0.0 53.2 jit_solution(12141232192908739602)
XLA Ops:
  0.6 0.0 copy-start
  0.6 0.0 copy-start.1
  0.7 3.0 %collective-permute-start.1 = (bf16[256,128]{1,0:T(8,128)(2,1)}, bf16[256,128]{1,0:T(8,128)(2,1)S(1)}, u32[]{:S(2)}, u32[]{:S(2)}) collective-permute-start(bf16[256,128]{1,0:T(8,128)(2,1)} %nodes.5), channel_id=1, source_target_pairs={{0,1},{1,0},{2,3},{3,2},{4,5},{5,4},{6,7},{7,6},{8,9},{9,8},{10,11... | collective-permute-start | bytes 196616 | tf_op jit(solution)/shard_map/ppermute | solution.py:94
  3.7 1.5 %collective-permute-start = (bf16[256,128]{1,0:T(8,128)(2,1)}, bf16[256,128]{1,0:T(8,128)(2,1)S(1)}, u32[]{:S(2)}, u32[]{:S(2)}) collective-permute-start(bf16[256,128]{1,0:T(8,128)(2,1)} %nodes.5), channel_id=1, source_target_pairs={{0,0},{1,2},{2,1},{3,4},{4,3},{5,6},{6,5},{7,7},{8,8},{9,10},{10,9... | collective-permute-start | bytes 196616 | tf_op jit(solution)/shard_map/ppermute | solution.py:93
  5.2 4.5 %shard_map.162 = (bf16[4096,128]{1,0:T(8,128)(2,1)S(1)}, bf16[4096,128]{1,0:T(8,128)(2,1)S(1)}, bf16[4096,128]{1,0:T(8,128)(2,1)S(1)}, bf16[4,128,1024]{2,1,0:T(...) custom-call(bf16[256,128]{1,0:T(8,128)(2,1)} %nodes.5, ...), custom_call_target="tpu_custom_call" | custom-call | tf_op jit(solution)/shard_map/pallas_call | solution.py:69
  9.7 0.0 collective-permute-done.1.even
  9.7 0.0 collective-permute-done.odd
  9.8 0.1 collective-permute-start.3
  9.8 0.7 %collective-permute-start.2 = (bf16[96,128]{1,0:T(8,128)(2,1)S(1)}, bf16[96,128]{1,0:T(8,128)(2,1)S(1)}, u32[]{:S(2)}, u32[]{:S(2)}) collective-permute-start(bf16[96,128]{1,0:T(8,128)(2,1)S(1)} %shard_map.163.column.own_column), channel_id=1, source_target_pairs={{0,0},{8,16},{16,8},{24,24},{1,1},{9,17},{17,9},{25,25},{2,2},{10,... | collective-permute-start | bytes 73736 | tf_op jit(solution)/shard_map/ppermute | solution.py:93
  11.2 0.2 shard_map.164
  11.4 0.0 collective-permute-done.3.even_column
  11.4 0.0 collective-permute-done.2.odd_column
  11.4 8.8 %shard_map.165 = (bf16[256,128]{1,0:T(8,128)(2,1)}, bf16[4096,128]{1,0:T(8,128)(2,1)}, f32[256,128]{1,0:T(8,128)S(1)}, bf16[8,176,128]{2,1,0:T(8,128)(2,1)S(1)}) custom-call(s32[1]{0:T(128)S(6)} %copy.18.edge_count, bf16[256,128]{1,0:T(8,128)(2,1)S(1)} %copy-done, bf16[96,128]{1,0:T(8,128)(2,1)S(1)} %shard_map.163.column.own_column, ...), custom_call_target="tpu_custom_call" | custom-call | tf_op jit(solution)/shard_map/pallas_call | solution.py:69
  20.2 16.6 %all_to_all.10.came = bf16[8,176,128]{2,1,0:T(8,128)(2,1)S(1)} all-to-all(bf16[8,176,128]{2,1,0:T(8,128)(2,1)S(1)} %get-tuple-element.68), channel_id=1, replica_groups=mesh['strip'=4,'z'=4,'y'=2] {'strip','y'}, dimensions={0} | all-to-all | bytes 720896 | tf_op jit(solution)/shard_map/all_to_all | solution.py:648
  36.8 0.1 shard_map.166
  36.9 1.9 %collective-permute-start.6 = (bf16[144,128]{1,0:T(8,128)(2,1)S(1)}, bf16[144,128]{1,0:T(8,128)(2,1)S(1)}, u32[]{:S(2)}, u32[]{:S(2)}) collective-permute-start(bf16[144,128]{1,0:T(8,128)(2,1)S(1)} %get-tuple-element.70.refs_0_), channel_id=1, source_target_pairs={{0,6},{2,4},{4,2},{6,0},{1,7},{3,5},{5,3},{7,1},{8,14},{10,12},{12... | collective-permute-start | bytes 110600 | tf_op jit(solution)/shard_map/ppermute | solution.py:653
  38.8 1.2 %collective-permute-start.5 = (bf16[144,128]{1,0:T(8,128)(2,1)S(1)}, bf16[144,128]{1,0:T(8,128)(2,1)S(1)}, u32[]{:S(2)}, u32[]{:S(2)}) collective-permute-start(bf16[144,128]{1,0:T(8,128)(2,1)S(1)} %get-tuple-element.70.refs_0_), channel_id=1, source_target_pairs={{0,4},{2,6},{4,0},{6,2},{1,5},{3,7},{5,1},{7,3},{8,12},{10,14},{12... | collective-permute-start | bytes 110600 | tf_op jit(solution)/shard_map/ppermute | solution.py:653
  40.0 1.3 %collective-permute-start.4 = (bf16[144,128]{1,0:T(8,128)(2,1)S(1)}, bf16[144,128]{1,0:T(8,128)(2,1)S(1)}, u32[]{:S(2)}, u32[]{:S(2)}) collective-permute-start(bf16[144,128]{1,0:T(8,128)(2,1)S(1)} %get-tuple-element.70.refs_0_), channel_id=1, source_target_pairs={{0,2},{2,0},{4,6},{6,4},{1,3},{3,1},{5,7},{7,5},{8,10},{10,8},{12,... | collective-permute-start | bytes 110600 | tf_op jit(solution)/shard_map/ppermute | solution.py:653
  41.3 1.5 %collective-permute-done.6.refs_3_ = bf16[144,128]{1,0:T(8,128)(2,1)S(1)} collective-permute-done((bf16[144,128]{1,0:T(8,128)(2,1)S(1)}, bf16[144,128]{1,0:T(8,128)(2,1)S(1)}, u32[]{:S(2)}, u32[]{:S(2)}) %collective-permute-start.6) | collective-permute-done | bytes 36896 | tf_op jit(solution)/shard_map/ppermute | solution.py:653
  42.8 1.0 %collective-permute-done.5.refs_2_ = bf16[144,128]{1,0:T(8,128)(2,1)S(1)} collective-permute-done((bf16[144,128]{1,0:T(8,128)(2,1)S(1)}, bf16[144,128]{1,0:T(8,128)(2,1)S(1)}, u32[]{:S(2)}, u32[]{:S(2)}) %collective-permute-start.5) | collective-permute-done | bytes 36896 | tf_op jit(solution)/shard_map/ppermute | solution.py:653
  43.9 0.4 collective-permute-done.4.refs_1_
  44.2 0.1 shard_map.167
  44.3 8.1 %all_to_all.11.came = bf16[8,112,128]{2,1,0:T(8,128)(2,1)S(1)} all-to-all(bf16[8,112,128]{2,1,0:T(8,128)(2,1)S(1)} %get-tuple-element.71), channel_id=1, replica_groups=mesh['strip'=4,'z'=4,'y'=2] {'strip','y'}, dimensions={0} | all-to-all | bytes 458752 | tf_op jit(solution)/shard_map/all_to_all | solution.py:662
  52.4 0.8 %shard_map.168 = (f32[256,128]{1,0:T(8,128)}, f32[384,128]{1,0:T(8,128)}, f32[128,128]{1,0:T(8,128)}, f32[256,128]{1,0:T(8,128)}, f32[128,128]{1,0:T(8,128)}) custom-call(bf16[8,112,128]{2,1,0:T(8,128)(2,1)S(1)} %all_to_all.11.came, f32[32,128]{1,0:T(8,128)S(1)} %get-tuple-element.72.rim_grad, f32[256,128]{1,0:T(8,128)S(1)} %get-tuple-element.73.local_grad), custom_call_target="tpu_custom_call" | custom-call | tf_op jit(solution)/shard_map/pallas_call | solution.py:69
  (11 shorter events, 0.0 us)
Async XLA Ops:
  0.6 9.1 %copy-start = (bf16[256,128]{1,0:T(8,128)(2,1)S(1)}, bf16[256,128]{1,0:T(8,128)(2,1)}, u32[]{:S(2)}) copy-start(bf16[256,128]{1,0:T(8,128)(2,1)} %nodes.5) | copy-start | bytes 196612
  0.6 10.5 %copy-start.1 = (bf16[384,128]{1,0:T(8,128)(2,1)S(1)}, bf16[384,128]{1,0:T(8,128)(2,1)}, u32[]{:S(2)}) copy-start(bf16[384,128]{1,0:T(8,128)(2,1)} %w_edge_in.3) | copy-start | bytes 294916
  0.7 10.5 %copy-start.3 = (bf16[256,128]{1,0:T(8,128)(2,1)S(1)}, bf16[256,128]{1,0:T(8,128)(2,1)}, u32[]{:S(2)}) copy-start(bf16[256,128]{1,0:T(8,128)(2,1)} %node_cot.3) | copy-start | bytes 196612
  0.7 10.5 %copy-start.5 = (bf16[128,128]{1,0:T(8,128)(2,1)S(1)}, bf16[128,128]{1,0:T(8,128)(2,1)}, u32[]{:S(2)}) copy-start(bf16[128,128]{1,0:T(8,128)(2,1)} %w_node_out.3) | copy-start | bytes 98308
  0.7 10.5 %copy-start.2 = (bf16[256,128]{1,0:T(8,128)(2,1)S(1)}, bf16[256,128]{1,0:T(8,128)(2,1)}, u32[]{:S(2)}) copy-start(bf16[256,128]{1,0:T(8,128)(2,1)} %w_node_in.3) | copy-start | bytes 196612
  0.7 10.5 %copy-start.4 = (bf16[128,128]{1,0:T(8,128)(2,1)S(1)}, bf16[128,128]{1,0:T(8,128)(2,1)}, u32[]{:S(2)}) copy-start(bf16[128,128]{1,0:T(8,128)(2,1)} %w_edge_out.3) | copy-start | bytes 98308
  0.7 9.0 %collective-permute-start.1 = (bf16[256,128]{1,0:T(8,128)(2,1)}, bf16[256,128]{1,0:T(8,128)(2,1)S(1)}, u32[]{:S(2)}, u32[]{:S(2)}) collective-permute-start(bf16[256,128]{1,0:T(8,128)(2,1)} %nodes.5), channel_id=1, source_target_pairs={{0,1},{1,0},{2,3},{3,2},{4,5},{5,4},{6,7},{7,6},{8,9},{9,8},{10,11... | collective-permute-start | bytes 196616 | tf_op jit(solution)/shard_map/ppermute | solution.py:94
  3.7 6.0 %collective-permute-start = (bf16[256,128]{1,0:T(8,128)(2,1)}, bf16[256,128]{1,0:T(8,128)(2,1)S(1)}, u32[]{:S(2)}, u32[]{:S(2)}) collective-permute-start(bf16[256,128]{1,0:T(8,128)(2,1)} %nodes.5), channel_id=1, source_target_pairs={{0,0},{1,2},{2,1},{3,4},{4,3},{5,6},{6,5},{7,7},{8,8},{9,10},{10,9... | collective-permute-start | bytes 196616 | tf_op jit(solution)/shard_map/ppermute | solution.py:93
  9.8 1.6 %collective-permute-start.3 = (bf16[96,128]{1,0:T(8,128)(2,1)S(1)}, bf16[96,128]{1,0:T(8,128)(2,1)S(1)}, u32[]{:S(2)}, u32[]{:S(2)}) collective-permute-start(bf16[96,128]{1,0:T(8,128)(2,1)S(1)} %shard_map.163.column.own_column), channel_id=1, source_target_pairs={{0,8},{8,0},{16,24},{24,16},{1,9},{9,1},{17,25},{25,17},{2,10},{10... | collective-permute-start | bytes 73736 | tf_op jit(solution)/shard_map/ppermute | solution.py:94
  9.8 1.5 %collective-permute-start.2 = (bf16[96,128]{1,0:T(8,128)(2,1)S(1)}, bf16[96,128]{1,0:T(8,128)(2,1)S(1)}, u32[]{:S(2)}, u32[]{:S(2)}) collective-permute-start(bf16[96,128]{1,0:T(8,128)(2,1)S(1)} %shard_map.163.column.own_column), channel_id=1, source_target_pairs={{0,0},{8,16},{16,8},{24,24},{1,1},{9,17},{17,9},{25,25},{2,2},{10,... | collective-permute-start | bytes 73736 | tf_op jit(solution)/shard_map/ppermute | solution.py:93
  36.9 5.9 %collective-permute-start.6 = (bf16[144,128]{1,0:T(8,128)(2,1)S(1)}, bf16[144,128]{1,0:T(8,128)(2,1)S(1)}, u32[]{:S(2)}, u32[]{:S(2)}) collective-permute-start(bf16[144,128]{1,0:T(8,128)(2,1)S(1)} %get-tuple-element.70.refs_0_), channel_id=1, source_target_pairs={{0,6},{2,4},{4,2},{6,0},{1,7},{3,5},{5,3},{7,1},{8,14},{10,12},{12... | collective-permute-start | bytes 110600 | tf_op jit(solution)/shard_map/ppermute | solution.py:653
  38.8 5.0 %collective-permute-start.5 = (bf16[144,128]{1,0:T(8,128)(2,1)S(1)}, bf16[144,128]{1,0:T(8,128)(2,1)S(1)}, u32[]{:S(2)}, u32[]{:S(2)}) collective-permute-start(bf16[144,128]{1,0:T(8,128)(2,1)S(1)} %get-tuple-element.70.refs_0_), channel_id=1, source_target_pairs={{0,4},{2,6},{4,0},{6,2},{1,5},{3,7},{5,1},{7,3},{8,12},{10,14},{12... | collective-permute-start | bytes 110600 | tf_op jit(solution)/shard_map/ppermute | solution.py:653
  40.0 4.2 %collective-permute-start.4 = (bf16[144,128]{1,0:T(8,128)(2,1)S(1)}, bf16[144,128]{1,0:T(8,128)(2,1)S(1)}, u32[]{:S(2)}, u32[]{:S(2)}) collective-permute-start(bf16[144,128]{1,0:T(8,128)(2,1)S(1)} %get-tuple-element.70.refs_0_), channel_id=1, source_target_pairs={{0,2},{2,0},{4,6},{6,4},{1,3},{3,1},{5,7},{7,5},{8,10},{10,8},{12,... | collective-permute-start | bytes 110600 | tf_op jit(solution)/shard_map/ppermute | solution.py:653

commit v14 on v13

--- a/solution.py
+++ b/solution.py
@@ -11,7 +11,7 @@
 
 EPS = 1e-05
 CHUNK = 1024
-SPLIT = 2
+SPLIT = 4
 UNROLL = 4
 PLANE = ("strip", "y")
 ALL = ("strip", "z", "y")
@@ -232,8 +232,8 @@
     edge_count,
     nodes,
     own_column,
+    even_column,
     odd_column,
-    even_column,
     edges,
     send_codes,
     recv_codes,
@@ -612,8 +612,8 @@
             edge_count,
             node_latents,
             own_column,
+            even_column,
             odd_column,
-            even_column,
             *early,
             w_edge_in,
             w_edge_out,

time: 53.5 us -> 55.4 us (1.036)
  blocking collectives: 24.7 us -> 21.8 us
  starting transfers between devices: 9.7 us -> 12.5 us
  Pallas kernels: 14.4 us -> 16.4 us
    all_to_all x2, blocking collectives: 24.7 us -> 21.8 us  [shards(): came = lax.all_to_all(parts, PLANE, 0, 0)]
    ppermute x2, starting transfers between devices: 3.1 us -> 5.95 us  [swapped(): from_even = lax.ppermute(value, axes, even)]
    pallas_call x7, Pallas kernels: 14.4 us -> 16.4 us  [call(): pl.pallas_call(kernel, out_shape=[pltpu.HBM(shape, dtype) if spec is HBM...]
  transfers between devices with their start and end apart: 7 -> 7, of which waited for: 3 -> 3; matrix products, arithmetic and copies ran while one was open for 0% -> 0% of each run, Pallas kernels for 9% -> 8%
where the time goes in v14:
time: 55.4 us; the launch traced here: 55.1 us
  blocking collectives  21.8 us (39%)
  Pallas kernels  16.4 us (30%)
  starting transfers between devices  12.5 us (23%)
  waiting for transfers between devices  2.89 us (5%)
  between operations  1.46 us (3%)
    all_to_all x2, blocking collectives, shards(): came = lax.all_to_all(parts, PLANE, 0, 0)  21.8 us
    pallas_call x7, Pallas kernels, call(): pl.pallas_call(kernel, out_shape=[pltpu.HBM(shape, dtype) if spec is HBM...  16.4 us
    ppermute x2, starting transfers between devices, swapped(): from_even = lax.ppermute(value, axes, even)  5.95 us
    ppermute x3, starting transfers between devices, shards(): lax.ppermute(message, 'z', [(z, z ^ k) for z in range(zs)])  4.45 us
    ppermute x3, waiting for transfers between devices, shards(): lax.ppermute(message, 'z', [(z, z ^ k) for z in range(zs)])  2.88 us
    ppermute x2, starting transfers between devices, swapped(): from_odd = lax.ppermute(value, axes, odd)  2.15 us
  transfers between devices with their start and end apart: 7, of which 3 were waited for; matrix products, arithmetic and copies ran while one was open for 0% of the time, Pallas kernels for 8%

profile of v14, /device:TPU:0, one launch (start us, length us, event | category | flops | bytes accessed | tf_op | source)
XLA Modules:
  0.0 55.1 jit_solution(12421126032872532643)
XLA Ops:
  0.6 0.0 copy-start
  0.6 0.0 copy-start.1
  0.7 3.0 %collective-permute-start.1 = (bf16[256,128]{1,0:T(8,128)(2,1)}, bf16[256,128]{1,0:T(8,128)(2,1)S(1)}, u32[]{:S(2)}, u32[]{:S(2)}) collective-permute-start(bf16[256,128]{1,0:T(8,128)(2,1)} %nodes.5), channel_id=1, source_target_pairs={{0,1},{1,0},{2,3},{3,2},{4,5},{5,4},{6,7},{7,6},{8,9},{9,8},{10,11... | collective-permute-start | bytes 196616 | tf_op jit(solution)/shard_map/ppermute | solution.py:94
  3.7 1.5 %collective-permute-start = (bf16[256,128]{1,0:T(8,128)(2,1)}, bf16[256,128]{1,0:T(8,128)(2,1)S(1)}, u32[]{:S(2)}, u32[]{:S(2)}) collective-permute-start(bf16[256,128]{1,0:T(8,128)(2,1)} %nodes.5), channel_id=1, source_target_pairs={{0,0},{1,2},{2,1},{3,4},{4,3},{5,6},{6,5},{7,7},{8,8},{9,10},{10,9... | collective-permute-start | bytes 196616 | tf_op jit(solution)/shard_map/ppermute | solution.py:93
  5.2 4.5 %shard_map.162 = (bf16[4096,128]{1,0:T(8,128)(2,1)S(1)}, bf16[4096,128]{1,0:T(8,128)(2,1)S(1)}, bf16[4096,128]{1,0:T(8,128)(2,1)S(1)}, bf16[4,128,1024]{2,1,0:T(...) custom-call(bf16[256,128]{1,0:T(8,128)(2,1)} %nodes.5, ...), custom_call_target="tpu_custom_call" | custom-call | tf_op jit(solution)/shard_map/pallas_call | solution.py:69
  9.7 0.0 collective-permute-done.1.even
  9.7 0.0 collective-permute-done.odd
  9.8 0.7 %collective-permute-start.3 = (bf16[96,128]{1,0:T(8,128)(2,1)S(1)}, bf16[96,128]{1,0:T(8,128)(2,1)S(1)}, u32[]{:S(2)}, u32[]{:S(2)}) collective-permute-start(bf16[96,128]{1,0:T(8,128)(2,1)S(1)} %shard_map.163.column.own_column), channel_id=1, source_target_pairs={{0,0},{8,16},{16,8},{24,24},{1,1},{9,17},{17,9},{25,25},{2,2},{10,... | collective-permute-start | bytes 73736 | tf_op jit(solution)/shard_map/ppermute | solution.py:93
  10.4 2.9 %collective-permute-start.2 = (bf16[96,128]{1,0:T(8,128)(2,1)S(1)}, bf16[96,128]{1,0:T(8,128)(2,1)S(1)}, u32[]{:S(2)}, u32[]{:S(2)}) collective-permute-start(bf16[96,128]{1,0:T(8,128)(2,1)S(1)} %shard_map.163.column.own_column), channel_id=1, source_target_pairs={{0,8},{8,0},{16,24},{24,16},{1,9},{9,1},{17,25},{25,17},{2,10},{10... | collective-permute-start | bytes 73736 | tf_op jit(solution)/shard_map/ppermute | solution.py:94
  14.0 0.2 shard_map.164
  14.2 0.0 collective-permute-done.3.odd_column
  14.2 0.0 collective-permute-done.2.even_column
  14.2 10.8 %shard_map.165 = (bf16[256,128]{1,0:T(8,128)(2,1)}, bf16[4096,128]{1,0:T(8,128)(2,1)}, f32[256,128]{1,0:T(8,128)S(1)}, bf16[8,176,128]{2,1,0:T(8,128)(2,1)S(1)}) custom-call(s32[1]{0:T(128)S(6)} %copy.18.edge_count, bf16[256,128]{1,0:T(8,128)(2,1)S(1)} %copy-done, bf16[96,128]{1,0:T(8,128)(2,1)S(1)} %shard_map.163.column.own_column, ...), custom_call_target="tpu_custom_call" | custom-call | tf_op jit(solution)/shard_map/pallas_call | solution.py:69
  25.1 13.7 %all_to_all.10.came = bf16[8,176,128]{2,1,0:T(8,128)(2,1)S(1)} all-to-all(bf16[8,176,128]{2,1,0:T(8,128)(2,1)S(1)} %get-tuple-element.68), channel_id=1, replica_groups=mesh['strip'=4,'z'=4,'y'=2] {'strip','y'}, dimensions={0} | all-to-all | bytes 720896 | tf_op jit(solution)/shard_map/all_to_all | solution.py:648
  38.8 0.1 shard_map.166
  38.8 2.0 %collective-permute-start.6 = (bf16[144,128]{1,0:T(8,128)(2,1)S(1)}, bf16[144,128]{1,0:T(8,128)(2,1)S(1)}, u32[]{:S(2)}, u32[]{:S(2)}) collective-permute-start(bf16[144,128]{1,0:T(8,128)(2,1)S(1)} %get-tuple-element.70.refs_0_), channel_id=1, source_target_pairs={{0,6},{2,4},{4,2},{6,0},{1,7},{3,5},{5,3},{7,1},{8,14},{10,12},{12... | collective-permute-start | bytes 110600 | tf_op jit(solution)/shard_map/ppermute | solution.py:653
  40.8 1.1 %collective-permute-start.5 = (bf16[144,128]{1,0:T(8,128)(2,1)S(1)}, bf16[144,128]{1,0:T(8,128)(2,1)S(1)}, u32[]{:S(2)}, u32[]{:S(2)}) collective-permute-start(bf16[144,128]{1,0:T(8,128)(2,1)S(1)} %get-tuple-element.70.refs_0_), channel_id=1, source_target_pairs={{0,4},{2,6},{4,0},{6,2},{1,5},{3,7},{5,1},{7,3},{8,12},{10,14},{12... | collective-permute-start | bytes 110600 | tf_op jit(solution)/shard_map/ppermute | solution.py:653
  41.9 1.3 %collective-permute-start.4 = (bf16[144,128]{1,0:T(8,128)(2,1)S(1)}, bf16[144,128]{1,0:T(8,128)(2,1)S(1)}, u32[]{:S(2)}, u32[]{:S(2)}) collective-permute-start(bf16[144,128]{1,0:T(8,128)(2,1)S(1)} %get-tuple-element.70.refs_0_), channel_id=1, source_target_pairs={{0,2},{2,0},{4,6},{6,4},{1,3},{3,1},{5,7},{7,5},{8,10},{10,8},{12,... | collective-permute-start | bytes 110600 | tf_op jit(solution)/shard_map/ppermute | solution.py:653
  43.3 1.4 %collective-permute-done.6.refs_3_ = bf16[144,128]{1,0:T(8,128)(2,1)S(1)} collective-permute-done((bf16[144,128]{1,0:T(8,128)(2,1)S(1)}, bf16[144,128]{1,0:T(8,128)(2,1)S(1)}, u32[]{:S(2)}, u32[]{:S(2)}) %collective-permute-start.6) | collective-permute-done | bytes 36896 | tf_op jit(solution)/shard_map/ppermute | solution.py:653
  44.7 1.1 %collective-permute-done.5.refs_2_ = bf16[144,128]{1,0:T(8,128)(2,1)S(1)} collective-permute-done((bf16[144,128]{1,0:T(8,128)(2,1)S(1)}, bf16[144,128]{1,0:T(8,128)(2,1)S(1)}, u32[]{:S(2)}, u32[]{:S(2)}) %collective-permute-start.5) | collective-permute-done | bytes 36896 | tf_op jit(solution)/shard_map/ppermute | solution.py:653
  45.8 0.4 collective-permute-done.4.refs_1_
  46.2 0.1 shard_map.167
  46.2 8.1 %all_to_all.11.came = bf16[8,112,128]{2,1,0:T(8,128)(2,1)S(1)} all-to-all(bf16[8,112,128]{2,1,0:T(8,128)(2,1)S(1)} %get-tuple-element.71), channel_id=1, replica_groups=mesh['strip'=4,'z'=4,'y'=2] {'strip','y'}, dimensions={0} | all-to-all | bytes 458752 | tf_op jit(solution)/shard_map/all_to_all | solution.py:662
  54.3 0.8 %shard_map.168 = (f32[256,128]{1,0:T(8,128)}, f32[384,128]{1,0:T(8,128)}, f32[128,128]{1,0:T(8,128)}, f32[256,128]{1,0:T(8,128)}, f32[128,128]{1,0:T(8,128)}) custom-call(bf16[8,112,128]{2,1,0:T(8,128)(2,1)S(1)} %all_to_all.11.came, f32[32,128]{1,0:T(8,128)S(1)} %get-tuple-element.72.rim_grad, f32[256,128]{1,0:T(8,128)S(1)} %get-tuple-element.73.local_grad), custom_call_target="tpu_custom_call" | custom-call | tf_op jit(solution)/shard_map/pallas_call | solution.py:69
  (11 shorter events, 0.0 us)
Async XLA Ops:
  0.6 9.1 %copy-start = (bf16[256,128]{1,0:T(8,128)(2,1)S(1)}, bf16[256,128]{1,0:T(8,128)(2,1)}, u32[]{:S(2)}) copy-start(bf16[256,128]{1,0:T(8,128)(2,1)} %nodes.5) | copy-start | bytes 196612
  0.6 13.4 %copy-start.1 = (bf16[384,128]{1,0:T(8,128)(2,1)S(1)}, bf16[384,128]{1,0:T(8,128)(2,1)}, u32[]{:S(2)}) copy-start(bf16[384,128]{1,0:T(8,128)(2,1)} %w_edge_in.3) | copy-start | bytes 294916
  0.7 13.4 %copy-start.3 = (bf16[256,128]{1,0:T(8,128)(2,1)S(1)}, bf16[256,128]{1,0:T(8,128)(2,1)}, u32[]{:S(2)}) copy-start(bf16[256,128]{1,0:T(8,128)(2,1)} %node_cot.3) | copy-start | bytes 196612
  0.7 13.4 %copy-start.5 = (bf16[128,128]{1,0:T(8,128)(2,1)S(1)}, bf16[128,128]{1,0:T(8,128)(2,1)}, u32[]{:S(2)}) copy-start(bf16[128,128]{1,0:T(8,128)(2,1)} %w_node_out.3) | copy-start | bytes 98308
  0.7 13.4 %copy-start.2 = (bf16[256,128]{1,0:T(8,128)(2,1)S(1)}, bf16[256,128]{1,0:T(8,128)(2,1)}, u32[]{:S(2)}) copy-start(bf16[256,128]{1,0:T(8,128)(2,1)} %w_node_in.3) | copy-start | bytes 196612
  0.7 13.4 %copy-start.4 = (bf16[128,128]{1,0:T(8,128)(2,1)S(1)}, bf16[128,128]{1,0:T(8,128)(2,1)}, u32[]{:S(2)}) copy-start(bf16[128,128]{1,0:T(8,128)(2,1)} %w_edge_out.3) | copy-start | bytes 98308
  0.7 9.0 %collective-permute-start.1 = (bf16[256,128]{1,0:T(8,128)(2,1)}, bf16[256,128]{1,0:T(8,128)(2,1)S(1)}, u32[]{:S(2)}, u32[]{:S(2)}) collective-permute-start(bf16[256,128]{1,0:T(8,128)(2,1)} %nodes.5), channel_id=1, source_target_pairs={{0,1},{1,0},{2,3},{3,2},{4,5},{5,4},{6,7},{7,6},{8,9},{9,8},{10,11... | collective-permute-start | bytes 196616 | tf_op jit(solution)/shard_map/ppermute | solution.py:94
  3.7 6.0 %collective-permute-start = (bf16[256,128]{1,0:T(8,128)(2,1)}, bf16[256,128]{1,0:T(8,128)(2,1)S(1)}, u32[]{:S(2)}, u32[]{:S(2)}) collective-permute-start(bf16[256,128]{1,0:T(8,128)(2,1)} %nodes.5), channel_id=1, source_target_pairs={{0,0},{1,2},{2,1},{3,4},{4,3},{5,6},{6,5},{7,7},{8,8},{9,10},{10,9... | collective-permute-start | bytes 196616 | tf_op jit(solution)/shard_map/ppermute | solution.py:93
  9.8 4.5 %collective-permute-start.3 = (bf16[96,128]{1,0:T(8,128)(2,1)S(1)}, bf16[96,128]{1,0:T(8,128)(2,1)S(1)}, u32[]{:S(2)}, u32[]{:S(2)}) collective-permute-start(bf16[96,128]{1,0:T(8,128)(2,1)S(1)} %shard_map.163.column.own_column), channel_id=1, source_target_pairs={{0,0},{8,16},{16,8},{24,24},{1,1},{9,17},{17,9},{25,25},{2,2},{10,... | collective-permute-start | bytes 73736 | tf_op jit(solution)/shard_map/ppermute | solution.py:93
  10.4 3.8 %collective-permute-start.2 = (bf16[96,128]{1,0:T(8,128)(2,1)S(1)}, bf16[96,128]{1,0:T(8,128)(2,1)S(1)}, u32[]{:S(2)}, u32[]{:S(2)}) collective-permute-start(bf16[96,128]{1,0:T(8,128)(2,1)S(1)} %shard_map.163.column.own_column), channel_id=1, source_target_pairs={{0,8},{8,0},{16,24},{24,16},{1,9},{9,1},{17,25},{25,17},{2,10},{10... | collective-permute-start | bytes 73736 | tf_op jit(solution)/shard_map/ppermute | solution.py:94
  38.8 5.9 %collective-permute-start.6 = (bf16[144,128]{1,0:T(8,128)(2,1)S(1)}, bf16[144,128]{1,0:T(8,128)(2,1)S(1)}, u32[]{:S(2)}, u32[]{:S(2)}) collective-permute-start(bf16[144,128]{1,0:T(8,128)(2,1)S(1)} %get-tuple-element.70.refs_0_), channel_id=1, source_target_pairs={{0,6},{2,4},{4,2},{6,0},{1,7},{3,5},{5,3},{7,1},{8,14},{10,12},{12... | collective-permute-start | bytes 110600 | tf_op jit(solution)/shard_map/ppermute | solution.py:653
  40.8 5.0 %collective-permute-start.5 = (bf16[144,128]{1,0:T(8,128)(2,1)S(1)}, bf16[144,128]{1,0:T(8,128)(2,1)S(1)}, u32[]{:S(2)}, u32[]{:S(2)}) collective-permute-start(bf16[144,128]{1,0:T(8,128)(2,1)S(1)} %get-tuple-element.70.refs_0_), channel_id=1, source_target_pairs={{0,4},{2,6},{4,0},{6,2},{1,5},{3,7},{5,1},{7,3},{8,12},{10,14},{12... | collective-permute-start | bytes 110600 | tf_op jit(solution)/shard_map/ppermute | solution.py:653
  41.9 4.2 %collective-permute-start.4 = (bf16[144,128]{1,0:T(8,128)(2,1)S(1)}, bf16[144,128]{1,0:T(8,128)(2,1)S(1)}, u32[]{:S(2)}, u32[]{:S(2)}) collective-permute-start(bf16[144,128]{1,0:T(8,128)(2,1)S(1)} %get-tuple-element.70.refs_0_), channel_id=1, source_target_pairs={{0,2},{2,0},{4,6},{6,4},{1,3},{3,1},{5,7},{7,5},{8,10},{10,8},{12,... | collective-permute-start | bytes 110600 | tf_op jit(solution)/shard_map/ppermute | solution.py:653

commit v15 on v14

--- a/solution.py
+++ b/solution.py
@@ -11,7 +11,7 @@
 
 EPS = 1e-05
 CHUNK = 1024
-SPLIT = 4
+SPLIT = 1
 UNROLL = 4
 PLANE = ("strip", "y")
 ALL = ("strip", "z", "y")

time: 55.4 us -> 52.7 us (0.951)
  Pallas kernels: 16.4 us -> 13.7 us
    pallas_call x7, Pallas kernels: 16.4 us -> 13.7 us  [call(): pl.pallas_call(kernel, out_shape=[pltpu.HBM(shape, dtype) if spec is HBM...]
  transfers between devices with their start and end apart: 7 -> 7, of which waited for: 3 -> 3; matrix products, arithmetic and copies ran while one was open for 0% -> 0% of each run, Pallas kernels for 8% -> 9%
where the time goes in v15:
time: 52.7 us; the launch traced here: 52.5 us
  blocking collectives  21.8 us (41%)
  Pallas kernels  13.7 us (26%)
  starting transfers between devices  12.5 us (24%)
  waiting for transfers between devices  2.89 us (5%)
  between operations  1.46 us (3%)
    all_to_all x2, blocking collectives, shards(): came = lax.all_to_all(parts, PLANE, 0, 0)  21.8 us
    pallas_call x7, Pallas kernels, call(): pl.pallas_call(kernel, out_shape=[pltpu.HBM(shape, dtype) if spec is HBM...  13.7 us
    ppermute x2, starting transfers between devices, swapped(): from_even = lax.ppermute(value, axes, even)  5.95 us
    ppermute x3, starting transfers between devices, shards(): lax.ppermute(message, 'z', [(z, z ^ k) for z in range(zs)])  4.45 us
    ppermute x3, waiting for transfers between devices, shards(): lax.ppermute(message, 'z', [(z, z ^ k) for z in range(zs)])  2.88 us
    ppermute x2, starting transfers between devices, swapped(): from_odd = lax.ppermute(value, axes, odd)  2.15 us
  transfers between devices with their start and end apart: 7, of which 3 were waited for; matrix products, arithmetic and copies ran while one was open for 0% of the time, Pallas kernels for 9%

profile of v15, /device:TPU:0, one launch (start us, length us, event | category | flops | bytes accessed | tf_op | source)
XLA Modules:
  0.0 52.5 jit_solution(15398552604868143654)
XLA Ops:
  0.6 0.0 copy-start
  0.6 0.0 copy-start.1
  0.7 3.0 %collective-permute-start.1 = (bf16[256,128]{1,0:T(8,128)(2,1)}, bf16[256,128]{1,0:T(8,128)(2,1)S(1)}, u32[]{:S(2)}, u32[]{:S(2)}) collective-permute-start(bf16[256,128]{1,0:T(8,128)(2,1)} %nodes.5), channel_id=1, source_target_pairs={{0,1},{1,0},{2,3},{3,2},{4,5},{5,4},{6,7},{7,6},{8,9},{9,8},{10,11... | collective-permute-start | bytes 196616 | tf_op jit(solution)/shard_map/ppermute | solution.py:94
  3.7 1.5 %collective-permute-start = (bf16[256,128]{1,0:T(8,128)(2,1)}, bf16[256,128]{1,0:T(8,128)(2,1)S(1)}, u32[]{:S(2)}, u32[]{:S(2)}) collective-permute-start(bf16[256,128]{1,0:T(8,128)(2,1)} %nodes.5), channel_id=1, source_target_pairs={{0,0},{1,2},{2,1},{3,4},{4,3},{5,6},{6,5},{7,7},{8,8},{9,10},{10,9... | collective-permute-start | bytes 196616 | tf_op jit(solution)/shard_map/ppermute | solution.py:93
  5.2 4.5 %shard_map.162 = (bf16[4096,128]{1,0:T(8,128)(2,1)S(1)}, bf16[4096,128]{1,0:T(8,128)(2,1)S(1)}, bf16[4096,128]{1,0:T(8,128)(2,1)S(1)}, bf16[4,128,1024]{2,1,0:T(...) custom-call(bf16[256,128]{1,0:T(8,128)(2,1)} %nodes.5, ...), custom_call_target="tpu_custom_call" | custom-call | tf_op jit(solution)/shard_map/pallas_call | solution.py:69
  9.7 0.0 collective-permute-done.1.even
  9.7 0.0 collective-permute-done.odd
  9.8 0.7 %collective-permute-start.3 = (bf16[96,128]{1,0:T(8,128)(2,1)S(1)}, bf16[96,128]{1,0:T(8,128)(2,1)S(1)}, u32[]{:S(2)}, u32[]{:S(2)}) collective-permute-start(bf16[96,128]{1,0:T(8,128)(2,1)S(1)} %shard_map.163.column.own_column), channel_id=1, source_target_pairs={{0,0},{8,16},{16,8},{24,24},{1,1},{9,17},{17,9},{25,25},{2,2},{10,... | collective-permute-start | bytes 73736 | tf_op jit(solution)/shard_map/ppermute | solution.py:93
  10.4 2.9 %collective-permute-start.2 = (bf16[96,128]{1,0:T(8,128)(2,1)S(1)}, bf16[96,128]{1,0:T(8,128)(2,1)S(1)}, u32[]{:S(2)}, u32[]{:S(2)}) collective-permute-start(bf16[96,128]{1,0:T(8,128)(2,1)S(1)} %shard_map.163.column.own_column), channel_id=1, source_target_pairs={{0,8},{8,0},{16,24},{24,16},{1,9},{9,1},{17,25},{25,17},{2,10},{10... | collective-permute-start | bytes 73736 | tf_op jit(solution)/shard_map/ppermute | solution.py:94
  14.0 0.2 shard_map.164
  14.2 0.0 collective-permute-done.3.odd_column
  14.2 0.0 collective-permute-done.2.even_column
  14.2 8.1 %shard_map.165 = (bf16[256,128]{1,0:T(8,128)(2,1)}, bf16[4096,128]{1,0:T(8,128)(2,1)}, f32[256,128]{1,0:T(8,128)S(1)}, bf16[8,176,128]{2,1,0:T(8,128)(2,1)S(1)}) custom-call(s32[1]{0:T(128)S(6)} %copy.18.edge_count, bf16[256,128]{1,0:T(8,128)(2,1)S(1)} %copy-done, bf16[96,128]{1,0:T(8,128)(2,1)S(1)} %shard_map.163.column.own_column, ...), custom_call_target="tpu_custom_call" | custom-call | tf_op jit(solution)/shard_map/pallas_call | solution.py:69
  22.4 13.7 %all_to_all.10.came = bf16[8,176,128]{2,1,0:T(8,128)(2,1)S(1)} all-to-all(bf16[8,176,128]{2,1,0:T(8,128)(2,1)S(1)} %get-tuple-element.68), channel_id=1, replica_groups=mesh['strip'=4,'z'=4,'y'=2] {'strip','y'}, dimensions={0} | all-to-all | bytes 720896 | tf_op jit(solution)/shard_map/all_to_all | solution.py:648
  36.1 0.1 shard_map.166
  36.2 2.0 %collective-permute-start.6 = (bf16[144,128]{1,0:T(8,128)(2,1)S(1)}, bf16[144,128]{1,0:T(8,128)(2,1)S(1)}, u32[]{:S(2)}, u32[]{:S(2)}) collective-permute-start(bf16[144,128]{1,0:T(8,128)(2,1)S(1)} %get-tuple-element.70.refs_0_), channel_id=1, source_target_pairs={{0,6},{2,4},{4,2},{6,0},{1,7},{3,5},{5,3},{7,1},{8,14},{10,12},{12... | collective-permute-start | bytes 110600 | tf_op jit(solution)/shard_map/ppermute | solution.py:653
  38.2 1.1 %collective-permute-start.5 = (bf16[144,128]{1,0:T(8,128)(2,1)S(1)}, bf16[144,128]{1,0:T(8,128)(2,1)S(1)}, u32[]{:S(2)}, u32[]{:S(2)}) collective-permute-start(bf16[144,128]{1,0:T(8,128)(2,1)S(1)} %get-tuple-element.70.refs_0_), channel_id=1, source_target_pairs={{0,4},{2,6},{4,0},{6,2},{1,5},{3,7},{5,1},{7,3},{8,12},{10,14},{12... | collective-permute-start | bytes 110600 | tf_op jit(solution)/shard_map/ppermute | solution.py:653
  39.3 1.3 %collective-permute-start.4 = (bf16[144,128]{1,0:T(8,128)(2,1)S(1)}, bf16[144,128]{1,0:T(8,128)(2,1)S(1)}, u32[]{:S(2)}, u32[]{:S(2)}) collective-permute-start(bf16[144,128]{1,0:T(8,128)(2,1)S(1)} %get-tuple-element.70.refs_0_), channel_id=1, source_target_pairs={{0,2},{2,0},{4,6},{6,4},{1,3},{3,1},{5,7},{7,5},{8,10},{10,8},{12,... | collective-permute-start | bytes 110600 | tf_op jit(solution)/shard_map/ppermute | solution.py:653
  40.6 1.4 %collective-permute-done.6.refs_3_ = bf16[144,128]{1,0:T(8,128)(2,1)S(1)} collective-permute-done((bf16[144,128]{1,0:T(8,128)(2,1)S(1)}, bf16[144,128]{1,0:T(8,128)(2,1)S(1)}, u32[]{:S(2)}, u32[]{:S(2)}) %collective-permute-start.6) | collective-permute-done | bytes 36896 | tf_op jit(solution)/shard_map/ppermute | solution.py:653
  42.1 1.1 %collective-permute-done.5.refs_2_ = bf16[144,128]{1,0:T(8,128)(2,1)S(1)} collective-permute-done((bf16[144,128]{1,0:T(8,128)(2,1)S(1)}, bf16[144,128]{1,0:T(8,128)(2,1)S(1)}, u32[]{:S(2)}, u32[]{:S(2)}) %collective-permute-start.5) | collective-permute-done | bytes 36896 | tf_op jit(solution)/shard_map/ppermute | solution.py:653
  43.1 0.4 collective-permute-done.4.refs_1_
  43.5 0.1 shard_map.167
  43.6 8.1 %all_to_all.11.came = bf16[8,112,128]{2,1,0:T(8,128)(2,1)S(1)} all-to-all(bf16[8,112,128]{2,1,0:T(8,128)(2,1)S(1)} %get-tuple-element.71), channel_id=1, replica_groups=mesh['strip'=4,'z'=4,'y'=2] {'strip','y'}, dimensions={0} | all-to-all | bytes 458752 | tf_op jit(solution)/shard_map/all_to_all | solution.py:662
  51.6 0.8 %shard_map.168 = (f32[256,128]{1,0:T(8,128)}, f32[384,128]{1,0:T(8,128)}, f32[128,128]{1,0:T(8,128)}, f32[256,128]{1,0:T(8,128)}, f32[128,128]{1,0:T(8,128)}) custom-call(bf16[8,112,128]{2,1,0:T(8,128)(2,1)S(1)} %all_to_all.11.came, f32[32,128]{1,0:T(8,128)S(1)} %get-tuple-element.72.rim_grad, f32[256,128]{1,0:T(8,128)S(1)} %get-tuple-element.73.local_grad), custom_call_target="tpu_custom_call" | custom-call | tf_op jit(solution)/shard_map/pallas_call | solution.py:69
  (11 shorter events, 0.0 us)
Async XLA Ops:
  0.6 9.1 %copy-start = (bf16[256,128]{1,0:T(8,128)(2,1)S(1)}, bf16[256,128]{1,0:T(8,128)(2,1)}, u32[]{:S(2)}) copy-start(bf16[256,128]{1,0:T(8,128)(2,1)} %nodes.5) | copy-start | bytes 196612
  0.6 13.4 %copy-start.1 = (bf16[384,128]{1,0:T(8,128)(2,1)S(1)}, bf16[384,128]{1,0:T(8,128)(2,1)}, u32[]{:S(2)}) copy-start(bf16[384,128]{1,0:T(8,128)(2,1)} %w_edge_in.3) | copy-start | bytes 294916
  0.7 13.4 %copy-start.3 = (bf16[256,128]{1,0:T(8,128)(2,1)S(1)}, bf16[256,128]{1,0:T(8,128)(2,1)}, u32[]{:S(2)}) copy-start(bf16[256,128]{1,0:T(8,128)(2,1)} %node_cot.3) | copy-start | bytes 196612
  0.7 13.4 %copy-start.5 = (bf16[128,128]{1,0:T(8,128)(2,1)S(1)}, bf16[128,128]{1,0:T(8,128)(2,1)}, u32[]{:S(2)}) copy-start(bf16[128,128]{1,0:T(8,128)(2,1)} %w_node_out.3) | copy-start | bytes 98308
  0.7 13.4 %copy-start.2 = (bf16[256,128]{1,0:T(8,128)(2,1)S(1)}, bf16[256,128]{1,0:T(8,128)(2,1)}, u32[]{:S(2)}) copy-start(bf16[256,128]{1,0:T(8,128)(2,1)} %w_node_in.3) | copy-start | bytes 196612
  0.7 13.4 %copy-start.4 = (bf16[128,128]{1,0:T(8,128)(2,1)S(1)}, bf16[128,128]{1,0:T(8,128)(2,1)}, u32[]{:S(2)}) copy-start(bf16[128,128]{1,0:T(8,128)(2,1)} %w_edge_out.3) | copy-start | bytes 98308
  0.7 9.0 %collective-permute-start.1 = (bf16[256,128]{1,0:T(8,128)(2,1)}, bf16[256,128]{1,0:T(8,128)(2,1)S(1)}, u32[]{:S(2)}, u32[]{:S(2)}) collective-permute-start(bf16[256,128]{1,0:T(8,128)(2,1)} %nodes.5), channel_id=1, source_target_pairs={{0,1},{1,0},{2,3},{3,2},{4,5},{5,4},{6,7},{7,6},{8,9},{9,8},{10,11... | collective-permute-start | bytes 196616 | tf_op jit(solution)/shard_map/ppermute | solution.py:94
  3.7 6.0 %collective-permute-start = (bf16[256,128]{1,0:T(8,128)(2,1)}, bf16[256,128]{1,0:T(8,128)(2,1)S(1)}, u32[]{:S(2)}, u32[]{:S(2)}) collective-permute-start(bf16[256,128]{1,0:T(8,128)(2,1)} %nodes.5), channel_id=1, source_target_pairs={{0,0},{1,2},{2,1},{3,4},{4,3},{5,6},{6,5},{7,7},{8,8},{9,10},{10,9... | collective-permute-start | bytes 196616 | tf_op jit(solution)/shard_map/ppermute | solution.py:93
  9.8 4.5 %collective-permute-start.3 = (bf16[96,128]{1,0:T(8,128)(2,1)S(1)}, bf16[96,128]{1,0:T(8,128)(2,1)S(1)}, u32[]{:S(2)}, u32[]{:S(2)}) collective-permute-start(bf16[96,128]{1,0:T(8,128)(2,1)S(1)} %shard_map.163.column.own_column), channel_id=1, source_target_pairs={{0,0},{8,16},{16,8},{24,24},{1,1},{9,17},{17,9},{25,25},{2,2},{10,... | collective-permute-start | bytes 73736 | tf_op jit(solution)/shard_map/ppermute | solution.py:93
  10.4 3.8 %collective-permute-start.2 = (bf16[96,128]{1,0:T(8,128)(2,1)S(1)}, bf16[96,128]{1,0:T(8,128)(2,1)S(1)}, u32[]{:S(2)}, u32[]{:S(2)}) collective-permute-start(bf16[96,128]{1,0:T(8,128)(2,1)S(1)} %shard_map.163.column.own_column), channel_id=1, source_target_pairs={{0,8},{8,0},{16,24},{24,16},{1,9},{9,1},{17,25},{25,17},{2,10},{10... | collective-permute-start | bytes 73736 | tf_op jit(solution)/shard_map/ppermute | solution.py:94
  36.2 5.9 %collective-permute-start.6 = (bf16[144,128]{1,0:T(8,128)(2,1)S(1)}, bf16[144,128]{1,0:T(8,128)(2,1)S(1)}, u32[]{:S(2)}, u32[]{:S(2)}) collective-permute-start(bf16[144,128]{1,0:T(8,128)(2,1)S(1)} %get-tuple-element.70.refs_0_), channel_id=1, source_target_pairs={{0,6},{2,4},{4,2},{6,0},{1,7},{3,5},{5,3},{7,1},{8,14},{10,12},{12... | collective-permute-start | bytes 110600 | tf_op jit(solution)/shard_map/ppermute | solution.py:653
  38.2 5.0 %collective-permute-start.5 = (bf16[144,128]{1,0:T(8,128)(2,1)S(1)}, bf16[144,128]{1,0:T(8,128)(2,1)S(1)}, u32[]{:S(2)}, u32[]{:S(2)}) collective-permute-start(bf16[144,128]{1,0:T(8,128)(2,1)S(1)} %get-tuple-element.70.refs_0_), channel_id=1, source_target_pairs={{0,4},{2,6},{4,0},{6,2},{1,5},{3,7},{5,1},{7,3},{8,12},{10,14},{12... | collective-permute-start | bytes 110600 | tf_op jit(solution)/shard_map/ppermute | solution.py:653
  39.3 4.2 %collective-permute-start.4 = (bf16[144,128]{1,0:T(8,128)(2,1)S(1)}, bf16[144,128]{1,0:T(8,128)(2,1)S(1)}, u32[]{:S(2)}, u32[]{:S(2)}) collective-permute-start(bf16[144,128]{1,0:T(8,128)(2,1)S(1)} %get-tuple-element.70.refs_0_), channel_id=1, source_target_pairs={{0,2},{2,0},{4,6},{6,4},{1,3},{3,1},{5,7},{7,5},{8,10},{10,8},{12,... | collective-permute-start | bytes 110600 | tf_op jit(solution)/shard_map/ppermute | solution.py:653

commit v16 on v15

--- a/solution.py
+++ b/solution.py
@@ -10,9 +10,9 @@
 from jax.sharding import PartitionSpec as P
 
 EPS = 1e-05
-CHUNK = 1024
+CHUNK = 2048
 SPLIT = 1
-UNROLL = 4
+UNROLL = 2
 PLANE = ("strip", "y")
 ALL = ("strip", "z", "y")
 F32 = jnp.float32

time: 52.7 us -> 52.6 us (level)
  transfers between devices with their start and end apart: 7 -> 7, of which waited for: 3 -> 3; matrix products, arithmetic and copies ran while one was open for 0% -> 0% of each run, Pallas kernels for 9% -> 8%
where the time goes in v16:
time: 52.6 us; the launch traced here: 52.3 us
  blocking collectives  21.8 us (41%)
  Pallas kernels  13.5 us (26%)
  starting transfers between devices  12.6 us (24%)
  waiting for transfers between devices  3.01 us (6%)
  between operations  1.46 us (3%)
    all_to_all x2, blocking collectives, shards(): came = lax.all_to_all(parts, PLANE, 0, 0)  21.8 us
    pallas_call x7, Pallas kernels, call(): pl.pallas_call(kernel, out_shape=[pltpu.HBM(shape, dtype) if spec is HBM...  13.5 us
    ppermute x2, starting transfers between devices, swapped(): from_even = lax.ppermute(value, axes, even)  5.95 us
    ppermute x3, starting transfers between devices, shards(): lax.ppermute(message, 'z', [(z, z ^ k) for z in range(zs)])  4.45 us
    ppermute x3, waiting for transfers between devices, shards(): lax.ppermute(message, 'z', [(z, z ^ k) for z in range(zs)])  3 us
    ppermute x2, starting transfers between devices, swapped(): from_odd = lax.ppermute(value, axes, odd)  2.15 us
  transfers between devices with their start and end apart: 7, of which 3 were waited for; matrix products, arithmetic and copies ran while one was open for 0% of the time, Pallas kernels for 8%

profile of v16, /device:TPU:0, one launch (start us, length us, event | category | flops | bytes accessed | tf_op | source)
XLA Modules:
  0.0 52.3 jit_solution(10226893735077242793)
XLA Ops:
  0.6 0.0 copy-start
  0.6 0.0 copy-start.1
  0.7 3.0 %collective-permute-start.1 = (bf16[256,128]{1,0:T(8,128)(2,1)}, bf16[256,128]{1,0:T(8,128)(2,1)S(1)}, u32[]{:S(2)}, u32[]{:S(2)}) collective-permute-start(bf16[256,128]{1,0:T(8,128)(2,1)} %nodes.5), channel_id=1, source_target_pairs={{0,1},{1,0},{2,3},{3,2},{4,5},{5,4},{6,7},{7,6},{8,9},{9,8},{10,11... | collective-permute-start | bytes 196616 | tf_op jit(solution)/shard_map/ppermute | solution.py:94
  3.7 1.5 %collective-permute-start = (bf16[256,128]{1,0:T(8,128)(2,1)}, bf16[256,128]{1,0:T(8,128)(2,1)S(1)}, u32[]{:S(2)}, u32[]{:S(2)}) collective-permute-start(bf16[256,128]{1,0:T(8,128)(2,1)} %nodes.5), channel_id=1, source_target_pairs={{0,0},{1,2},{2,1},{3,4},{4,3},{5,6},{6,5},{7,7},{8,8},{9,10},{10,9... | collective-permute-start | bytes 196616 | tf_op jit(solution)/shard_map/ppermute | solution.py:93
  5.2 4.1 %shard_map.162 = (bf16[4096,128]{1,0:T(8,128)(2,1)S(1)}, bf16[4096,128]{1,0:T(8,128)(2,1)S(1)}, bf16[4096,128]{1,0:T(8,128)(2,1)S(1)}, bf16[2,128,2048]{2,1,0:T(...) custom-call(bf16[256,128]{1,0:T(8,128)(2,1)} %nodes.5, ...), custom_call_target="tpu_custom_call" | custom-call | tf_op jit(solution)/shard_map/pallas_call | solution.py:69
  9.4 0.0 collective-permute-done.1.even
  9.4 0.0 collective-permute-done.odd
  9.4 0.7 %collective-permute-start.3 = (bf16[96,128]{1,0:T(8,128)(2,1)S(1)}, bf16[96,128]{1,0:T(8,128)(2,1)S(1)}, u32[]{:S(2)}, u32[]{:S(2)}) collective-permute-start(bf16[96,128]{1,0:T(8,128)(2,1)S(1)} %shard_map.163.column.own_column), channel_id=1, source_target_pairs={{0,0},{8,16},{16,8},{24,24},{1,1},{9,17},{17,9},{25,25},{2,2},{10,... | collective-permute-start | bytes 73736 | tf_op jit(solution)/shard_map/ppermute | solution.py:93
  10.1 2.9 %collective-permute-start.2 = (bf16[96,128]{1,0:T(8,128)(2,1)S(1)}, bf16[96,128]{1,0:T(8,128)(2,1)S(1)}, u32[]{:S(2)}, u32[]{:S(2)}) collective-permute-start(bf16[96,128]{1,0:T(8,128)(2,1)S(1)} %shard_map.163.column.own_column), channel_id=1, source_target_pairs={{0,8},{8,0},{16,24},{24,16},{1,9},{9,1},{17,25},{25,17},{2,10},{10... | collective-permute-start | bytes 73736 | tf_op jit(solution)/shard_map/ppermute | solution.py:94
  13.7 0.2 shard_map.164
  13.9 0.0 collective-permute-done.3.odd_column
  13.9 0.0 collective-permute-done.2.even_column
  13.9 8.2 %shard_map.165 = (bf16[256,128]{1,0:T(8,128)(2,1)}, bf16[4096,128]{1,0:T(8,128)(2,1)}, f32[256,128]{1,0:T(8,128)S(1)}, bf16[8,176,128]{2,1,0:T(8,128)(2,1)S(1)}) custom-call(s32[1]{0:T(128)S(6)} %copy.18.edge_count, bf16[256,128]{1,0:T(8,128)(2,1)S(1)} %copy-done, bf16[96,128]{1,0:T(8,128)(2,1)S(1)} %shard_map.163.column.own_column, ...), custom_call_target="tpu_custom_call" | custom-call | tf_op jit(solution)/shard_map/pallas_call | solution.py:69
  22.1 13.7 %all_to_all.10.came = bf16[8,176,128]{2,1,0:T(8,128)(2,1)S(1)} all-to-all(bf16[8,176,128]{2,1,0:T(8,128)(2,1)S(1)} %get-tuple-element.68), channel_id=1, replica_groups=mesh['strip'=4,'z'=4,'y'=2] {'strip','y'}, dimensions={0} | all-to-all | bytes 720896 | tf_op jit(solution)/shard_map/all_to_all | solution.py:648
  35.9 0.1 shard_map.166
  35.9 2.3 %collective-permute-start.6 = (bf16[144,128]{1,0:T(8,128)(2,1)S(1)}, bf16[144,128]{1,0:T(8,128)(2,1)S(1)}, u32[]{:S(2)}, u32[]{:S(2)}) collective-permute-start(bf16[144,128]{1,0:T(8,128)(2,1)S(1)} %get-tuple-element.70.refs_0_), channel_id=1, source_target_pairs={{0,6},{2,4},{4,2},{6,0},{1,7},{3,5},{5,3},{7,1},{8,14},{10,12},{12... | collective-permute-start | bytes 110600 | tf_op jit(solution)/shard_map/ppermute | solution.py:653
  38.3 0.8 %collective-permute-start.5 = (bf16[144,128]{1,0:T(8,128)(2,1)S(1)}, bf16[144,128]{1,0:T(8,128)(2,1)S(1)}, u32[]{:S(2)}, u32[]{:S(2)}) collective-permute-start(bf16[144,128]{1,0:T(8,128)(2,1)S(1)} %get-tuple-element.70.refs_0_), channel_id=1, source_target_pairs={{0,4},{2,6},{4,0},{6,2},{1,5},{3,7},{5,1},{7,3},{8,12},{10,14},{12... | collective-permute-start | bytes 110600 | tf_op jit(solution)/shard_map/ppermute | solution.py:653
  39.0 1.3 %collective-permute-start.4 = (bf16[144,128]{1,0:T(8,128)(2,1)S(1)}, bf16[144,128]{1,0:T(8,128)(2,1)S(1)}, u32[]{:S(2)}, u32[]{:S(2)}) collective-permute-start(bf16[144,128]{1,0:T(8,128)(2,1)S(1)} %get-tuple-element.70.refs_0_), channel_id=1, source_target_pairs={{0,2},{2,0},{4,6},{6,4},{1,3},{3,1},{5,7},{7,5},{8,10},{10,8},{12,... | collective-permute-start | bytes 110600 | tf_op jit(solution)/shard_map/ppermute | solution.py:653
  40.4 1.5 %collective-permute-done.6.refs_3_ = bf16[144,128]{1,0:T(8,128)(2,1)S(1)} collective-permute-done((bf16[144,128]{1,0:T(8,128)(2,1)S(1)}, bf16[144,128]{1,0:T(8,128)(2,1)S(1)}, u32[]{:S(2)}, u32[]{:S(2)}) %collective-permute-start.6) | collective-permute-done | bytes 36896 | tf_op jit(solution)/shard_map/ppermute | solution.py:653
  41.8 1.4 %collective-permute-done.5.refs_2_ = bf16[144,128]{1,0:T(8,128)(2,1)S(1)} collective-permute-done((bf16[144,128]{1,0:T(8,128)(2,1)S(1)}, bf16[144,128]{1,0:T(8,128)(2,1)S(1)}, u32[]{:S(2)}, u32[]{:S(2)}) %collective-permute-start.5) | collective-permute-done | bytes 36896 | tf_op jit(solution)/shard_map/ppermute | solution.py:653
  43.2 0.2 collective-permute-done.4.refs_1_
  43.4 0.1 shard_map.167
  43.4 8.1 %all_to_all.11.came = bf16[8,112,128]{2,1,0:T(8,128)(2,1)S(1)} all-to-all(bf16[8,112,128]{2,1,0:T(8,128)(2,1)S(1)} %get-tuple-element.71), channel_id=1, replica_groups=mesh['strip'=4,'z'=4,'y'=2] {'strip','y'}, dimensions={0} | all-to-all | bytes 458752 | tf_op jit(solution)/shard_map/all_to_all | solution.py:662
  51.5 0.8 %shard_map.168 = (f32[256,128]{1,0:T(8,128)}, f32[384,128]{1,0:T(8,128)}, f32[128,128]{1,0:T(8,128)}, f32[256,128]{1,0:T(8,128)}, f32[128,128]{1,0:T(8,128)}) custom-call(bf16[8,112,128]{2,1,0:T(8,128)(2,1)S(1)} %all_to_all.11.came, f32[32,128]{1,0:T(8,128)S(1)} %get-tuple-element.72.rim_grad, f32[256,128]{1,0:T(8,128)S(1)} %get-tuple-element.73.local_grad), custom_call_target="tpu_custom_call" | custom-call | tf_op jit(solution)/shard_map/pallas_call | solution.py:69
  (11 shorter events, 0.0 us)
Async XLA Ops:
  0.6 8.7 %copy-start = (bf16[256,128]{1,0:T(8,128)(2,1)S(1)}, bf16[256,128]{1,0:T(8,128)(2,1)}, u32[]{:S(2)}) copy-start(bf16[256,128]{1,0:T(8,128)(2,1)} %nodes.5) | copy-start | bytes 196612
  0.6 13.0 %copy-start.1 = (bf16[384,128]{1,0:T(8,128)(2,1)S(1)}, bf16[384,128]{1,0:T(8,128)(2,1)}, u32[]{:S(2)}) copy-start(bf16[384,128]{1,0:T(8,128)(2,1)} %w_edge_in.3) | copy-start | bytes 294916
  0.7 13.0 %copy-start.3 = (bf16[256,128]{1,0:T(8,128)(2,1)S(1)}, bf16[256,128]{1,0:T(8,128)(2,1)}, u32[]{:S(2)}) copy-start(bf16[256,128]{1,0:T(8,128)(2,1)} %node_cot.3) | copy-start | bytes 196612
  0.7 13.0 %copy-start.5 = (bf16[128,128]{1,0:T(8,128)(2,1)S(1)}, bf16[128,128]{1,0:T(8,128)(2,1)}, u32[]{:S(2)}) copy-start(bf16[128,128]{1,0:T(8,128)(2,1)} %w_node_out.3) | copy-start | bytes 98308
  0.7 13.0 %copy-start.2 = (bf16[256,128]{1,0:T(8,128)(2,1)S(1)}, bf16[256,128]{1,0:T(8,128)(2,1)}, u32[]{:S(2)}) copy-start(bf16[256,128]{1,0:T(8,128)(2,1)} %w_node_in.3) | copy-start | bytes 196612
  0.7 13.0 %copy-start.4 = (bf16[128,128]{1,0:T(8,128)(2,1)S(1)}, bf16[128,128]{1,0:T(8,128)(2,1)}, u32[]{:S(2)}) copy-start(bf16[128,128]{1,0:T(8,128)(2,1)} %w_edge_out.3) | copy-start | bytes 98308
  0.7 8.7 %collective-permute-start.1 = (bf16[256,128]{1,0:T(8,128)(2,1)}, bf16[256,128]{1,0:T(8,128)(2,1)S(1)}, u32[]{:S(2)}, u32[]{:S(2)}) collective-permute-start(bf16[256,128]{1,0:T(8,128)(2,1)} %nodes.5), channel_id=1, source_target_pairs={{0,1},{1,0},{2,3},{3,2},{4,5},{5,4},{6,7},{7,6},{8,9},{9,8},{10,11... | collective-permute-start | bytes 196616 | tf_op jit(solution)/shard_map/ppermute | solution.py:94
  3.7 5.6 %collective-permute-start = (bf16[256,128]{1,0:T(8,128)(2,1)}, bf16[256,128]{1,0:T(8,128)(2,1)S(1)}, u32[]{:S(2)}, u32[]{:S(2)}) collective-permute-start(bf16[256,128]{1,0:T(8,128)(2,1)} %nodes.5), channel_id=1, source_target_pairs={{0,0},{1,2},{2,1},{3,4},{4,3},{5,6},{6,5},{7,7},{8,8},{9,10},{10,9... | collective-permute-start | bytes 196616 | tf_op jit(solution)/shard_map/ppermute | solution.py:93
  9.4 4.5 %collective-permute-start.3 = (bf16[96,128]{1,0:T(8,128)(2,1)S(1)}, bf16[96,128]{1,0:T(8,128)(2,1)S(1)}, u32[]{:S(2)}, u32[]{:S(2)}) collective-permute-start(bf16[96,128]{1,0:T(8,128)(2,1)S(1)} %shard_map.163.column.own_column), channel_id=1, source_target_pairs={{0,0},{8,16},{16,8},{24,24},{1,1},{9,17},{17,9},{25,25},{2,2},{10,... | collective-permute-start | bytes 73736 | tf_op jit(solution)/shard_map/ppermute | solution.py:93
  10.1 3.8 %collective-permute-start.2 = (bf16[96,128]{1,0:T(8,128)(2,1)S(1)}, bf16[96,128]{1,0:T(8,128)(2,1)S(1)}, u32[]{:S(2)}, u32[]{:S(2)}) collective-permute-start(bf16[96,128]{1,0:T(8,128)(2,1)S(1)} %shard_map.163.column.own_column), channel_id=1, source_target_pairs={{0,8},{8,0},{16,24},{24,16},{1,9},{9,1},{17,25},{25,17},{2,10},{10... | collective-permute-start | bytes 73736 | tf_op jit(solution)/shard_map/ppermute | solution.py:94
  35.9 5.9 %collective-permute-start.6 = (bf16[144,128]{1,0:T(8,128)(2,1)S(1)}, bf16[144,128]{1,0:T(8,128)(2,1)S(1)}, u32[]{:S(2)}, u32[]{:S(2)}) collective-permute-start(bf16[144,128]{1,0:T(8,128)(2,1)S(1)} %get-tuple-element.70.refs_0_), channel_id=1, source_target_pairs={{0,6},{2,4},{4,2},{6,0},{1,7},{3,5},{5,3},{7,1},{8,14},{10,12},{12... | collective-permute-start | bytes 110600 | tf_op jit(solution)/shard_map/ppermute | solution.py:653
  38.3 4.9 %collective-permute-start.5 = (bf16[144,128]{1,0:T(8,128)(2,1)S(1)}, bf16[144,128]{1,0:T(8,128)(2,1)S(1)}, u32[]{:S(2)}, u32[]{:S(2)}) collective-permute-start(bf16[144,128]{1,0:T(8,128)(2,1)S(1)} %get-tuple-element.70.refs_0_), channel_id=1, source_target_pairs={{0,4},{2,6},{4,0},{6,2},{1,5},{3,7},{5,1},{7,3},{8,12},{10,14},{12... | collective-permute-start | bytes 110600 | tf_op jit(solution)/shard_map/ppermute | solution.py:653
  39.0 4.4 %collective-permute-start.4 = (bf16[144,128]{1,0:T(8,128)(2,1)S(1)}, bf16[144,128]{1,0:T(8,128)(2,1)S(1)}, u32[]{:S(2)}, u32[]{:S(2)}) collective-permute-start(bf16[144,128]{1,0:T(8,128)(2,1)S(1)} %get-tuple-element.70.refs_0_), channel_id=1, source_target_pairs={{0,2},{2,0},{4,6},{6,4},{1,3},{3,1},{5,7},{7,5},{8,10},{10,8},{12,... | collective-permute-start | bytes 110600 | tf_op jit(solution)/shard_map/ppermute | solution.py:653

commit v17 on v15

--- a/solution.py
+++ b/solution.py
@@ -155,8 +155,8 @@
     tables[count_p:] = w_edge_in[2 * width :]
     line = lax.broadcasted_iota(jnp.int32, (8, chunk), 0)
 
-    def one(step, carry):
-        rows = pl.ds(pl.multiple_of(step * chunk, chunk), chunk)
+    def one(step):
+        rows = slice(step * chunk, (step + 1) * chunk)
         sender = jnp.broadcast_to(senders[step], (8, chunk))
         receiver = jnp.broadcast_to(receivers[step], (8, chunk))
         owner = lax.shift_right_logical(sender, place_bits)
@@ -171,20 +171,24 @@
         index = jnp.where(line == 2, jnp.where(near, spot, -1 - spot), index)
         info[step] = index
         columns = index.T
-        for copy in fetch(step):
-            copy.wait()
         edge = edges[rows]
         cot = edge_cot[rows].astype(F32)
         recv = jnp.broadcast_to(columns[:, 1:2], edge.shape).astype(F32).astype(BF16)
         recv_codes[rows] = recv
         send_codes[rows] = jnp.broadcast_to(columns[:, 2:3], edge.shape).astype(F32).astype(BF16)
         recv = found(recv, count_p // width)
-        pre_part[rows] = mm(jnp.concatenate([recv, edge], axis=1), tables[...])
         edges_t[step] = edge.T
         cot_part[rows] = (cot - jnp.mean(cot, axis=1, keepdims=True)).astype(BF16)
-        return carry
-
-    lax.fori_loop(0, chunks, one, 0, unroll=UNROLL)
+        return jnp.concatenate([recv, edge], axis=1)
+
+    group = 2 if chunks % 2 == 0 else 1
+    for first in range(0, chunks, group):
+        steps = range(first, first + group)
+        for step in steps:
+            for copy in fetch(step):
+                copy.wait()
+        left = jnp.concatenate([one(step) for step in steps], axis=0)
+        pre_part[first * chunk : (first + group) * chunk] = mm(left, tables[...])
 
 
 def prepare_kernel(
@@ -477,8 +481,8 @@
     message[share:] = total[share + border :].astype(BF16)
 
 
-def line_sum_kernel(factor, mine, *refs):
-    messages, (out, rim_grad, held) = refs[:-3], refs[-3:]
+def line_sum_kernel(factor, mine, first, *refs):
+    messages, (out, rim_grad, held) = (first, *refs[-4::-1]), refs[-3:]
     border = mine.shape[0]
     share = out.shape[1]
     for k, message in enumerate(messages):
@@ -655,7 +659,7 @@
     parts, rim_grad = call(
         functools.partial(line_sum_kernel, factor),
         [((slots, share, width), BF16), ((border, width), F32)],
-        [mine, *messages],
+        [mine, messages[0], *messages[:0:-1]],
         [VMEM] * (1 + zs),
         [pltpu.VMEM((zs, share + border, width), F32)],
     )

time: 52.7 us -> 54.1 us (1.027)
  waiting for transfers between devices: 2.89 us -> 4.03 us
    ppermute x3, waiting for transfers between devices: 2.88 us -> 4.02 us  [shards(): lax.ppermute(message, 'z', [(z, z ^ k) for z in range(zs)])]
  transfers between devices with their start and end apart: 7 -> 7, of which waited for: 3 -> 2; matrix products, arithmetic and copies ran while one was open for 0% -> 0% of each run, Pallas kernels for 9% -> 9%
where the time goes in v17:
time: 54.1 us; the launch traced here: 53.8 us
  blocking collectives  21.8 us (40%)
  Pallas kernels  13.9 us (26%)
  starting transfers between devices  12.6 us (23%)
  waiting for transfers between devices  4.03 us (7%)
  between operations  1.46 us (3%)
    all_to_all x2, blocking collectives, shards(): came = lax.all_to_all(parts, PLANE, 0, 0)  21.8 us
    pallas_call x7, Pallas kernels, call(): pl.pallas_call(kernel, out_shape=[pltpu.HBM(shape, dtype) if spec is HBM...  13.9 us
    ppermute x2, starting transfers between devices, swapped(): from_even = lax.ppermute(value, axes, even)  5.95 us
    ppermute x3, starting transfers between devices, shards(): lax.ppermute(message, 'z', [(z, z ^ k) for z in range(zs)])  4.45 us
    ppermute x3, waiting for transfers between devices, shards(): lax.ppermute(message, 'z', [(z, z ^ k) for z in range(zs)])  4.02 us
    ppermute x2, starting transfers between devices, swapped(): from_odd = lax.ppermute(value, axes, odd)  2.15 us
  transfers between devices with their start and end apart: 7, of which 2 were waited for; matrix products, arithmetic and copies ran while one was open for 0% of the time, Pallas kernels for 9%

profile of v17, /device:TPU:0, one launch (start us, length us, event | category | flops | bytes accessed | tf_op | source)
XLA Modules:
  0.0 53.8 jit_solution(13265346612485104128)
XLA Ops:
  0.6 0.0 copy-start
  0.6 0.0 copy-start.1
  0.7 3.0 %collective-permute-start.1 = (bf16[256,128]{1,0:T(8,128)(2,1)}, bf16[256,128]{1,0:T(8,128)(2,1)S(1)}, u32[]{:S(2)}, u32[]{:S(2)}) collective-permute-start(bf16[256,128]{1,0:T(8,128)(2,1)} %nodes.5), channel_id=1, source_target_pairs={{0,1},{1,0},{2,3},{3,2},{4,5},{5,4},{6,7},{7,6},{8,9},{9,8},{10,11... | collective-permute-start | bytes 196616 | tf_op jit(solution)/shard_map/ppermute | solution.py:94
  3.7 1.5 %collective-permute-start = (bf16[256,128]{1,0:T(8,128)(2,1)}, bf16[256,128]{1,0:T(8,128)(2,1)S(1)}, u32[]{:S(2)}, u32[]{:S(2)}) collective-permute-start(bf16[256,128]{1,0:T(8,128)(2,1)} %nodes.5), channel_id=1, source_target_pairs={{0,0},{1,2},{2,1},{3,4},{4,3},{5,6},{6,5},{7,7},{8,8},{9,10},{10,9... | collective-permute-start | bytes 196616 | tf_op jit(solution)/shard_map/ppermute | solution.py:93
  5.2 4.7 %shard_map.162 = (bf16[4096,128]{1,0:T(8,128)(2,1)S(1)}, bf16[4096,128]{1,0:T(8,128)(2,1)S(1)}, bf16[4096,128]{1,0:T(8,128)(2,1)S(1)}, bf16[4,128,1024]{2,1,0:T(...) custom-call(bf16[256,128]{1,0:T(8,128)(2,1)} %nodes.5, ...), custom_call_target="tpu_custom_call" | custom-call | tf_op jit(solution)/shard_map/pallas_call | solution.py:69
  9.9 0.0 collective-permute-done.1.even
  9.9 0.0 collective-permute-done.odd
  10.0 0.7 %collective-permute-start.3 = (bf16[96,128]{1,0:T(8,128)(2,1)S(1)}, bf16[96,128]{1,0:T(8,128)(2,1)S(1)}, u32[]{:S(2)}, u32[]{:S(2)}) collective-permute-start(bf16[96,128]{1,0:T(8,128)(2,1)S(1)} %shard_map.163.column.own_column), channel_id=1, source_target_pairs={{0,0},{8,16},{16,8},{24,24},{1,1},{9,17},{17,9},{25,25},{2,2},{10,... | collective-permute-start | bytes 73736 | tf_op jit(solution)/shard_map/ppermute | solution.py:93
  10.6 2.9 %collective-permute-start.2 = (bf16[96,128]{1,0:T(8,128)(2,1)S(1)}, bf16[96,128]{1,0:T(8,128)(2,1)S(1)}, u32[]{:S(2)}, u32[]{:S(2)}) collective-permute-start(bf16[96,128]{1,0:T(8,128)(2,1)S(1)} %shard_map.163.column.own_column), channel_id=1, source_target_pairs={{0,8},{8,0},{16,24},{24,16},{1,9},{9,1},{17,25},{25,17},{2,10},{10... | collective-permute-start | bytes 73736 | tf_op jit(solution)/shard_map/ppermute | solution.py:94
  14.3 0.2 shard_map.164
  14.4 0.0 collective-permute-done.3.odd_column
  14.4 0.0 collective-permute-done.2.even_column
  14.4 8.1 %shard_map.165 = (bf16[256,128]{1,0:T(8,128)(2,1)}, bf16[4096,128]{1,0:T(8,128)(2,1)}, f32[256,128]{1,0:T(8,128)S(1)}, bf16[8,176,128]{2,1,0:T(8,128)(2,1)S(1)}) custom-call(s32[1]{0:T(128)S(6)} %copy.18.edge_count, bf16[256,128]{1,0:T(8,128)(2,1)S(1)} %copy-done, bf16[96,128]{1,0:T(8,128)(2,1)S(1)} %shard_map.163.column.own_column, ...), custom_call_target="tpu_custom_call" | custom-call | tf_op jit(solution)/shard_map/pallas_call | solution.py:69
  22.6 13.7 %all_to_all.10.came = bf16[8,176,128]{2,1,0:T(8,128)(2,1)S(1)} all-to-all(bf16[8,176,128]{2,1,0:T(8,128)(2,1)S(1)} %get-tuple-element.68), channel_id=1, replica_groups=mesh['strip'=4,'z'=4,'y'=2] {'strip','y'}, dimensions={0} | all-to-all | bytes 720896 | tf_op jit(solution)/shard_map/all_to_all | solution.py:652
  36.3 0.1 shard_map.166
  36.4 1.6 %collective-permute-start.6 = (bf16[144,128]{1,0:T(8,128)(2,1)S(1)}, bf16[144,128]{1,0:T(8,128)(2,1)S(1)}, u32[]{:S(2)}, u32[]{:S(2)}) collective-permute-start(bf16[144,128]{1,0:T(8,128)(2,1)S(1)} %get-tuple-element.70.first), channel_id=1, source_target_pairs={{0,2},{2,0},{4,6},{6,4},{1,3},{3,1},{5,7},{7,5},{8,10},{10,8},{12,... | collective-permute-start | bytes 110600 | tf_op jit(solution)/shard_map/ppermute | solution.py:657
  38.0 1.1 %collective-permute-start.5 = (bf16[144,128]{1,0:T(8,128)(2,1)S(1)}, bf16[144,128]{1,0:T(8,128)(2,1)S(1)}, u32[]{:S(2)}, u32[]{:S(2)}) collective-permute-start(bf16[144,128]{1,0:T(8,128)(2,1)S(1)} %get-tuple-element.70.first), channel_id=1, source_target_pairs={{0,4},{2,6},{4,0},{6,2},{1,5},{3,7},{5,1},{7,3},{8,12},{10,14},{12... | collective-permute-start | bytes 110600 | tf_op jit(solution)/shard_map/ppermute | solution.py:657
  39.1 1.7 %collective-permute-start.4 = (bf16[144,128]{1,0:T(8,128)(2,1)S(1)}, bf16[144,128]{1,0:T(8,128)(2,1)S(1)}, u32[]{:S(2)}, u32[]{:S(2)}) collective-permute-start(bf16[144,128]{1,0:T(8,128)(2,1)S(1)} %get-tuple-element.70.first), channel_id=1, source_target_pairs={{0,6},{2,4},{4,2},{6,0},{1,7},{3,5},{5,3},{7,1},{8,14},{10,12},{12... | collective-permute-start | bytes 110600 | tf_op jit(solution)/shard_map/ppermute | solution.py:657
  40.8 0.0 collective-permute-done.6.refs_2_
  40.8 3.2 %collective-permute-done.5.refs_1_ = bf16[144,128]{1,0:T(8,128)(2,1)S(1)} collective-permute-done((bf16[144,128]{1,0:T(8,128)(2,1)S(1)}, bf16[144,128]{1,0:T(8,128)(2,1)S(1)}, u32[]{:S(2)}, u32[]{:S(2)}) %collective-permute-start.5) | collective-permute-done | bytes 36896 | tf_op jit(solution)/shard_map/ppermute | solution.py:657
  44.0 0.9 %collective-permute-done.4.refs_0_ = bf16[144,128]{1,0:T(8,128)(2,1)S(1)} collective-permute-done((bf16[144,128]{1,0:T(8,128)(2,1)S(1)}, bf16[144,128]{1,0:T(8,128)(2,1)S(1)}, u32[]{:S(2)}, u32[]{:S(2)}) %collective-permute-start.4) | collective-permute-done | bytes 36896 | tf_op jit(solution)/shard_map/ppermute | solution.py:657
  44.9 0.1 shard_map.167
  44.9 8.1 %all_to_all.11.came = bf16[8,112,128]{2,1,0:T(8,128)(2,1)S(1)} all-to-all(bf16[8,112,128]{2,1,0:T(8,128)(2,1)S(1)} %get-tuple-element.71), channel_id=1, replica_groups=mesh['strip'=4,'z'=4,'y'=2] {'strip','y'}, dimensions={0} | all-to-all | bytes 458752 | tf_op jit(solution)/shard_map/all_to_all | solution.py:666
  53.0 0.8 %shard_map.168 = (f32[256,128]{1,0:T(8,128)}, f32[384,128]{1,0:T(8,128)}, f32[128,128]{1,0:T(8,128)}, f32[256,128]{1,0:T(8,128)}, f32[128,128]{1,0:T(8,128)}) custom-call(bf16[8,112,128]{2,1,0:T(8,128)(2,1)S(1)} %all_to_all.11.came, f32[32,128]{1,0:T(8,128)S(1)} %get-tuple-element.72.rim_grad, f32[256,128]{1,0:T(8,128)S(1)} %get-tuple-element.73.local_grad), custom_call_target="tpu_custom_call" | custom-call | tf_op jit(solution)/shard_map/pallas_call | solution.py:69
  (11 shorter events, 0.0 us)
Async XLA Ops:
  0.6 9.3 %copy-start = (bf16[256,128]{1,0:T(8,128)(2,1)S(1)}, bf16[256,128]{1,0:T(8,128)(2,1)}, u32[]{:S(2)}) copy-start(bf16[256,128]{1,0:T(8,128)(2,1)} %nodes.5) | copy-start | bytes 196612
  0.6 13.6 %copy-start.1 = (bf16[384,128]{1,0:T(8,128)(2,1)S(1)}, bf16[384,128]{1,0:T(8,128)(2,1)}, u32[]{:S(2)}) copy-start(bf16[384,128]{1,0:T(8,128)(2,1)} %w_edge_in.3) | copy-start | bytes 294916
  0.7 13.6 %copy-start.3 = (bf16[256,128]{1,0:T(8,128)(2,1)S(1)}, bf16[256,128]{1,0:T(8,128)(2,1)}, u32[]{:S(2)}) copy-start(bf16[256,128]{1,0:T(8,128)(2,1)} %node_cot.3) | copy-start | bytes 196612
  0.7 13.6 %copy-start.5 = (bf16[128,128]{1,0:T(8,128)(2,1)S(1)}, bf16[128,128]{1,0:T(8,128)(2,1)}, u32[]{:S(2)}) copy-start(bf16[128,128]{1,0:T(8,128)(2,1)} %w_node_out.3) | copy-start | bytes 98308
  0.7 13.6 %copy-start.2 = (bf16[256,128]{1,0:T(8,128)(2,1)S(1)}, bf16[256,128]{1,0:T(8,128)(2,1)}, u32[]{:S(2)}) copy-start(bf16[256,128]{1,0:T(8,128)(2,1)} %w_node_in.3) | copy-start | bytes 196612
  0.7 13.6 %copy-start.4 = (bf16[128,128]{1,0:T(8,128)(2,1)S(1)}, bf16[128,128]{1,0:T(8,128)(2,1)}, u32[]{:S(2)}) copy-start(bf16[128,128]{1,0:T(8,128)(2,1)} %w_edge_out.3) | copy-start | bytes 98308
  0.7 9.2 %collective-permute-start.1 = (bf16[256,128]{1,0:T(8,128)(2,1)}, bf16[256,128]{1,0:T(8,128)(2,1)S(1)}, u32[]{:S(2)}, u32[]{:S(2)}) collective-permute-start(bf16[256,128]{1,0:T(8,128)(2,1)} %nodes.5), channel_id=1, source_target_pairs={{0,1},{1,0},{2,3},{3,2},{4,5},{5,4},{6,7},{7,6},{8,9},{9,8},{10,11... | collective-permute-start | bytes 196616 | tf_op jit(solution)/shard_map/ppermute | solution.py:94
  3.7 6.2 %collective-permute-start = (bf16[256,128]{1,0:T(8,128)(2,1)}, bf16[256,128]{1,0:T(8,128)(2,1)S(1)}, u32[]{:S(2)}, u32[]{:S(2)}) collective-permute-start(bf16[256,128]{1,0:T(8,128)(2,1)} %nodes.5), channel_id=1, source_target_pairs={{0,0},{1,2},{2,1},{3,4},{4,3},{5,6},{6,5},{7,7},{8,8},{9,10},{10,9... | collective-permute-start | bytes 196616 | tf_op jit(solution)/shard_map/ppermute | solution.py:93
  10.0 4.5 %collective-permute-start.3 = (bf16[96,128]{1,0:T(8,128)(2,1)S(1)}, bf16[96,128]{1,0:T(8,128)(2,1)S(1)}, u32[]{:S(2)}, u32[]{:S(2)}) collective-permute-start(bf16[96,128]{1,0:T(8,128)(2,1)S(1)} %shard_map.163.column.own_column), channel_id=1, source_target_pairs={{0,0},{8,16},{16,8},{24,24},{1,1},{9,17},{17,9},{25,25},{2,2},{10,... | collective-permute-start | bytes 73736 | tf_op jit(solution)/shard_map/ppermute | solution.py:93
  10.6 3.8 %collective-permute-start.2 = (bf16[96,128]{1,0:T(8,128)(2,1)S(1)}, bf16[96,128]{1,0:T(8,128)(2,1)S(1)}, u32[]{:S(2)}, u32[]{:S(2)}) collective-permute-start(bf16[96,128]{1,0:T(8,128)(2,1)S(1)} %shard_map.163.column.own_column), channel_id=1, source_target_pairs={{0,8},{8,0},{16,24},{24,16},{1,9},{9,1},{17,25},{25,17},{2,10},{10... | collective-permute-start | bytes 73736 | tf_op jit(solution)/shard_map/ppermute | solution.py:94
  36.4 4.5 %collective-permute-start.6 = (bf16[144,128]{1,0:T(8,128)(2,1)S(1)}, bf16[144,128]{1,0:T(8,128)(2,1)S(1)}, u32[]{:S(2)}, u32[]{:S(2)}) collective-permute-start(bf16[144,128]{1,0:T(8,128)(2,1)S(1)} %get-tuple-element.70.first), channel_id=1, source_target_pairs={{0,2},{2,0},{4,6},{6,4},{1,3},{3,1},{5,7},{7,5},{8,10},{10,8},{12,... | collective-permute-start | bytes 110600 | tf_op jit(solution)/shard_map/ppermute | solution.py:657
  38.0 6.0 %collective-permute-start.5 = (bf16[144,128]{1,0:T(8,128)(2,1)S(1)}, bf16[144,128]{1,0:T(8,128)(2,1)S(1)}, u32[]{:S(2)}, u32[]{:S(2)}) collective-permute-start(bf16[144,128]{1,0:T(8,128)(2,1)S(1)} %get-tuple-element.70.first), channel_id=1, source_target_pairs={{0,4},{2,6},{4,0},{6,2},{1,5},{3,7},{5,1},{7,3},{8,12},{10,14},{12... | collective-permute-start | bytes 110600 | tf_op jit(solution)/shard_map/ppermute | solution.py:657
  39.1 5.8 %collective-permute-start.4 = (bf16[144,128]{1,0:T(8,128)(2,1)S(1)}, bf16[144,128]{1,0:T(8,128)(2,1)S(1)}, u32[]{:S(2)}, u32[]{:S(2)}) collective-permute-start(bf16[144,128]{1,0:T(8,128)(2,1)S(1)} %get-tuple-element.70.first), channel_id=1, source_target_pairs={{0,6},{2,4},{4,2},{6,0},{1,7},{3,5},{5,3},{7,1},{8,14},{10,12},{12... | collective-permute-start | bytes 110600 | tf_op jit(solution)/shard_map/ppermute | solution.py:657

commit v18 on v15

--- a/solution.py
+++ b/solution.py
@@ -119,7 +119,9 @@
     sems,
 ):
     count_p, width = nodes_in.shape
-    chunks, _, chunk = info.shape
+    pieces, _, piece = info.shape
+    chunks, _, chunk = senders_in.shape
+    group = chunk // piece
     border = count_p // 8
     my_strip = lax.axis_index("strip")
     subs = lax.axis_size("z") * lax.axis_size("y")
@@ -169,7 +171,8 @@
         spot = jnp.where(near, within, spot * border + jnp.minimum(within, border - 1))
         index = jnp.where(line == 0, spot, receiver)
         index = jnp.where(line == 2, jnp.where(near, spot, -1 - spot), index)
-        info[step] = index
+        for part in range(group):
+            info[step * group + part] = index[:, part * piece : (part + 1) * piece]
         columns = index.T
         for copy in fetch(step):
             copy.wait()
@@ -180,11 +183,12 @@
         send_codes[rows] = jnp.broadcast_to(columns[:, 2:3], edge.shape).astype(F32).astype(BF16)
         recv = found(recv, count_p // width)
         pre_part[rows] = mm(jnp.concatenate([recv, edge], axis=1), tables[...])
-        edges_t[step] = edge.T
+        for part in range(group):
+            edges_t[step * group + part] = edge[part * piece : (part + 1) * piece].T
         cot_part[rows] = (cot - jnp.mean(cot, axis=1, keepdims=True)).astype(BF16)
         return carry
 
-    lax.fori_loop(0, chunks, one, 0, unroll=UNROLL)
+    lax.fori_loop(0, chunks, one, 0, unroll=chunks)
 
 
 def prepare_kernel(
@@ -535,6 +539,7 @@
     even, odd = swapped(node_latents, ("z", "y"))
     chunk = min(CHUNK, count_e)
     chunks = count_e // chunk
+    steps = chunks // 2 if chunks % 2 == 0 else chunks
     early = call(
         early_kernel,
         [
@@ -550,8 +555,8 @@
             node_latents,
             edge_latents,
             edge_cotangent,
-            senders.reshape(chunks, 1, chunk),
-            receivers.reshape(chunks, 1, chunk),
+            senders.reshape(steps, 1, count_e // steps),
+            receivers.reshape(steps, 1, count_e // steps),
             w_edge_in,
         ],
         [HBM] * 6,
@@ -559,11 +564,11 @@
             pltpu.VMEM((count_p + width, width), BF16),
             pltpu.VMEM((count_p, width), BF16),
             pltpu.VMEM((count_e, width), BF16),
-            pltpu.VMEM((chunks, 1, chunk), jnp.int32),
-            pltpu.VMEM((chunks, 1, chunk), jnp.int32),
+            pltpu.VMEM((steps, 1, count_e // steps), jnp.int32),
+            pltpu.VMEM((steps, 1, count_e // steps), jnp.int32),
             pltpu.VMEM((3 * width, width), BF16),
             SEM((4,)),
-            SEM((2, chunks)),
+            SEM((2, steps)),
         ],
     )
 

time: 52.7 us -> 52.5 us (level)
  transfers between devices with their start and end apart: 7 -> 7, of which waited for: 3 -> 3; matrix products, arithmetic and copies ran while one was open for 0% -> 0% of each run, Pallas kernels for 9% -> 8%
where the time goes in v18:
time: 52.5 us; the launch traced here: 52.2 us
  blocking collectives  21.8 us (42%)
  Pallas kernels  13.4 us (26%)
  starting transfers between devices  12.6 us (24%)
  waiting for transfers between devices  3.01 us (6%)
  between operations  1.46 us (3%)
    all_to_all x2, blocking collectives, shards(): came = lax.all_to_all(parts, PLANE, 0, 0)  21.8 us
    pallas_call x7, Pallas kernels, call(): pl.pallas_call(kernel, out_shape=[pltpu.HBM(shape, dtype) if spec is HBM...  13.4 us
    ppermute x2, starting transfers between devices, swapped(): from_even = lax.ppermute(value, axes, even)  5.95 us
    ppermute x3, starting transfers between devices, shards(): lax.ppermute(message, 'z', [(z, z ^ k) for z in range(zs)])  4.45 us
    ppermute x3, waiting for transfers between devices, shards(): lax.ppermute(message, 'z', [(z, z ^ k) for z in range(zs)])  3 us
    ppermute x2, starting transfers between devices, swapped(): from_odd = lax.ppermute(value, axes, odd)  2.15 us
  transfers between devices with their start and end apart: 7, of which 3 were waited for; matrix products, arithmetic and copies ran while one was open for 0% of the time, Pallas kernels for 8%

profile of v18, /device:TPU:0, one launch (start us, length us, event | category | flops | bytes accessed | tf_op | source)
XLA Modules:
  0.0 52.2 jit_solution(14110847971967408323)
XLA Ops:
  0.6 0.0 copy-start
  0.6 0.0 copy-start.1
  0.7 3.0 %collective-permute-start.1 = (bf16[256,128]{1,0:T(8,128)(2,1)}, bf16[256,128]{1,0:T(8,128)(2,1)S(1)}, u32[]{:S(2)}, u32[]{:S(2)}) collective-permute-start(bf16[256,128]{1,0:T(8,128)(2,1)} %nodes.5), channel_id=1, source_target_pairs={{0,1},{1,0},{2,3},{3,2},{4,5},{5,4},{6,7},{7,6},{8,9},{9,8},{10,11... | collective-permute-start | bytes 196616 | tf_op jit(solution)/shard_map/ppermute | solution.py:94
  3.7 1.5 %collective-permute-start = (bf16[256,128]{1,0:T(8,128)(2,1)}, bf16[256,128]{1,0:T(8,128)(2,1)S(1)}, u32[]{:S(2)}, u32[]{:S(2)}) collective-permute-start(bf16[256,128]{1,0:T(8,128)(2,1)} %nodes.5), channel_id=1, source_target_pairs={{0,0},{1,2},{2,1},{3,4},{4,3},{5,6},{6,5},{7,7},{8,8},{9,10},{10,9... | collective-permute-start | bytes 196616 | tf_op jit(solution)/shard_map/ppermute | solution.py:93
  5.2 4.1 %shard_map.162 = (bf16[4096,128]{1,0:T(8,128)(2,1)S(1)}, bf16[4096,128]{1,0:T(8,128)(2,1)S(1)}, bf16[4096,128]{1,0:T(8,128)(2,1)S(1)}, bf16[4,128,1024]{2,1,0:T(...) custom-call(bf16[256,128]{1,0:T(8,128)(2,1)} %nodes.5, ...), custom_call_target="tpu_custom_call" | custom-call | tf_op jit(solution)/shard_map/pallas_call | solution.py:69
  9.4 0.0 collective-permute-done.1.even
  9.4 0.0 collective-permute-done.odd
  9.4 0.7 %collective-permute-start.3 = (bf16[96,128]{1,0:T(8,128)(2,1)S(1)}, bf16[96,128]{1,0:T(8,128)(2,1)S(1)}, u32[]{:S(2)}, u32[]{:S(2)}) collective-permute-start(bf16[96,128]{1,0:T(8,128)(2,1)S(1)} %shard_map.163.column.own_column), channel_id=1, source_target_pairs={{0,0},{8,16},{16,8},{24,24},{1,1},{9,17},{17,9},{25,25},{2,2},{10,... | collective-permute-start | bytes 73736 | tf_op jit(solution)/shard_map/ppermute | solution.py:93
  10.1 2.9 %collective-permute-start.2 = (bf16[96,128]{1,0:T(8,128)(2,1)S(1)}, bf16[96,128]{1,0:T(8,128)(2,1)S(1)}, u32[]{:S(2)}, u32[]{:S(2)}) collective-permute-start(bf16[96,128]{1,0:T(8,128)(2,1)S(1)} %shard_map.163.column.own_column), channel_id=1, source_target_pairs={{0,8},{8,0},{16,24},{24,16},{1,9},{9,1},{17,25},{25,17},{2,10},{10... | collective-permute-start | bytes 73736 | tf_op jit(solution)/shard_map/ppermute | solution.py:94
  13.7 0.2 shard_map.164
  13.9 0.0 collective-permute-done.3.odd_column
  13.9 0.0 collective-permute-done.2.even_column
  13.9 8.1 %shard_map.165 = (bf16[256,128]{1,0:T(8,128)(2,1)}, bf16[4096,128]{1,0:T(8,128)(2,1)}, f32[256,128]{1,0:T(8,128)S(1)}, bf16[8,176,128]{2,1,0:T(8,128)(2,1)S(1)}) custom-call(s32[1]{0:T(128)S(6)} %copy.18.edge_count, bf16[256,128]{1,0:T(8,128)(2,1)S(1)} %copy-done, bf16[96,128]{1,0:T(8,128)(2,1)S(1)} %shard_map.163.column.own_column, ...), custom_call_target="tpu_custom_call" | custom-call | tf_op jit(solution)/shard_map/pallas_call | solution.py:69
  22.0 13.7 %all_to_all.10.came = bf16[8,176,128]{2,1,0:T(8,128)(2,1)S(1)} all-to-all(bf16[8,176,128]{2,1,0:T(8,128)(2,1)S(1)} %get-tuple-element.68), channel_id=1, replica_groups=mesh['strip'=4,'z'=4,'y'=2] {'strip','y'}, dimensions={0} | all-to-all | bytes 720896 | tf_op jit(solution)/shard_map/all_to_all | solution.py:653
  35.8 0.1 shard_map.166
  35.8 2.3 %collective-permute-start.6 = (bf16[144,128]{1,0:T(8,128)(2,1)S(1)}, bf16[144,128]{1,0:T(8,128)(2,1)S(1)}, u32[]{:S(2)}, u32[]{:S(2)}) collective-permute-start(bf16[144,128]{1,0:T(8,128)(2,1)S(1)} %get-tuple-element.70.refs_0_), channel_id=1, source_target_pairs={{0,6},{2,4},{4,2},{6,0},{1,7},{3,5},{5,3},{7,1},{8,14},{10,12},{12... | collective-permute-start | bytes 110600 | tf_op jit(solution)/shard_map/ppermute | solution.py:658
  38.2 0.8 %collective-permute-start.5 = (bf16[144,128]{1,0:T(8,128)(2,1)S(1)}, bf16[144,128]{1,0:T(8,128)(2,1)S(1)}, u32[]{:S(2)}, u32[]{:S(2)}) collective-permute-start(bf16[144,128]{1,0:T(8,128)(2,1)S(1)} %get-tuple-element.70.refs_0_), channel_id=1, source_target_pairs={{0,4},{2,6},{4,0},{6,2},{1,5},{3,7},{5,1},{7,3},{8,12},{10,14},{12... | collective-permute-start | bytes 110600 | tf_op jit(solution)/shard_map/ppermute | solution.py:658
  38.9 1.3 %collective-permute-start.4 = (bf16[144,128]{1,0:T(8,128)(2,1)S(1)}, bf16[144,128]{1,0:T(8,128)(2,1)S(1)}, u32[]{:S(2)}, u32[]{:S(2)}) collective-permute-start(bf16[144,128]{1,0:T(8,128)(2,1)S(1)} %get-tuple-element.70.refs_0_), channel_id=1, source_target_pairs={{0,2},{2,0},{4,6},{6,4},{1,3},{3,1},{5,7},{7,5},{8,10},{10,8},{12,... | collective-permute-start | bytes 110600 | tf_op jit(solution)/shard_map/ppermute | solution.py:658
  40.3 1.5 %collective-permute-done.6.refs_3_ = bf16[144,128]{1,0:T(8,128)(2,1)S(1)} collective-permute-done((bf16[144,128]{1,0:T(8,128)(2,1)S(1)}, bf16[144,128]{1,0:T(8,128)(2,1)S(1)}, u32[]{:S(2)}, u32[]{:S(2)}) %collective-permute-start.6) | collective-permute-done | bytes 36896 | tf_op jit(solution)/shard_map/ppermute | solution.py:658
  41.7 1.4 %collective-permute-done.5.refs_2_ = bf16[144,128]{1,0:T(8,128)(2,1)S(1)} collective-permute-done((bf16[144,128]{1,0:T(8,128)(2,1)S(1)}, bf16[144,128]{1,0:T(8,128)(2,1)S(1)}, u32[]{:S(2)}, u32[]{:S(2)}) %collective-permute-start.5) | collective-permute-done | bytes 36896 | tf_op jit(solution)/shard_map/ppermute | solution.py:658
  43.1 0.2 collective-permute-done.4.refs_1_
  43.3 0.1 shard_map.167
  43.3 8.1 %all_to_all.11.came = bf16[8,112,128]{2,1,0:T(8,128)(2,1)S(1)} all-to-all(bf16[8,112,128]{2,1,0:T(8,128)(2,1)S(1)} %get-tuple-element.71), channel_id=1, replica_groups=mesh['strip'=4,'z'=4,'y'=2] {'strip','y'}, dimensions={0} | all-to-all | bytes 458752 | tf_op jit(solution)/shard_map/all_to_all | solution.py:667
  51.4 0.8 %shard_map.168 = (f32[256,128]{1,0:T(8,128)}, f32[384,128]{1,0:T(8,128)}, f32[128,128]{1,0:T(8,128)}, f32[256,128]{1,0:T(8,128)}, f32[128,128]{1,0:T(8,128)}) custom-call(bf16[8,112,128]{2,1,0:T(8,128)(2,1)S(1)} %all_to_all.11.came, f32[32,128]{1,0:T(8,128)S(1)} %get-tuple-element.72.rim_grad, f32[256,128]{1,0:T(8,128)S(1)} %get-tuple-element.73.local_grad), custom_call_target="tpu_custom_call" | custom-call | tf_op jit(solution)/shard_map/pallas_call | solution.py:69
  (11 shorter events, 0.0 us)
Async XLA Ops:
  0.6 8.7 %copy-start = (bf16[256,128]{1,0:T(8,128)(2,1)S(1)}, bf16[256,128]{1,0:T(8,128)(2,1)}, u32[]{:S(2)}) copy-start(bf16[256,128]{1,0:T(8,128)(2,1)} %nodes.5) | copy-start | bytes 196612
  0.6 13.0 %copy-start.1 = (bf16[384,128]{1,0:T(8,128)(2,1)S(1)}, bf16[384,128]{1,0:T(8,128)(2,1)}, u32[]{:S(2)}) copy-start(bf16[384,128]{1,0:T(8,128)(2,1)} %w_edge_in.3) | copy-start | bytes 294916
  0.7 13.0 %copy-start.3 = (bf16[256,128]{1,0:T(8,128)(2,1)S(1)}, bf16[256,128]{1,0:T(8,128)(2,1)}, u32[]{:S(2)}) copy-start(bf16[256,128]{1,0:T(8,128)(2,1)} %node_cot.3) | copy-start | bytes 196612
  0.7 13.0 %copy-start.5 = (bf16[128,128]{1,0:T(8,128)(2,1)S(1)}, bf16[128,128]{1,0:T(8,128)(2,1)}, u32[]{:S(2)}) copy-start(bf16[128,128]{1,0:T(8,128)(2,1)} %w_node_out.3) | copy-start | bytes 98308
  0.7 13.0 %copy-start.2 = (bf16[256,128]{1,0:T(8,128)(2,1)S(1)}, bf16[256,128]{1,0:T(8,128)(2,1)}, u32[]{:S(2)}) copy-start(bf16[256,128]{1,0:T(8,128)(2,1)} %w_node_in.3) | copy-start | bytes 196612
  0.7 13.0 %copy-start.4 = (bf16[128,128]{1,0:T(8,128)(2,1)S(1)}, bf16[128,128]{1,0:T(8,128)(2,1)}, u32[]{:S(2)}) copy-start(bf16[128,128]{1,0:T(8,128)(2,1)} %w_edge_out.3) | copy-start | bytes 98308
  0.7 8.7 %collective-permute-start.1 = (bf16[256,128]{1,0:T(8,128)(2,1)}, bf16[256,128]{1,0:T(8,128)(2,1)S(1)}, u32[]{:S(2)}, u32[]{:S(2)}) collective-permute-start(bf16[256,128]{1,0:T(8,128)(2,1)} %nodes.5), channel_id=1, source_target_pairs={{0,1},{1,0},{2,3},{3,2},{4,5},{5,4},{6,7},{7,6},{8,9},{9,8},{10,11... | collective-permute-start | bytes 196616 | tf_op jit(solution)/shard_map/ppermute | solution.py:94
  3.7 5.6 %collective-permute-start = (bf16[256,128]{1,0:T(8,128)(2,1)}, bf16[256,128]{1,0:T(8,128)(2,1)S(1)}, u32[]{:S(2)}, u32[]{:S(2)}) collective-permute-start(bf16[256,128]{1,0:T(8,128)(2,1)} %nodes.5), channel_id=1, source_target_pairs={{0,0},{1,2},{2,1},{3,4},{4,3},{5,6},{6,5},{7,7},{8,8},{9,10},{10,9... | collective-permute-start | bytes 196616 | tf_op jit(solution)/shard_map/ppermute | solution.py:93
  9.4 4.5 %collective-permute-start.3 = (bf16[96,128]{1,0:T(8,128)(2,1)S(1)}, bf16[96,128]{1,0:T(8,128)(2,1)S(1)}, u32[]{:S(2)}, u32[]{:S(2)}) collective-permute-start(bf16[96,128]{1,0:T(8,128)(2,1)S(1)} %shard_map.163.column.own_column), channel_id=1, source_target_pairs={{0,0},{8,16},{16,8},{24,24},{1,1},{9,17},{17,9},{25,25},{2,2},{10,... | collective-permute-start | bytes 73736 | tf_op jit(solution)/shard_map/ppermute | solution.py:93
  10.1 3.8 %collective-permute-start.2 = (bf16[96,128]{1,0:T(8,128)(2,1)S(1)}, bf16[96,128]{1,0:T(8,128)(2,1)S(1)}, u32[]{:S(2)}, u32[]{:S(2)}) collective-permute-start(bf16[96,128]{1,0:T(8,128)(2,1)S(1)} %shard_map.163.column.own_column), channel_id=1, source_target_pairs={{0,8},{8,0},{16,24},{24,16},{1,9},{9,1},{17,25},{25,17},{2,10},{10... | collective-permute-start | bytes 73736 | tf_op jit(solution)/shard_map/ppermute | solution.py:94
  35.8 5.9 %collective-permute-start.6 = (bf16[144,128]{1,0:T(8,128)(2,1)S(1)}, bf16[144,128]{1,0:T(8,128)(2,1)S(1)}, u32[]{:S(2)}, u32[]{:S(2)}) collective-permute-start(bf16[144,128]{1,0:T(8,128)(2,1)S(1)} %get-tuple-element.70.refs_0_), channel_id=1, source_target_pairs={{0,6},{2,4},{4,2},{6,0},{1,7},{3,5},{5,3},{7,1},{8,14},{10,12},{12... | collective-permute-start | bytes 110600 | tf_op jit(solution)/shard_map/ppermute | solution.py:658
  38.2 4.9 %collective-permute-start.5 = (bf16[144,128]{1,0:T(8,128)(2,1)S(1)}, bf16[144,128]{1,0:T(8,128)(2,1)S(1)}, u32[]{:S(2)}, u32[]{:S(2)}) collective-permute-start(bf16[144,128]{1,0:T(8,128)(2,1)S(1)} %get-tuple-element.70.refs_0_), channel_id=1, source_target_pairs={{0,4},{2,6},{4,0},{6,2},{1,5},{3,7},{5,1},{7,3},{8,12},{10,14},{12... | collective-permute-start | bytes 110600 | tf_op jit(solution)/shard_map/ppermute | solution.py:658
  38.9 4.4 %collective-permute-start.4 = (bf16[144,128]{1,0:T(8,128)(2,1)S(1)}, bf16[144,128]{1,0:T(8,128)(2,1)S(1)}, u32[]{:S(2)}, u32[]{:S(2)}) collective-permute-start(bf16[144,128]{1,0:T(8,128)(2,1)S(1)} %get-tuple-element.70.refs_0_), channel_id=1, source_target_pairs={{0,2},{2,0},{4,6},{6,4},{1,3},{3,1},{5,7},{7,5},{8,10},{10,8},{12,... | collective-permute-start | bytes 110600 | tf_op jit(solution)/shard_map/ppermute | solution.py:658
